TPU v7x, 32 devices: a whole 2x2x4 slice. The times are simulated.
32 devices in a mesh: width: 4 (over y, x), seq: 8 (over z, core).
Axes of the slice: x: 2, y: 2, z: 4, core: 2. Of those that a mesh axis runs over, the one named last changes fastest.
Arguments:
- tokens: bfloat16 [8192, 2048], P(('width', 'seq')), may hold values from -6 to 6
- cotangent: bfloat16 [8192, 2048], P(('width', 'seq')), may hold values from -6 to 6
- starts: int32 [32, 2], P(('width', 'seq')), may hold values from 0 to 1, as said below
- valid: int32 [32, 2], P(('width', 'seq')), may hold values from 1 to 128, as said below
- norm_gain: float32 [2048], replicated, may hold values from 0.5 to 1.5
- w_zx: bfloat16 [2048, 8192], P('seq'), may hold values from -0.125 to 0.125
- w_bc: bfloat16 [2048, 256], P('seq'), may hold values from -0.125 to 0.125
- w_dt: bfloat16 [2048, 64], P('seq'), may hold values from -0.125 to 0.125
- conv_w: float32 [4352, 4], replicated, may hold values from -3 to 3
- conv_b: float32 [4352], replicated, may hold values from -3 to 3
- dt_bias: float32 [64], replicated, may hold values from -2 to 0.5
- a_log: float32 [64], replicated
- d_skip: float32 [64], replicated, may hold values from 0.5 to 1.5
- gate_gain: float32 [4096], replicated, may hold values from 0.5 to 1.5
- w_out: bfloat16 [4096, 2048], P('seq'), may hold values from -0.125 to 0.125
Outputs:
- output: bfloat16 [8192, 2048], P(('width', 'seq'))
- input_grad: float32 [8192, 2048], P(('width', 'seq'))
- grad_norm_gain: float32 [2048], P('seq')
- grad_w_zx: float32 [2048, 8192], P('seq')
- grad_w_bc: float32 [2048, 256], P('seq')
- grad_w_dt: float32 [2048, 64], P('seq')
- grad_conv_w: float32 [4352, 4], P('seq')
- grad_conv_b: float32 [4352], P('seq')
- grad_dt_bias: float32 [64], P('seq')
- grad_a_log: float32 [64], P('seq')
- grad_d_skip: float32 [64], P('seq')
- grad_gate_gain: float32 [4096], P('seq')
- grad_w_out: float32 [4096, 2048], P('seq')
Inputs may be any that keep to these rules, and one draw needn't show every extreme that they name: `starts`: block 0 of every lane begins a sequence; in each group one lane holds a single sequence over all 8 blocks; in the other lanes no sequence spans more than 4 blocks and one spans exactly 4. `valid`: below 128 only in a block after which a new sequence begins or the lane ends.
All inputs are finite; a program needn't handle non-finite values.
Results may differ from a plain program's by a relative error of at most 0.012.
The roundings to bfloat16 on the way count: a program that leaves them out, or rounds other values in their place, can miss the bound.
Values may be sent and summed in bfloat16 or wider, within the bound.
A program may use at most 576 MiB of HBM per device.

v0:
```python
from functools import partial

import jax
import jax.numpy as jnp
from jax import lax
from jax.sharding import PartitionSpec as P

H = 64
HEAD_DIM = 64
N = 128
KCONV = 4
BLOCK = 128
E = 4096


epsilon = 1e-05
highest = lax.Precision.HIGHEST


def passed_along(array, axis, by):
    peers = lax.axis_size(axis)
    pairs = [(i, i + by) for i in range(peers) if 0 <= i + by < peers]
    return lax.ppermute(array, axis, pairs)


def carried_in(part, axis, combine, identity, reverse):
    count = lax.axis_size(axis)
    place = lax.axis_index(axis)
    ahead = count - 1 - place if reverse else place
    gathered = jax.tree.map(lambda a: lax.all_gather(a, axis), part)
    state = jax.tree.map(lambda a, e: jnp.zeros_like(a) + jnp.asarray(e, a.dtype), part, identity)

    def one(lap, state):
        source = count - 1 - lap if reverse else lap
        return combine(
            state, jax.tree.map(lambda a: lax.dynamic_index_in_dim(a, source, 0, False), gathered)
        )

    return lax.fori_loop(0, ahead, one, state)


def round_value(v):
    return lax.optimization_barrier(v.astype(jnp.bfloat16)).astype(jnp.float32)


def keep_round(v):
    return (round_value(v), None)


def pass_grad(kept, grad):
    return (grad,)


def same_value(v):
    return v


def keep_same(v):
    return (v, None)


def round_grad(kept, grad):
    return (round_value(grad),)


def low(v):
    wrapped = jax.custom_vjp(round_value)
    wrapped.defvjp(keep_round, pass_grad)
    return wrapped(v)


def low_back(v):
    wrapped = jax.custom_vjp(same_value)
    wrapped.defvjp(keep_same, round_grad)
    return wrapped(v)


def rms_front(x_rows, norm_gain):
    mean_square = jnp.mean(x_rows * x_rows, axis=-1, keepdims=True)
    return x_rows * lax.rsqrt(mean_square + epsilon) * norm_gain


def rim_of(zx_pre, bc_pre, chan_mask):
    return jnp.concatenate(
        [zx_pre[:, BLOCK - KCONV + 1 :, E:] * chan_mask, bc_pre[:, BLOCK - KCONV + 1 :, :]], axis=-1
    )


def piece_front(
    zx_pre,
    bc_pre,
    dt_raw,
    rim_rows,
    conv_w,
    conv_b,
    dt_bias,
    a_log,
    chan_mask,
    head_mask,
    keep_rows,
):
    z_gate = zx_pre[..., :E] * chan_mask
    pre_conv = jnp.concatenate([zx_pre[..., E:] * chan_mask, bc_pre], axis=-1)
    padded = jnp.concatenate([rim_rows * keep_rows[:, None, None], pre_conv], axis=1)
    conv_out = conv_b + padded[:, 0:BLOCK, :] * conv_w[:, 0]
    for offset in range(1, KCONV):
        conv_out = conv_out + padded[:, offset : offset + BLOCK, :] * conv_w[:, offset]
    active = jax.nn.silu(conv_out)
    x_conv = low(active[..., :E] * chan_mask)
    b_conv = low(active[..., E : E + N])
    c_conv = low(active[..., E + N :])
    dt_step = jax.nn.softplus(dt_raw + dt_bias) * head_mask
    log_step = -jnp.exp(a_log) * dt_step
    return (z_gate, x_conv, b_conv, c_conv, dt_step, log_step)


def block_state(x_conv, b_conv, dt_step, log_step):
    cumulative = jnp.cumsum(log_step, axis=1)
    to_end = jnp.exp(cumulative[:, -1:, :] - cumulative) * dt_step
    weighted = low(x_conv.reshape(x_conv.shape[0], BLOCK, H, HEAD_DIM) * to_end[..., None])
    state_sum = jnp.einsum("lqhp,lqn->lhpn", weighted, b_conv, precision=highest)
    return (state_sum, cumulative[:, -1, :])


def piece_mix(
    z_gate, x_conv, b_conv, c_conv, dt_step, log_step, state_in, d_skip, gate_gain, chan_count
):
    lane_count = x_conv.shape[0]
    cumulative = jnp.cumsum(log_step, axis=1)
    cum_heads = jnp.swapaxes(cumulative, 1, 2)
    causal = jnp.arange(BLOCK)[:, None] >= jnp.arange(BLOCK)[None, :]
    spread = cum_heads[:, :, :, None] - cum_heads[:, :, None, :]
    decays = jnp.where(causal, jnp.exp(jnp.where(causal, spread, 0.0)), 0.0)
    inner_cb = jnp.einsum("lqn,lsn->lqs", c_conv, b_conv, precision=highest)
    scores = low(inner_cb[:, None] * decays * jnp.swapaxes(dt_step, 1, 2)[:, :, None, :])
    x_heads = x_conv.reshape(lane_count, BLOCK, H, HEAD_DIM)
    within = jnp.einsum("lhqs,lshp->lqhp", scores, x_heads, precision=highest)
    carried = (
        jnp.einsum("lqn,lhpn->lqhp", c_conv, state_in, precision=highest)
        * jnp.exp(cumulative)[..., None]
    )
    mixed_sum = low_back(within + carried) + d_skip[:, None] * x_heads
    gated_rows = mixed_sum.reshape(lane_count, BLOCK, E) * jax.nn.silu(z_gate)
    mean_square = jnp.sum(gated_rows * gated_rows, axis=-1, keepdims=True) / chan_count
    return low(gated_rows * lax.rsqrt(mean_square + epsilon) * gate_gain)


def mix_lanes(lane_inputs, d_skip, gate_gain, chan_count):

    def one_lane(pieces):
        lane_gate, lane_xconv, lane_bconv, lane_cconv, lane_step, lane_decay, lane_state = pieces
        return piece_mix(
            lane_gate[None],
            lane_xconv[None],
            lane_bconv[None],
            lane_cconv[None],
            lane_step[None],
            lane_decay[None],
            lane_state[None],
            d_skip,
            gate_gain,
            chan_count,
        )[0]

    return lax.map(one_lane, lane_inputs)


def mix_back_lanes(lane_inputs, mixed_grad, d_skip, gate_gain, chan_count):

    def lane_mix(z_gate, x_conv, b_conv, c_conv, dt_step, log_step, state_in, skip_coef, gain_coef):
        return piece_mix(
            z_gate[None],
            x_conv[None],
            b_conv[None],
            c_conv[None],
            dt_step[None],
            log_step[None],
            state_in[None],
            skip_coef,
            gain_coef,
            chan_count,
        )[0]

    def one_lane(pieces):
        (
            lane_gate,
            lane_xconv,
            lane_bconv,
            lane_cconv,
            lane_step,
            lane_decay,
            lane_state,
            lane_grad,
        ) = pieces
        unused, pull_lane = jax.vjp(
            lane_mix,
            lane_gate,
            lane_xconv,
            lane_bconv,
            lane_cconv,
            lane_step,
            lane_decay,
            lane_state,
            d_skip,
            gate_gain,
        )
        return pull_lane(lane_grad)

    lane_grads = lax.map(one_lane, lane_inputs + (mixed_grad,))
    return (lane_grads[:7], jnp.sum(lane_grads[7], axis=0), jnp.sum(lane_grads[8], axis=0))


def chain_combine(earlier, latter):
    return (earlier[0] * latter[0], latter[0][:, :, None, None] * earlier[1] + latter[1])


def share_out(out_grad):
    return lax.psum_scatter(out_grad, "seq", scatter_dimension=0, tiled=True)


def contract_rows(left, right):
    return lax.dot_general(
        left, right, (((0,), (0,)), ((), ())), preferred_element_type=jnp.float32
    )


def contract_cols(left, right):
    return lax.dot_general(
        left, right, (((1,), (1,)), ((), ())), preferred_element_type=jnp.float32
    )


def body(
    tokens,
    cotangent,
    starts,
    valid,
    norm_gain,
    w_zx,
    w_bc,
    w_dt,
    conv_w,
    conv_b,
    dt_bias,
    a_log,
    d_skip,
    gate_gain,
    w_out,
):
    lane_count = starts.shape[1]
    width_index = lax.axis_index("width")
    shift_bits = lax.axis_size("width") - 1 - width_index
    active_heads = jnp.right_shift(jnp.int32(H), shift_bits)
    chan_mask = (jnp.arange(E) // HEAD_DIM < active_heads).astype(jnp.float32)
    head_mask = (jnp.arange(H) < active_heads).astype(jnp.float32)
    chan_count = (active_heads * HEAD_DIM).astype(jnp.float32)
    keep_rows = 1.0 - starts[0].astype(jnp.float32)
    row_mask = (jnp.arange(BLOCK)[None, :] < valid[0][:, None]).astype(jnp.float32).reshape(-1, 1)
    x_rows = tokens.astype(jnp.float32)
    normed, norm_back = jax.vjp(rms_front, x_rows, norm_gain)
    normed_low = normed.astype(jnp.bfloat16)
    zx_full, bc_full, dt_full, out_full = (
        lax.all_gather(w_zx, "seq", axis=0, tiled=True),
        lax.all_gather(w_bc, "seq", axis=0, tiled=True),
        lax.all_gather(w_dt, "seq", axis=0, tiled=True),
        lax.all_gather(w_out, "seq", axis=0, tiled=True),
    )
    zx_pre = jnp.dot(normed_low, zx_full, preferred_element_type=jnp.float32).reshape(
        lane_count, BLOCK, 2 * E
    )
    bc_pre = jnp.dot(normed_low, bc_full, preferred_element_type=jnp.float32).reshape(
        lane_count, BLOCK, 2 * N
    )
    dt_raw = jnp.dot(normed_low, dt_full, preferred_element_type=jnp.float32).reshape(
        lane_count, BLOCK, H
    )
    rim_rows = passed_along(rim_of(zx_pre, bc_pre, chan_mask), "seq", 1)
    front_fn = partial(piece_front, chan_mask=chan_mask, head_mask=head_mask, keep_rows=keep_rows)
    front_out, front_back = jax.vjp(
        front_fn, zx_pre, bc_pre, dt_raw, rim_rows, conv_w, conv_b, dt_bias, a_log
    )
    z_gate, x_conv, b_conv, c_conv, dt_step, log_step = front_out
    (state_sum, log_total), state_back = jax.vjp(block_state, x_conv, b_conv, dt_step, log_step)
    carry_rate = jnp.exp(log_total) * keep_rows[:, None]
    identity = (jnp.ones_like(carry_rate), jnp.zeros_like(state_sum))
    prefix_pair = carried_in((carry_rate, state_sum), "seq", chain_combine, identity, False)
    state_in = prefix_pair[1] * keep_rows[:, None, None, None]
    lane_inputs = (z_gate, x_conv, b_conv, c_conv, dt_step, log_step, state_in)
    mixed_low = mix_lanes(lane_inputs, d_skip, gate_gain, chan_count)
    mixed_flat = mixed_low.reshape(-1, E).astype(jnp.bfloat16)
    branch = jnp.dot(mixed_flat, out_full, preferred_element_type=jnp.float32)
    output = (x_rows + row_mask * branch).astype(jnp.bfloat16)
    cot_rows = cotangent.astype(jnp.float32)
    branch_grad = (cot_rows * row_mask).astype(jnp.bfloat16)
    out_grad = contract_rows(mixed_flat, branch_grad)
    mixed_grad = contract_cols(branch_grad, out_full).reshape(lane_count, BLOCK, E)
    lane_grads, grad_skip, grad_gain = mix_back_lanes(
        lane_inputs, mixed_grad, d_skip, gate_gain, chan_count
    )
    grad_gate, grad_x, grad_b, grad_c, grad_dt, grad_log, grad_state = lane_grads
    later_pair = carried_in(
        (carry_rate, grad_state * keep_rows[:, None, None, None]),
        "seq",
        chain_combine,
        identity,
        True,
    )
    later_grad = later_pair[1]
    grad_total = jnp.exp(log_total) * jnp.sum(later_grad * state_in, axis=(2, 3))
    grad_x_more, grad_b_more, grad_dt_more, grad_log_more = state_back((later_grad, grad_total))
    grad_zx, grad_bc, grad_dtraw, grad_rim, grad_convw, grad_convb, grad_dtbias, grad_alog = (
        front_back(
            (
                grad_gate,
                grad_x + grad_x_more,
                grad_b + grad_b_more,
                grad_c,
                grad_dt + grad_dt_more,
                grad_log + grad_log_more,
            )
        )
    )
    rim_grad = passed_along(grad_rim.astype(jnp.bfloat16), "seq", -1).astype(grad_rim.dtype)
    grad_zx = grad_zx.at[:, BLOCK - KCONV + 1 :, E:].add(rim_grad[..., :E] * chan_mask)
    grad_bc = grad_bc.at[:, BLOCK - KCONV + 1 :, :].add(rim_grad[..., E:])
    zx_low = grad_zx.reshape(-1, 2 * E).astype(jnp.bfloat16)
    bc_low = grad_bc.reshape(-1, 2 * N).astype(jnp.bfloat16)
    dt_low = grad_dtraw.reshape(-1, H).astype(jnp.bfloat16)
    zx_weight_grad = contract_rows(normed_low, zx_low)
    bc_weight_grad = contract_rows(normed_low, bc_low)
    dt_weight_grad = contract_rows(normed_low, dt_low)
    normed_grad = (
        contract_cols(zx_low, zx_full)
        + contract_cols(bc_low, bc_full)
        + contract_cols(dt_low, dt_full)
    )
    grad_x_rows, grad_norm = norm_back(normed_grad)
    input_grad = cot_rows + grad_x_rows
    out_shard = share_out(out_grad)
    row_shards = (
        lax.psum_scatter(grad_norm, "seq", scatter_dimension=0, tiled=True),
        lax.psum_scatter(zx_weight_grad, "seq", scatter_dimension=0, tiled=True),
        lax.psum_scatter(bc_weight_grad, "seq", scatter_dimension=0, tiled=True),
        lax.psum_scatter(dt_weight_grad, "seq", scatter_dimension=0, tiled=True),
        lax.psum_scatter(grad_convw, "seq", scatter_dimension=0, tiled=True),
        lax.psum_scatter(grad_convb, "seq", scatter_dimension=0, tiled=True),
        lax.psum_scatter(grad_dtbias, "seq", scatter_dimension=0, tiled=True),
        lax.psum_scatter(grad_alog, "seq", scatter_dimension=0, tiled=True),
        lax.psum_scatter(grad_skip, "seq", scatter_dimension=0, tiled=True),
        lax.psum_scatter(grad_gain, "seq", scatter_dimension=0, tiled=True),
    )
    summed = lax.psum(
        (
            row_shards[0],
            row_shards[1],
            row_shards[2],
            row_shards[3],
            row_shards[4],
            row_shards[5],
            row_shards[6],
            row_shards[7],
            row_shards[8],
            row_shards[9],
            out_shard,
        ),
        "width",
    )
    return (
        output,
        input_grad,
        summed[0],
        summed[1],
        summed[2],
        summed[3],
        summed[4],
        summed[5],
        summed[6],
        summed[7],
        summed[8],
        summed[9],
        summed[10],
    )


def solution(mesh):
    in_specs = (
        P(("width", "seq"), None),
        P(("width", "seq"), None),
        P(("width", "seq"), None),
        P(("width", "seq"), None),
        P(),
        P("seq", None),
        P("seq", None),
        P("seq", None),
        P(),
        P(),
        P(),
        P(),
        P(),
        P(),
        P("seq", None),
    )
    out_specs = (
        P(("width", "seq"), None),
        P(("width", "seq"), None),
        P("seq"),
        P("seq", None),
        P("seq", None),
        P("seq", None),
        P("seq", None),
        P("seq"),
        P("seq"),
        P("seq"),
        P("seq"),
        P("seq"),
        P("seq", None),
    )
    return jax.shard_map(body, mesh=mesh, in_specs=in_specs, out_specs=out_specs, check_vma=False)
```

profile of v0, /device:TPU:9, one launch (start us, length us, event | category | flops | bytes accessed | tf_op | source)
XLA Modules:
  0.0 2688.1 jit_solution(11758217119221314912)
XLA Ops:
  9.6 15.0 all_gather.32
  35.6 285.3 %all-gather.8.cloned.1.call-done = bf16[2048,8192]{1,0:T(8,128)(2,1)} async-done(((bf16[256,8192]{1,0:T(8,128)(2,1)}), bf16[2048,8192]{1,0:T(8,128)(2,1)}) %all-gather.8.cloned.1.call-update) | async-done | bytes 33554448 | tf_op jit(solution)/shard_map/all_gather | solution.py:263
  320.9 17.6 fusion.125
  344.8 6.6 slice_multiply_fusion.1
  372.4 13.3 all_gather.33
  385.8 87.6 %all-gather.12.cloned.1.call-done = bf16[4096,2048]{1,0:T(8,128)(2,1)} async-done(((bf16[512,2048]{1,0:T(8,128)(2,1)}), bf16[4096,2048]{1,0:T(8,128)(2,1)}) %all-gather.12.cloned.1.call-update) | async-done | bytes 16777232 | tf_op jit(solution)/shard_map/all_gather | solution.py:266
  473.4 10.4 fusion.93
  490.0 271.6 %all-gather.14.cloned.1.call-done = f32[16,64,64,128]{3,2,1,0:T(8,128)} async-done(((f32[2,64,64,128]{3,2,1,0:T(8,128)}), f32[16,64,64,128]{3,2,1,0:T(8,128)}) %all-gather.14.cloned.1.call-update) | async-done | bytes 33554448 | tf_op jit(solution)/shard_map/all_gather | solution.py:30
  764.1 17.7 while.68
  794.4 140.7 %while.70 = (s32[]{:T(128)}, f32[2,128,4096]{2,1,0:T(8,128)}, f32[2,128,4096]{2,1,0:T(8,128)}, f32[2,128,128]{2,1,0:T(8,128)}, f32[2,128,128]{2,1,0:T(8,128)}, /...) while((s32[]{:T(128)}, f32[2,128,4096]{2,1,0:T(8,128)}, ...), condition=%wide.region_21.22_spmd.clone, body=%wide.region_8.21_spmd.sunk.clone | while | flops 4284477952 | bytes 209170992 | solution.py:209
  805.0 7.2 fusion.262
  875.0 7.2 fusion.262
  942.5 308.0 %all-gather.16.cloned.1.call-done = f32[16,64,64,128]{3,2,1,0:T(8,128)} async-done(((f32[2,64,64,128]{3,2,1,0:T(8,128)}), f32[16,64,64,128]{3,2,1,0:T(8,128)}) %all-gather.16.cloned.1.call-update) | async-done | bytes 33554448 | tf_op jit(solution)/shard_map/all_gather | solution.py:30
  1253.0 26.6 while.71
  1279.6 8.7 multiply_reduce_fusion.12
  1305.4 6.2 multiply_reduce_fusion.9
  1311.8 6.6 broadcast_multiply_fusion
  1324.5 9.1 collective-permute-start.1
  1337.7 44.5 %while.69 = (s32[]{:T(128)}, bf16[2,128,4096]{2,1,0:T(8,128)(2,1)}, f32[2,128,4096]{1,2,0:T(8,128)}, f32[2,128,128]{2,1,0:T(8,128)S(1)}, f32[2,128,128]{2,1,0:T(...) while((s32[]{:T(128)}, bf16[2,128,4096]{2,1,0:T(8,128)(2,1)}, ...), condition=%wide.region_7.8_spmd.clone, body=%wide.region_4.7_spmd.sunk.clone | while | flops 1650466944 | bytes 69030352 | solution.py:165
  1350.5 6.6 fusion.242
  1372.5 6.6 fusion.242
  1382.2 18.1 fusion.91
  1400.3 7.3 pad_add_fusion.1
  1413.8 26.6 fusion.119
  1443.5 295.7 %reduce-scatter.14.cloned.1.call-done = f32[512,2048]{1,0:T(8,128)} async-done(((f32[4096,2048]{1,0:T(8,128)}), f32[512,2048]{1,0:T(8,128)}) %reduce-scatter.14.cloned.1.call-update) | async-done | bytes 4194320 | tf_op jit(solution)/shard_map/reduce_scatter | solution.py:218
  1739.1 640.9 %reduce-scatter.8.cloned.1.call-done = f32[256,8192]{1,0:T(8,128)} async-done(((f32[2048,8192]{1,0:T(8,128)}), f32[256,8192]{1,0:T(8,128)}) %reduce-scatter.8.cloned.1.call-update) | async-done | bytes 8388624 | tf_op jit(solution)/shard_map/reduce_scatter | solution.py:342
  2384.0 9.5 fusion.82
  2393.5 15.8 fusion.138
  2411.2 23.2 all-reduce.21
  2439.3 14.0 all-reduce.22
  2453.3 216.8 %all-reduce.26.cloned.1.call-done = (f32[256,8192]{1,0:T(8,128)}, f32[256,256]{1,0:T(8,128)}, f32[256,64]{0,1:T(8,128)}, f32[512,2048]{1,0:T(8,128)}) async-done(((f32[256,8192]{1,0:T(8,128)}, f32[256,256]{1,0:T(8,128)}, f32[256,64]{0,1:T(8,128)}, f32[512,2048]{1,0:T(8,128)}), (f32[256,8192]{1,0:T(8,128)}, f32[256,256]{1,0:T(8,128)}, f32[256,64]{0,1:T(8,128)}, ...) | async-done | bytes 12910608 | tf_op jit(solution)/shard_map/psum | solution.py:352
  2670.1 7.8 copy.310
  (539 shorter events, 318.9 us)
Async XLA Ops:
  7.2 26.6 all-gather.10.cloned.1.call-start
  8.0 312.9 %all-gather.8.cloned.1.call-start = ((), (), s32[]{:S(2)}) async-start(), calls=%async_computation.5 | async-start | bytes 37748736 | tf_op jit(solution)/shard_map/all_gather | solution.py:263
  8.7 19.3 copy-start.83
  8.7 19.5 copy-start.111
  8.7 464.7 %all-gather.12.cloned.1.call-start = ((), (), s32[]{:S(2)}) async-start(), calls=%async_computation.7 | async-start | bytes 18874368 | tf_op jit(solution)/shard_map/all_gather | solution.py:266
  9.5 752.1 %all-gather.14.cloned.1.call-start = ((), (), s32[]{:S(2)}) async-start(), calls=%async_computation.12 | async-start | bytes 37748736 | tf_op jit(solution)/shard_map/all_gather | solution.py:30
  25.4 313.1 %copy-start.75 = (f32[256]{0:T(256)}, f32[256]{0:T(256)S(1)}, u32[]{:S(2)}) copy-start(f32[256]{0:T(256)S(1)} %fusion.113) | copy-start | bytes 3076
  26.7 345.0 %copy-start.28 = (f32[2,128,64]{2,1,0:T(8,128)}, f32[2,128,64]{2,1,0:T(8,128)S(1)}, u32[]{:S(2)}) copy-start(f32[2,128,64]{2,1,0:T(8,128)S(1)} %get-tuple-element.653) | copy-start | bytes 196612
  27.8 310.7 %copy-start.95 = (f32[2,1,64]{2,1,0:T(1,128)}, f32[2,1,64]{2,1,0:T(1,128)S(1)}, u32[]{:S(2)}) copy-start(f32[2,1,64]{2,1,0:T(1,128)S(1)} %get-tuple-element.673) | copy-start | bytes 1540
  28.0 336.6 %copy-start.49 = (f32[2,128,64]{1,2,0:T(8,128)}, f32[2,128,64]{1,2,0:T(8,128)S(1)}, u32[]{:S(2)}) copy-start(f32[2,128,64]{1,2,0:T(8,128)S(1)} %copy.153) | copy-start | bytes 196612
  28.0 332.4 %copy-start.43 = (f32[4096]{0:T(1024)}, f32[4096]{0:T(1024)S(1)}, u32[]{:S(2)}) copy-start(f32[4096]{0:T(1024)S(1)} %fusion.111) | copy-start | bytes 49156
  28.2 327.3 %copy-start.60 = (f32[4352]{0:T(1024)}, f32[4352]{0:T(1024)S(1)}, u32[]{:S(2)}) copy-start(f32[4352]{0:T(1024)S(1)} %get-tuple-element.532) | copy-start | bytes 52228
  28.2 327.3 %copy-start.62 = (f32[4352]{0:T(1024)}, f32[4352]{0:T(1024)S(1)}, u32[]{:S(2)}) copy-start(f32[4352]{0:T(1024)S(1)} %get-tuple-element.533) | copy-start | bytes 52228
  28.2 327.3 %copy-start.64 = (f32[4352]{0:T(1024)}, f32[4352]{0:T(1024)S(1)}, u32[]{:S(2)}) copy-start(f32[4352]{0:T(1024)S(1)} %get-tuple-element.534) | copy-start | bytes 52228
  28.2 327.3 %copy-start.66 = (f32[4352]{0:T(1024)}, f32[4352]{0:T(1024)S(1)}, u32[]{:S(2)}) copy-start(f32[4352]{0:T(1024)S(1)} %get-tuple-element.535) | copy-start | bytes 52228
  28.5 753.3 %copy-start.92 = (f32[2]{0:T(128)}, f32[2]{0:T(128)S(1)}, u32[]{:S(2)}) copy-start(f32[2]{0:T(128)S(1)} %subtract_bitcast_fusion) | copy-start | bytes 28
  35.6 320.0 %copy-start.30 = (f32[256,256]{1,0:T(8,128)}, f32[256,256]{1,0:T(8,128)S(1)}, u32[]{:S(2)}) copy-start(f32[256,256]{1,0:T(8,128)S(1)} %fusion.123) | copy-start | bytes 786436
  339.5 15.4 collective-permute-start
  364.6 125.4 %copy-start.38 = (bf16[2,128,128]{2,1,0:T(8,128)(2,1)}, bf16[2,128,128]{2,1,0:T(8,128)(2,1)S(1)}, u32[]{:S(2)}) copy-start(bf16[2,128,128]{2,1,0:T(8,128)(2,1)S(1)} %get-tuple-element.670) | copy-start | bytes 196612
  368.9 104.5 %copy-start.26 = (bf16[256,2048]{1,0:T(8,128)(2,1)S(1)}, bf16[256,2048]{1,0:T(8,128)(2,1)}, u32[]{:S(2)}) copy-start(bf16[256,2048]{1,0:T(8,128)(2,1)} %param.28) | copy-start | bytes 3145732
  371.6 878.9 %all-gather.16.cloned.1.call-start = ((), (), s32[]{:S(2)}) async-start(), calls=%async_computation.13 | async-start | bytes 37748736 | tf_op jit(solution)/shard_map/all_gather | solution.py:30
  385.8 98.0 %copy-start.107 = (f32[256]{0:T(256)}, f32[256]{0:T(256)S(1)}, u32[]{:S(2)}) copy-start(f32[256]{0:T(256)S(1)} %fusion.112) | copy-start | bytes 3076
  940.1 503.3 %reduce-scatter.12.cloned.1.call-start = ((), (), s32[]{:S(2)}) async-start(), calls=%async_computation.10 | async-start | bytes 589824 | tf_op jit(solution)/shard_map/reduce_scatter | solution.py:344
  1253.0 26.6 copy-start.39
  1253.0 26.6 copy-start.50
  1323.0 120.5 %reduce-scatter.10.cloned.1.call-start = ((), (), s32[]{:S(2)}) async-start(), calls=%async_computation.9 | async-start | bytes 2359296 | tf_op jit(solution)/shard_map/reduce_scatter | solution.py:343
  1324.5 10.3 collective-permute-start.1
  1337.7 401.5 %reduce-scatter.14.cloned.1.call-start = ((), (), s32[]{:S(2)}) async-start(), calls=%async_computation.11 | async-start | bytes 37748736 | tf_op jit(solution)/shard_map/reduce_scatter | solution.py:218
  1400.3 979.7 %reduce-scatter.8.cloned.1.call-start = ((), (), s32[]{:S(2)}) async-start(), calls=%async_computation.8 | async-start | bytes 75497472 | tf_op jit(solution)/shard_map/reduce_scatter | solution.py:342
  1440.4 997.8 %reduce-scatter.16.cloned.1.call-start = ((), (), s32[]{:S(2)}) async-start(), calls=%async_computation.14 | async-start | bytes 2506752
  1443.4 1226.7 %all-reduce.26.cloned.1.call-start = ((), (), s32[]{:S(2)}) async-start(), calls=%async_computation.15 | async-start | bytes 25821184 | tf_op jit(solution)/shard_map/psum | solution.py:352
  2409.4 25.5 copy-start.98
  (128 other events, 764.4 us)
Sparse Core Ops, SparseCore 0:
  9.7 24.1 all-gather.9
  35.4 285.4 all-gather.7
  322.5 150.8 all-gather.11
  474.9 286.6 all-gather.13
  940.2 310.1 all-gather.15
  1323.1 44.8 reduce-scatter.11
  1370.4 35.4 reduce-scatter.9
  1408.4 330.6 reduce-scatter.13
  1741.5 638.4 reduce-scatter.7
  2382.9 31.2 reduce-scatter.15
  2418.2 251.8 all-reduce.25
where the time goes:
time: 2700 us; the launch traced here: 2690 us
  waiting for transfers between devices  2120 us (79%)
  matrix products  191 us (7%)
  other arithmetic  151 us (6%)
  local copies, waits for them, and re-layouts  128 us (5%)
  blocking collectives  65.5 us (2%)
    reduce_scatter x1, waiting for transfers between devices, body(): lax.psum_scatter(zx_weight_grad, 'seq', scatter_dimension=0, tiled=True)  641 us
    all_gather x2, waiting for transfers between devices, carried_in(): gathered = jax.tree.map(lambda a: lax.all_gather(a, axis), part)  580 us
    reduce_scatter x1, waiting for transfers between devices, share_out(): return lax.psum_scatter(out_grad, 'seq', scatter_dimension=0, tiled=True)  296 us
    all_gather x1, waiting for transfers between devices, body(): lax.all_gather(w_zx, 'seq', axis=0, tiled=True)  285 us
    psum x1, waiting for transfers between devices, body(): lax.psum((row_shards[0], row_shards[1], row_shards[2], row_shards[3], row...  217 us
    all_gather x1, waiting for transfers between devices, body(): lax.all_gather(w_out, 'seq', axis=0, tiled=True)  87.6 us
  transfers between devices with their start and end apart: 13, of which 9 were waited for; matrix products, arithmetic and copies ran while one was open for 8% of the time, Pallas kernels for 0%

commit v1 on v0

--- a/solution.py
+++ b/solution.py
@@ -3,6 +3,8 @@
 import jax
 import jax.numpy as jnp
 from jax import lax
+from jax.experimental import pallas as pl
+from jax.experimental.pallas import tpu as pltpu
 from jax.sharding import PartitionSpec as P
 
 H = 64
@@ -11,10 +13,463 @@
 KCONV = 4
 BLOCK = 128
 E = 4096
-
+SUB = 8
 
 epsilon = 1e-05
 highest = lax.Precision.HIGHEST
+f32 = jnp.float32
+bf16 = jnp.bfloat16
+
+NN = ((1,), (0,))
+NT = ((1,), (1,))
+TN = ((0,), (0,))
+
+
+def mm(left, right, dims=NN, precision=None):
+    return lax.dot_general(left, right, (dims, ((), ())), precision=precision, preferred_element_type=f32)
+
+
+def split2(value):
+    high = value.astype(bf16)
+    return high, (value - high.astype(f32)).astype(bf16)
+
+
+def mm_right(left, right, dims=NN):
+    high, low = split2(right)
+    return mm(left, high, dims) + mm(left, low, dims)
+
+
+def mm_left(left, right, dims=NN):
+    high, low = split2(left)
+    return mm(high, right, dims) + mm(low, right, dims)
+
+
+def softplus(v):
+    small = jnp.exp(-jnp.abs(v))
+    log1p = jnp.where(small < 1e-4, small - 0.5 * small * small, jnp.log(1.0 + small))
+    return jnp.maximum(v, 0.0) + log1p
+
+
+def sigmoid(v):
+    return 1.0 / (1.0 + jnp.exp(-v))
+
+
+def grids():
+    row = lax.broadcasted_iota(jnp.int32, (BLOCK, BLOCK), 0)
+    col = lax.broadcasted_iota(jnp.int32, (BLOCK, BLOCK), 1)
+    return row, col
+
+
+def halves(pair, lane):
+    zero = jnp.zeros_like(pair)
+    return jnp.where(lane < HEAD_DIM, pair, zero), jnp.where(lane < HEAD_DIM, zero, pair)
+
+
+def decay_of(cum, cum_t, head, causal):
+    return jnp.exp(jnp.where(causal, cum[:, head : head + 1] - cum_t[head : head + 1, :], -1e30))
+
+
+TAP, BIAS, SKIP, GAIN, MASK = 0, 4, 5, 6, 7
+DT_BIAS, NEG_A, HEAD_MASK = 0, 1, 2
+
+
+def forward_kernel(
+    keep_ref, zx_ref, bcd_ref, grad_ref, chan_ref, bc_par_ref, head_ref, spread_ref,
+    conv_ref, mix_ref, bc_ref, step_ref, state_ref, tail_ref, sums_ref,
+    state, tail_x, tail_b, pad_x, pad_b,
+    *, lanes, heads,
+):
+    c = pl.program_id(0)
+    width = heads * HEAD_DIM
+    row, col = grids()
+    causal = row >= col
+    tril = causal.astype(f32)
+    spread = spread_ref[...]
+
+    @pl.when(c == 0)
+    def _():
+        state[...] = jnp.zeros_like(state)
+        tail_x[...] = jnp.zeros_like(tail_x)
+        tail_b[...] = jnp.zeros_like(tail_b)
+
+    for lane in range(lanes):
+        rows = pl.ds(lane * BLOCK, BLOCK)
+        keep = keep_ref[c, lane]
+        pre = zx_ref[rows, width:]
+        pad_x[lane, 0:SUB] = tail_x[lane] * keep
+        pad_x[lane, SUB:] = pre
+        tail_ref[0, lane] = tail_x[lane] * keep
+        tail_x[lane] = pre[BLOCK - SUB :, :]
+        conv = chan_ref[BIAS : BIAS + 1, :]
+        for k in range(KCONV):
+            conv = conv + pad_x[lane, SUB - KCONV + 1 + k : SUB - KCONV + 1 + k + BLOCK, :] * chan_ref[k : k + 1, :]
+        conv_ref[rows, :] = conv
+        x_low = (conv * sigmoid(conv) * chan_ref[MASK : MASK + 1, :]).astype(bf16)
+
+        pre_b = bcd_ref[rows, : 2 * N]
+        pad_b[lane, 0:SUB] = tail_b[lane] * keep
+        pad_b[lane, SUB:] = pre_b
+        tail_b[lane] = pre_b[BLOCK - SUB :, :]
+        conv_b = bc_par_ref[BIAS : BIAS + 1, :]
+        for k in range(KCONV):
+            conv_b = conv_b + pad_b[lane, SUB - KCONV + 1 + k : SUB - KCONV + 1 + k + BLOCK, :] * bc_par_ref[k : k + 1, :]
+        bc_low = (conv_b * sigmoid(conv_b)).astype(bf16)
+        bc_ref[rows, :] = bc_low
+        b_low, c_low = bc_low[:, :N], bc_low[:, N:]
+
+        raw = bcd_ref[rows, 2 * N :] + head_ref[DT_BIAS : DT_BIAS + 1, :]
+        dt = softplus(raw) * head_ref[HEAD_MASK : HEAD_MASK + 1, :]
+        cum = mm(tril, head_ref[NEG_A : NEG_A + 1, :] * dt, precision=highest)
+        step_ref[rows, :BLOCK] = cum
+        step_ref[rows, BLOCK:] = dt
+        cum_t, dt_t = cum.T, dt.T
+        last = cum[BLOCK - 1 :, :]
+        carry_x = mm_left(jnp.exp(cum), spread)
+        end_x = mm_left(jnp.exp(last - cum) * dt, spread)
+        last_x = carry_x[BLOCK - 1 :, :]
+
+        inner = mm(c_low, b_low, NT)
+        parts = []
+        for j in range(heads // 2):
+            pair = x_low[:, 2 * HEAD_DIM * j : 2 * HEAD_DIM * (j + 1)]
+            scores = [
+                (inner * decay_of(cum, cum_t, h, causal) * dt_t[h : h + 1, :]).astype(bf16)
+                for h in (2 * j, 2 * j + 1)
+            ]
+            parts.append(mm(jnp.concatenate(scores, axis=1), jnp.concatenate(halves(pair, col), axis=0)))
+        within = jnp.concatenate(parts, axis=1)
+
+        state_in = state[lane] * keep
+        state_ref[0, lane] = state_in
+        carried = mm_right(c_low, state_in) * carry_x
+        x_f = x_low.astype(f32)
+        mixed = within + carried + chan_ref[SKIP : SKIP + 1, :] * x_f
+        mix_ref[rows, :] = mixed
+        weighted = (x_f * end_x).astype(bf16)
+        state[lane] = last_x * state_in + mm(b_low, weighted, TN)
+
+        z = zx_ref[rows, :width]
+        gated = mixed * (z * sigmoid(z))
+        ones = jnp.ones((SUB, width), bf16)
+        square = mm_right(ones, gated * gated, NT)
+        cross = mm_right(ones, grad_ref[rows, :] * chan_ref[GAIN : GAIN + 1, :] * gated, NT)
+        sub = lax.broadcasted_iota(jnp.int32, (SUB, BLOCK), 0)
+        sums_ref[0, lane] = jnp.where(sub == 0, square, jnp.where(sub == 1, cross, 0.0))
+
+
+def backward_kernel(
+    keep_ref, zx_ref, bcd_ref, grad_ref, chan_ref, head_ref, spread_ref,
+    conv_ref, mix_ref, bc_ref, step_ref, state_ref, tail_ref, scale_ref,
+    dzx_ref, ddt_ref, dbc_ref, dchan_ref, dhead_ref,
+    state_grad, next_conv, pad_x, pad_d,
+    *, lanes, heads, blocks,
+):
+    lap = pl.program_id(0)
+    c = blocks - 1 - lap
+    width = heads * HEAD_DIM
+    row, col = grids()
+    causal = row >= col
+    triu = (col >= row).astype(f32)
+    spread = spread_ref[...]
+
+    @pl.when(lap == 0)
+    def _():
+        state_grad[...] = jnp.zeros_like(state_grad)
+        next_conv[...] = jnp.zeros_like(next_conv)
+        dchan_ref[...] = jnp.zeros_like(dchan_ref)
+        dhead_ref[...] = jnp.zeros_like(dhead_ref)
+
+    def total(value):
+        return jnp.sum(value, axis=0, keepdims=True)
+
+    for lane in range(lanes):
+        rows = pl.ds(lane * BLOCK, BLOCK)
+        keep = keep_ref[c, lane]
+        z = zx_ref[rows, :width]
+        conv = conv_ref[rows, :]
+        mixed = mix_ref[rows, :]
+        grad = grad_ref[rows, :]
+        gain = chan_ref[GAIN : GAIN + 1, :]
+        skip = chan_ref[SKIP : SKIP + 1, :]
+        rate = scale_ref[rows, 0:1]
+        pull = scale_ref[rows, 1:2]
+        gate = sigmoid(z)
+        silu = z * gate
+        gated = mixed * silu
+        dgated = grad * gain * rate - gated * pull
+        dzx_ref[rows, :width] = (dgated * mixed * (gate * (1.0 + z * (1.0 - gate)))).astype(bf16)
+        dmixed = dgated * silu
+        act = sigmoid(conv)
+        x_low = (conv * act * chan_ref[MASK : MASK + 1, :]).astype(bf16)
+        x_f = x_low.astype(f32)
+        dchan_ref[GAIN : GAIN + 1, :] += total(grad * gated * rate)
+        dchan_ref[SKIP : SKIP + 1, :] += total(dmixed * x_f)
+        dlow = dmixed.astype(bf16)
+        dlow_f = dlow.astype(f32)
+
+        b_low, c_low = bc_ref[rows, :N], bc_ref[rows, N:]
+        cum, dt = step_ref[rows, :BLOCK], step_ref[rows, BLOCK:]
+        cum_t, dt_t = cum.T, dt.T
+        last = cum[BLOCK - 1 :, :]
+        to_last = jnp.exp(last - cum)
+        carry_x = mm_left(jnp.exp(cum), spread)
+        end_x = mm_left(to_last * dt, spread)
+        last_x = carry_x[BLOCK - 1 :, :]
+
+        inner = mm(c_low, b_low, NT)
+        dinner = jnp.zeros((BLOCK, BLOCK), f32)
+        parts, dt_rows = [], []
+        for j in range(heads // 2):
+            lanes_j = slice(2 * HEAD_DIM * j, 2 * HEAD_DIM * (j + 1))
+            pair, dpair = x_low[:, lanes_j], dlow[:, lanes_j]
+            dstack = jnp.concatenate(halves(dpair, col), axis=0)
+            dscores = mm(dstack, pair, NT)
+            scores = []
+            for i, h in enumerate((2 * j, 2 * j + 1)):
+                decay = decay_of(cum, cum_t, h, causal)
+                step = dt_t[h : h + 1, :]
+                scores.append((inner * decay * step).astype(bf16))
+                part = dscores[i * BLOCK : (i + 1) * BLOCK] * decay
+                dinner = dinner + part * step
+                dt_rows.append(total(part * inner))
+            parts.append(mm(jnp.concatenate(scores, axis=0), dstack, TN))
+        dx_within = jnp.concatenate(parts, axis=1)
+        dt_rows.append(jnp.zeros((BLOCK - heads, BLOCK), f32))
+        ddt_within = jnp.concatenate(dt_rows, axis=0).T
+
+        state_in = state_ref[0, lane]
+        sgrad = state_grad[lane]
+        in_high, in_low = split2(state_in)
+        sg_high, sg_low = split2(sgrad)
+        dcarry = dlow_f * carry_x
+        dc_high, dc_low = split2(dcarry)
+        di_high, di_low = split2(dinner)
+        dc = mm(dc_high, in_high, NT) + mm(dc_high, in_low, NT) + mm(dc_low, in_high, NT)
+        dc = dc + mm(di_high, b_low) + mm(di_low, b_low)
+        weighted = (x_f * end_x).astype(bf16)
+        db = mm(weighted, sg_high, NT) + mm(weighted, sg_low, NT)
+        db = db + mm(di_high, c_low, TN) + mm(di_low, c_low, TN)
+        dbc_ref[rows, :N] = db
+        dbc_ref[rows, N:] = dc
+        dweighted = mm(b_low, sg_high) + mm(b_low, sg_low)
+        dx = dx_within + dweighted * end_x
+        dcum = mm_left(dlow_f * (mixed - skip * x_f) - x_f * dx, spread, NT)
+        dend = mm_left(dweighted * x_f, spread, NT)
+        touch = jnp.broadcast_to(total(sgrad * state_in), (SUB, width))
+        dlast = total(dend * to_last * dt) + jnp.exp(last) * mm_left(touch, spread, NT)[0:1]
+        dlog = mm(triu, dcum, precision=highest) + dlast
+        neg_a = head_ref[NEG_A : NEG_A + 1, :]
+        ddt = ddt_within + dend * to_last + dlog * neg_a
+        raw = bcd_ref[rows, 2 * N :] + head_ref[DT_BIAS : DT_BIAS + 1, :]
+        draw = ddt * sigmoid(raw) * head_ref[HEAD_MASK : HEAD_MASK + 1, :]
+        ddt_ref[rows, :] = draw.astype(bf16)
+        dhead_ref[0:1, :] += total(draw)
+        dhead_ref[1:2, :] += total(dlog * neg_a * dt)
+        state_grad[lane] = keep * (mm(c_low, dc_high, TN) + mm(c_low, dc_low, TN) + last_x * sgrad)
+
+        dx = dx + skip * dmixed
+        dconv = dx * chan_ref[MASK : MASK + 1, :] * (act * (1.0 + conv * (1.0 - act)))
+        pad_d[lane, :BLOCK] = dconv
+        pad_d[lane, BLOCK:] = next_conv[lane]
+        next_conv[lane] = dconv[:SUB] * keep
+        pad_x[lane, :SUB] = tail_ref[0, lane]
+        pad_x[lane, SUB:] = zx_ref[rows, width:]
+        dpre = jnp.zeros((BLOCK, width), f32)
+        for k in range(KCONV):
+            dpre = dpre + pad_d[lane, KCONV - 1 - k : KCONV - 1 - k + BLOCK, :] * chan_ref[k : k + 1, :]
+            dchan_ref[k : k + 1, :] += total(dconv * pad_x[lane, SUB - KCONV + 1 + k : SUB - KCONV + 1 + k + BLOCK, :])
+        dchan_ref[BIAS : BIAS + 1, :] += total(dconv)
+        dzx_ref[rows, width:] = dpre.astype(bf16)
+
+
+def run_forward(keep, zx, bcd, grad, chan, bc_par, head, spread, lanes, heads):
+    rows, width = grad.shape
+    step = lanes * BLOCK
+    blocks = rows // step
+    by_block = lambda cols: pl.BlockSpec((step, cols), lambda c: (c, 0))
+    whole = lambda a: pl.BlockSpec(a.shape, lambda c: (0,) * a.ndim)
+    per_lane = lambda r, cols: pl.BlockSpec((1, lanes, r, cols), lambda c: (c, 0, 0, 0))
+    return pl.pallas_call(
+        partial(forward_kernel, lanes=lanes, heads=heads),
+        grid=(blocks,),
+        in_specs=[
+            pl.BlockSpec(memory_space=pltpu.SMEM), by_block(2 * width), by_block(2 * N + BLOCK), by_block(width),
+            whole(chan), whole(bc_par), whole(head), whole(spread),
+        ],
+        out_specs=[
+            by_block(width), by_block(width), by_block(2 * N), by_block(2 * BLOCK),
+            per_lane(N, width), per_lane(SUB, width), per_lane(SUB, BLOCK),
+        ],
+        out_shape=[
+            jax.ShapeDtypeStruct((rows, width), f32), jax.ShapeDtypeStruct((rows, width), f32),
+            jax.ShapeDtypeStruct((rows, 2 * N), bf16), jax.ShapeDtypeStruct((rows, 2 * BLOCK), f32),
+            jax.ShapeDtypeStruct((blocks, lanes, N, width), f32), jax.ShapeDtypeStruct((blocks, lanes, SUB, width), f32),
+            jax.ShapeDtypeStruct((blocks, lanes, SUB, BLOCK), f32),
+        ],
+        scratch_shapes=[
+            pltpu.VMEM((lanes, N, width), f32), pltpu.VMEM((lanes, SUB, width), f32), pltpu.VMEM((lanes, SUB, 2 * N), f32),
+            pltpu.VMEM((lanes, BLOCK + SUB, width), f32), pltpu.VMEM((lanes, BLOCK + SUB, 2 * N), f32),
+        ],
+        compiler_params=pltpu.CompilerParams(vmem_limit_bytes=40 << 20, dimension_semantics=("arbitrary",)),
+        cost_estimate=pl.CostEstimate(flops=rows * width * 2048, bytes_accessed=rows * width * 32, transcendentals=rows * width * 4),
+        name="mix_forward",
+    )(keep, zx, bcd, grad, chan, bc_par, head, spread)
+
+
+def run_backward(keep, zx, bcd, grad, chan, head, spread, conv, mix, bc, step_arr, state, tail, scale, lanes, heads):
+    rows, width = grad.shape
+    step = lanes * BLOCK
+    blocks = rows // step
+    by_block = lambda cols: pl.BlockSpec((step, cols), lambda c: (blocks - 1 - c, 0))
+    whole = lambda a: pl.BlockSpec(a.shape, lambda c: (0,) * a.ndim)
+    fixed = lambda shape: pl.BlockSpec(shape, lambda c: (0,) * len(shape))
+    per_lane = lambda r, cols: pl.BlockSpec((1, lanes, r, cols), lambda c: (blocks - 1 - c, 0, 0, 0))
+    return pl.pallas_call(
+        partial(backward_kernel, lanes=lanes, heads=heads, blocks=blocks),
+        grid=(blocks,),
+        in_specs=[
+            pl.BlockSpec(memory_space=pltpu.SMEM), by_block(2 * width), by_block(2 * N + BLOCK), by_block(width),
+            whole(chan), whole(head), whole(spread),
+            by_block(width), by_block(width), by_block(2 * N), by_block(2 * BLOCK),
+            per_lane(N, width), per_lane(SUB, width), by_block(SUB),
+        ],
+        out_specs=[by_block(2 * width), by_block(BLOCK), by_block(2 * N), fixed((SUB, width)), fixed((SUB, BLOCK))],
+        out_shape=[
+            jax.ShapeDtypeStruct((rows, 2 * width), bf16), jax.ShapeDtypeStruct((rows, BLOCK), bf16),
+            jax.ShapeDtypeStruct((rows, 2 * N), f32), jax.ShapeDtypeStruct((SUB, width), f32),
+            jax.ShapeDtypeStruct((SUB, BLOCK), f32),
+        ],
+        scratch_shapes=[
+            pltpu.VMEM((lanes, N, width), f32), pltpu.VMEM((lanes, SUB, width), f32),
+            pltpu.VMEM((lanes, BLOCK + SUB, width), f32), pltpu.VMEM((lanes, BLOCK + SUB, width), f32),
+        ],
+        compiler_params=pltpu.CompilerParams(vmem_limit_bytes=48 << 20, dimension_semantics=("arbitrary",)),
+        cost_estimate=pl.CostEstimate(flops=rows * width * 6144, bytes_accessed=rows * width * 40, transcendentals=rows * width * 6),
+        name="mix_backward",
+    )(keep, zx, bcd, grad, chan, head, spread, conv, mix, bc, step_arr, state, tail, scale)
+
+
+def bc_front(bc_pre, taps, bias, keep):
+    rim = bc_pre[:, :, BLOCK - KCONV + 1 :, :]
+    before = jnp.concatenate([jnp.zeros_like(rim[:1]), rim[:-1]], axis=0) * keep[:, :, None, None]
+    padded = jnp.concatenate([before, bc_pre], axis=2)
+    out = bias
+    for k in range(KCONV):
+        out = out + padded[:, :, k : k + BLOCK, :] * taps[k]
+    return jax.nn.silu(out)
+
+
+def packed_rows(rows, count):
+    flat = jnp.stack(rows)
+    return jnp.pad(flat, ((0, count - len(rows)), (0, 0)))
+
+
+def heads_body(
+    tokens, cotangent, starts, valid, norm_gain, w_zx, w_bc, w_dt, conv_w, conv_b, dt_bias, a_log, d_skip, gate_gain, w_out
+):
+    peers = lax.axis_size("seq")
+    widths = lax.axis_size("width")
+    place = lax.axis_index("seq")
+    lanes = starts.shape[1]
+    heads = H // peers
+    chans = heads * HEAD_DIM
+    own, model = tokens.shape
+    rows = own * peers
+    active = jnp.right_shift(jnp.int32(H), widths - 1 - lax.axis_index("width"))
+    count = (active * HEAD_DIM).astype(f32)
+    first = place * heads
+
+    x_rows = tokens.astype(f32)
+    rate = lax.rsqrt(jnp.mean(x_rows * x_rows, axis=-1, keepdims=True) + epsilon)
+    normed_own = (x_rows * rate * norm_gain).astype(bf16)
+    row_mask = (jnp.arange(BLOCK)[None, :] < valid[0][:, None]).astype(f32).reshape(-1, 1)
+    cot_rows = cotangent.astype(f32)
+    bgrad_own = (cot_rows * row_mask).astype(bf16)
+
+    weights = lax.all_to_all(w_zx.reshape(-1, 2, peers, chans), "seq", 2, 0, tiled=True).reshape(model, 2 * chans)
+    normed = lax.all_gather(normed_own, "seq", axis=0, tiled=True)
+    bgrad = lax.all_gather(bgrad_own, "seq", axis=0, tiled=True)
+    bc_dt = lax.all_gather(jnp.concatenate([w_bc, w_dt], axis=1), "seq", axis=0, tiled=True)
+    keep = 1.0 - lax.all_gather(starts, "seq", axis=0, tiled=True).astype(f32)
+    weights_bc = bc_dt[:, : 2 * N]
+    weights_dt = jnp.pad(lax.dynamic_slice_in_dim(bc_dt, 2 * N + first, heads, 1), ((0, 0), (0, BLOCK - heads)))
+
+    taps_x = lax.dynamic_slice_in_dim(conv_w, first * HEAD_DIM, chans, 0).T
+    of_chans = lambda a: lax.dynamic_slice_in_dim(a, first * HEAD_DIM, chans, 0)
+    of_heads = lambda a: jnp.pad(lax.dynamic_slice_in_dim(a, first, heads, 0), (0, BLOCK - heads))
+    head_on = (jnp.arange(BLOCK) < jnp.minimum(active - first, heads)).astype(f32)
+    chan_on = (jnp.arange(chans) // HEAD_DIM < active - first).astype(f32)
+    skip_x = jnp.repeat(lax.dynamic_slice_in_dim(d_skip, first, heads, 0), HEAD_DIM)
+    chan = packed_rows([*taps_x, of_chans(conv_b), skip_x, of_chans(gate_gain), chan_on], SUB)
+    bc_par = packed_rows([*conv_w[E:].T, conv_b[E:]], SUB)
+    head = packed_rows([of_heads(dt_bias), of_heads(-jnp.exp(a_log)), head_on], SUB)
+    spread = (jnp.arange(chans)[None, :] // HEAD_DIM == jnp.arange(BLOCK)[:, None]).astype(bf16)
+
+    zx = mm(normed, weights)
+    bcd = mm(normed, jnp.concatenate([weights_bc, weights_dt], axis=1))
+    mixed_grad = mm(bgrad, w_out, NT)
+    conv, mix, bc, steps, state, tail, sums = run_forward(
+        keep, zx, bcd, mixed_grad, chan, bc_par, head, spread, lanes, heads
+    )
+    sums = lax.psum(sums[:, :, :2, :], "seq")
+    gate_rate = lax.rsqrt(sums[:, :, 0] / count + epsilon).reshape(rows, 1)
+    gate_pull = gate_rate * gate_rate * gate_rate * sums[:, :, 1].reshape(rows, 1) / count
+    scale = jnp.pad(jnp.concatenate([gate_rate, gate_pull], axis=1), ((0, 0), (0, SUB - 2)))
+    mixed_low = lax.optimization_barrier(
+        (mix * jax.nn.silu(zx[:, :chans]) * gate_rate * chan[GAIN]).astype(bf16)
+    )
+    branch = lax.psum_scatter(mm(mixed_low, w_out).astype(bf16), "seq", scatter_dimension=0, tiled=True).astype(f32)
+    output = (x_rows + row_mask * branch).astype(bf16)
+    out_grad = lax.psum(mm(mixed_low, bgrad, TN).astype(bf16), "width").astype(f32)
+
+    dzx, ddt, dbc, dchan, dhead = run_backward(
+        keep, zx, bcd, mixed_grad, chan, head, spread, conv, mix, bc, steps, state, tail, scale, lanes, heads
+    )
+
+    dbc = lax.psum(dbc, "seq").reshape(peers, lanes, BLOCK, 2 * N)
+    bc_pre = bcd[:, : 2 * N].reshape(peers, lanes, BLOCK, 2 * N)
+    unused, bc_back = jax.vjp(partial(bc_front, keep=keep), bc_pre, conv_w[E:].T, conv_b[E:])
+    dbc_pre, dtaps_bc, dbias_bc = bc_back(dbc)
+    bc_grad = lax.optimization_barrier(dbc_pre.reshape(rows, 2 * N).astype(bf16))
+
+    wide = jnp.concatenate([mm(normed, dzx, TN).astype(bf16), mm(normed, ddt, TN).astype(bf16)], axis=1)
+    wide = wide.reshape(peers, widths, own // widths, -1)
+    wide = lax.psum_scatter(wide, "width", scatter_dimension=1, tiled=True)[:, 0]
+    wide = lax.all_to_all(wide, "seq", 0, 0, tiled=True)
+    wide = lax.all_gather(wide, "width", axis=1, tiled=True).astype(f32)
+    grad_zx = wide[:, :, : 2 * chans].reshape(peers, own, 2, chans).transpose(1, 2, 0, 3).reshape(own, 2 * E)
+    grad_dt = wide[:, :, 2 * chans : 2 * chans + heads].transpose(1, 0, 2).reshape(own, H)
+    normed_cols = lax.dynamic_slice_in_dim(normed, place * own, own, 1)
+    grad_bc = lax.psum(mm(normed_cols, bc_grad, TN), "width")
+
+    wide_grad = mm(dzx, weights, NT) + mm(ddt, weights_dt, NT)
+    normed_grad = lax.psum_scatter(wide_grad.astype(bf16), "seq", scatter_dimension=0, tiled=True).astype(f32)
+    normed_grad = normed_grad + mm(lax.dynamic_slice_in_dim(bc_grad, place * own, own, 0), weights_bc, NT)
+    unit = x_rows * rate
+    pulled = normed_grad * norm_gain
+    input_grad = cot_rows + rate * (pulled - unit * jnp.mean(pulled * unit, axis=-1, keepdims=True))
+    grad_norm = jnp.sum(w_zx.astype(f32) * grad_zx, axis=1) + jnp.sum(w_bc.astype(f32) * grad_bc, axis=1)
+    grad_norm = grad_norm + jnp.sum(w_dt.astype(f32) * grad_dt, axis=1)
+    grad_norm = grad_norm / lax.dynamic_slice_in_dim(norm_gain, place * own, own, 0)
+
+    once = (place == 0).astype(f32)
+    at_heads = lambda a: lax.dynamic_update_slice_in_dim(jnp.zeros((H,), f32), a, first, 0)
+    at_chans = lambda a: lax.dynamic_update_slice_in_dim(jnp.zeros((E,), f32), a, first * HEAD_DIM, 0)
+    taps = [jnp.concatenate([at_chans(dchan[k]), dtaps_bc[k] * once]) for k in range(KCONV)]
+    bias = jnp.concatenate([at_chans(dchan[BIAS]), dbias_bc * once])
+    skip = jnp.sum(dchan[SKIP].reshape(heads, HEAD_DIM), axis=1)
+    small = [*taps, bias, at_chans(dchan[GAIN]), at_heads(dhead[0, :heads]), at_heads(dhead[1, :heads]), at_heads(skip)]
+    sizes = [a.shape[0] for a in small]
+    summed = lax.psum(jnp.concatenate(small), ("width", "seq"))
+    pieces = []
+    for size in sizes:
+        pieces.append(lax.dynamic_slice_in_dim(summed, sum(a.shape[0] * peers for a in pieces) + place * (size // peers), size // peers, 0))
+    grad_taps = jnp.stack(pieces[:KCONV], axis=1)
+    grad_bias, grad_gain, grad_dtb, grad_alog, grad_skip = pieces[KCONV:]
+    return (
+        output, input_grad, grad_norm, grad_zx, grad_bc, grad_dt, grad_taps, grad_bias, grad_dtb, grad_alog, grad_skip,
+        grad_gain, out_grad,
+    )
 
 
 def passed_along(array, axis, by):
@@ -26,17 +481,16 @@
 def carried_in(part, axis, combine, identity, reverse):
     count = lax.axis_size(axis)
     place = lax.axis_index(axis)
-    ahead = count - 1 - place if reverse else place
-    gathered = jax.tree.map(lambda a: lax.all_gather(a, axis), part)
+    at = count - 1 - place if reverse else place
+    by = -1 if reverse else 1
     state = jax.tree.map(lambda a, e: jnp.zeros_like(a) + jnp.asarray(e, a.dtype), part, identity)
 
     def one(lap, state):
-        source = count - 1 - lap if reverse else lap
-        return combine(
-            state, jax.tree.map(lambda a: lax.dynamic_index_in_dim(a, source, 0, False), gathered)
-        )
-
-    return lax.fori_loop(0, ahead, one, state)
+        sent = combine(state, part)
+        got = jax.tree.map(lambda a: passed_along(a, axis, by), sent)
+        return jax.tree.map(lambda old, new: jnp.where(at == lap + 1, new, old), state, got)
+
+    return lax.fori_loop(0, count - 1, one, state)
 
 
 def round_value(v):
@@ -230,7 +684,7 @@
     )
 
 
-def body(
+def rows_body(
     tokens,
     cotangent,
     starts,
@@ -415,4 +869,5 @@
         P("seq"),
         P("seq", None),
     )
+    body = heads_body if H % (2 * mesh.shape["seq"]) == 0 else rows_body
     return jax.shard_map(body, mesh=mesh, in_specs=in_specs, out_specs=out_specs, check_vma=False)

time: 2700 us -> 1050 us (0.39)
  waiting for transfers between devices: 2120 us -> 506 us
  blocking collectives: 65.5 us -> 186 us
  other arithmetic: 151 us -> 48 us
  matrix products: 191 us -> 108 us
  Pallas kernels: 0 us -> 58.5 us
    all_gather x5 -> x4, waiting for transfers between devices: 958 us -> 92.4 us  [the longest x1 54.3 us: heads_body(): wide = lax.all_gather(wide, 'width', axis=1, tiled=True).astype(f32)]
    reduce_scatter x4 -> x2, waiting for transfers between devices: 937 us -> 131 us  [the longest x1 86.7 us: heads_body(): lax.psum_scatter(mm(mixed_low, w_out).astype(bf16), 'seq', scatter_dimens...]
    unnamed x12 -> x11, waiting for transfers between devices: 2.19 us -> 144 us
    all_gather x2 -> x1, blocking collectives: 28.3 us -> 162 us  [heads_body(): keep = 1.0 - lax.all_gather(starts, 'seq', axis=0, tiled=True).astype(f32)]
    psum x1 -> x3, waiting for transfers between devices: 217 us -> 121 us  [the longest x1 70.2 us: heads_body(): summed = lax.psum(jnp.concatenate(small), ('width', 'seq'))]
    dot_general x38 -> x11, matrix products: 191 us -> 108 us  [mm(): lax.dot_general(left, right, (dims, ((), ())), precision=precision, prefe...]
    pallas_call x0 -> x2, Pallas kernels: none -> 58.5 us  [the longest x1 33.8 us: run_backward(): pl.pallas_call(partial(backward_kernel, lanes=lanes, heads=heads, blocks=...]
    add x10 -> x1, other arithmetic: 44.9 us -> 4.6 us  [heads_body(): cot_rows + rate * (pulled - unit * jnp.mean(pulled * unit, axis=-1, keepd...]
  transfers between devices with their start and end apart: 13 -> 12, of which waited for: 9 -> 9; matrix products, arithmetic and copies ran while one was open for 8% -> 21% of each run, Pallas kernels for 0% -> 0%
where the time goes in v1:
time: 1050 us; the launch traced here: 1040 us
  waiting for transfers between devices  506 us (48%)
  blocking collectives  186 us (18%)
  matrix products  108 us (10%)
  local copies, waits for them, and re-layouts  104 us (10%)
  Pallas kernels  58.5 us (6%)
  other arithmetic  48 us (5%)
  between operations  14.9 us (1%)
  starting transfers between devices  11.6 us (1%)
    all_gather x1, blocking collectives, heads_body(): keep = 1.0 - lax.all_gather(starts, 'seq', axis=0, tiled=True).astype(f32)  162 us
    unnamed x11, waiting for transfers between devices  144 us
    dot_general x11, matrix products, mm(): lax.dot_general(left, right, (dims, ((), ())), precision=precision, prefe...  108 us
    reduce_scatter x1, waiting for transfers between devices, heads_body(): lax.psum_scatter(mm(mixed_low, w_out).astype(bf16), 'seq', scatter_dimens...  86.7 us
    psum x1, waiting for transfers between devices, heads_body(): summed = lax.psum(jnp.concatenate(small), ('width', 'seq'))  70.2 us
    all_gather x1, waiting for transfers between devices, heads_body(): wide = lax.all_gather(wide, 'width', axis=1, tiled=True).astype(f32)  54.3 us
    reduce_scatter x1, waiting for transfers between devices, heads_body(): lax.psum_scatter(wide_grad.astype(bf16), 'seq', scatter_dimension=0, tile...  44.4 us
    psum x1, waiting for transfers between devices, heads_body(): grad_bc = lax.psum(mm(normed_cols, bc_grad, TN), 'width')  42.2 us
  transfers between devices with their start and end apart: 12, of which 9 were waited for; matrix products, arithmetic and copies ran while one was open for 21% of the time, Pallas kernels for 0%

profile of v1, /device:TPU:9, one launch (start us, length us, event | category | flops | bytes accessed | tf_op | source)
XLA Modules:
  0.0 1037.0 jit_solution(9325085524718919222)
XLA Ops:
  17.3 6.4 copy.85
  28.3 5.8 all-to-all-start
  34.1 161.8 %all-gather = s32[8,1,2]{2,1,0:T(1,128)S(1)} all-gather(s32[1,1,2]{2,1,0:T(1,128)S(1)} %bitcast.136), channel_id=1, replica_groups=mesh['width'=4,'seq'=8] {'seq'}, dimensions={0}, use_global_device_ids=true | all-gather | bytes 72 | tf_op jit(solution)/shard_map/all_gather | solution.py:393
  213.6 9.9 fusion.16.bcd_ref
  223.6 11.4 %fusion.44.zx_ref = f32[2048,1024]{1,0:T(8,128)} fusion(bf16[2048,2048]{1,0:T(8,128)(2,1)S(1)} %copy-done.30, bf16[2048,1024]{0,1:T(8,128)(2,1)S(1)} %bitcast.105), kind=kOutput, calls=%fused_computation.122 | convolution fusion | flops 8589934592 | bytes 20971520 | tf_op jit(solution)/shard_map/dot_general | solution.py:29
  235.0 38.1 %all-gather.10.cloned.1.call-done = bf16[2048,2048]{1,0:T(8,128)(2,1)} async-done(((bf16[256,2048]{1,0:T(8,128)(2,1)}), bf16[2048,2048]{1,0:T(8,128)(2,1)}) %all-gather.10.cloned.1.call-update) | async-done | bytes 8388624 | tf_op jit(solution)/shard_map/all_gather | solution.py:391
  273.1 9.8 fusion.45.grad_ref
  282.9 24.6 %mix_forward.1 = (f32[2048,512]{1,0:T(8,128)S(1)}, f32[2048,512]{1,0:T(8,128)}, bf16[2048,256]{1,0:T(8,128)(2,1)S(1)}, f32[2048,256]{1,0:T(8,128)S(1)}, f32[8,2,...) custom-call(f32[8,2]{1,0:T(8,128)S(1)} %copy-done.7, f32[2048,1024]{1,0:T(8,128)} %fusion.44.zx_ref, ...), custom_call_target="tpu_custom_call" | custom-call | flops 2147483648 | bytes 33554432 | tf_op jit(solution)/shard_map/mix_forward/pallas_call | solution.py:292
  311.5 24.0 %psum.35 = f32[8,2,2,128]{3,2,1,0:T(2,128)} all-reduce(f32[8,2,2,128]{3,2,1,0:T(2,128)} %slice.96), channel_id=1, replica_groups=mesh['width'=4,'seq'=8] {'seq'}, use_global_device_ids=true, to_apply=%region_1.2 | all-reduce | flops 4096 | bytes 32768 | tf_op jit(solution)/shard_map/psum | solution.py:414
  340.9 33.8 %mix_backward.1 = (bf16[2048,1024]{1,0:T(8,128)(2,1)}, bf16[2048,128]{1,0:T(8,128)(2,1)S(1)}, f32[2048,256]{1,0:T(8,128)S(1)}, f32[8,512]{1,0:T(8,128)S(1)}, f32[8,128]{1,0:T(8,128)S(1)}) custom-call(f32[8,2]{1,0:T(8,128)S(1)} %copy-done.8, f32[2048,1024]{1,0:T(8,128)} %fusion.44.zx_ref, f32[2048,384]{1,0:T(8,128)} %fusion.16.bcd_ref, ...), custom_call_target="tpu_custom_call" | custom-call | flops 6442450944 | bytes 41943040 | tf_op jit(solution)/shard_map/mix_backward/pallas_call | solution.py:327
  378.2 21.2 %convolution_convert_fusion.1 = bf16[2048,1024]{0,1:T(8,128)(2,1)S(1)} fusion(bf16[2048,2048]{1,0:T(8,128)(2,1)} %all-gather.6.cloned.1.call-done, bf16[2048,1024]{1,0:T(8,128)(2,1)} %get-tuple-element.32), kind=kOutput, calls=%fused_computation.5 | convolution fusion | flops 8592031744 | bytes 16777216 | tf_op jit(solution)/shard_map/dot_general | solution.py:29
  399.5 4.8 convolution_convert_fusion.3
  406.8 6.8 copy.93
  417.8 10.1 convolution_convert_fusion.2
  435.9 8.6 all-reduce.24.cloned.1.call-done
  444.5 9.3 multiply_reduce_fusion.3
  453.8 143.4 %all-reduce.30.cloned.1.call-done = (bf16[8,4,64,1152]{3,2,1,0:T(8,128)(2,1)}, bf16[512,2048]{1,0:T(8,128)(2,1)}) async-done(((bf16[8,4,64,1152]{3,2,1,0:T(8,128)(2,1)}, bf16[512,2048]{1,0:T(8,128)(2,1)}), (bf16[8,4,64,1152]{3,2,1,0:T(8,128)(2,1)}, bf16[512,2048]{1,0:T(8,128)(2,1)})) %all-reduce.30.cloned.1.call-update) | async-done | bytes 6815760
  600.2 5.5 all-to-all-start.1
  614.0 17.8 %all-to-all-done.1 = bf16[8,64,1152]{2,1,0:T(8,128)(2,1)} async-done(((bf16[8,64,1152]{2,1,0:T(8,128)(2,1)}), bf16[8,64,1152]{2,1,0:T(8,128)(2,1)}, u32[]{:S(2)}, u32[]{:S(2)}) %all-to-all-start.1) | async-done | bytes 1179680 | tf_op jit(solution)/shard_map/all_to_all | solution.py:438
  631.8 15.3 %fusion.46 = f32[2048,2048]{1,0:T(8,128)} fusion(bf16[2048,1024]{1,0:T(8,128)(2,1)} %get-tuple-element.32, bf16[2048,1024]{0,1:T(8,128)(2,1)} %bitcast.104), kind=kOutput, calls=%fused_computation.124 | convolution fusion | flops 8589934592 | bytes 25165824 | tf_op jit(solution)/shard_map/dot_general | solution.py:29
  647.2 11.4 %add_convert_fusion = bf16[2048,2048]{1,0:T(8,128)(2,1)} fusion(f32[2048,2048]{1,0:T(8,128)} %fusion.46, bf16[2048,128]{1,0:T(8,128)(2,1)S(1)} %copy-done.6, bf16[2048,8]{1,0:T(8,128)(2,1)S(1)} %copy-done.21), kind=kOutput, calls=%fused_computation | convolution fusion | flops 1082130432 | bytes 25722880 | tf_op jit(solution)/shard_map/dot_general | solution.py:29
  658.7 8.4 convolution_convert_fusion
  667.1 70.2 %all-reduce.28.cloned.1.call-done = f32[26048]{0:T(1024)} async-done(((f32[26048]{0:T(1024)}), f32[26048]{0:T(1024)}) %all-reduce.28.cloned.1.call-update) | async-done | bytes 104208 | tf_op jit(solution)/shard_map/psum | solution.py:463
  742.1 42.2 %all-reduce.26.cloned.1.call-done = f32[256,256]{1,0:T(8,128)} async-done(((f32[256,256]{1,0:T(8,128)}), f32[256,256]{1,0:T(8,128)}) %all-reduce.26.cloned.1.call-update) | async-done | bytes 262160 | tf_op jit(solution)/shard_map/psum | solution.py:443
  789.5 54.3 %all-gather.12.cloned.1.call-done = bf16[8,256,1152]{2,1,0:T(8,128)(2,1)} async-done(((bf16[8,64,1152]{2,1,0:T(8,128)(2,1)}), bf16[8,256,1152]{2,1,0:T(8,128)(2,1)}) %all-gather.12.cloned.1.call-update) | async-done | bytes 4718608 | tf_op jit(solution)/shard_map/all_gather | solution.py:439
  843.9 6.6 slice.130
  850.5 11.9 %reshape.261 = f32[8,256,2,512]{3,2,1,0:T(2,128)} reshape(f32[8,256,1024]{2,1,0:T(8,128)} %slice.130) | data formatting | bytes 16777216 | tf_op jit(solution)/shard_map/reshape | solution.py:440
  862.4 8.5 copy.94
  870.9 11.2 %copy.99 = f32[32,8,16,512]{3,1,2,0:T(8,128)} copy(f32[32,8,16,512]{3,2,1,0:T(8,128)S(1)} %bitcast.96) | data formatting | bytes 16777216
  883.5 5.8 multiply_reduce_fusion
  890.0 44.4 %reduce-scatter.8.cloned.1.call-done = bf16[256,2048]{1,0:T(8,128)(2,1)} async-done(((bf16[2048,2048]{1,0:T(8,128)(2,1)}), bf16[256,2048]{1,0:T(8,128)(2,1)}) %reduce-scatter.8.cloned.1.call-update) | async-done | bytes 1048592 | tf_op jit(solution)/shard_map/reduce_scatter | solution.py:446
  937.9 86.7 %reduce-scatter.6.cloned.1.call-done = bf16[256,2048]{1,0:T(8,128)(2,1)} async-done(((bf16[2048,2048]{1,0:T(8,128)(2,1)}), bf16[256,2048]{1,0:T(8,128)(2,1)}) %reduce-scatter.6.cloned.1.call-update) | async-done | bytes 1048592 | tf_op jit(solution)/shard_map/reduce_scatter | solution.py:421
  (224 shorter events, 92.2 us)
Async XLA Ops:
  7.2 265.9 %copy-start = (bf16[512,2048]{1,0:T(8,128)(2,1)S(1)}, bf16[512,2048]{1,0:T(8,128)(2,1)}, u32[]{:S(2)}) copy-start(bf16[512,2048]{1,0:T(8,128)(2,1)} %param.29) | copy-start | bytes 6291460
  7.2 195.4 %all-gather.8.cloned.1.call-start = ((), (), s32[]{:S(2)}) async-start(), calls=%async_computation.5 | async-start | bytes 1769472 | tf_op jit(solution)/shard_map/all_gather | solution.py:392
  10.0 203.7 %all-gather.6.cloned.1.call-start = ((), (), s32[]{:S(2)}) async-start(), calls=%async_computation.4 | async-start | bytes 9437184 | tf_op jit(solution)/shard_map/all_gather | solution.py:390
  14.1 259.0 %all-gather.10.cloned.1.call-start = ((), (), s32[]{:S(2)}) async-start(), calls=%async_computation.6 | async-start | bytes 9437184 | tf_op jit(solution)/shard_map/all_gather | solution.py:391
  28.3 167.6 %copy-start.44 = (f32[64]{0:T(128)S(1)}, f32[64]{0:T(128)}, u32[]{:S(2)}) copy-start(f32[64]{0:T(128)} %param.26) | copy-start | bytes 772
  28.3 167.7 %copy-start.45 = (f32[64]{0:T(128)S(1)}, f32[64]{0:T(128)}, u32[]{:S(2)}) copy-start(f32[64]{0:T(128)} %param.25) | copy-start | bytes 772
  28.3 167.7 %copy-start.46 = (f32[64]{0:T(128)S(1)}, f32[64]{0:T(128)}, u32[]{:S(2)}) copy-start(f32[64]{0:T(128)} %param.27) | copy-start | bytes 772
  28.3 177.3 %all-to-all-start = ((bf16[256,2,8,512]{0,3,1,2:T(8,128)(2,1)}), bf16[256,2,8,512]{0,3,1,2:T(8,128)(2,1)}, u32[]{:S(2)}, u32[]{:S(2)}) async-start(bf16[256,2,8,512]{0,3,1,2:T(8,128)(2,1)} %copy.86), calls=%async_computation | async-start | bytes 8388608 | tf_op jit(solution)/shard_map/all_to_all | solution.py:389
  34.1 410.4 %all-reduce.24.cloned.1.call-start = ((), (), s32[]{:S(2)}) async-start(), calls=%async_computation.9 | async-start | bytes 4194304 | tf_op jit(solution)/shard_map/psum | solution.py:429
  213.6 9.9 copy-start.22
  213.6 9.9 copy-start.30
  273.1 9.8 copy-start.1
  273.1 9.8 copy-start.7
  273.1 9.8 copy-start.10
  273.1 9.8 copy-start.12
  378.1 219.1 %all-reduce.30.cloned.1.call-start = ((), (), s32[]{:S(2)}) async-start(), calls=%async_computation.13 | async-start | bytes 13631488
  378.2 21.3 %copy-start.6 = (bf16[2048,128]{1,0:T(8,128)(2,1)S(1)}, bf16[2048,128]{1,0:T(8,128)(2,1)}, u32[]{:S(2)}) copy-start(bf16[2048,128]{1,0:T(8,128)(2,1)} %copy-done.5) | copy-start | bytes 1572868
  417.8 10.1 copy-start.23
  429.2 15.3 %copy-start.39 = (f32[256]{0:T(256)S(1)}, f32[256]{0:T(256)}, u32[]{:S(2)}) copy-start(f32[256]{0:T(256)} %copy-done.38) | copy-start | bytes 3076
  600.2 31.5 %all-to-all-start.1 = ((bf16[8,64,1152]{2,1,0:T(8,128)(2,1)}), bf16[8,64,1152]{2,1,0:T(8,128)(2,1)}, u32[]{:S(2)}, u32[]{:S(2)}) async-start(bf16[8,64,1152]{2,1,0:T(8,128)(2,1)} %dynamic-slice_bitcast_fusion), calls=%async_computation.3 | async-start | bytes 2359296 | tf_op jit(solution)/shard_map/all_to_all | solution.py:438
  605.7 131.6 %all-reduce.28.cloned.1.call-start = ((), (), s32[]{:S(2)}) async-start(), calls=%async_computation.12 | async-start | bytes 212992 | tf_op jit(solution)/shard_map/psum | solution.py:463
  606.5 177.9 %all-reduce.26.cloned.1.call-start = ((), (), s32[]{:S(2)}) async-start(), calls=%async_computation.11 | async-start | bytes 524288 | tf_op jit(solution)/shard_map/psum | solution.py:443
  613.9 229.9 %all-gather.12.cloned.1.call-start = ((), (), s32[]{:S(2)}) async-start(), calls=%async_computation.10 | async-start | bytes 5898240 | tf_op jit(solution)/shard_map/all_gather | solution.py:439
  631.8 15.4 %copy-start.21 = (bf16[2048,8]{1,0:T(8,128)(2,1)S(1)}, bf16[2048,8]{1,0:T(8,128)(2,1)}, u32[]{:S(2)}) copy-start(bf16[2048,8]{1,0:T(8,128)(2,1)} %copy-done.20) | copy-start | bytes 98308
  631.8 302.6 %reduce-scatter.8.cloned.1.call-start = ((), (), s32[]{:S(2)}) async-start(), calls=%async_computation.8 | async-start | bytes 9437184 | tf_op jit(solution)/shard_map/reduce_scatter | solution.py:446
  658.6 366.0 %reduce-scatter.6.cloned.1.call-start = ((), (), s32[]{:S(2)}) async-start(), calls=%async_computation.7 | async-start | bytes 9437184 | tf_op jit(solution)/shard_map/reduce_scatter | solution.py:421
  667.1 117.3 %copy-start.25 = (bf16[256,256]{1,0:T(8,128)(2,1)S(1)}, bf16[256,256]{1,0:T(8,128)(2,1)}, u32[]{:S(2)}) copy-start(bf16[256,256]{1,0:T(8,128)(2,1)} %param.21) | copy-start | bytes 393220
  862.4 19.7 %slice-start = ((s8[4718592]{0:T(1024)(128)(4,1)}), s8[4194304]{0:T(1024)(128)(4,1)S(1)}, s32[]{:S(2)}) async-start(s8[4718592]{0:T(1024)(128)(4,1)} %bitcast.91), calls=%async_computation.14 | async-start | bytes 8388608
  870.9 11.2 %slice-start.1 = ((s8[4718592]{0:T(1024)(128)(4,1)}), s8[524288]{0:T(1024)(128)(4,1)S(1)}, s32[]{:S(2)}) async-start(s8[4718592]{0:T(1024)(128)(4,1)} %bitcast.91), calls=%async_computation.15 | async-start | bytes 1048576
  883.5 50.9 %copy-start.17 = (bf16[256,2048]{1,0:T(8,128)(2,1)S(1)}, bf16[256,2048]{1,0:T(8,128)(2,1)}, u32[]{:S(2)}) copy-start(bf16[256,2048]{1,0:T(8,128)(2,1)} %param.15) | copy-start | bytes 3145732
  883.5 50.8 %copy-start.37 = (f32[256]{0:T(256)S(1)}, f32[256]{0:T(256)}, u32[]{:S(2)}) copy-start(f32[256]{0:T(256)} %copy-done.36) | copy-start | bytes 3076
  890.0 134.7 %copy-start.41 = (f32[256]{0:T(256)S(1)}, f32[256]{0:T(256)}, u32[]{:S(2)}) copy-start(f32[256]{0:T(256)} %copy-done.40) | copy-start | bytes 3076
  (31 other events, 74.8 us)
Sparse Core Ops, SparseCore 0:
  10.3 26.5 all-gather.7
  39.0 142.9 all-gather.5
  184.2 88.7 all-gather.9
  378.2 66.2 all-reduce.23
  447.9 149.2 all-reduce.29
  611.7 125.5 all-reduce.27
  740.8 43.4 all-reduce.25
  786.3 57.4 all-gather.11
  846.3 88.0 reduce-scatter.7
  936.6 87.9 reduce-scatter.5

commit v2 on v1

--- a/solution.py
+++ b/solution.py
@@ -74,7 +74,7 @@
 
 
 def forward_kernel(
-    keep_ref, zx_ref, bcd_ref, grad_ref, chan_ref, bc_par_ref, head_ref, spread_ref,
+    keep_ref, zx_ref, grad_ref, chan_ref, bc_par_ref, head_ref, spread_ref,
     conv_ref, mix_ref, bc_ref, step_ref, state_ref, tail_ref, sums_ref,
     state, tail_x, tail_b, pad_x, pad_b,
     *, lanes, heads,
@@ -95,7 +95,7 @@
     for lane in range(lanes):
         rows = pl.ds(lane * BLOCK, BLOCK)
         keep = keep_ref[c, lane]
-        pre = zx_ref[rows, width:]
+        pre = zx_ref[rows, width : 2 * width]
         pad_x[lane, 0:SUB] = tail_x[lane] * keep
         pad_x[lane, SUB:] = pre
         tail_ref[0, lane] = tail_x[lane] * keep
@@ -106,7 +106,7 @@
         conv_ref[rows, :] = conv
         x_low = (conv * sigmoid(conv) * chan_ref[MASK : MASK + 1, :]).astype(bf16)
 
-        pre_b = bcd_ref[rows, : 2 * N]
+        pre_b = zx_ref[rows, 2 * width + BLOCK :]
         pad_b[lane, 0:SUB] = tail_b[lane] * keep
         pad_b[lane, SUB:] = pre_b
         tail_b[lane] = pre_b[BLOCK - SUB :, :]
@@ -117,7 +117,7 @@
         bc_ref[rows, :] = bc_low
         b_low, c_low = bc_low[:, :N], bc_low[:, N:]
 
-        raw = bcd_ref[rows, 2 * N :] + head_ref[DT_BIAS : DT_BIAS + 1, :]
+        raw = zx_ref[rows, 2 * width : 2 * width + BLOCK] + head_ref[DT_BIAS : DT_BIAS + 1, :]
         dt = softplus(raw) * head_ref[HEAD_MASK : HEAD_MASK + 1, :]
         cum = mm(tril, head_ref[NEG_A : NEG_A + 1, :] * dt, precision=highest)
         step_ref[rows, :BLOCK] = cum
@@ -158,9 +158,9 @@
 
 
 def backward_kernel(
-    keep_ref, zx_ref, bcd_ref, grad_ref, chan_ref, head_ref, spread_ref,
+    keep_ref, zx_ref, grad_ref, chan_ref, head_ref, spread_ref,
     conv_ref, mix_ref, bc_ref, step_ref, state_ref, tail_ref, scale_ref,
-    dzx_ref, ddt_ref, dbc_ref, dchan_ref, dhead_ref,
+    dzx_ref, dbc_ref, dchan_ref, dhead_ref,
     state_grad, next_conv, pad_x, pad_d,
     *, lanes, heads, blocks,
 ):
@@ -249,8 +249,8 @@
         weighted = (x_f * end_x).astype(bf16)
         db = mm(weighted, sg_high, NT) + mm(weighted, sg_low, NT)
         db = db + mm(di_high, c_low, TN) + mm(di_low, c_low, TN)
-        dbc_ref[rows, :N] = db
-        dbc_ref[rows, N:] = dc
+        dbc_ref[:N, rows] = db.T.astype(bf16)
+        dbc_ref[N:, rows] = dc.T.astype(bf16)
         dweighted = mm(b_low, sg_high) + mm(b_low, sg_low)
         dx = dx_within + dweighted * end_x
         dcum = mm_left(dlow_f * (mixed - skip * x_f) - x_f * dx, spread, NT)
@@ -260,9 +260,9 @@
         dlog = mm(triu, dcum, precision=highest) + dlast
         neg_a = head_ref[NEG_A : NEG_A + 1, :]
         ddt = ddt_within + dend * to_last + dlog * neg_a
-        raw = bcd_ref[rows, 2 * N :] + head_ref[DT_BIAS : DT_BIAS + 1, :]
+        raw = zx_ref[rows, 2 * width : 2 * width + BLOCK] + head_ref[DT_BIAS : DT_BIAS + 1, :]
         draw = ddt * sigmoid(raw) * head_ref[HEAD_MASK : HEAD_MASK + 1, :]
-        ddt_ref[rows, :] = draw.astype(bf16)
+        dzx_ref[rows, 2 * width :] = draw.astype(bf16)
         dhead_ref[0:1, :] += total(draw)
         dhead_ref[1:2, :] += total(dlog * neg_a * dt)
         state_grad[lane] = keep * (mm(c_low, dc_high, TN) + mm(c_low, dc_low, TN) + last_x * sgrad)
@@ -273,16 +273,54 @@
         pad_d[lane, BLOCK:] = next_conv[lane]
         next_conv[lane] = dconv[:SUB] * keep
         pad_x[lane, :SUB] = tail_ref[0, lane]
-        pad_x[lane, SUB:] = zx_ref[rows, width:]
+        pad_x[lane, SUB:] = zx_ref[rows, width : 2 * width]
         dpre = jnp.zeros((BLOCK, width), f32)
         for k in range(KCONV):
             dpre = dpre + pad_d[lane, KCONV - 1 - k : KCONV - 1 - k + BLOCK, :] * chan_ref[k : k + 1, :]
             dchan_ref[k : k + 1, :] += total(dconv * pad_x[lane, SUB - KCONV + 1 + k : SUB - KCONV + 1 + k + BLOCK, :])
         dchan_ref[BIAS : BIAS + 1, :] += total(dconv)
-        dzx_ref[rows, width:] = dpre.astype(bf16)
-
-
-def run_forward(keep, zx, bcd, grad, chan, bc_par, head, spread, lanes, heads):
+        dzx_ref[rows, width : 2 * width] = dpre.astype(bf16)
+
+
+def entry_kernel(valid_ref, start_ref, x_ref, cot_ref, gain_ref, bc_ref, dt_ref, normed_ref, bgrad_ref, third_ref, starts_ref, *, peers):
+    rows = x_ref.shape[0]
+    lanes = rows // BLOCK
+    x = x_ref[...].astype(f32)
+    normed_ref[...] = (x * lax.rsqrt(jnp.mean(x * x, axis=-1, keepdims=True) + epsilon) * gain_ref[...]).astype(bf16)
+    row = lax.broadcasted_iota(jnp.int32, (BLOCK, 1), 0)
+    for lane in range(lanes):
+        at = slice(lane * BLOCK, (lane + 1) * BLOCK)
+        mask = (row < valid_ref[0, lane]).astype(f32)
+        bgrad_ref[at, :] = (cot_ref[at, :].astype(f32) * mask).astype(bf16)
+    bc, dt = bc_ref[...].astype(f32), dt_ref[...].astype(f32)
+    share, heads = bc.shape[1] // peers, dt.shape[1] // peers
+    rest = jnp.zeros((rows, BLOCK - share - heads), f32)
+    for s in range(peers):
+        tile = [dt[:, s * heads : (s + 1) * heads], bc[:, s * share : (s + 1) * share], rest]
+        third_ref[s] = jnp.concatenate(tile, axis=1).astype(bf16)
+    lane = lax.broadcasted_iota(jnp.int32, (SUB, BLOCK), 1)
+    tile = jnp.zeros((SUB, BLOCK), f32)
+    for l in range(lanes):
+        tile = jnp.where(lane == l, start_ref[0, l].astype(f32), tile)
+    starts_ref[...] = tile
+
+
+def entry(valid, starts, tokens, cotangent, gain, w_bc, w_dt, peers):
+    smem, vmem = pl.BlockSpec(memory_space=pltpu.SMEM), pl.BlockSpec(memory_space=pltpu.VMEM)
+    return pl.pallas_call(
+        partial(entry_kernel, peers=peers),
+        in_specs=[smem] * 2 + [vmem] * 5,
+        out_specs=[vmem] * 4,
+        out_shape=[
+            jax.ShapeDtypeStruct(tokens.shape, bf16), jax.ShapeDtypeStruct(tokens.shape, bf16),
+            jax.ShapeDtypeStruct((peers, w_bc.shape[0], BLOCK), bf16), jax.ShapeDtypeStruct((SUB, BLOCK), f32),
+        ],
+        compiler_params=pltpu.CompilerParams(vmem_limit_bytes=32 << 20),
+        name="entry",
+    )(valid, starts, tokens, cotangent, gain[None], w_bc, w_dt)
+
+
+def run_forward(keep, zx, grad, chan, bc_par, head, spread, lanes, heads):
     rows, width = grad.shape
     step = lanes * BLOCK
     blocks = rows // step
@@ -293,7 +331,7 @@
         partial(forward_kernel, lanes=lanes, heads=heads),
         grid=(blocks,),
         in_specs=[
-            pl.BlockSpec(memory_space=pltpu.SMEM), by_block(2 * width), by_block(2 * N + BLOCK), by_block(width),
+            pl.BlockSpec(memory_space=pltpu.SMEM), by_block(zx.shape[1]), by_block(width),
             whole(chan), whole(bc_par), whole(head), whole(spread),
         ],
         out_specs=[
@@ -313,10 +351,10 @@
         compiler_params=pltpu.CompilerParams(vmem_limit_bytes=40 << 20, dimension_semantics=("arbitrary",)),
         cost_estimate=pl.CostEstimate(flops=rows * width * 2048, bytes_accessed=rows * width * 32, transcendentals=rows * width * 4),
         name="mix_forward",
-    )(keep, zx, bcd, grad, chan, bc_par, head, spread)
-
-
-def run_backward(keep, zx, bcd, grad, chan, head, spread, conv, mix, bc, step_arr, state, tail, scale, lanes, heads):
+    )(keep, zx, grad, chan, bc_par, head, spread)
+
+
+def run_backward(keep, zx, grad, chan, head, spread, conv, mix, bc, step_arr, state, tail, scale, lanes, heads):
     rows, width = grad.shape
     step = lanes * BLOCK
     blocks = rows // step
@@ -328,15 +366,18 @@
         partial(backward_kernel, lanes=lanes, heads=heads, blocks=blocks),
         grid=(blocks,),
         in_specs=[
-            pl.BlockSpec(memory_space=pltpu.SMEM), by_block(2 * width), by_block(2 * N + BLOCK), by_block(width),
+            pl.BlockSpec(memory_space=pltpu.SMEM), by_block(2 * width + BLOCK), by_block(width),
             whole(chan), whole(head), whole(spread),
             by_block(width), by_block(width), by_block(2 * N), by_block(2 * BLOCK),
             per_lane(N, width), per_lane(SUB, width), by_block(SUB),
         ],
-        out_specs=[by_block(2 * width), by_block(BLOCK), by_block(2 * N), fixed((SUB, width)), fixed((SUB, BLOCK))],
+        out_specs=[
+            by_block(2 * width + BLOCK), pl.BlockSpec((2 * N, step), lambda c: (0, blocks - 1 - c)),
+            fixed((SUB, width)), fixed((SUB, BLOCK)),
+        ],
         out_shape=[
-            jax.ShapeDtypeStruct((rows, 2 * width), bf16), jax.ShapeDtypeStruct((rows, BLOCK), bf16),
-            jax.ShapeDtypeStruct((rows, 2 * N), f32), jax.ShapeDtypeStruct((SUB, width), f32),
+            jax.ShapeDtypeStruct((rows, 2 * width + BLOCK), bf16),
+            jax.ShapeDtypeStruct((2 * N, rows), bf16), jax.ShapeDtypeStruct((SUB, width), f32),
             jax.ShapeDtypeStruct((SUB, BLOCK), f32),
         ],
         scratch_shapes=[
@@ -346,17 +387,516 @@
         compiler_params=pltpu.CompilerParams(vmem_limit_bytes=48 << 20, dimension_semantics=("arbitrary",)),
         cost_estimate=pl.CostEstimate(flops=rows * width * 6144, bytes_accessed=rows * width * 40, transcendentals=rows * width * 6),
         name="mix_backward",
-    )(keep, zx, bcd, grad, chan, head, spread, conv, mix, bc, step_arr, state, tail, scale)
-
-
-def bc_front(bc_pre, taps, bias, keep):
-    rim = bc_pre[:, :, BLOCK - KCONV + 1 :, :]
-    before = jnp.concatenate([jnp.zeros_like(rim[:1]), rim[:-1]], axis=0) * keep[:, :, None, None]
-    padded = jnp.concatenate([before, bc_pre], axis=2)
-    out = bias
-    for k in range(KCONV):
-        out = out + padded[:, :, k : k + BLOCK, :] * taps[k]
-    return jax.nn.silu(out)
+    )(keep, zx, grad, chan, head, spread, conv, mix, bc, step_arr, state, tail, scale)
+
+
+MESH = pl.DeviceIdType.MESH
+
+
+def greet(others):
+    barrier = pltpu.get_barrier_semaphore()
+    for other in others:
+        pl.semaphore_signal(barrier, inc=1, device_id=other, device_id_type=MESH)
+    pl.semaphore_wait(barrier, len(others))
+
+
+def gather_kernel(
+    zx_ref, third_ref, bc_ref, own_ref, start_ref, w_ref, rows_ref, starts_ref,
+    w_send, w_recv, st_send, st_recv, own_sem, wide_send, wide_recv,
+    up_send, up_recv, down_send, down_recv, mate_send, mate_recv,
+    *, peers, widths, chans,
+):
+    width, place = lax.axis_index("width"), lax.axis_index("seq")
+    chips = peers // 2
+    chip = place // 2
+    quarter = zx_ref.shape[0] // widths
+    ring = [lax.rem(place + by, peers) for by in range(1, peers)]
+    cross = [jnp.bitwise_xor(width, m) for m in range(1, widths)]
+    greet([(width, s) for s in ring] + [(w, place) for w in cross])
+    mine = pl.ds(pl.multiple_of(width * quarter, quarter), quarter)
+
+    def remote(src, dst, send, recv, device):
+        return pltpu.make_async_remote_copy(
+            src_ref=src, dst_ref=dst, send_sem=send, recv_sem=recv, device_id=device, device_id_type=MESH
+        )
+
+    def columns(half, s):
+        return pl.ds(pl.multiple_of(half * peers * chans + s * chans, 128), chans)
+
+    wide = 2 * chans
+    spots = [pl.ds(0, chans), pl.ds(chans, chans), pl.ds(wide, BLOCK), pl.ds(wide + BLOCK, 2 * N)]
+
+    def parts(s):
+        return [zx_ref.at[mine, columns(0, s)], zx_ref.at[mine, columns(1, s)], third_ref.at[s, mine], bc_ref.at[mine]]
+
+    pushes = []
+    for i, s in enumerate(ring):
+        for k, (part, spot) in enumerate(zip(parts(s), spots)):
+            pushes.append(remote(part, w_ref.at[place, width, :, spot], w_send.at[k, i], w_recv.at[k, i], (width, s)))
+        pushes.append(remote(start_ref, starts_ref.at[place], st_send.at[i], st_recv.at[i], (width, s)))
+    for push in pushes:
+        push.start()
+    keeps = [
+        pltpu.make_async_copy(part, w_ref.at[place, width, :, spot], own_sem.at[k])
+        for k, (part, spot) in enumerate(zip(parts(place), spots))
+    ]
+    keeps.append(pltpu.make_async_copy(start_ref, starts_ref.at[place], own_sem.at[4]))
+    keeps.append(pltpu.make_async_copy(own_ref, rows_ref.at[place], own_sem.at[5]))
+    for keep in keeps:
+        keep.start()
+
+    def hop(ref, s, step, by):
+        send, recv = (up_send, up_recv) if by > 0 else (down_send, down_recv)
+        return remote(ref, rows_ref.at[s], send.at[step], recv.at[step], (width, jnp.clip(place + 2 * by, 0, peers - 1)))
+
+    def over(ref, s, slot):
+        return remote(ref, rows_ref.at[s], mate_send.at[slot], mate_recv.at[slot], (width, jnp.bitwise_xor(place, 1)))
+
+    def inside(by):
+        return chip + 1 < chips if by > 0 else chip > 0
+
+    def reached(by, step):
+        return chip >= step if by > 0 else chip + step < chips
+
+    for by in (1, -1):
+        @pl.when(inside(by))
+        def _():
+            hop(own_ref, place, 0, by).start()
+    over(own_ref, place, 0).start()
+
+    for push in pushes:
+        push.wait_recv()
+    for keep in keeps:
+        keep.wait()
+    shares = []
+    for m, w in enumerate(cross):
+        shares.append(remote(w_ref.at[:, width], w_ref.at[:, width], wide_send.at[m], wide_recv.at[m], (w, place)))
+    for share in shares:
+        share.start()
+
+    for step in range(1, chips):
+        for by in (1, -1):
+            @pl.when(reached(by, step))
+            def _():
+                s = jnp.clip(place - 2 * by * step, 0, peers - 1)
+                ref = rows_ref.at[s]
+                hop(ref, s, step - 1, by).wait_recv()
+
+                @pl.when(inside(by))
+                def _():
+                    hop(ref, s, step, by).start()
+                over(ref, s, 2 * step - (by > 0)).start()
+
+    for share in shares:
+        share.wait()
+    for push in pushes:
+        push.wait_send()
+    over(own_ref, place, 0).wait()
+    for step in range(chips):
+        for by in (1, -1):
+            if step:
+                @pl.when(reached(by, step))
+                def _():
+                    s = jnp.clip(place - 2 * by * step, 0, peers - 1)
+                    over(rows_ref.at[s], s, 2 * step - (by > 0)).wait()
+
+            @pl.when(inside(by) & reached(by, step))
+            def _():
+                s = jnp.clip(place - 2 * by * step, 0, peers - 1)
+                hop(rows_ref.at[s], s, step, by).wait_send()
+
+
+def gathered_in(w_zx, third, w_bc, own_rows, start_tile, chans):
+    peers, widths = lax.axis_size("seq"), lax.axis_size("width")
+    own, model = own_rows.shape
+    quarter = own // widths
+    dma = pltpu.SemaphoreType.DMA
+    chips = peers // 2
+    anywhere = pl.BlockSpec(memory_space=pl.ANY)
+    return pl.pallas_call(
+        partial(gather_kernel, peers=peers, widths=widths, chans=chans),
+        in_specs=[anywhere] * 5,
+        out_specs=[anywhere] * 3,
+        out_shape=[
+            jax.ShapeDtypeStruct((peers, widths, quarter, 2 * chans + BLOCK + 2 * N), bf16),
+            jax.ShapeDtypeStruct((peers, own, model), bf16),
+            jax.ShapeDtypeStruct((peers,) + start_tile.shape, f32),
+        ],
+        scratch_shapes=[
+            dma((4, peers - 1)), dma((4, peers - 1)), dma((peers - 1,)), dma((peers - 1,)),
+            dma((6,)), dma((widths - 1,)), dma((widths - 1,)),
+            dma((chips,)), dma((chips,)), dma((chips,)), dma((chips,)), dma((2 * chips,)), dma((2 * chips,)),
+        ],
+        compiler_params=pltpu.CompilerParams(collective_id=1, has_side_effects=True),
+        name="gather_in",
+    )(w_zx, third, w_bc, own_rows, start_tile)
+
+
+ROWS_AT_ONCE = 16
+
+
+def add_into(dst, others, rows):
+    @pl.loop(0, rows // ROWS_AT_ONCE)
+    def _(i):
+        at = pl.ds(pl.multiple_of(i * ROWS_AT_ONCE, ROWS_AT_ONCE), ROWS_AT_ONCE)
+        value = dst[at].astype(f32)
+        for other in others:
+            value = value + other[at].astype(f32)
+        dst[at] = value.astype(dst.dtype)
+
+
+def scatter_kernel(
+    part_ref, wide_ref, third_ref, x_ref, cot_ref, gain_ref, rows_ref, out_ref, out_third_ref,
+    mine, from_core, up, down, own0, own1, own2, got0, got1, got2, piece0, piece1, piece2,
+    local_sem, core_send, core_recv, up_send, up_recv, down_send, down_recv,
+    own_sem, q_send, q_recv, p_send, p_recv, o_send, o_recv,
+    *, peers, widths,
+):
+    width, place = lax.axis_index("width"), lax.axis_index("seq")
+    chips = peers // 2
+    chip, core = place // 2, lax.rem(place, 2)
+    mate = (width, jnp.bitwise_xor(place, 1))
+    ring = [lax.rem(place + by, peers) for by in range(1, peers)]
+    cross = [jnp.bitwise_xor(width, m) for m in range(1, widths)]
+    greet([(width, s) for s in ring] + [(w, place) for w in cross])
+    half = wide_ref.shape[3] // 2
+    sets = [
+        (wide_ref, out_ref, pl.ds(0, half), own0, got0, piece0),
+        (wide_ref, out_ref, pl.ds(half, half), own1, got1, piece1),
+        (third_ref, out_third_ref, pl.ds(0, BLOCK), own2, got2, piece2),
+    ]
+
+    def remote(src, dst, send, recv, device):
+        return pltpu.make_async_remote_copy(
+            src_ref=src, dst_ref=dst, send_sem=send, recv_sem=recv, device_id=device, device_id_type=MESH
+        )
+
+    locals_ = [pltpu.make_async_copy(part_ref.at[2 * q + core], mine.at[q], local_sem.at[q]) for q in range(chips)]
+    to_core = [
+        remote(part_ref.at[2 * q + 1 - core], from_core.at[q], core_send.at[q], core_recv.at[q], mate) for q in range(chips)
+    ]
+    own_in, to_width = [], []
+    for k, (src, dst, cols, own, got, piece) in enumerate(sets):
+        own_in.append(pltpu.make_async_copy(src.at[:, width, :, cols], own, own_sem.at[0, k]))
+        to_width.append([
+            remote(src.at[:, w, :, cols], got.at[m], q_send.at[k, m], q_recv.at[k, m], (w, place)) for m, w in enumerate(cross)
+        ])
+    for copy in locals_ + to_core + own_in + to_width[0] + to_width[1] + to_width[2]:
+        copy.start()
+    rows = mine.shape[1]
+    for q in range(chips):
+        locals_[q].wait()
+        to_core[q].wait_recv()
+        add_into(mine.at[q], [from_core.at[q]], rows)
+
+    def flow(by):
+        return (up, up_send, up_recv) if by > 0 else (down, down_send, down_recv)
+
+    def sends(by, step):
+        far = chips - step
+        return chip + far < chips if by > 0 else chip >= far
+
+    def later(by):
+        return chip > 0 if by > 0 else chip + 1 < chips
+
+    def hop(src, by, step):
+        buffer, send, recv = flow(by)
+        return remote(
+            src, buffer.at[step - 1], send.at[step - 1], recv.at[step - 1], (width, jnp.clip(place + 2 * by, 0, peers - 1))
+        )
+
+    def staged(by, step):
+        return flow(by)[0].at[step - 2]
+
+    def run_hops(step):
+        for by in (1, -1):
+            owner = jnp.clip(chip + by * (chips - step), 0, chips - 1)
+
+            def direct():
+                hop(mine.at[owner], by, step).start()
+
+            def relayed():
+                hop(staged(by, step), by, step - 1).wait_recv()
+                add_into(staged(by, step), [mine.at[owner]], rows)
+                hop(staged(by, step), by, step).start()
+
+            if step == 1:
+                pl.when(sends(by, step))(direct)
+            else:
+                pl.when(sends(by, step) & jnp.logical_not(later(by)))(direct)
+                pl.when(sends(by, step) & later(by))(relayed)
+
+    to_owner, to_all, kept = [None] * 3, [None] * 3, []
+
+    def exchange(k):
+        src, dst, cols, own, got, piece = sets[k]
+        own_in[k].wait()
+        for copy in to_width[k]:
+            copy.wait_recv()
+        for s in range(peers):
+            add_into(own.at[s], [got.at[m, s] for m in range(widths - 1)], own.shape[1])
+        to_owner[k] = [
+            remote(own.at[s], piece.at[place], p_send.at[k, i], p_recv.at[k, i], (width, s)) for i, s in enumerate(ring)
+        ]
+        keep = pltpu.make_async_copy(own.at[place], piece.at[place], own_sem.at[1, k])
+        for copy in to_owner[k] + [keep]:
+            copy.start()
+        kept.append(keep)
+
+    def spread(k):
+        src, dst, cols, own, got, piece = sets[k]
+        for copy in to_owner[k]:
+            copy.wait_recv()
+        kept[k].wait()
+        to_all[k] = [
+            remote(piece, dst.at[:, width, :, cols], o_send.at[k, m], o_recv.at[k, m], (w, place)) for m, w in enumerate(cross)
+        ]
+        to_all[k].append(pltpu.make_async_copy(piece, dst.at[:, width, :, cols], own_sem.at[2, k]))
+        for copy in to_all[k]:
+            copy.start()
+
+    run_hops(1)
+    exchange(0)
+    if chips > 2:
+        run_hops(2)
+    spread(0)
+    exchange(1)
+    exchange(2)
+    for step in range(3, chips):
+        run_hops(step)
+    spread(1)
+    spread(2)
+
+    for by in (1, -1):
+        @pl.when(later(by))
+        def _():
+            buffer = flow(by)[0].at[chips - 2]
+            hop(buffer, by, chips - 1).wait_recv()
+            add_into(mine.at[chip], [buffer], rows)
+
+    gain = gain_ref[...]
+
+    @pl.loop(0, rows // ROWS_AT_ONCE)
+    def _(i):
+        at = pl.ds(pl.multiple_of(i * ROWS_AT_ONCE, ROWS_AT_ONCE), ROWS_AT_ONCE)
+        x = x_ref[at, :].astype(f32)
+        rate = lax.rsqrt(jnp.mean(x * x, axis=-1, keepdims=True) + epsilon)
+        unit = x * rate
+        pulled = mine[chip, at].astype(f32) * gain
+        inner = jnp.mean(pulled * unit, axis=-1, keepdims=True)
+        rows_ref[at, :] = cot_ref[at, :].astype(f32) + rate * (pulled - unit * inner)
+
+    for step in range(1, chips):
+        for by in (1, -1):
+            @pl.when(sends(by, step))
+            def _():
+                hop(mine.at[0], by, step).wait_send()
+    for copy in to_core:
+        copy.wait_send()
+    for k in range(len(sets)):
+        for copy in to_width[k] + to_owner[k]:
+            copy.wait_send()
+        for copy in to_all[k]:
+            copy.wait()
+
+
+def scattered_out(part, wide, third, x_rows, cotangent, gain):
+    peers, widths = lax.axis_size("seq"), lax.axis_size("width")
+    chips = peers // 2
+    dma = pltpu.SemaphoreType.DMA
+    anywhere = pl.BlockSpec(memory_space=pl.ANY)
+    vmem = pl.BlockSpec(memory_space=pltpu.VMEM)
+    block = part.shape[1:]
+    half = wide.shape[3] // 2
+    pieces = [(peers, wide.shape[2], cols) for cols in (half, half, third.shape[3])]
+    return pl.pallas_call(
+        partial(scatter_kernel, peers=peers, widths=widths),
+        in_specs=[anywhere] * 3 + [vmem] * 3,
+        out_specs=[vmem, anywhere, anywhere],
+        out_shape=[
+            jax.ShapeDtypeStruct(block, f32), jax.ShapeDtypeStruct(wide.shape, bf16), jax.ShapeDtypeStruct(third.shape, bf16)
+        ],
+        scratch_shapes=[
+            pltpu.VMEM((chips,) + block, bf16), pltpu.VMEM((chips,) + block, bf16),
+            pltpu.VMEM((chips - 1,) + block, bf16), pltpu.VMEM((chips - 1,) + block, bf16),
+            *[pltpu.VMEM(piece, bf16) for piece in pieces],
+            *[pltpu.VMEM((widths - 1,) + piece, bf16) for piece in pieces],
+            *[pltpu.VMEM(piece, bf16) for piece in pieces],
+            dma((chips,)), dma((chips,)), dma((chips,)),
+            dma((chips - 1,)), dma((chips - 1,)), dma((chips - 1,)), dma((chips - 1,)),
+            dma((3, 3)), dma((3, widths - 1)), dma((3, widths - 1)), dma((3, peers - 1)), dma((3, peers - 1)),
+            dma((3, widths - 1)), dma((3, widths - 1)),
+        ],
+        compiler_params=pltpu.CompilerParams(collective_id=2, has_side_effects=True, vmem_limit_bytes=48 << 20),
+        name="scatter_out",
+    )(part, wide, third, x_rows, cotangent, gain)
+
+
+def bc_kernel(got_ref, pre_ref, par_ref, keep_ref, ddt_ref, third_ref, dpar_ref, pre_t, *, at):
+    chans, times = pre_t.shape
+    for i in range(times // BLOCK):
+        rows = slice(i * BLOCK, (i + 1) * BLOCK)
+        pre_t[:, rows] = pre_ref[rows, :].T[at : at + chans]
+    dbc = got_ref[0].astype(f32)
+    for s in range(1, got_ref.shape[0]):
+        dbc = dbc + got_ref[s].astype(f32)
+    pre = pre_t[...]
+    in_block = lax.rem(lax.broadcasted_iota(jnp.int32, (chans, times), 1), BLOCK)
+    keep, keep_next = keep_ref[0:1, :], keep_ref[1:2, :]
+    conv = jnp.broadcast_to(par_ref[:, BIAS : BIAS + 1], (chans, times))
+    shifted = []
+    for j in range(KCONV):
+        moved = pre
+        if j:
+            moved = jnp.where(in_block >= j, pltpu.roll(pre, j, 1), keep * pltpu.roll(pre, BLOCK + j, 1))
+        shifted.append(moved)
+        conv = conv + moved * par_ref[:, KCONV - 1 - j : KCONV - j]
+    act = sigmoid(conv)
+    dconv = dbc * (act * (1.0 + conv * (1.0 - act)))
+    dpre = dconv * par_ref[:, KCONV - 1 : KCONV]
+    lane = lax.broadcasted_iota(jnp.int32, (chans, BLOCK), 1)
+    dpar = jnp.where(lane == BIAS, jnp.sum(dconv, axis=1, keepdims=True), 0.0)
+    for j in range(KCONV):
+        dpar = dpar + jnp.where(lane == KCONV - 1 - j, jnp.sum(dconv * shifted[j], axis=1, keepdims=True), 0.0)
+        if j:
+            back = jnp.where(
+                in_block < BLOCK - j, pltpu.roll(dconv, times - j, 1), keep_next * pltpu.roll(dconv, times - BLOCK - j, 1)
+            )
+            dpre = dpre + back * par_ref[:, KCONV - 1 - j : KCONV - j]
+    dpar_ref[...] = dpar
+    for i in range(times // BLOCK):
+        tile = dpre[:, i * BLOCK : (i + 1) * BLOCK]
+        below = jnp.zeros((BLOCK - at - chans, BLOCK), f32)
+        tile = jnp.concatenate([jnp.zeros((at, BLOCK), f32), tile, below], axis=0).T
+        rows = slice(i * BLOCK, (i + 1) * BLOCK)
+        third_ref[rows, :] = (tile + ddt_ref[rows, :].astype(f32)).astype(bf16)
+
+
+def bc_backward(got, zx, par, keep, dzx, at, chans):
+    rows = dzx.shape[0]
+    share = got.shape[1]
+    third = pl.BlockSpec((rows, BLOCK), lambda i: (0, 2 * chans // BLOCK))
+    whole = lambda a: pl.BlockSpec(a.shape, lambda i: (0,) * a.ndim)
+    return pl.pallas_call(
+        partial(bc_kernel, at=at),
+        grid=(1,),
+        in_specs=[whole(got), third, whole(par), whole(keep), third],
+        out_specs=[pl.BlockSpec((rows, BLOCK), lambda i: (0, 0)), pl.BlockSpec((share, BLOCK), lambda i: (0, 0))],
+        out_shape=[jax.ShapeDtypeStruct((rows, BLOCK), bf16), jax.ShapeDtypeStruct((share, BLOCK), f32)],
+        scratch_shapes=[pltpu.VMEM((share, rows), f32)],
+        compiler_params=pltpu.CompilerParams(vmem_limit_bytes=32 << 20),
+        name="bc_backward",
+    )(got, zx, par, keep, dzx)
+
+
+def sum_kernel(own_ref, out_ref, got, send_sem, recv_sem, *, peers):
+    place = lax.axis_index("seq")
+    width = lax.axis_index("width")
+    barrier = pltpu.get_barrier_semaphore()
+    for by in range(1, peers):
+        pl.semaphore_signal(
+            barrier, inc=1, device_id=(width, lax.rem(place + by, peers)), device_id_type=pl.DeviceIdType.MESH
+        )
+    pl.semaphore_wait(barrier, peers - 1)
+    copies = []
+    for by in range(1, peers):
+        copies.append(
+            pltpu.make_async_remote_copy(
+                src_ref=own_ref, dst_ref=got.at[by - 1], send_sem=send_sem.at[by - 1], recv_sem=recv_sem.at[by - 1],
+                device_id=(width, lax.rem(place + by, peers)), device_id_type=pl.DeviceIdType.MESH,
+            )
+        )
+        copies[-1].start()
+    total = own_ref[...]
+    for by in range(1, peers):
+        copies[by - 1].wait()
+        total = total + got[by - 1]
+    out_ref[...] = total
+
+
+def summed_small(value):
+    peers = lax.axis_size("seq")
+    return pl.pallas_call(
+        partial(sum_kernel, peers=peers),
+        out_shape=jax.ShapeDtypeStruct(value.shape, f32),
+        in_specs=[pl.BlockSpec(memory_space=pltpu.VMEM)],
+        out_specs=pl.BlockSpec(memory_space=pltpu.VMEM),
+        scratch_shapes=[
+            pltpu.VMEM((peers - 1,) + value.shape, f32),
+            pltpu.SemaphoreType.DMA((peers - 1,)), pltpu.SemaphoreType.DMA((peers - 1,)),
+        ],
+        compiler_params=pltpu.CompilerParams(collective_id=0, has_side_effects=True),
+        name="row_sums",
+    )(value)
+
+
+def laid_kernel(in_ref, third_ref, w_ref, bc_ref, dt_ref, gain_ref, out_ref, out_bc_ref, out_dt_ref, norm_ref, *, heads, share):
+    peers, rows, wide = in_ref.shape[0], in_ref.shape[2], in_ref.shape[3]
+    chans = wide // 2
+    lane = jnp.zeros((rows, BLOCK), f32)
+    for s in range(peers):
+        for half in (0, 1):
+            at = (half * peers + s) * chans
+            value = in_ref[s, 0, :, half * chans : (half + 1) * chans].astype(f32)
+            out_ref[:, at : at + chans] = value
+            value = value * w_ref[:, at : at + chans].astype(f32)
+            for j in range(chans // BLOCK):
+                lane = lane + value[:, j * BLOCK : (j + 1) * BLOCK]
+    third = [third_ref[s, 0].astype(f32) for s in range(peers)]
+    bc = jnp.concatenate([t[:, heads : heads + share] for t in third], axis=1)
+    dt = jnp.concatenate([t[:, :heads] for t in third], axis=1)
+    out_bc_ref[...] = bc
+    out_dt_ref[...] = dt
+    total = jnp.sum(lane, axis=1, keepdims=True) + jnp.sum(bc * bc_ref[...].astype(f32), axis=1, keepdims=True)
+    total = total + jnp.sum(dt * dt_ref[...].astype(f32), axis=1, keepdims=True)
+    norm_ref[...] = total / gain_ref[...]
+
+
+def laid_out(wide, third, w_zx, w_bc, w_dt, gain, heads):
+    peers, widths, quarter, cols = wide.shape
+    rows = widths * quarter
+    steps = 2 * widths
+    cut = rows // steps
+    share = w_bc.shape[1] // peers
+    by_rows = lambda a: pl.BlockSpec((cut, a.shape[1]), lambda i: (i, 0))
+    by_piece = lambda a: pl.BlockSpec((peers, 1, cut, a.shape[3]), lambda i: (0, i // 2, i % 2, 0))
+    shapes = [jax.ShapeDtypeStruct(a.shape, f32) for a in (w_zx, w_bc, w_dt, gain)]
+    return pl.pallas_call(
+        partial(laid_kernel, heads=heads, share=share),
+        grid=(steps,),
+        in_specs=[by_piece(wide), by_piece(third)] + [by_rows(a) for a in (w_zx, w_bc, w_dt, gain)],
+        out_specs=[by_rows(a) for a in shapes],
+        out_shape=shapes,
+        compiler_params=pltpu.CompilerParams(vmem_limit_bytes=32 << 20),
+        name="lay_out",
+    )(wide, third, w_zx, w_bc, w_dt, gain)
+
+
+def crossed(value, axis, mask):
+    return lax.ppermute(value, axis, [(i, i ^ mask) for i in range(lax.axis_size(axis))])
+
+
+def pick(value, index):
+    return lax.dynamic_index_in_dim(value, index, 0, False)
+
+
+def quarters_sent(value):
+    widths, width = lax.axis_size("width"), lax.axis_index("width")
+    value = value.reshape((widths, value.shape[0] // widths) + value.shape[1:])
+    sent = [crossed(pick(value, jnp.bitwise_xor(width, m)), "width", m) for m in range(1, widths)]
+    return [pick(value, width)] + sent
+
+
+def quarters_back(total):
+    widths = lax.axis_size("width")
+    return [total] + [crossed(total, "width", m) for m in range(1, widths)]
+
+
+def quarters_joined(pieces):
+    width = lax.axis_index("width")
+    stacked = jnp.stack(pieces)
+    whole = jnp.stack([pick(stacked, jnp.bitwise_xor(width, j)) for j in range(len(pieces))])
+    return whole.reshape((-1,) + whole.shape[2:]).astype(f32)
 
 
 def packed_rows(rows, count):
@@ -379,20 +919,15 @@
     count = (active * HEAD_DIM).astype(f32)
     first = place * heads
 
-    x_rows = tokens.astype(f32)
-    rate = lax.rsqrt(jnp.mean(x_rows * x_rows, axis=-1, keepdims=True) + epsilon)
-    normed_own = (x_rows * rate * norm_gain).astype(bf16)
+    share = 2 * N // peers
+    used = heads + share
+    normed_own, bgrad_own, third_src, start_tile = entry(valid, starts, tokens, cotangent, norm_gain, w_bc, w_dt, peers)
     row_mask = (jnp.arange(BLOCK)[None, :] < valid[0][:, None]).astype(f32).reshape(-1, 1)
-    cot_rows = cotangent.astype(f32)
-    bgrad_own = (cot_rows * row_mask).astype(bf16)
-
-    weights = lax.all_to_all(w_zx.reshape(-1, 2, peers, chans), "seq", 2, 0, tiled=True).reshape(model, 2 * chans)
-    normed = lax.all_gather(normed_own, "seq", axis=0, tiled=True)
+    weights, normed, starts_all = gathered_in(w_zx, third_src, w_bc, normed_own, start_tile, chans)
+    weights = weights.reshape(model, -1)
+    normed = normed.reshape(rows, model)
     bgrad = lax.all_gather(bgrad_own, "seq", axis=0, tiled=True)
-    bc_dt = lax.all_gather(jnp.concatenate([w_bc, w_dt], axis=1), "seq", axis=0, tiled=True)
-    keep = 1.0 - lax.all_gather(starts, "seq", axis=0, tiled=True).astype(f32)
-    weights_bc = bc_dt[:, : 2 * N]
-    weights_dt = jnp.pad(lax.dynamic_slice_in_dim(bc_dt, 2 * N + first, heads, 1), ((0, 0), (0, BLOCK - heads)))
+    keep = 1.0 - starts_all[:, 0, :lanes]
 
     taps_x = lax.dynamic_slice_in_dim(conv_w, first * HEAD_DIM, chans, 0).T
     of_chans = lambda a: lax.dynamic_slice_in_dim(a, first * HEAD_DIM, chans, 0)
@@ -406,12 +941,11 @@
     spread = (jnp.arange(chans)[None, :] // HEAD_DIM == jnp.arange(BLOCK)[:, None]).astype(bf16)
 
     zx = mm(normed, weights)
-    bcd = mm(normed, jnp.concatenate([weights_bc, weights_dt], axis=1))
     mixed_grad = mm(bgrad, w_out, NT)
     conv, mix, bc, steps, state, tail, sums = run_forward(
-        keep, zx, bcd, mixed_grad, chan, bc_par, head, spread, lanes, heads
-    )
-    sums = lax.psum(sums[:, :, :2, :], "seq")
+        keep, zx, mixed_grad, chan, bc_par, head, spread, lanes, heads
+    )
+    sums = summed_small(sums[:, :, :2, :].reshape(-1, BLOCK)).reshape(peers, lanes, 2, BLOCK)
     gate_rate = lax.rsqrt(sums[:, :, 0] / count + epsilon).reshape(rows, 1)
     gate_pull = gate_rate * gate_rate * gate_rate * sums[:, :, 1].reshape(rows, 1) / count
     scale = jnp.pad(jnp.concatenate([gate_rate, gate_pull], axis=1), ((0, 0), (0, SUB - 2)))
@@ -419,51 +953,54 @@
         (mix * jax.nn.silu(zx[:, :chans]) * gate_rate * chan[GAIN]).astype(bf16)
     )
     branch = lax.psum_scatter(mm(mixed_low, w_out).astype(bf16), "seq", scatter_dimension=0, tiled=True).astype(f32)
-    output = (x_rows + row_mask * branch).astype(bf16)
-    out_grad = lax.psum(mm(mixed_low, bgrad, TN).astype(bf16), "width").astype(f32)
-
-    dzx, ddt, dbc, dchan, dhead = run_backward(
-        keep, zx, bcd, mixed_grad, chan, head, spread, conv, mix, bc, steps, state, tail, scale, lanes, heads
-    )
-
-    dbc = lax.psum(dbc, "seq").reshape(peers, lanes, BLOCK, 2 * N)
-    bc_pre = bcd[:, : 2 * N].reshape(peers, lanes, BLOCK, 2 * N)
-    unused, bc_back = jax.vjp(partial(bc_front, keep=keep), bc_pre, conv_w[E:].T, conv_b[E:])
-    dbc_pre, dtaps_bc, dbias_bc = bc_back(dbc)
-    bc_grad = lax.optimization_barrier(dbc_pre.reshape(rows, 2 * N).astype(bf16))
-
-    wide = jnp.concatenate([mm(normed, dzx, TN).astype(bf16), mm(normed, ddt, TN).astype(bf16)], axis=1)
-    wide = wide.reshape(peers, widths, own // widths, -1)
-    wide = lax.psum_scatter(wide, "width", scatter_dimension=1, tiled=True)[:, 0]
-    wide = lax.all_to_all(wide, "seq", 0, 0, tiled=True)
-    wide = lax.all_gather(wide, "width", axis=1, tiled=True).astype(f32)
-    grad_zx = wide[:, :, : 2 * chans].reshape(peers, own, 2, chans).transpose(1, 2, 0, 3).reshape(own, 2 * E)
-    grad_dt = wide[:, :, 2 * chans : 2 * chans + heads].transpose(1, 0, 2).reshape(own, H)
-    normed_cols = lax.dynamic_slice_in_dim(normed, place * own, own, 1)
-    grad_bc = lax.psum(mm(normed_cols, bc_grad, TN), "width")
-
-    wide_grad = mm(dzx, weights, NT) + mm(ddt, weights_dt, NT)
-    normed_grad = lax.psum_scatter(wide_grad.astype(bf16), "seq", scatter_dimension=0, tiled=True).astype(f32)
-    normed_grad = normed_grad + mm(lax.dynamic_slice_in_dim(bc_grad, place * own, own, 0), weights_bc, NT)
-    unit = x_rows * rate
-    pulled = normed_grad * norm_gain
-    input_grad = cot_rows + rate * (pulled - unit * jnp.mean(pulled * unit, axis=-1, keepdims=True))
-    grad_norm = jnp.sum(w_zx.astype(f32) * grad_zx, axis=1) + jnp.sum(w_bc.astype(f32) * grad_bc, axis=1)
-    grad_norm = grad_norm + jnp.sum(w_dt.astype(f32) * grad_dt, axis=1)
-    grad_norm = grad_norm / lax.dynamic_slice_in_dim(norm_gain, place * own, own, 0)
-
-    once = (place == 0).astype(f32)
+    output = (tokens.astype(f32) + row_mask * branch).astype(bf16)
+    out_part = mm(mixed_low, bgrad, TN).astype(bf16)
+    scale, out_part = lax.optimization_barrier((scale, out_part))
+    out_quarters = quarters_sent(out_part)
+
+    dzx, dbc, dchan, dhead = run_backward(
+        keep, zx, mixed_grad, chan, head, spread, conv, mix, bc, steps, state, tail, scale, lanes, heads
+    )
+    dzx, dbc, out_quarters = lax.optimization_barrier((dzx, dbc, out_quarters))
+    out_pieces = quarters_back(sum(q.astype(f32) for q in out_quarters).astype(bf16))
+
+    got = lax.all_to_all(dbc.reshape(peers, share, rows), "seq", 0, 0, tiled=True)
+    of_share = lambda a: lax.dynamic_slice_in_dim(a, E + place * share, share, 0)
+    share_par = jnp.pad(jnp.concatenate([of_share(conv_w), of_share(conv_b)[:, None]], axis=1), ((0, 0), (0, BLOCK - BIAS - 1)))
+    over_time = lambda a: jnp.repeat(a.reshape(-1), BLOCK)
+    keep_next = jnp.concatenate([keep[1:], jnp.zeros_like(keep[:1])], axis=0)
+    third, dshare = bc_backward(
+        got, zx, share_par, packed_rows([over_time(keep), over_time(keep_next)], SUB), dzx, heads, chans
+    )
+
     at_heads = lambda a: lax.dynamic_update_slice_in_dim(jnp.zeros((H,), f32), a, first, 0)
     at_chans = lambda a: lax.dynamic_update_slice_in_dim(jnp.zeros((E,), f32), a, first * HEAD_DIM, 0)
-    taps = [jnp.concatenate([at_chans(dchan[k]), dtaps_bc[k] * once]) for k in range(KCONV)]
-    bias = jnp.concatenate([at_chans(dchan[BIAS]), dbias_bc * once])
+    at_share = lambda a: lax.dynamic_update_slice_in_dim(jnp.zeros((2 * N,), f32), a, place * share, 0)
     skip = jnp.sum(dchan[SKIP].reshape(heads, HEAD_DIM), axis=1)
-    small = [*taps, bias, at_chans(dchan[GAIN]), at_heads(dhead[0, :heads]), at_heads(dhead[1, :heads]), at_heads(skip)]
-    sizes = [a.shape[0] for a in small]
-    summed = lax.psum(jnp.concatenate(small), ("width", "seq"))
-    pieces = []
-    for size in sizes:
-        pieces.append(lax.dynamic_slice_in_dim(summed, sum(a.shape[0] * peers for a in pieces) + place * (size // peers), size // peers, 0))
+    small = [jnp.concatenate([at_chans(dchan[k]), at_share(dshare[:, k])]) for k in range(KCONV + 1)]
+    small += [at_chans(dchan[GAIN]), at_heads(dhead[0, :heads]), at_heads(dhead[1, :heads]), at_heads(skip)]
+    sizes = [a.shape[0] // peers for a in small]
+    small = jnp.concatenate([a.reshape(peers, -1) for a in small], axis=1)
+    per_row = -(-small.shape[1] // own)
+    small = jnp.pad(small, ((0, 0), (0, own * per_row - small.shape[1]))).reshape(model, per_row)
+
+    wide = mm(normed, dzx[:, : 2 * chans], TN).astype(bf16)
+    wide, out_pieces = lax.optimization_barrier((wide, out_pieces))
+    out_grad = quarters_joined(out_pieces)
+    wide_third = jnp.concatenate(
+        [mm(normed, third, TN)[:, :used], small, jnp.zeros((model, BLOCK - used - per_row), f32)], axis=1
+    ).astype(bf16)
+    part = mm(lax.dynamic_update_slice(dzx, third, (0, 2 * chans)), weights[:, : 2 * chans + BLOCK], NT).astype(bf16)
+    by_owner = lambda a: a.reshape(peers, widths, own // widths, -1)
+    part, output, out_grad = lax.optimization_barrier((part, output, out_grad))
+    input_grad, wide, wide_third = scattered_out(
+        part.reshape(peers, own, model), by_owner(wide), by_owner(wide_third), tokens, cotangent, norm_gain[None]
+    )
+    gain_rows = lax.dynamic_slice_in_dim(norm_gain, place * own, own, 0)[:, None]
+    grad_zx, grad_bc, grad_dt, grad_norm = laid_out(wide, wide_third, w_zx, w_bc, w_dt, gain_rows, heads)
+    grad_norm = grad_norm[:, 0]
+    summed = jnp.sum(wide_third.reshape(peers, own, BLOCK)[:, :, used : used + per_row].astype(f32), axis=0).reshape(-1)
+    pieces = [summed[sum(sizes[:i]) : sum(sizes[: i + 1])] for i in range(len(sizes))]
     grad_taps = jnp.stack(pieces[:KCONV], axis=1)
     grad_bias, grad_gain, grad_dtb, grad_alog, grad_skip = pieces[KCONV:]
     return (

time: 1050 us -> 573 us (0.55)
  the two profiles are of different devices: /device:TPU:9 before, /device:TPU:0 now
where the time goes in v2:
time: 573 us; the launch traced here: 563 us
  Pallas kernels  361 us (63%)
  matrix products  79.8 us (14%)
  local copies, waits for them, and re-layouts  57.6 us (10%)
  waiting for transfers between devices  20.4 us (4%)
  other arithmetic  17.7 us (3%)
  between operations  15.2 us (3%)
  starting transfers between devices  11.1 us (2%)
    pallas_call x1, Pallas kernels, gathered_in(): pl.pallas_call(partial(gather_kernel, peers=peers, widths=widths, chans=c...  179 us
    pallas_call x1, Pallas kernels, scattered_out(): pl.pallas_call(partial(scatter_kernel, peers=peers, widths=widths), in_sp...  107 us
    dot_general x7, matrix products, mm(): lax.dot_general(left, right, (dims, ((), ())), precision=precision, prefe...  79.8 us
    unnamed x94, local copies, waits for them, and re-layouts  35.6 us
    pallas_call x1, Pallas kernels, run_backward(): pl.pallas_call(partial(backward_kernel, lanes=lanes, heads=heads, blocks=...  34.1 us
    pallas_call x1, Pallas kernels, run_forward(): pl.pallas_call(partial(forward_kernel, lanes=lanes, heads=heads), grid=(b...  24.4 us
    all_to_all x1, waiting for transfers between devices, heads_body(): lax.all_to_all(dbc.reshape(peers, share, rows), 'seq', 0, 0, tiled=True)  16.6 us
  transfers between devices with their start and end apart: 9, of which 2 were waited for; matrix products, arithmetic and copies ran while one was open for 16% of the time, Pallas kernels for 38%

profile of v2, /device:TPU:0, one launch (start us, length us, event | category | flops | bytes accessed | tf_op | source)
XLA Modules:
  0.0 563.0 jit_solution(597379678587725436)
XLA Ops:
  13.6 2.5 entry.1
  21.7 179.3 %gather_in.1 = (bf16[8,4,64,1408]{3,2,1,0:T(8,128)(2,1)}, bf16[8,256,2048]{2,1,0:T(8,128)(2,1)}, f32[8,8,128]{2,1,0:T(8,128)}) custom-call(bf16[256,8192]{1,0:T(8,128)(2,1)} %w_ref.1, bf16[8,256,128]{2,1,0:T(8,128)(2,1)} %copy-done.19, bf16[256,256]{1,0:T(8,128)(2,1)} %bc_ref.5, bf16[256,2048]{1,0:T(8,128)(2,1)} %copy-done.17, f32[8,128]{1,0:T(8,128)} %copy-done.29), custom_call_target="tpu_custom_call" | custom-call | tf_op jit(solution)/shard_map/gather_in/pallas_call | solution.py:516
  204.2 18.5 %fusion.17.zx_ref.pre_ref = f32[2048,1408]{1,0:T(8,128)} fusion(bf16[2048,2048]{1,0:T(8,128)(2,1)} %bitcast.109, bf16[2048,1408]{1,0:T(8,128)(2,1)} %bitcast.112), kind=kOutput, calls=%fused_computation.81 | convolution fusion | flops 11811160064 | bytes 25690112 | tf_op jit(solution)/shard_map/dot_general | solution.py:29
  222.7 9.5 %fusion.18.grad_ref = f32[2048,512]{1,0:T(8,128)} fusion(bf16[2048,2048]{1,0:T(8,128)(2,1)} %all-gather.2.cloned.1.call-done, bf16[512,2048]{1,0:T(8,128)(2,1)S(1)} %copy-done), kind=kOutput, calls=%fused_computation.82 | convolution fusion | flops 4294967296 | bytes 14680064 | tf_op jit(solution)/shard_map/dot_general | solution.py:29
  232.2 24.4 %mix_forward.1 = (f32[2048,512]{1,0:T(8,128)S(1)}, f32[2048,512]{1,0:T(8,128)S(1)}, bf16[2048,256]{1,0:T(8,128)(2,1)S(1)}, f32[2048,256]{1,0:T(8,128)S(1)}, f32[...) custom-call(f32[8,2]{1,0:T(8,128)S(1)} %copy.66.keep_ref, ...), custom_call_target="tpu_custom_call" | custom-call | flops 2147483648 | bytes 33554432 | tf_op jit(solution)/shard_map/mix_forward/pallas_call | solution.py:330
  256.7 2.0 copy-done.4
  258.6 2.1 copy-done.11
  263.3 7.2 %row_sums.1 = f32[32,128]{1,0:T(8,128)} custom-call(f32[32,128]{1,0:T(8,128)} %bitcast.92), custom_call_target="tpu_custom_call" | custom-call | tf_op jit(solution)/shard_map/row_sums/pallas_call | solution.py:819
  272.0 4.2 multiply_convert_fusion
  277.6 6.9 %convolution_convert_fusion = bf16[2048,2048]{1,0:T(8,128)(2,1)} fusion(bf16[2048,512]{1,0:T(8,128)(2,1)S(1)} %multiply_convert_fusion, bf16[512,2048]{1,0:T(8,128)(2,1)S(1)} %copy-done), kind=kOutput, calls=%fused_computation | convolution fusion | flops 4299161600 | bytes 12582912 | tf_op jit(solution)/shard_map/dot_general | solution.py:29
  289.9 9.2 %convolution_convert_fusion.2 = bf16[512,2048]{1,0:T(8,128)(2,1)S(1)} fusion(bf16[2048,512]{1,0:T(8,128)(2,1)} %copy-done.34, bf16[2048,2048]{1,0:T(8,128)(2,1)} %all-gather.2.cloned.1.call-done), kind=kOutput, calls=%fused_computation.7 | convolution fusion | flops 4296015872 | bytes 12582912 | tf_op jit(solution)/shard_map/dot_general | solution.py:29
  302.0 1.6 collective-permute-start.1
  304.1 34.1 %mix_backward.1 = (bf16[2048,1152]{1,0:T(8,128)(2,1)}, bf16[256,2048]{1,0:T(8,128)(2,1)S(1)}, f32[8,512]{1,0:T(8,128)S(1)}, f32[8,128]{1,0:T(8,128)S(1)}) custom-call(f32[8,2]{1,0:T(8,128)S(1)} %copy-done.26, f32[2048,1408]{1,0:T(8,128)} %fusion.17.zx_ref.pre_ref, f32[2048,512]{1,0:T(8,128)} %fusion.18.grad_ref, f32[8,512]{1,0:T(8,128)S(1)} %stack.69.chan_ref, ...), custom_call_target="tpu_custom_call" | custom-call | flops 6442450944 | bytes 41943040 | tf_op jit(solution)/shard_map/mix_backward/pallas_call | solution.py:365
  343.3 1.9 add_convert_fusion.1
  346.7 1.6 collective-permute-start.4
  348.7 4.0 all-to-all-start
  352.7 14.1 %fusion.3 = bf16[2048,1024]{1,0:T(8,128)(2,1)} fusion(bf16[2048,2048]{1,0:T(8,128)(2,1)} %bitcast.110, bf16[2048,1152]{1,0:T(8,128)(2,1)} %get-tuple-element.74.ddt_ref), kind=kOutput, calls=%fused_computation.6 | convolution fusion | flops 8592031744 | bytes 16777216 | tf_op jit(solution)/shard_map/dot_general | solution.py:29
  366.9 3.8 collective-permute-done.4
  371.6 1.8 pad_maximum_fusion
  373.9 2.7 bitcast_convert_fusion
  376.6 16.6 %all-to-all-done.got_ref = bf16[8,32,2048]{2,1,0:T(8,128)(2,1)S(1)} async-done(((bf16[8,32,2048]{2,1,0:T(8,128)(2,1)}), bf16[8,32,2048]{2,1,0:T(8,128)(2,1)S(1)}, u32[]{:S(2)}, u32[]{:S(2)}) %all-to-all-start) | async-done | bytes 1048608 | tf_op jit(solution)/shard_map/all_to_all | solution.py:967
  393.2 4.3 copy-done.2
  397.5 2.3 copy-done.7
  399.8 1.5 bc_backward.1
  404.5 4.7 fusion.19
  410.8 16.9 %convolution_convert_fusion.1 = bf16[2048,2048]{1,0:T(8,128)(2,1)} fusion(bf16[2048,1152]{1,0:T(8,128)(2,1)} %constant_dynamic-update-slice_fusion, bf16[2048,1408]{1,0:T(8,128)(2,1)} %bitcast.113), kind=kOutput, calls=%fused_computation.1 | convolution fusion | flops 9667870720 | bytes 17825792 | tf_op jit(solution)/shard_map/dot_general | solution.py:29
  427.7 2.6 add_convert_fusion
  430.2 107.2 %scatter_out.1 = (f32[256,2048]{1,0:T(8,128)S(1)}, bf16[8,4,64,1024]{3,2,1,0:T(8,128)(2,1)}, bf16[8,4,64,128]{3,2,1,0:T(8,128)(2,1)S(1)}) custom-call(bf16[8,256,2048]{2,1,0:T(8,128)(2,1)} %bitcast.80, bf16[8,4,64,1024]{3,2,1,0:T(8,128)(2,1)} %bitcast.81, bf16[8,4,64,128]{3,2,1,0:T(8,128)(2,1)S(1)} %maximum_maximum_fusion.third_ref, ...), custom_call_target="tpu_custom_call" | custom-call | tf_op jit(solution)/shard_map/scatter_out/pallas_call | solution.py:712
  541.1 2.2 copy-done.3
  543.2 2.2 copy-done.10
  545.4 5.2 lay_out.1
  552.6 3.1 copy.97
  (220 shorter events, 47.9 us)
Async XLA Ops:
  7.2 215.6 %copy-start = (bf16[512,2048]{1,0:T(8,128)(2,1)S(1)}, bf16[512,2048]{1,0:T(8,128)(2,1)}, u32[]{:S(2)}) copy-start(bf16[512,2048]{1,0:T(8,128)(2,1)} %param.29) | copy-start | bytes 6291460
  7.2 215.5 %all-gather.2.cloned.1.call-start = ((), (), s32[]{:S(2)}) async-start(), calls=%async_computation.2 | async-start | bytes 9437184 | tf_op jit(solution)/shard_map/all_gather | solution.py:929
  13.6 190.6 %slice-start = ((f32[4352]{0:T(1024)}), f32[256]{0:T(256)S(1)}, s32[]{:S(2)}) async-start(f32[4352]{0:T(1024)} %param.24), calls=%async_computation.4 | async-start | bytes 2048 | tf_op jit(solution)/shard_map/slice | solution.py:939
  18.5 409.1 %reduce-scatter.2.cloned.1.call-start = ((), (), s32[]{:S(2)}) async-start(), calls=%async_computation.3 | async-start | bytes 9437184 | tf_op jit(solution)/shard_map/reduce_scatter | solution.py:955
  201.9 30.3 %copy-start.25 = (f32[8,2]{1,0:T(8,128)}, f32[8,2]{1,0:T(8,128)S(1)}, u32[]{:S(2)}) copy-start(f32[8,2]{1,0:T(8,128)S(1)} %copy.66.keep_ref) | copy-start | bytes 196
  203.5 28.8 %copy-start.27 = (f32[8,128]{1,0:T(8,128)}, f32[8,128]{1,0:T(8,128)S(1)}, u32[]{:S(2)}) copy-start(f32[8,128]{1,0:T(8,128)S(1)} %select_maximum_fusion.2.head_ref) | copy-start | bytes 12292
  272.0 4.2 copy-start.39
  284.5 4.1 copy-start.32
  284.5 4.9 copy-start.40
  284.5 4.9 copy-start.41
  299.1 4.9 copy-start.13
  299.2 4.9 copy-start.21
  299.2 4.9 copy-start.26
  299.2 4.9 copy-start.28
  300.6 42.7 %collective-permute-start = (bf16[128,2048]{1,0:T(8,128)(2,1)}, bf16[128,2048]{1,0:T(8,128)(2,1)}, u32[]{:S(2)}, u32[]{:S(2)}) collective-permute-start(bf16[128,2048]{1,0:T(8,128)(2,1)} %get-tuple-element.149), channel_id=1, source_target_pairs={{0,8},{8,0},{16,24},{24,16},{1,9},{9,1},{17,25},{25,17},{2,10},{10... | collective-permute-start | bytes 1572872 | tf_op jit(solution)/shard_map/ppermute | solution.py:876
  302.0 41.3 %collective-permute-start.1 = (bf16[128,2048]{1,0:T(8,128)(2,1)}, bf16[128,2048]{1,0:T(8,128)(2,1)}, u32[]{:S(2)}, u32[]{:S(2)}) collective-permute-start(bf16[128,2048]{1,0:T(8,128)(2,1)} %get-tuple-element.148), channel_id=1, source_target_pairs={{0,16},{8,24},{16,0},{24,8},{1,17},{9,25},{17,1},{25,9},{2,18},{10... | collective-permute-start | bytes 1572872 | tf_op jit(solution)/shard_map/ppermute | solution.py:876
  303.6 39.7 %collective-permute-start.2 = (bf16[128,2048]{1,0:T(8,128)(2,1)}, bf16[128,2048]{1,0:T(8,128)(2,1)}, u32[]{:S(2)}, u32[]{:S(2)}) collective-permute-start(bf16[128,2048]{1,0:T(8,128)(2,1)} %get-tuple-element.147), channel_id=1, source_target_pairs={{0,24},{8,16},{16,8},{24,0},{1,25},{9,17},{17,9},{25,1},{2,26},{10... | collective-permute-start | bytes 1572872 | tf_op jit(solution)/shard_map/ppermute | solution.py:876
  345.2 21.7 %copy-start.35 = (bf16[128,2048]{1,0:T(8,128)(2,1)}, bf16[128,2048]{1,0:T(8,128)(2,1)S(1)}, u32[]{:S(2)}) copy-start(bf16[128,2048]{1,0:T(8,128)(2,1)S(1)} %add_convert_fusion.1) | copy-start | bytes 1572868
  345.2 21.7 %collective-permute-start.3 = (bf16[128,2048]{1,0:T(8,128)(2,1)S(1)}, bf16[128,2048]{1,0:T(8,128)(2,1)S(1)}, u32[]{:S(2)}, u32[]{:S(2)}) collective-permute-start(bf16[128,2048]{1,0:T(8,128)(2,1)S(1)} %add_convert_fusion.1), channel_id=1, source_target_pairs={{0,8},{8,0},{16,24},{24,16},{1,9},{9,1},{17,25},{25,17},{2,10},{10... | collective-permute-start | bytes 1572872 | tf_op jit(solution)/shard_map/ppermute | solution.py:876
  346.7 24.0 %collective-permute-start.4 = (bf16[128,2048]{1,0:T(8,128)(2,1)S(1)}, bf16[128,2048]{1,0:T(8,128)(2,1)S(1)}, u32[]{:S(2)}, u32[]{:S(2)}) collective-permute-start(bf16[128,2048]{1,0:T(8,128)(2,1)S(1)} %add_convert_fusion.1), channel_id=1, source_target_pairs={{0,16},{8,24},{16,0},{24,8},{1,17},{9,25},{17,1},{25,9},{2,18},{10... | collective-permute-start | bytes 1572872 | tf_op jit(solution)/shard_map/ppermute | solution.py:876
  348.2 22.4 %collective-permute-start.5 = (bf16[128,2048]{1,0:T(8,128)(2,1)S(1)}, bf16[128,2048]{1,0:T(8,128)(2,1)S(1)}, u32[]{:S(2)}, u32[]{:S(2)}) collective-permute-start(bf16[128,2048]{1,0:T(8,128)(2,1)S(1)} %add_convert_fusion.1), channel_id=1, source_target_pairs={{0,24},{8,16},{16,8},{24,0},{1,25},{9,17},{17,9},{25,1},{2,26},{10... | collective-permute-start | bytes 1572872 | tf_op jit(solution)/shard_map/ppermute | solution.py:876
  348.7 44.4 %all-to-all-start = ((bf16[8,32,2048]{2,1,0:T(8,128)(2,1)}), bf16[8,32,2048]{2,1,0:T(8,128)(2,1)S(1)}, u32[]{:S(2)}, u32[]{:S(2)}) async-start(bf16[8,32,2048]{2,1,0:T(8,128)(2,1)} %bitcast.76), calls=%async_computation | async-start | bytes 2097152 | tf_op jit(solution)/shard_map/all_to_all | solution.py:967
  366.9 3.8 copy-start.36
  373.9 19.3 %copy-start.22 = (f32[32,128]{1,0:T(8,128)S(1)}, f32[32,128]{1,0:T(8,128)}, u32[]{:S(2)}) copy-start(f32[32,128]{1,0:T(8,128)} %pad.38.par_ref) | copy-start | bytes 49156
  393.2 4.3 copy-start.2
  404.5 5.9 %copy-start.44 = (bf16[128]{0:T(256)(128)(2,1)S(1)}, bf16[128]{0:T(256)(128)(2,1)}, u32[]{:S(2)}) copy-start(bf16[128]{0:T(256)(128)(2,1)} %pad.47.clone) | copy-start | bytes 772
  410.7 16.9 %copy-start.6 = (bf16[256,2048]{1,0:T(8,128)(2,1)S(1)}, bf16[256,2048]{1,0:T(8,128)(2,1)}, u32[]{:S(2)}) copy-start(bf16[256,2048]{1,0:T(8,128)(2,1)} %x_ref.3) | copy-start | bytes 3145732
  410.7 16.9 %copy-start.43 = (f32[256]{0:T(256)S(1)}, f32[256]{0:T(256)}, u32[]{:S(2)}) copy-start(f32[256]{0:T(256)} %fusion.12) | copy-start | bytes 3076
  410.7 19.5 %copy-start.9 = (bf16[256,2048]{1,0:T(8,128)(2,1)S(1)}, bf16[256,2048]{1,0:T(8,128)(2,1)}, u32[]{:S(2)}) copy-start(bf16[256,2048]{1,0:T(8,128)(2,1)} %cot_ref.3) | copy-start | bytes 3145732
  410.8 19.5 %copy-start.24 = (f32[2048]{0:T(1024)S(1)}, f32[2048]{0:T(1024)}, u32[]{:S(2)}) copy-start(f32[2048]{0:T(1024)} %param.19) | copy-start | bytes 24580
  430.2 110.8 %copy-start.16 = (bf16[256,256]{1,0:T(8,128)(2,1)S(1)}, bf16[256,256]{1,0:T(8,128)(2,1)}, u32[]{:S(2)}) copy-start(bf16[256,256]{1,0:T(8,128)(2,1)} %bc_ref.5) | copy-start | bytes 393220
  545.4 10.3 %copy-start.1 = (bf16[512,2048]{1,0:T(8,128)(2,1)S(1)}, bf16[512,2048]{1,0:T(8,128)(2,1)}, u32[]{:S(2)}) copy-start(bf16[512,2048]{1,0:T(8,128)(2,1)} %param.29) | copy-start | bytes 6291460
  (23 other events, 27.2 us)
Sparse Core Ops, SparseCore 0:
  18.6 129.8 all-gather.1
  284.6 104.6 reduce-scatter.1

commit v3 on v2

--- a/solution.py
+++ b/solution.py
@@ -73,88 +73,104 @@
 DT_BIAS, NEG_A, HEAD_MASK = 0, 1, 2
 
 
-def forward_kernel(
-    keep_ref, zx_ref, grad_ref, chan_ref, bc_par_ref, head_ref, spread_ref,
-    conv_ref, mix_ref, bc_ref, step_ref, state_ref, tail_ref, sums_ref,
+def forward_block(
+    keep_row, zx_ref, chan_ref, bc_par_ref, head_ref, spread,
+    conv_ref, mix_ref, bc_ref, step_ref, state_ref, tail_ref,
     state, tail_x, tail_b, pad_x, pad_b,
-    *, lanes, heads,
+    *, lane, heads,
 ):
-    c = pl.program_id(0)
     width = heads * HEAD_DIM
     row, col = grids()
     causal = row >= col
     tril = causal.astype(f32)
-    spread = spread_ref[...]
-
-    @pl.when(c == 0)
-    def _():
-        state[...] = jnp.zeros_like(state)
-        tail_x[...] = jnp.zeros_like(tail_x)
-        tail_b[...] = jnp.zeros_like(tail_b)
-
-    for lane in range(lanes):
-        rows = pl.ds(lane * BLOCK, BLOCK)
-        keep = keep_ref[c, lane]
-        pre = zx_ref[rows, width : 2 * width]
-        pad_x[lane, 0:SUB] = tail_x[lane] * keep
-        pad_x[lane, SUB:] = pre
-        tail_ref[0, lane] = tail_x[lane] * keep
-        tail_x[lane] = pre[BLOCK - SUB :, :]
-        conv = chan_ref[BIAS : BIAS + 1, :]
-        for k in range(KCONV):
-            conv = conv + pad_x[lane, SUB - KCONV + 1 + k : SUB - KCONV + 1 + k + BLOCK, :] * chan_ref[k : k + 1, :]
-        conv_ref[rows, :] = conv
-        x_low = (conv * sigmoid(conv) * chan_ref[MASK : MASK + 1, :]).astype(bf16)
-
-        pre_b = zx_ref[rows, 2 * width + BLOCK :]
-        pad_b[lane, 0:SUB] = tail_b[lane] * keep
-        pad_b[lane, SUB:] = pre_b
-        tail_b[lane] = pre_b[BLOCK - SUB :, :]
-        conv_b = bc_par_ref[BIAS : BIAS + 1, :]
-        for k in range(KCONV):
-            conv_b = conv_b + pad_b[lane, SUB - KCONV + 1 + k : SUB - KCONV + 1 + k + BLOCK, :] * bc_par_ref[k : k + 1, :]
-        bc_low = (conv_b * sigmoid(conv_b)).astype(bf16)
-        bc_ref[rows, :] = bc_low
-        b_low, c_low = bc_low[:, :N], bc_low[:, N:]
-
-        raw = zx_ref[rows, 2 * width : 2 * width + BLOCK] + head_ref[DT_BIAS : DT_BIAS + 1, :]
-        dt = softplus(raw) * head_ref[HEAD_MASK : HEAD_MASK + 1, :]
-        cum = mm(tril, head_ref[NEG_A : NEG_A + 1, :] * dt, precision=highest)
-        step_ref[rows, :BLOCK] = cum
-        step_ref[rows, BLOCK:] = dt
-        cum_t, dt_t = cum.T, dt.T
-        last = cum[BLOCK - 1 :, :]
-        carry_x = mm_left(jnp.exp(cum), spread)
-        end_x = mm_left(jnp.exp(last - cum) * dt, spread)
-        last_x = carry_x[BLOCK - 1 :, :]
-
-        inner = mm(c_low, b_low, NT)
-        parts = []
-        for j in range(heads // 2):
-            pair = x_low[:, 2 * HEAD_DIM * j : 2 * HEAD_DIM * (j + 1)]
-            scores = [
-                (inner * decay_of(cum, cum_t, h, causal) * dt_t[h : h + 1, :]).astype(bf16)
-                for h in (2 * j, 2 * j + 1)
-            ]
-            parts.append(mm(jnp.concatenate(scores, axis=1), jnp.concatenate(halves(pair, col), axis=0)))
-        within = jnp.concatenate(parts, axis=1)
-
-        state_in = state[lane] * keep
-        state_ref[0, lane] = state_in
-        carried = mm_right(c_low, state_in) * carry_x
-        x_f = x_low.astype(f32)
-        mixed = within + carried + chan_ref[SKIP : SKIP + 1, :] * x_f
-        mix_ref[rows, :] = mixed
-        weighted = (x_f * end_x).astype(bf16)
-        state[lane] = last_x * state_in + mm(b_low, weighted, TN)
-
-        z = zx_ref[rows, :width]
-        gated = mixed * (z * sigmoid(z))
-        ones = jnp.ones((SUB, width), bf16)
-        square = mm_right(ones, gated * gated, NT)
-        cross = mm_right(ones, grad_ref[rows, :] * chan_ref[GAIN : GAIN + 1, :] * gated, NT)
-        sub = lax.broadcasted_iota(jnp.int32, (SUB, BLOCK), 0)
-        sums_ref[0, lane] = jnp.where(sub == 0, square, jnp.where(sub == 1, cross, 0.0))
+    rows = pl.ds(lane * BLOCK, BLOCK)
+    keep = jnp.concatenate([keep_row] * (width // BLOCK), axis=1)
+    keep_b = jnp.concatenate([keep_row] * (2 * N // BLOCK), axis=1)
+
+    pre = zx_ref[rows, width : 2 * width]
+    before = tail_x[lane] * keep
+    pad_x[lane, 0:SUB] = before
+    pad_x[lane, SUB:] = pre
+    tail_ref[lane] = before
+    tail_x[lane] = pre[BLOCK - SUB :, :]
+    conv = chan_ref[BIAS : BIAS + 1, :]
+    for k in range(KCONV):
+        conv = conv + pad_x[lane, SUB - KCONV + 1 + k : SUB - KCONV + 1 + k + BLOCK, :] * chan_ref[k : k + 1, :]
+    conv_ref[rows, :] = conv
+    x_low = (conv * sigmoid(conv) * chan_ref[MASK : MASK + 1, :]).astype(bf16)
+
+    pre_b = zx_ref[rows, 2 * width + BLOCK :]
+    pad_b[lane, 0:SUB] = tail_b[lane] * keep_b
+    pad_b[lane, SUB:] = pre_b
+    tail_b[lane] = pre_b[BLOCK - SUB :, :]
+    conv_b = bc_par_ref[BIAS : BIAS + 1, :]
+    for k in range(KCONV):
+        conv_b = conv_b + pad_b[lane, SUB - KCONV + 1 + k : SUB - KCONV + 1 + k + BLOCK, :] * bc_par_ref[k : k + 1, :]
+    bc_low = (conv_b * sigmoid(conv_b)).astype(bf16)
+    bc_ref[rows, :] = bc_low
+    b_low, c_low = bc_low[:, :N], bc_low[:, N:]
+
+    raw = zx_ref[rows, 2 * width : 2 * width + BLOCK] + head_ref[DT_BIAS : DT_BIAS + 1, :]
+    dt = softplus(raw) * head_ref[HEAD_MASK : HEAD_MASK + 1, :]
+    cum = mm(tril, head_ref[NEG_A : NEG_A + 1, :] * dt, precision=highest)
+    step_ref[rows, :BLOCK] = cum
+    step_ref[rows, BLOCK:] = dt
+    cum_t, dt_t = cum.T, dt.T
+    last = cum[BLOCK - 1 :, :]
+    carry_x = mm_left(jnp.exp(cum), spread)
+    end_x = mm_left(jnp.exp(last - cum) * dt, spread)
+    last_x = carry_x[BLOCK - 1 :, :]
+
+    inner = mm(c_low, b_low, NT)
+    parts = []
+    for j in range(heads // 2):
+        pair = x_low[:, 2 * HEAD_DIM * j : 2 * HEAD_DIM * (j + 1)]
+        scores = [
+            (inner * decay_of(cum, cum_t, h, causal) * dt_t[h : h + 1, :]).astype(bf16)
+            for h in (2 * j, 2 * j + 1)
+        ]
+        parts.append(mm(jnp.concatenate(scores, axis=1), jnp.concatenate(halves(pair, col), axis=0)))
+    within = jnp.concatenate(parts, axis=1)
+
+    state_in = state[lane] * keep
+    state_ref[lane] = state_in
+    carried = mm_right(c_low, state_in) * carry_x
+    x_f = x_low.astype(f32)
+    mix_ref[rows, :] = within + carried + chan_ref[SKIP : SKIP + 1, :] * x_f
+    weighted = (x_f * end_x).astype(bf16)
+    state[lane] = last_x * state_in + mm(b_low, weighted, TN)
+
+
+def grad_kernel(bgrad_ref, w_ref, zx_ref, mix_ref, chan_ref, grad_ref, sums_ref):
+    grad = mm(bgrad_ref[...], w_ref[...], NT)
+    grad_ref[...] = grad
+    z = zx_ref[...]
+    gated = mix_ref[...] * (z * sigmoid(z))
+    ones = jnp.ones((SUB, gated.shape[1]), bf16)
+    square = mm_right(ones, gated * gated, NT)
+    cross = mm_right(ones, grad * chan_ref[GAIN : GAIN + 1, :] * gated, NT)
+    sub = lax.broadcasted_iota(jnp.int32, (SUB, BLOCK), 0)
+    for lane in range(gated.shape[0] // BLOCK):
+        at = slice(lane * BLOCK, (lane + 1) * BLOCK)
+        sums_ref[0, lane] = jnp.where(sub == 0, square[:, at], jnp.where(sub == 1, cross[:, at], 0.0))
+
+
+def run_grad(bgrad, w_out, zx, mix, chan, lanes):
+    rows, width = mix.shape
+    step = lanes * BLOCK
+    blocks = rows // step
+    by_block = lambda cols: pl.BlockSpec((step, cols), lambda c: (c, 0))
+    whole = lambda a: pl.BlockSpec(a.shape, lambda c: (0,) * a.ndim)
+    return pl.pallas_call(
+        grad_kernel,
+        grid=(blocks,),
+        in_specs=[by_block(bgrad.shape[1]), whole(w_out), by_block(width), by_block(width), whole(chan)],
+        out_specs=[by_block(width), pl.BlockSpec((1, lanes, SUB, BLOCK), lambda c: (c, 0, 0, 0))],
+        out_shape=[jax.ShapeDtypeStruct((rows, width), f32), jax.ShapeDtypeStruct((blocks, lanes, SUB, BLOCK), f32)],
+        compiler_params=pltpu.CompilerParams(vmem_limit_bytes=32 << 20),
+        cost_estimate=pl.CostEstimate(flops=2 * rows * width * bgrad.shape[1], bytes_accessed=rows * width * 24, transcendentals=rows * width),
+        name="mixed_grad",
+    )(bgrad, w_out, zx, mix, chan)
 
 
 def backward_kernel(
@@ -298,10 +314,10 @@
     for s in range(peers):
         tile = [dt[:, s * heads : (s + 1) * heads], bc[:, s * share : (s + 1) * share], rest]
         third_ref[s] = jnp.concatenate(tile, axis=1).astype(bf16)
-    lane = lax.broadcasted_iota(jnp.int32, (SUB, BLOCK), 1)
+    sub = lax.broadcasted_iota(jnp.int32, (SUB, BLOCK), 0)
     tile = jnp.zeros((SUB, BLOCK), f32)
-    for l in range(lanes):
-        tile = jnp.where(lane == l, start_ref[0, l].astype(f32), tile)
+    for lane in range(lanes):
+        tile = jnp.where(sub == lane, start_ref[0, lane].astype(f32), tile)
     starts_ref[...] = tile
 
 
@@ -318,40 +334,6 @@
         compiler_params=pltpu.CompilerParams(vmem_limit_bytes=32 << 20),
         name="entry",
     )(valid, starts, tokens, cotangent, gain[None], w_bc, w_dt)
-
-
-def run_forward(keep, zx, grad, chan, bc_par, head, spread, lanes, heads):
-    rows, width = grad.shape
-    step = lanes * BLOCK
-    blocks = rows // step
-    by_block = lambda cols: pl.BlockSpec((step, cols), lambda c: (c, 0))
-    whole = lambda a: pl.BlockSpec(a.shape, lambda c: (0,) * a.ndim)
-    per_lane = lambda r, cols: pl.BlockSpec((1, lanes, r, cols), lambda c: (c, 0, 0, 0))
-    return pl.pallas_call(
-        partial(forward_kernel, lanes=lanes, heads=heads),
-        grid=(blocks,),
-        in_specs=[
-            pl.BlockSpec(memory_space=pltpu.SMEM), by_block(zx.shape[1]), by_block(width),
-            whole(chan), whole(bc_par), whole(head), whole(spread),
-        ],
-        out_specs=[
-            by_block(width), by_block(width), by_block(2 * N), by_block(2 * BLOCK),
-            per_lane(N, width), per_lane(SUB, width), per_lane(SUB, BLOCK),
-        ],
-        out_shape=[
-            jax.ShapeDtypeStruct((rows, width), f32), jax.ShapeDtypeStruct((rows, width), f32),
-            jax.ShapeDtypeStruct((rows, 2 * N), bf16), jax.ShapeDtypeStruct((rows, 2 * BLOCK), f32),
-            jax.ShapeDtypeStruct((blocks, lanes, N, width), f32), jax.ShapeDtypeStruct((blocks, lanes, SUB, width), f32),
-            jax.ShapeDtypeStruct((blocks, lanes, SUB, BLOCK), f32),
-        ],
-        scratch_shapes=[
-            pltpu.VMEM((lanes, N, width), f32), pltpu.VMEM((lanes, SUB, width), f32), pltpu.VMEM((lanes, SUB, 2 * N), f32),
-            pltpu.VMEM((lanes, BLOCK + SUB, width), f32), pltpu.VMEM((lanes, BLOCK + SUB, 2 * N), f32),
-        ],
-        compiler_params=pltpu.CompilerParams(vmem_limit_bytes=40 << 20, dimension_semantics=("arbitrary",)),
-        cost_estimate=pl.CostEstimate(flops=rows * width * 2048, bytes_accessed=rows * width * 32, transcendentals=rows * width * 4),
-        name="mix_forward",
-    )(keep, zx, grad, chan, bc_par, head, spread)
 
 
 def run_backward(keep, zx, grad, chan, head, spread, conv, mix, bc, step_arr, state, tail, scale, lanes, heads):
@@ -400,25 +382,105 @@
     pl.semaphore_wait(barrier, len(others))
 
 
-def gather_kernel(
-    zx_ref, third_ref, bc_ref, own_ref, start_ref, w_ref, rows_ref, starts_ref,
-    w_send, w_recv, st_send, st_recv, own_sem, wide_send, wide_recv,
-    up_send, up_recv, down_send, down_recv, mate_send, mate_recv,
-    *, peers, widths, chans,
+def remote(src, dst, send, recv, device):
+    return pltpu.make_async_remote_copy(
+        src_ref=src, dst_ref=dst, send_sem=send, recv_sem=recv, device_id=device, device_id_type=MESH
+    )
+
+
+class Rows:
+    def __init__(self, own_ref, all_ref, sems, peers):
+        self.own, self.all, self.sems, self.peers = own_ref, all_ref, sems, peers
+        self.width, self.place = lax.axis_index("width"), lax.axis_index("seq")
+        self.chips, self.chip = peers // 2, self.place // 2
+
+    def hop(self, ref, s, step, by):
+        send, recv = self.sems[0 if by > 0 else 2], self.sems[1 if by > 0 else 3]
+        device = (self.width, jnp.clip(self.place + 2 * by, 0, self.peers - 1))
+        return remote(ref, self.all.at[s], send.at[step], recv.at[step], device)
+
+    def over(self, ref, s, slot):
+        device = (self.width, jnp.bitwise_xor(self.place, 1))
+        return remote(ref, self.all.at[s], self.sems[4].at[slot], self.sems[5].at[slot], device)
+
+    def inside(self, by):
+        return self.chip + 1 < self.chips if by > 0 else self.chip > 0
+
+    def reached(self, by, step):
+        return self.chip >= step if by > 0 else self.chip + step < self.chips
+
+    def source(self, by, step):
+        return jnp.clip(self.place - 2 * by * step, 0, self.peers - 1)
+
+    def keep(self):
+        return pltpu.make_async_copy(self.own, self.all.at[self.place], self.sems[6])
+
+    def start(self):
+        self.keep().start()
+        for by in (1, -1):
+            @pl.when(self.inside(by))
+            def _():
+                self.hop(self.own, self.place, 0, by).start()
+        self.over(self.own, self.place, 0).start()
+
+    def pass_on(self, step):
+        for by in (1, -1):
+            @pl.when(self.reached(by, step))
+            def _():
+                s = self.source(by, step)
+                ref = self.all.at[s]
+                self.hop(ref, s, step - 1, by).wait_recv()
+
+                @pl.when(self.inside(by))
+                def _():
+                    self.hop(ref, s, step, by).start()
+                self.over(ref, s, 2 * step - (by > 0)).start()
+
+    def arrived(self):
+        self.keep().wait()
+        self.over(self.own, self.place, 0).wait()
+        for step in range(1, self.chips):
+            for by in (1, -1):
+                @pl.when(self.reached(by, step))
+                def _():
+                    s = self.source(by, step)
+                    self.over(self.all.at[s], s, 2 * step - (by > 0)).wait()
+
+    def sent(self):
+        for step in range(self.chips):
+            for by in (1, -1):
+                @pl.when(self.inside(by) & self.reached(by, step))
+                def _():
+                    s = self.source(by, step)
+                    self.hop(self.all.at[s], s, step, by).wait_send()
+
+
+ROW_SEMS = 7
+
+
+def row_sems(chips):
+    dma = pltpu.SemaphoreType.DMA
+    return [dma((chips,)), dma((chips,)), dma((chips,)), dma((chips,)), dma((2 * chips,)), dma((2 * chips,)), dma(())]
+
+
+def front_kernel(
+    zx_ref, third_ref, bc_ref, own_ref, grad_ref, start_ref, chan_ref, bc_par_ref, head_ref, spread_ref,
+    w_ref, rows_ref, grads_ref, starts_ref, out_zx, out_conv, out_mix, out_bc, out_step, out_state, out_tail,
+    w_v, rows_v, starts_v, zx_v, conv_v, mix_v, bc_v, step_v, state_v, tail_v,
+    state, tail_x, tail_b, pad_x, pad_b,
+    w_send, w_recv, st_send, st_recv, own_sem, wide_send, wide_recv, in_sem, out_sem, *sems,
+    peers, widths, lanes, heads,
 ):
     width, place = lax.axis_index("width"), lax.axis_index("seq")
     chips = peers // 2
-    chip = place // 2
+    chans = heads * HEAD_DIM
     quarter = zx_ref.shape[0] // widths
     ring = [lax.rem(place + by, peers) for by in range(1, peers)]
     cross = [jnp.bitwise_xor(width, m) for m in range(1, widths)]
     greet([(width, s) for s in ring] + [(w, place) for w in cross])
     mine = pl.ds(pl.multiple_of(width * quarter, quarter), quarter)
-
-    def remote(src, dst, send, recv, device):
-        return pltpu.make_async_remote_copy(
-            src_ref=src, dst_ref=dst, send_sem=send, recv_sem=recv, device_id=device, device_id_type=MESH
-        )
+    rows = Rows(own_ref, rows_ref, sems[:ROW_SEMS], peers)
+    grads = Rows(grad_ref, grads_ref, sems[ROW_SEMS:], peers)
 
     def columns(half, s):
         return pl.ds(pl.multiple_of(half * peers * chans + s * chans, 128), chans)
@@ -441,95 +503,116 @@
         for k, (part, spot) in enumerate(zip(parts(place), spots))
     ]
     keeps.append(pltpu.make_async_copy(start_ref, starts_ref.at[place], own_sem.at[4]))
-    keeps.append(pltpu.make_async_copy(own_ref, rows_ref.at[place], own_sem.at[5]))
     for keep in keeps:
         keep.start()
-
-    def hop(ref, s, step, by):
-        send, recv = (up_send, up_recv) if by > 0 else (down_send, down_recv)
-        return remote(ref, rows_ref.at[s], send.at[step], recv.at[step], (width, jnp.clip(place + 2 * by, 0, peers - 1)))
-
-    def over(ref, s, slot):
-        return remote(ref, rows_ref.at[s], mate_send.at[slot], mate_recv.at[slot], (width, jnp.bitwise_xor(place, 1)))
-
-    def inside(by):
-        return chip + 1 < chips if by > 0 else chip > 0
-
-    def reached(by, step):
-        return chip >= step if by > 0 else chip + step < chips
-
-    for by in (1, -1):
-        @pl.when(inside(by))
-        def _():
-            hop(own_ref, place, 0, by).start()
-    over(own_ref, place, 0).start()
+    rows.start()
 
     for push in pushes:
         push.wait_recv()
     for keep in keeps:
         keep.wait()
-    shares = []
-    for m, w in enumerate(cross):
-        shares.append(remote(w_ref.at[:, width], w_ref.at[:, width], wide_send.at[m], wide_recv.at[m], (w, place)))
+    shares = [
+        remote(w_ref.at[:, width], w_ref.at[:, width], wide_send.at[m], wide_recv.at[m], (w, place)) for m, w in enumerate(cross)
+    ]
     for share in shares:
         share.start()
-
+    for step in range(1, chips - 1):
+        rows.pass_on(step)
+    grads.start()
+    for share in shares:
+        share.wait_recv()
+    in_w = pltpu.make_async_copy(w_ref, w_v, own_sem.at[0])
+    in_starts = pltpu.make_async_copy(starts_ref, starts_v, own_sem.at[1])
+    in_w.start()
+    in_starts.start()
+    rows.pass_on(chips - 1)
+    rows.arrived()
+    loads = [pltpu.make_async_copy(rows_ref.at[c], rows_v.at[c], in_sem.at[c]) for c in range(peers)]
+    for load in loads:
+        load.start()
+    for array in (state, tail_x, tail_b):
+        array[...] = jnp.zeros_like(array)
+    in_w.wait()
+    in_starts.wait()
+
+    outs = [
+        (zx_v, out_zx), (conv_v, out_conv), (mix_v, out_mix), (bc_v, out_bc), (step_v, out_step), (state_v, out_state), (tail_v, out_tail)
+    ]
+
+    def out_copies(c):
+        return [pltpu.make_async_copy(src.at[c], dst.at[c], out_sem.at[k, c]) for k, (src, dst) in enumerate(outs)]
+
+    def compute(first, last):
+        @pl.loop(first, last)
+        def _(c):
+            pltpu.make_async_copy(rows_ref.at[c], rows_v.at[c], in_sem.at[c]).wait()
+            weights = w_v[...].reshape(w_v.shape[0] * w_v.shape[1] * w_v.shape[2], w_v.shape[3])
+            zx_v[c] = mm(rows_v[c], weights)
+            spread = spread_ref[...]
+            for lane in range(lanes):
+                forward_block(
+                    1.0 - starts_v[c, lane : lane + 1, :], zx_v.at[c], chan_ref, bc_par_ref, head_ref, spread,
+                    conv_v.at[c], mix_v.at[c], bc_v.at[c], step_v.at[c], state_v.at[c], tail_v.at[c],
+                    state, tail_x, tail_b, pad_x, pad_b, lane=lane, heads=heads,
+                )
+            for copy in out_copies(c):
+                copy.start()
+
+    per = -(-peers // 2)
     for step in range(1, chips):
-        for by in (1, -1):
-            @pl.when(reached(by, step))
-            def _():
-                s = jnp.clip(place - 2 * by * step, 0, peers - 1)
-                ref = rows_ref.at[s]
-                hop(ref, s, step - 1, by).wait_recv()
-
-                @pl.when(inside(by))
-                def _():
-                    hop(ref, s, step, by).start()
-                over(ref, s, 2 * step - (by > 0)).start()
-
+        first, last = min((step - 1) * per, peers), min(step * per, peers)
+        if step == chips - 1:
+            last = peers
+        if first < last:
+            compute(first, last)
+        grads.pass_on(step)
+
+    grads.arrived()
     for share in shares:
-        share.wait()
+        share.wait_send()
     for push in pushes:
         push.wait_send()
-    over(own_ref, place, 0).wait()
-    for step in range(chips):
-        for by in (1, -1):
-            if step:
-                @pl.when(reached(by, step))
-                def _():
-                    s = jnp.clip(place - 2 * by * step, 0, peers - 1)
-                    over(rows_ref.at[s], s, 2 * step - (by > 0)).wait()
-
-            @pl.when(inside(by) & reached(by, step))
-            def _():
-                s = jnp.clip(place - 2 * by * step, 0, peers - 1)
-                hop(rows_ref.at[s], s, step, by).wait_send()
-
-
-def gathered_in(w_zx, third, w_bc, own_rows, start_tile, chans):
+    rows.sent()
+    grads.sent()
+
+    @pl.loop(0, peers)
+    def _(c):
+        for copy in out_copies(c):
+            copy.wait()
+
+
+def front(w_zx, third, w_bc, own_rows, own_grads, start_tile, chan, bc_par, head, spread, lanes, heads):
     peers, widths = lax.axis_size("seq"), lax.axis_size("width")
     own, model = own_rows.shape
     quarter = own // widths
+    chans = heads * HEAD_DIM
+    cols = 2 * chans + BLOCK + 2 * N
     dma = pltpu.SemaphoreType.DMA
-    chips = peers // 2
-    anywhere = pl.BlockSpec(memory_space=pl.ANY)
+    anywhere, vmem = pl.BlockSpec(memory_space=pl.ANY), pl.BlockSpec(memory_space=pltpu.VMEM)
+    gathered = [
+        ((peers, widths, quarter, cols), bf16), ((peers, own, model), bf16), ((peers, own, model), bf16),
+        ((peers,) + start_tile.shape, f32),
+    ]
+    computed = [
+        ((peers, own, cols), f32), ((peers, own, chans), f32), ((peers, own, chans), f32), ((peers, own, 2 * N), bf16),
+        ((peers, own, 2 * BLOCK), f32), ((peers, lanes, N, chans), f32), ((peers, lanes, SUB, chans), f32),
+    ]
     return pl.pallas_call(
-        partial(gather_kernel, peers=peers, widths=widths, chans=chans),
-        in_specs=[anywhere] * 5,
-        out_specs=[anywhere] * 3,
-        out_shape=[
-            jax.ShapeDtypeStruct((peers, widths, quarter, 2 * chans + BLOCK + 2 * N), bf16),
-            jax.ShapeDtypeStruct((peers, own, model), bf16),
-            jax.ShapeDtypeStruct((peers,) + start_tile.shape, f32),
+        partial(front_kernel, peers=peers, widths=widths, lanes=lanes, heads=heads),
+        in_specs=[anywhere] * 6 + [vmem] * 4,
+        out_specs=[anywhere] * (len(gathered) + len(computed)),
+        out_shape=[jax.ShapeDtypeStruct(*a) for a in gathered + computed],
+        scratch_shapes=[
+            *[pltpu.VMEM(*a) for a in (gathered[0], gathered[1], gathered[3], *computed)],
+            pltpu.VMEM((lanes, N, chans), f32), pltpu.VMEM((lanes, SUB, chans), f32), pltpu.VMEM((lanes, SUB, 2 * N), f32),
+            pltpu.VMEM((lanes, BLOCK + SUB, chans), f32), pltpu.VMEM((lanes, BLOCK + SUB, 2 * N), f32),
+            dma((4, peers - 1)), dma((4, peers - 1)), dma((peers - 1,)), dma((peers - 1,)),
+            dma((5,)), dma((widths - 1,)), dma((widths - 1,)), dma((peers,)), dma((len(computed), peers)),
+            *row_sems(peers // 2), *row_sems(peers // 2),
         ],
-        scratch_shapes=[
-            dma((4, peers - 1)), dma((4, peers - 1)), dma((peers - 1,)), dma((peers - 1,)),
-            dma((6,)), dma((widths - 1,)), dma((widths - 1,)),
-            dma((chips,)), dma((chips,)), dma((chips,)), dma((chips,)), dma((2 * chips,)), dma((2 * chips,)),
-        ],
-        compiler_params=pltpu.CompilerParams(collective_id=1, has_side_effects=True),
-        name="gather_in",
-    )(w_zx, third, w_bc, own_rows, start_tile)
+        compiler_params=pltpu.CompilerParams(collective_id=1, has_side_effects=True, vmem_limit_bytes=60 << 20),
+        name="front",
+    )(w_zx, third, w_bc, own_rows, own_grads, start_tile, chan, bc_par, head, spread)
 
 
 ROWS_AT_ONCE = 16
@@ -923,12 +1006,6 @@
     used = heads + share
     normed_own, bgrad_own, third_src, start_tile = entry(valid, starts, tokens, cotangent, norm_gain, w_bc, w_dt, peers)
     row_mask = (jnp.arange(BLOCK)[None, :] < valid[0][:, None]).astype(f32).reshape(-1, 1)
-    weights, normed, starts_all = gathered_in(w_zx, third_src, w_bc, normed_own, start_tile, chans)
-    weights = weights.reshape(model, -1)
-    normed = normed.reshape(rows, model)
-    bgrad = lax.all_gather(bgrad_own, "seq", axis=0, tiled=True)
-    keep = 1.0 - starts_all[:, 0, :lanes]
-
     taps_x = lax.dynamic_slice_in_dim(conv_w, first * HEAD_DIM, chans, 0).T
     of_chans = lambda a: lax.dynamic_slice_in_dim(a, first * HEAD_DIM, chans, 0)
     of_heads = lambda a: jnp.pad(lax.dynamic_slice_in_dim(a, first, heads, 0), (0, BLOCK - heads))
@@ -940,11 +1017,15 @@
     head = packed_rows([of_heads(dt_bias), of_heads(-jnp.exp(a_log)), head_on], SUB)
     spread = (jnp.arange(chans)[None, :] // HEAD_DIM == jnp.arange(BLOCK)[:, None]).astype(bf16)
 
-    zx = mm(normed, weights)
-    mixed_grad = mm(bgrad, w_out, NT)
-    conv, mix, bc, steps, state, tail, sums = run_forward(
-        keep, zx, mixed_grad, chan, bc_par, head, spread, lanes, heads
-    )
+    weights, normed, bgrad, starts_all, *computed = front(
+        w_zx, third_src, w_bc, normed_own, bgrad_own, start_tile, chan, bc_par, head, spread, lanes, heads
+    )
+    weights = weights.reshape(model, -1)
+    normed, bgrad = normed.reshape(rows, model), bgrad.reshape(rows, model)
+    keep = 1.0 - starts_all[:, :lanes, 0]
+    zx, conv, mix, bc, steps = [a.reshape(rows, a.shape[-1]) for a in computed[:5]]
+    state, tail = computed[5:]
+    mixed_grad, sums = run_grad(bgrad, w_out, zx, mix, chan, lanes)
     sums = summed_small(sums[:, :, :2, :].reshape(-1, BLOCK)).reshape(peers, lanes, 2, BLOCK)
     gate_rate = lax.rsqrt(sums[:, :, 0] / count + epsilon).reshape(rows, 1)
     gate_pull = gate_rate * gate_rate * gate_rate * sums[:, :, 1].reshape(rows, 1) / count

time: 573 us -> 528 us (0.921)
  the two profiles are of different devices: /device:TPU:0 before, /device:TPU:9 now
where the time goes in v3:
time: 528 us; the launch traced here: 522 us
  Pallas kernels  349 us (66%)
  local copies, waits for them, and re-layouts  58.1 us (11%)
  matrix products  52.4 us (10%)
  waiting for transfers between devices  18.4 us (3%)
  other arithmetic  17.4 us (3%)
  between operations  14.8 us (3%)
  starting transfers between devices  11.6 us (2%)
    pallas_call x1, Pallas kernels, front(): pl.pallas_call(partial(front_kernel, peers=peers, widths=widths, lanes=la...  173 us
    pallas_call x1, Pallas kernels, scattered_out(): pl.pallas_call(partial(scatter_kernel, peers=peers, widths=widths), in_sp...  109 us
    dot_general x5, matrix products, mm(): lax.dot_general(left, right, (dims, ((), ())), precision=precision, prefe...  52.4 us
    unnamed x70, local copies, waits for them, and re-layouts  36.2 us
    pallas_call x1, Pallas kernels, run_backward(): pl.pallas_call(partial(backward_kernel, lanes=lanes, heads=heads, blocks=...  34.1 us
    all_to_all x1, waiting for transfers between devices, heads_body(): lax.all_to_all(dbc.reshape(peers, share, rows), 'seq', 0, 0, tiled=True)  17.1 us
    pallas_call x1, Pallas kernels, summed_small(): pl.pallas_call(partial(sum_kernel, peers=peers), out_shape=jax.ShapeDtype...  13.9 us
  transfers between devices with their start and end apart: 8, of which 2 were waited for; matrix products, arithmetic and copies ran while one was open for 12% of the time, Pallas kernels for 7%

profile of v3, /device:TPU:9, one launch (start us, length us, event | category | flops | bytes accessed | tf_op | source)
XLA Modules:
  0.0 521.7 jit_solution(7012494853822693534)
XLA Ops:
  22.0 1.5 entry.1
  26.9 173.4 %front.1 = (bf16[8,4,64,1408]{3,2,1,0:T(8,128)(2,1)}, bf16[8,256,2048]{2,1,0:T(8,128)(2,1)}, bf16[8,256,2048]{2,1,0:T(8,128)(2,1)}, f32[8,8,128]{2,1,0:T(8,128)}...) custom-call(bf16[256,8192]{1,0:T(8,128)(2,1)} %w_ref.3, ...), custom_call_target="tpu_custom_call" | custom-call | tf_op jit(solution)/shard_map/front/pallas_call | solution.py:600
  200.3 2.2 copy-done.1
  202.5 3.4 copy-done.5
  205.8 9.8 %mixed_grad.1 = (f32[2048,512]{1,0:T(8,128)S(1)}, f32[8,2,8,128]{3,2,1,0:T(8,128)S(1)}) custom-call(bf16[2048,2048]{1,0:T(8,128)(2,1)S(1)} %bitcast.85, bf16[512,2048]{1,0:T(8,128)(2,1)S(1)} %copy-done.14, f32[2048,1408]{1,0:T(8,128)} %bitcast.78, f32[2048,512]{1,0:T(8,128)S(1)} %bitcast.83, f32[8,512]{1,0:T(8,128)S(1)} %copy-done.24), custom_call_target="tpu_custom_call" | custom-call | flops 4294967296 | bytes 25165824 | tf_op jit(solution)/shard_map/mixed_grad/pallas_call | solution.py:164
  215.6 2.0 copy-done.10
  218.3 13.9 %row_sums.1 = f32[32,128]{1,0:T(8,128)} custom-call(f32[32,128]{1,0:T(8,128)} %bitcast.106), custom_call_target="tpu_custom_call" | custom-call | tf_op jit(solution)/shard_map/row_sums/pallas_call | solution.py:902
  233.0 4.2 multiply_convert_fusion
  237.3 1.3 copy-done.32
  238.6 6.9 %convolution_convert_fusion = bf16[2048,2048]{1,0:T(8,128)(2,1)} fusion(bf16[2048,512]{1,0:T(8,128)(2,1)S(1)} %multiply_convert_fusion, bf16[512,2048]{1,0:T(8,128)(2,1)S(1)} %copy-done.14), kind=kOutput, calls=%fused_computation | convolution fusion | flops 4299161600 | bytes 12582912 | tf_op jit(solution)/shard_map/dot_general | solution.py:29
  246.0 9.9 %convolution_convert_fusion.2 = bf16[512,2048]{1,0:T(8,128)(2,1)} fusion(bf16[2048,512]{1,0:T(8,128)(2,1)} %copy-done.32, bf16[2048,2048]{1,0:T(8,128)(2,1)} %bitcast.84), kind=kOutput, calls=%fused_computation.7 | convolution fusion | flops 4296015872 | bytes 12582912 | tf_op jit(solution)/shard_map/dot_general | solution.py:29
  255.9 3.0 dynamic-slice_bitcast_fusion
  266.7 34.1 %mix_backward.1 = (bf16[2048,1152]{1,0:T(8,128)(2,1)}, bf16[256,2048]{1,0:T(8,128)(2,1)S(1)}, f32[8,512]{1,0:T(8,128)S(1)}, f32[8,128]{1,0:T(8,128)S(1)}) custom-call(f32[8,2]{1,0:T(8,128)S(1)} %copy.63.keep_ref, f32[2048,1408]{1,0:T(8,128)} %bitcast.80, f32[2048,512]{1,0:T(8,128)} %copy-done.10, f32[8,512]{1,0:T(8,128)S(1)} %copy-done.24, ...), custom_call_target="tpu_custom_call" | custom-call | flops 6442450944 | bytes 41943040 | tf_op jit(solution)/shard_map/mix_backward/pallas_call | solution.py:347
  304.7 1.9 add_convert_fusion.1
  306.6 1.3 collective-permute-start.3
  309.3 6.2 %all-to-all-start = ((bf16[8,32,2048]{2,1,0:T(8,128)(2,1)}), bf16[8,32,2048]{2,1,0:T(8,128)(2,1)S(1)}, u32[]{:S(2)}, u32[]{:S(2)}) async-start(bf16[8,32,2048]{2,1,0:T(8,128)(2,1)} %bitcast.89), calls=%async_computation | async-start | bytes 2097152 | tf_op jit(solution)/shard_map/all_to_all | solution.py:1048
  315.5 14.1 %fusion.3 = bf16[2048,1024]{1,0:T(8,128)(2,1)} fusion(bf16[2048,2048]{1,0:T(8,128)(2,1)} %bitcast.123, bf16[2048,1152]{1,0:T(8,128)(2,1)} %get-tuple-element.78.ddt_ref), kind=kOutput, calls=%fused_computation.6 | convolution fusion | flops 8592031744 | bytes 16777216 | tf_op jit(solution)/shard_map/dot_general | solution.py:29
  329.7 1.3 collective-permute-done.5
  331.7 2.7 bitcast_convert_fusion
  334.4 17.1 %all-to-all-done.got_ref = bf16[8,32,2048]{2,1,0:T(8,128)(2,1)S(1)} async-done(((bf16[8,32,2048]{2,1,0:T(8,128)(2,1)}), bf16[8,32,2048]{2,1,0:T(8,128)(2,1)S(1)}, u32[]{:S(2)}, u32[]{:S(2)}) %all-to-all-start) | async-done | bytes 1048608 | tf_op jit(solution)/shard_map/all_to_all | solution.py:1048
  351.5 4.4 copy-done
  355.8 2.4 copy-done.6
  358.2 1.5 bc_backward.1
  359.7 4.7 fusion.17
  369.1 16.9 %convolution_convert_fusion.1 = bf16[2048,2048]{1,0:T(8,128)(2,1)} fusion(bf16[2048,1152]{1,0:T(8,128)(2,1)} %constant_dynamic-update-slice_fusion, bf16[2048,1408]{1,0:T(8,128)(2,1)} %bitcast.125), kind=kOutput, calls=%fused_computation.1 | convolution fusion | flops 9667870720 | bytes 17825792 | tf_op jit(solution)/shard_map/dot_general | solution.py:29
  386.0 2.6 add_convert_fusion
  388.6 109.5 %scatter_out.1 = (f32[256,2048]{1,0:T(8,128)S(1)}, bf16[8,4,64,1024]{3,2,1,0:T(8,128)(2,1)}, bf16[8,4,64,128]{3,2,1,0:T(8,128)(2,1)S(1)}) custom-call(bf16[8,256,2048]{2,1,0:T(8,128)(2,1)} %bitcast.93, bf16[8,4,64,1024]{3,2,1,0:T(8,128)(2,1)} %bitcast.94, bf16[8,4,64,128]{3,2,1,0:T(8,128)(2,1)S(1)} %maximum_maximum_fusion.third_ref, ...), custom_call_target="tpu_custom_call" | custom-call | tf_op jit(solution)/shard_map/scatter_out/pallas_call | solution.py:795
  498.1 1.3 copy-done.12
  501.7 2.2 copy-done.2
  503.9 2.2 copy-done.9
  506.1 5.2 lay_out.1
  513.3 1.3 copy.94
  (190 shorter events, 42.6 us)
Async XLA Ops:
  7.2 378.8 %reduce-scatter.2.cloned.1.call-start = ((), (), s32[]{:S(2)}) async-start(), calls=%async_computation.2 | async-start | bytes 9437184 | tf_op jit(solution)/shard_map/reduce_scatter | solution.py:1036
  16.6 1.2 copy-start.3
  17.9 1.2 copy-start.7
  22.0 178.3 %copy-start.14 = (bf16[512,2048]{1,0:T(8,128)(2,1)S(1)}, bf16[512,2048]{1,0:T(8,128)(2,1)}, u32[]{:S(2)}) copy-start(bf16[512,2048]{1,0:T(8,128)(2,1)} %w_ref.2) | copy-start | bytes 6291460
  22.0 178.3 %copy-start.24 = (f32[8,512]{1,0:T(8,128)S(1)}, f32[8,512]{1,0:T(8,128)}, u32[]{:S(2)}) copy-start(f32[8,512]{1,0:T(8,128)} %stack.69.chan_ref) | copy-start | bytes 49156
  23.5 1.0 copy-start.19
  200.3 2.2 copy-start.1
  202.5 3.4 copy-start.5
  215.6 2.0 copy-start.10
  237.2 1.3 copy-start.32
  255.9 8.6 %copy-start.11 = (f32[8,256,256]{2,1,0:T(8,128)S(1)}, f32[8,256,256]{2,1,0:T(8,128)}, u32[]{:S(2)}) copy-start(f32[8,256,256]{2,1,0:T(8,128)} %get-tuple-element.70) | copy-start | bytes 6291460
  255.9 8.6 %copy-start.17 = (bf16[128,512]{1,0:T(8,128)(2,1)S(1)}, bf16[128,512]{1,0:T(8,128)(2,1)}, u32[]{:S(2)}) copy-start(bf16[128,512]{1,0:T(8,128)(2,1)} %fusion.6.spread_ref) | copy-start | bytes 393220
  255.9 8.6 %copy-start.27 = (f32[8,128]{1,0:T(8,128)S(1)}, f32[8,128]{1,0:T(8,128)}, u32[]{:S(2)}) copy-start(f32[8,128]{1,0:T(8,128)} %select_maximum_fusion.2.head_ref) | copy-start | bytes 12292
  258.9 45.8 %collective-permute-start = (bf16[128,2048]{1,0:T(8,128)(2,1)}, bf16[128,2048]{1,0:T(8,128)(2,1)}, u32[]{:S(2)}, u32[]{:S(2)}) collective-permute-start(bf16[128,2048]{1,0:T(8,128)(2,1)} %get-tuple-element.155), channel_id=1, source_target_pairs={{0,8},{8,0},{16,24},{24,16},{1,9},{9,1},{17,25},{25,17},{2,10},{10... | collective-permute-start | bytes 1572872 | tf_op jit(solution)/shard_map/ppermute | solution.py:959
  260.1 44.6 %collective-permute-start.1 = (bf16[128,2048]{1,0:T(8,128)(2,1)}, bf16[128,2048]{1,0:T(8,128)(2,1)}, u32[]{:S(2)}, u32[]{:S(2)}) collective-permute-start(bf16[128,2048]{1,0:T(8,128)(2,1)} %get-tuple-element.154), channel_id=1, source_target_pairs={{0,16},{8,24},{16,0},{24,8},{1,17},{9,25},{17,1},{25,9},{2,18},{10... | collective-permute-start | bytes 1572872 | tf_op jit(solution)/shard_map/ppermute | solution.py:959
  261.4 43.3 %collective-permute-start.2 = (bf16[128,2048]{1,0:T(8,128)(2,1)}, bf16[128,2048]{1,0:T(8,128)(2,1)}, u32[]{:S(2)}, u32[]{:S(2)}) collective-permute-start(bf16[128,2048]{1,0:T(8,128)(2,1)} %get-tuple-element.153), channel_id=1, source_target_pairs={{0,24},{8,16},{16,8},{24,0},{1,25},{9,17},{17,9},{25,1},{2,26},{10... | collective-permute-start | bytes 1572872 | tf_op jit(solution)/shard_map/ppermute | solution.py:959
  264.5 1.2 copy-start.18
  266.7 36.3 %copy-start.26 = (f32[2048]{0:T(1024)S(1)}, f32[2048]{0:T(1024)}, u32[]{:S(2)}) copy-start(f32[2048]{0:T(1024)} %param.19) | copy-start | bytes 24580
  266.7 37.8 %copy-start.31 = (s32[1,2]{1,0:T(1,128)S(1)}, s32[1,2]{1,0:T(1,128)}, u32[]{:S(2)}) copy-start(s32[1,2]{1,0:T(1,128)} %valid_ref.1) | copy-start | bytes 28
  306.6 23.1 %collective-permute-start.3 = (bf16[128,2048]{1,0:T(8,128)(2,1)S(1)}, bf16[128,2048]{1,0:T(8,128)(2,1)S(1)}, u32[]{:S(2)}, u32[]{:S(2)}) collective-permute-start(bf16[128,2048]{1,0:T(8,128)(2,1)S(1)} %add_convert_fusion.1), channel_id=1, source_target_pairs={{0,8},{8,0},{16,24},{24,16},{1,9},{9,1},{17,25},{25,17},{2,10},{10... | collective-permute-start | bytes 1572872 | tf_op jit(solution)/shard_map/ppermute | solution.py:959
  307.9 21.8 %collective-permute-start.4 = (bf16[128,2048]{1,0:T(8,128)(2,1)S(1)}, bf16[128,2048]{1,0:T(8,128)(2,1)S(1)}, u32[]{:S(2)}, u32[]{:S(2)}) collective-permute-start(bf16[128,2048]{1,0:T(8,128)(2,1)S(1)} %add_convert_fusion.1), channel_id=1, source_target_pairs={{0,16},{8,24},{16,0},{24,8},{1,17},{9,25},{17,1},{25,9},{2,18},{10... | collective-permute-start | bytes 1572872 | tf_op jit(solution)/shard_map/ppermute | solution.py:959
  309.1 21.9 %collective-permute-start.5 = (bf16[128,2048]{1,0:T(8,128)(2,1)S(1)}, bf16[128,2048]{1,0:T(8,128)(2,1)S(1)}, u32[]{:S(2)}, u32[]{:S(2)}) collective-permute-start(bf16[128,2048]{1,0:T(8,128)(2,1)S(1)} %add_convert_fusion.1), channel_id=1, source_target_pairs={{0,24},{8,16},{16,8},{24,0},{1,25},{9,17},{17,9},{25,1},{2,26},{10... | collective-permute-start | bytes 1572872 | tf_op jit(solution)/shard_map/ppermute | solution.py:959
  309.3 42.2 %all-to-all-start = ((bf16[8,32,2048]{2,1,0:T(8,128)(2,1)}), bf16[8,32,2048]{2,1,0:T(8,128)(2,1)S(1)}, u32[]{:S(2)}, u32[]{:S(2)}) async-start(bf16[8,32,2048]{2,1,0:T(8,128)(2,1)} %bitcast.89), calls=%async_computation | async-start | bytes 2097152 | tf_op jit(solution)/shard_map/all_to_all | solution.py:1048
  351.5 4.4 copy-start
  355.8 2.4 copy-start.6
  369.1 16.9 %copy-start.4 = (bf16[256,2048]{1,0:T(8,128)(2,1)S(1)}, bf16[256,2048]{1,0:T(8,128)(2,1)}, u32[]{:S(2)}) copy-start(bf16[256,2048]{1,0:T(8,128)(2,1)} %x_ref.3) | copy-start | bytes 3145732
  369.1 19.5 %copy-start.8 = (bf16[256,2048]{1,0:T(8,128)(2,1)S(1)}, bf16[256,2048]{1,0:T(8,128)(2,1)}, u32[]{:S(2)}) copy-start(bf16[256,2048]{1,0:T(8,128)(2,1)} %cot_ref.3) | copy-start | bytes 3145732
  388.6 113.1 %copy-start.16 = (bf16[256,256]{1,0:T(8,128)(2,1)S(1)}, bf16[256,256]{1,0:T(8,128)(2,1)}, u32[]{:S(2)}) copy-start(bf16[256,256]{1,0:T(8,128)(2,1)} %bc_ref.5) | copy-start | bytes 393220
  498.1 1.3 copy-start.12
  501.7 2.2 copy-start.2
  503.9 2.2 copy-start.9
  506.1 7.2 %copy-start.13 = (f32[256,2048]{1,0:T(8,128)S(1)}, f32[256,2048]{1,0:T(8,128)}, u32[]{:S(2)}) copy-start(f32[256,2048]{1,0:T(8,128)} %copy-done.12) | copy-start | bytes 6291460
  (9 other events, 7.2 us)
Sparse Core Ops, SparseCore 0:
  245.6 110.6 reduce-scatter.1

commit v4 on v3

--- a/solution.py
+++ b/solution.py
@@ -6,6 +6,7 @@
 from jax.experimental import pallas as pl
 from jax.experimental.pallas import tpu as pltpu
 from jax.sharding import PartitionSpec as P
+import numpy as np
 
 H = 64
 HEAD_DIM = 64
@@ -139,38 +140,6 @@
     mix_ref[rows, :] = within + carried + chan_ref[SKIP : SKIP + 1, :] * x_f
     weighted = (x_f * end_x).astype(bf16)
     state[lane] = last_x * state_in + mm(b_low, weighted, TN)
-
-
-def grad_kernel(bgrad_ref, w_ref, zx_ref, mix_ref, chan_ref, grad_ref, sums_ref):
-    grad = mm(bgrad_ref[...], w_ref[...], NT)
-    grad_ref[...] = grad
-    z = zx_ref[...]
-    gated = mix_ref[...] * (z * sigmoid(z))
-    ones = jnp.ones((SUB, gated.shape[1]), bf16)
-    square = mm_right(ones, gated * gated, NT)
-    cross = mm_right(ones, grad * chan_ref[GAIN : GAIN + 1, :] * gated, NT)
-    sub = lax.broadcasted_iota(jnp.int32, (SUB, BLOCK), 0)
-    for lane in range(gated.shape[0] // BLOCK):
-        at = slice(lane * BLOCK, (lane + 1) * BLOCK)
-        sums_ref[0, lane] = jnp.where(sub == 0, square[:, at], jnp.where(sub == 1, cross[:, at], 0.0))
-
-
-def run_grad(bgrad, w_out, zx, mix, chan, lanes):
-    rows, width = mix.shape
-    step = lanes * BLOCK
-    blocks = rows // step
-    by_block = lambda cols: pl.BlockSpec((step, cols), lambda c: (c, 0))
-    whole = lambda a: pl.BlockSpec(a.shape, lambda c: (0,) * a.ndim)
-    return pl.pallas_call(
-        grad_kernel,
-        grid=(blocks,),
-        in_specs=[by_block(bgrad.shape[1]), whole(w_out), by_block(width), by_block(width), whole(chan)],
-        out_specs=[by_block(width), pl.BlockSpec((1, lanes, SUB, BLOCK), lambda c: (c, 0, 0, 0))],
-        out_shape=[jax.ShapeDtypeStruct((rows, width), f32), jax.ShapeDtypeStruct((blocks, lanes, SUB, BLOCK), f32)],
-        compiler_params=pltpu.CompilerParams(vmem_limit_bytes=32 << 20),
-        cost_estimate=pl.CostEstimate(flops=2 * rows * width * bgrad.shape[1], bytes_accessed=rows * width * 24, transcendentals=rows * width),
-        name="mixed_grad",
-    )(bgrad, w_out, zx, mix, chan)
 
 
 def backward_kernel(
@@ -298,44 +267,6 @@
         dzx_ref[rows, width : 2 * width] = dpre.astype(bf16)
 
 
-def entry_kernel(valid_ref, start_ref, x_ref, cot_ref, gain_ref, bc_ref, dt_ref, normed_ref, bgrad_ref, third_ref, starts_ref, *, peers):
-    rows = x_ref.shape[0]
-    lanes = rows // BLOCK
-    x = x_ref[...].astype(f32)
-    normed_ref[...] = (x * lax.rsqrt(jnp.mean(x * x, axis=-1, keepdims=True) + epsilon) * gain_ref[...]).astype(bf16)
-    row = lax.broadcasted_iota(jnp.int32, (BLOCK, 1), 0)
-    for lane in range(lanes):
-        at = slice(lane * BLOCK, (lane + 1) * BLOCK)
-        mask = (row < valid_ref[0, lane]).astype(f32)
-        bgrad_ref[at, :] = (cot_ref[at, :].astype(f32) * mask).astype(bf16)
-    bc, dt = bc_ref[...].astype(f32), dt_ref[...].astype(f32)
-    share, heads = bc.shape[1] // peers, dt.shape[1] // peers
-    rest = jnp.zeros((rows, BLOCK - share - heads), f32)
-    for s in range(peers):
-        tile = [dt[:, s * heads : (s + 1) * heads], bc[:, s * share : (s + 1) * share], rest]
-        third_ref[s] = jnp.concatenate(tile, axis=1).astype(bf16)
-    sub = lax.broadcasted_iota(jnp.int32, (SUB, BLOCK), 0)
-    tile = jnp.zeros((SUB, BLOCK), f32)
-    for lane in range(lanes):
-        tile = jnp.where(sub == lane, start_ref[0, lane].astype(f32), tile)
-    starts_ref[...] = tile
-
-
-def entry(valid, starts, tokens, cotangent, gain, w_bc, w_dt, peers):
-    smem, vmem = pl.BlockSpec(memory_space=pltpu.SMEM), pl.BlockSpec(memory_space=pltpu.VMEM)
-    return pl.pallas_call(
-        partial(entry_kernel, peers=peers),
-        in_specs=[smem] * 2 + [vmem] * 5,
-        out_specs=[vmem] * 4,
-        out_shape=[
-            jax.ShapeDtypeStruct(tokens.shape, bf16), jax.ShapeDtypeStruct(tokens.shape, bf16),
-            jax.ShapeDtypeStruct((peers, w_bc.shape[0], BLOCK), bf16), jax.ShapeDtypeStruct((SUB, BLOCK), f32),
-        ],
-        compiler_params=pltpu.CompilerParams(vmem_limit_bytes=32 << 20),
-        name="entry",
-    )(valid, starts, tokens, cotangent, gain[None], w_bc, w_dt)
-
-
 def run_backward(keep, zx, grad, chan, head, spread, conv, mix, bc, step_arr, state, tail, scale, lanes, heads):
     rows, width = grad.shape
     step = lanes * BLOCK
@@ -351,7 +282,7 @@
             pl.BlockSpec(memory_space=pltpu.SMEM), by_block(2 * width + BLOCK), by_block(width),
             whole(chan), whole(head), whole(spread),
             by_block(width), by_block(width), by_block(2 * N), by_block(2 * BLOCK),
-            per_lane(N, width), per_lane(SUB, width), by_block(SUB),
+            per_lane(N, width), per_lane(SUB, width), by_block(BLOCK),
         ],
         out_specs=[
             by_block(2 * width + BLOCK), pl.BlockSpec((2 * N, step), lambda c: (0, blocks - 1 - c)),
@@ -376,10 +307,12 @@
 
 
 def greet(others):
-    barrier = pltpu.get_barrier_semaphore()
     for other in others:
-        pl.semaphore_signal(barrier, inc=1, device_id=other, device_id_type=MESH)
-    pl.semaphore_wait(barrier, len(others))
+        pl.semaphore_signal(pltpu.get_barrier_semaphore(), inc=1, device_id=other, device_id_type=MESH)
+
+
+def met(others):
+    pl.semaphore_wait(pltpu.get_barrier_semaphore(), len(others))
 
 
 def remote(src, dst, send, recv, device):
@@ -436,15 +369,20 @@
                     self.hop(ref, s, step, by).start()
                 self.over(ref, s, 2 * step - (by > 0)).start()
 
+    def mate(self, by, step):
+        if not step:
+            return self.over(self.own, self.place, 0)
+        s = self.source(by, step)
+        return self.over(self.all.at[s], s, 2 * step - (by > 0))
+
     def arrived(self):
         self.keep().wait()
-        self.over(self.own, self.place, 0).wait()
+        self.mate(1, 0).wait_recv()
         for step in range(1, self.chips):
             for by in (1, -1):
                 @pl.when(self.reached(by, step))
                 def _():
-                    s = self.source(by, step)
-                    self.over(self.all.at[s], s, 2 * step - (by > 0)).wait()
+                    self.mate(by, step).wait_recv()
 
     def sent(self):
         for step in range(self.chips):
@@ -453,6 +391,12 @@
                 def _():
                     s = self.source(by, step)
                     self.hop(self.all.at[s], s, step, by).wait_send()
+        self.mate(1, 0).wait_send()
+        for step in range(1, self.chips):
+            for by in (1, -1):
+                @pl.when(self.reached(by, step))
+                def _():
+                    self.mate(by, step).wait_send()
 
 
 ROW_SEMS = 7
@@ -464,11 +408,14 @@
 
 
 def front_kernel(
-    zx_ref, third_ref, bc_ref, own_ref, grad_ref, start_ref, chan_ref, bc_par_ref, head_ref, spread_ref,
-    w_ref, rows_ref, grads_ref, starts_ref, out_zx, out_conv, out_mix, out_bc, out_step, out_state, out_tail,
-    w_v, rows_v, starts_v, zx_v, conv_v, mix_v, bc_v, step_v, state_v, tail_v,
+    valid_ref, start_ref, x_ref, cot_ref, norm_gain_ref, bc_ref, dt_ref, taps_ref, bias_ref, dtb_ref, alog_ref, skip_ref,
+    gain_ref, spread_ref, zx_ref, wout_ref,
+    w_ref, rows_ref, grads_ref, starts_ref, chan_ref, head_ref,
+    out_zx, out_mix, out_grad, out_scale, out_low, out_part, out_conv, out_bc, out_step, out_state, out_tail,
+    w_v, rows_v, starts_v, wout_v, own_v, grad_v, third_v, start_v, bc_par,
+    zx_v, mix_v, mgrad_v, scale_v, low_v, conv_v, bc_v, step_v, state_v, tail_v, sums, sums_got,
     state, tail_x, tail_b, pad_x, pad_b,
-    w_send, w_recv, st_send, st_recv, own_sem, wide_send, wide_recv, in_sem, out_sem, *sems,
+    w_send, w_recv, st_send, st_recv, own_sem, wide_send, wide_recv, in_sem, out_sem, slot_sem, sum_send, sum_recv, *sems,
     peers, widths, lanes, heads,
 ):
     width, place = lax.axis_index("width"), lax.axis_index("seq")
@@ -477,35 +424,77 @@
     quarter = zx_ref.shape[0] // widths
     ring = [lax.rem(place + by, peers) for by in range(1, peers)]
     cross = [jnp.bitwise_xor(width, m) for m in range(1, widths)]
-    greet([(width, s) for s in ring] + [(w, place) for w in cross])
+    others = [(width, s) for s in ring] + [(w, place) for w in cross]
+    greet(others)
+
+    x = x_ref[...].astype(f32)
+    own_v[...] = (x * lax.rsqrt(jnp.mean(x * x, axis=-1, keepdims=True) + epsilon) * norm_gain_ref[...]).astype(bf16)
+    row = lax.broadcasted_iota(jnp.int32, (BLOCK, 1), 0)
+    sub = lax.broadcasted_iota(jnp.int32, (SUB, BLOCK), 0)
+    tile = jnp.zeros((SUB, BLOCK), f32)
+    for lane in range(lanes):
+        at = slice(lane * BLOCK, (lane + 1) * BLOCK)
+        mask = (row < valid_ref[0, lane]).astype(f32)
+        grad_v[at, :] = (cot_ref[at, :].astype(f32) * mask).astype(bf16)
+        tile = jnp.where(sub == lane, start_ref[0, lane].astype(f32), tile)
+    start_v[...] = tile
+    bc, dt = bc_ref[...].astype(f32), dt_ref[...].astype(f32)
+    share = bc.shape[1] // peers
+    rest = jnp.zeros((bc.shape[0], BLOCK - share - heads), f32)
+    for s in range(peers):
+        columns = [dt[:, s * heads : (s + 1) * heads], bc[:, s * share : (s + 1) * share], rest]
+        third_v[s] = jnp.concatenate(columns, axis=1).astype(bf16)
+    met(others)
+
     mine = pl.ds(pl.multiple_of(width * quarter, quarter), quarter)
-    rows = Rows(own_ref, rows_ref, sems[:ROW_SEMS], peers)
-    grads = Rows(grad_ref, grads_ref, sems[ROW_SEMS:], peers)
-
-    def columns(half, s):
+    rows = Rows(own_v, rows_ref, sems[:ROW_SEMS], peers)
+    grads = Rows(grad_v, grads_ref, sems[ROW_SEMS:], peers)
+
+    def columns_of(half, s):
         return pl.ds(pl.multiple_of(half * peers * chans + s * chans, 128), chans)
 
     wide = 2 * chans
     spots = [pl.ds(0, chans), pl.ds(chans, chans), pl.ds(wide, BLOCK), pl.ds(wide + BLOCK, 2 * N)]
 
     def parts(s):
-        return [zx_ref.at[mine, columns(0, s)], zx_ref.at[mine, columns(1, s)], third_ref.at[s, mine], bc_ref.at[mine]]
+        return [zx_ref.at[mine, columns_of(0, s)], zx_ref.at[mine, columns_of(1, s)], third_v.at[s, mine], bc_ref.at[mine]]
 
     pushes = []
     for i, s in enumerate(ring):
         for k, (part, spot) in enumerate(zip(parts(s), spots)):
             pushes.append(remote(part, w_ref.at[place, width, :, spot], w_send.at[k, i], w_recv.at[k, i], (width, s)))
-        pushes.append(remote(start_ref, starts_ref.at[place], st_send.at[i], st_recv.at[i], (width, s)))
+        pushes.append(remote(start_v, starts_ref.at[place], st_send.at[i], st_recv.at[i], (width, s)))
     for push in pushes:
         push.start()
     keeps = [
         pltpu.make_async_copy(part, w_ref.at[place, width, :, spot], own_sem.at[k])
         for k, (part, spot) in enumerate(zip(parts(place), spots))
     ]
-    keeps.append(pltpu.make_async_copy(start_ref, starts_ref.at[place], own_sem.at[4]))
+    keeps.append(pltpu.make_async_copy(start_v, starts_ref.at[place], own_sem.at[4]))
     for keep in keeps:
         keep.start()
     rows.start()
+
+    active = jnp.right_shift(jnp.int32(H), widths - 1 - width)
+    first = place * heads
+    here = columns_of(0, place)
+    spread = spread_ref[...]
+    pick_row = lax.broadcasted_iota(jnp.int32, (H, BLOCK), 0)
+    pick_lane = lax.broadcasted_iota(jnp.int32, (H, BLOCK), 1)
+    chosen = ((pick_row == pick_lane + first) & (pick_lane < heads)).astype(f32)
+    per_head = jnp.concatenate(
+        [dtb_ref[...], -jnp.exp(alog_ref[...]), jnp.ones((1, H), f32), skip_ref[...], jnp.zeros((SUB - 4, H), f32)], axis=0
+    )
+    per_head = mm(per_head, chosen, precision=highest)
+    head_lane = lax.broadcasted_iota(jnp.int32, (SUB, BLOCK), 1)
+    head_ref[...] = jnp.where((sub == HEAD_MASK) & (head_lane + first >= active), 0.0, per_head)
+    on_chans = mm(head_ref[...], spread.astype(f32), precision=highest)
+    chan_ref[...] = jnp.concatenate(
+        [taps_ref[:, here], bias_ref[:, here], on_chans[3:4], gain_ref[:, here], on_chans[HEAD_MASK : HEAD_MASK + 1]], axis=0
+    )
+    bc_par[...] = jnp.concatenate(
+        [taps_ref[:, E:], bias_ref[:, E:], jnp.zeros((SUB - KCONV - 1, 2 * N), f32)], axis=0
+    )
 
     for push in pushes:
         push.wait_recv()
@@ -514,105 +503,206 @@
     shares = [
         remote(w_ref.at[:, width], w_ref.at[:, width], wide_send.at[m], wide_recv.at[m], (w, place)) for m, w in enumerate(cross)
     ]
-    for share in shares:
-        share.start()
+    for copy in shares:
+        copy.start()
     for step in range(1, chips - 1):
         rows.pass_on(step)
     grads.start()
-    for share in shares:
-        share.wait_recv()
+    for copy in shares:
+        copy.wait_recv()
     in_w = pltpu.make_async_copy(w_ref, w_v, own_sem.at[0])
     in_starts = pltpu.make_async_copy(starts_ref, starts_v, own_sem.at[1])
-    in_w.start()
-    in_starts.start()
+    in_wout = pltpu.make_async_copy(wout_ref, wout_v, own_sem.at[2])
+    for copy in (in_w, in_starts, in_wout):
+        copy.start()
     rows.pass_on(chips - 1)
     rows.arrived()
-    loads = [pltpu.make_async_copy(rows_ref.at[c], rows_v.at[c], in_sem.at[c]) for c in range(peers)]
-    for load in loads:
-        load.start()
+
+    def load(src, s):
+        return pltpu.make_async_copy(src.at[s], rows_v.at[s], in_sem.at[s])
+
+    for c in range(peers):
+        load(rows_ref, c).start()
     for array in (state, tail_x, tail_b):
         array[...] = jnp.zeros_like(array)
-    in_w.wait()
-    in_starts.wait()
-
-    outs = [
-        (zx_v, out_zx), (conv_v, out_conv), (mix_v, out_mix), (bc_v, out_bc), (step_v, out_step), (state_v, out_state), (tail_v, out_tail)
-    ]
-
-    def out_copies(c):
-        return [pltpu.make_async_copy(src.at[c], dst.at[c], out_sem.at[k, c]) for k, (src, dst) in enumerate(outs)]
-
-    def compute(first, last):
-        @pl.loop(first, last)
+    for copy in (in_w, in_starts, in_wout):
+        copy.wait()
+
+    def out_copy(k, src, dst, c):
+        return pltpu.make_async_copy(src.at[c], dst.at[c], out_sem.at[k, c])
+
+    slots = [(conv_v, out_conv), (bc_v, out_bc), (step_v, out_step), (state_v, out_state), (tail_v, out_tail)]
+
+    def slot_copies(c):
+        slot = lax.rem(c, 2)
+        return [pltpu.make_async_copy(src.at[slot], dst.at[c], slot_sem.at[k, slot]) for k, (src, dst) in enumerate(slots)]
+
+    def compute(begin, end):
+        @pl.loop(begin, end)
         def _(c):
-            pltpu.make_async_copy(rows_ref.at[c], rows_v.at[c], in_sem.at[c]).wait()
+            load(rows_ref, c).wait()
+
+            @pl.when(c >= 2)
+            def _():
+                for copy in slot_copies(c - 2):
+                    copy.wait()
             weights = w_v[...].reshape(w_v.shape[0] * w_v.shape[1] * w_v.shape[2], w_v.shape[3])
             zx_v[c] = mm(rows_v[c], weights)
-            spread = spread_ref[...]
+            slot = lax.rem(c, 2)
             for lane in range(lanes):
                 forward_block(
-                    1.0 - starts_v[c, lane : lane + 1, :], zx_v.at[c], chan_ref, bc_par_ref, head_ref, spread,
-                    conv_v.at[c], mix_v.at[c], bc_v.at[c], step_v.at[c], state_v.at[c], tail_v.at[c],
+                    1.0 - starts_v[c, lane : lane + 1, :], zx_v.at[c], chan_ref, bc_par, head_ref, spread_ref[...],
+                    conv_v.at[slot], mix_v.at[c], bc_v.at[slot], step_v.at[slot], state_v.at[slot], tail_v.at[slot],
                     state, tail_x, tail_b, pad_x, pad_b, lane=lane, heads=heads,
                 )
-            for copy in out_copies(c):
+            out_copy(0, zx_v, out_zx, c).start()
+            out_copy(1, mix_v, out_mix, c).start()
+            for copy in slot_copies(c):
                 copy.start()
+
+    def gated_of(c):
+        z = zx_v[c, :, :chans]
+        return mix_v[c] * (z * sigmoid(z))
+
+    def mix_grad(s):
+        load(grads_ref, s).wait()
+        grad = mm(rows_v[s], wout_v[...], NT)
+        mgrad_v[s] = grad
+        out_copy(2, mgrad_v, out_grad, s).start()
+        gated = gated_of(s)
+        ones = jnp.ones((SUB, chans), bf16)
+        square = mm_right(ones, gated * gated, NT)
+        pulled = mm_right(ones, grad * chan_ref[GAIN : GAIN + 1, :] * gated, NT)
+        for lane in range(lanes):
+            at = slice(lane * BLOCK, (lane + 1) * BLOCK)
+            sums[0, pl.ds(s * lanes + lane, 1), :] = square[:1, at]
+            sums[1, pl.ds(s * lanes + lane, 1), :] = pulled[:1, at]
 
     per = -(-peers // 2)
     for step in range(1, chips):
-        first, last = min((step - 1) * per, peers), min(step * per, peers)
+        begin, end = min((step - 1) * per, peers), min(step * per, peers)
         if step == chips - 1:
-            last = peers
-        if first < last:
-            compute(first, last)
-        grads.pass_on(step)
-
-    grads.arrived()
-    for share in shares:
-        share.wait_send()
-    for push in pushes:
-        push.wait_send()
+            end = peers
+        if begin < end:
+            compute(begin, end)
+        if step < chips - 1:
+            grads.pass_on(step)
+
+    def at_distance(step, act):
+        if not step:
+            act(place, None)
+            act(jnp.bitwise_xor(place, 1), (1, 0))
+        for by in (1, -1):
+            if step:
+                @pl.when(grads.reached(by, step))
+                def _():
+                    s = grads.source(by, step)
+                    act(s, None)
+                    act(jnp.bitwise_xor(s, 1), (by, step))
+
+    def begin_load(s, mate):
+        if mate is not None:
+            grads.mate(*mate).wait_recv()
+        load(grads_ref, s).start()
+
+    grads.keep().wait()
+    for step in range(chips - 1):
+        at_distance(step, begin_load)
+    for step in range(chips - 1):
+        at_distance(step, lambda s, mate: mix_grad(s))
+    grads.pass_on(chips - 1)
+    at_distance(chips - 1, begin_load)
+    at_distance(chips - 1, lambda s, mate: mix_grad(s))
+
+    give = [remote(sums, sums_got.at[i], sum_send.at[i], sum_recv.at[i], (width, s)) for i, s in enumerate(ring)]
+    for copy in give:
+        copy.start()
+    for copy in give:
+        copy.wait_recv()
+    total = sums[...]
+    for i in range(peers - 1):
+        total = total + sums_got[i]
+    count = (active * HEAD_DIM).astype(f32)
+    rate = lax.rsqrt(total[0] / count + epsilon)
+    pull = rate * rate * rate * total[1] / count
+    blank = jnp.zeros((BLOCK - 2 * lanes * peers, BLOCK), f32)
+    by_time = jnp.concatenate([rate, pull, blank], axis=0).T
+    lane_at = lax.broadcasted_iota(jnp.int32, (BLOCK, BLOCK), 1)
+    for c in range(peers):
+        for lane in range(lanes):
+            i = c * lanes + lane
+            j = lanes * peers + i
+            scale_v[c, lane * BLOCK : (lane + 1) * BLOCK, :] = jnp.where(
+                lane_at == 0, by_time[:, i : i + 1], jnp.where(lane_at == 1, by_time[:, j : j + 1], 0.0)
+            )
+
+    @pl.loop(0, peers)
+    def _(c):
+        low = (gated_of(c) * scale_v[c, :, 0:1] * chan_ref[GAIN : GAIN + 1, :]).astype(bf16)
+        low_v[c] = low
+        rows_v[c] = mm(low, wout_v[...]).astype(bf16)
+        out_copy(3, scale_v, out_scale, c).start()
+        out_copy(4, low_v, out_low, c).start()
+        out_copy(5, rows_v, out_part, c).start()
+
+    for copy in shares + pushes + give:
+        copy.wait_send()
     rows.sent()
     grads.sent()
+    for c in (peers - 2, peers - 1):
+        for copy in slot_copies(c):
+            copy.wait()
 
     @pl.loop(0, peers)
     def _(c):
-        for copy in out_copies(c):
-            copy.wait()
-
-
-def front(w_zx, third, w_bc, own_rows, own_grads, start_tile, chan, bc_par, head, spread, lanes, heads):
+        for k, (src, dst) in enumerate(
+            [(zx_v, out_zx), (mix_v, out_mix), (mgrad_v, out_grad), (scale_v, out_scale), (low_v, out_low), (rows_v, out_part)]
+        ):
+            out_copy(k, src, dst, c).wait()
+
+
+def front(valid, starts, tokens, cotangent, norm_gain, w_bc, w_dt, taps, bias, dt_bias, a_log, d_skip, gate_gain, spread, w_zx, w_out):
     peers, widths = lax.axis_size("seq"), lax.axis_size("width")
-    own, model = own_rows.shape
+    own, model = tokens.shape
+    lanes = starts.shape[1]
     quarter = own // widths
-    chans = heads * HEAD_DIM
+    chans = w_out.shape[0]
+    heads = chans // HEAD_DIM
     cols = 2 * chans + BLOCK + 2 * N
     dma = pltpu.SemaphoreType.DMA
     anywhere, vmem = pl.BlockSpec(memory_space=pl.ANY), pl.BlockSpec(memory_space=pltpu.VMEM)
-    gathered = [
-        ((peers, widths, quarter, cols), bf16), ((peers, own, model), bf16), ((peers, own, model), bf16),
-        ((peers,) + start_tile.shape, f32),
+    smem = pl.BlockSpec(memory_space=pltpu.SMEM)
+    w_all = ((peers, widths, quarter, cols), bf16)
+    rows_all = ((peers, own, model), bf16)
+    starts_all = ((peers, SUB, BLOCK), f32)
+    per_chan, low = ((peers, own, chans), f32), ((peers, own, chans), bf16)
+    whole = [((peers, own, cols), f32), per_chan, per_chan, ((peers, own, BLOCK), f32), low]
+    streamed = [
+        ((own, chans), f32), ((own, 2 * N), bf16), ((own, 2 * BLOCK), f32), ((lanes, N, chans), f32), ((lanes, SUB, chans), f32)
     ]
-    computed = [
-        ((peers, own, cols), f32), ((peers, own, chans), f32), ((peers, own, chans), f32), ((peers, own, 2 * N), bf16),
-        ((peers, own, 2 * BLOCK), f32), ((peers, lanes, N, chans), f32), ((peers, lanes, SUB, chans), f32),
-    ]
+    outs = [w_all, rows_all, rows_all, starts_all, ((SUB, chans), f32), ((SUB, BLOCK), f32), *whole, rows_all]
+    outs += [((peers,) + a[0], a[1]) for a in streamed]
+    scratch = [w_all, rows_all, starts_all, ((chans, model), bf16), ((own, model), bf16), ((own, model), bf16)]
+    scratch += [((peers, own, BLOCK), bf16), ((SUB, BLOCK), f32), ((SUB, 2 * N), f32), *whole]
+    scratch += [((2,) + a[0], a[1]) for a in streamed]
+    scratch += [((2, peers * lanes, BLOCK), f32), ((peers - 1, 2, peers * lanes, BLOCK), f32)]
+    scratch += [((lanes, N, chans), f32), ((lanes, SUB, chans), f32), ((lanes, SUB, 2 * N), f32)]
+    scratch += [((lanes, BLOCK + SUB, chans), f32), ((lanes, BLOCK + SUB, 2 * N), f32)]
     return pl.pallas_call(
         partial(front_kernel, peers=peers, widths=widths, lanes=lanes, heads=heads),
-        in_specs=[anywhere] * 6 + [vmem] * 4,
-        out_specs=[anywhere] * (len(gathered) + len(computed)),
-        out_shape=[jax.ShapeDtypeStruct(*a) for a in gathered + computed],
+        in_specs=[smem] * 2 + [vmem] * 12 + [anywhere] * 2,
+        out_specs=[anywhere] * 4 + [vmem] * 2 + [anywhere] * 11,
+        out_shape=[jax.ShapeDtypeStruct(*a) for a in outs],
         scratch_shapes=[
-            *[pltpu.VMEM(*a) for a in (gathered[0], gathered[1], gathered[3], *computed)],
-            pltpu.VMEM((lanes, N, chans), f32), pltpu.VMEM((lanes, SUB, chans), f32), pltpu.VMEM((lanes, SUB, 2 * N), f32),
-            pltpu.VMEM((lanes, BLOCK + SUB, chans), f32), pltpu.VMEM((lanes, BLOCK + SUB, 2 * N), f32),
+            *[pltpu.VMEM(*a) for a in scratch],
             dma((4, peers - 1)), dma((4, peers - 1)), dma((peers - 1,)), dma((peers - 1,)),
-            dma((5,)), dma((widths - 1,)), dma((widths - 1,)), dma((peers,)), dma((len(computed), peers)),
+            dma((5,)), dma((widths - 1,)), dma((widths - 1,)), dma((peers,)), dma((6, peers)), dma((5, 2)),
+            dma((peers - 1,)), dma((peers - 1,)),
             *row_sems(peers // 2), *row_sems(peers // 2),
         ],
-        compiler_params=pltpu.CompilerParams(collective_id=1, has_side_effects=True, vmem_limit_bytes=60 << 20),
+        compiler_params=pltpu.CompilerParams(collective_id=1, has_side_effects=True, vmem_limit_bytes=62 << 20),
         name="front",
-    )(w_zx, third, w_bc, own_rows, own_grads, start_tile, chan, bc_par, head, spread)
+    )(valid, starts, tokens, cotangent, norm_gain, w_bc, w_dt, taps, bias, dt_bias, a_log, d_skip, gate_gain, spread, w_zx, w_out)
 
 
 ROWS_AT_ONCE = 16
@@ -641,7 +731,9 @@
     mate = (width, jnp.bitwise_xor(place, 1))
     ring = [lax.rem(place + by, peers) for by in range(1, peers)]
     cross = [jnp.bitwise_xor(width, m) for m in range(1, widths)]
-    greet([(width, s) for s in ring] + [(w, place) for w in cross])
+    others = [(width, s) for s in ring] + [(w, place) for w in cross]
+    greet(others)
+    met(others)
     half = wide_ref.shape[3] // 2
     sets = [
         (wide_ref, out_ref, pl.ds(0, half), own0, got0, piece0),
@@ -872,47 +964,6 @@
     )(got, zx, par, keep, dzx)
 
 
-def sum_kernel(own_ref, out_ref, got, send_sem, recv_sem, *, peers):
-    place = lax.axis_index("seq")
-    width = lax.axis_index("width")
-    barrier = pltpu.get_barrier_semaphore()
-    for by in range(1, peers):
-        pl.semaphore_signal(
-            barrier, inc=1, device_id=(width, lax.rem(place + by, peers)), device_id_type=pl.DeviceIdType.MESH
-        )
-    pl.semaphore_wait(barrier, peers - 1)
-    copies = []
-    for by in range(1, peers):
-        copies.append(
-            pltpu.make_async_remote_copy(
-                src_ref=own_ref, dst_ref=got.at[by - 1], send_sem=send_sem.at[by - 1], recv_sem=recv_sem.at[by - 1],
-                device_id=(width, lax.rem(place + by, peers)), device_id_type=pl.DeviceIdType.MESH,
-            )
-        )
-        copies[-1].start()
-    total = own_ref[...]
-    for by in range(1, peers):
-        copies[by - 1].wait()
-        total = total + got[by - 1]
-    out_ref[...] = total
-
-
-def summed_small(value):
-    peers = lax.axis_size("seq")
-    return pl.pallas_call(
-        partial(sum_kernel, peers=peers),
-        out_shape=jax.ShapeDtypeStruct(value.shape, f32),
-        in_specs=[pl.BlockSpec(memory_space=pltpu.VMEM)],
-        out_specs=pl.BlockSpec(memory_space=pltpu.VMEM),
-        scratch_shapes=[
-            pltpu.VMEM((peers - 1,) + value.shape, f32),
-            pltpu.SemaphoreType.DMA((peers - 1,)), pltpu.SemaphoreType.DMA((peers - 1,)),
-        ],
-        compiler_params=pltpu.CompilerParams(collective_id=0, has_side_effects=True),
-        name="row_sums",
-    )(value)
-
-
 def laid_kernel(in_ref, third_ref, w_ref, bc_ref, dt_ref, gain_ref, out_ref, out_bc_ref, out_dt_ref, norm_ref, *, heads, share):
     peers, rows, wide = in_ref.shape[0], in_ref.shape[2], in_ref.shape[3]
     chans = wide // 2
@@ -998,42 +1049,21 @@
     chans = heads * HEAD_DIM
     own, model = tokens.shape
     rows = own * peers
-    active = jnp.right_shift(jnp.int32(H), widths - 1 - lax.axis_index("width"))
-    count = (active * HEAD_DIM).astype(f32)
     first = place * heads
-
     share = 2 * N // peers
     used = heads + share
-    normed_own, bgrad_own, third_src, start_tile = entry(valid, starts, tokens, cotangent, norm_gain, w_bc, w_dt, peers)
     row_mask = (jnp.arange(BLOCK)[None, :] < valid[0][:, None]).astype(f32).reshape(-1, 1)
-    taps_x = lax.dynamic_slice_in_dim(conv_w, first * HEAD_DIM, chans, 0).T
-    of_chans = lambda a: lax.dynamic_slice_in_dim(a, first * HEAD_DIM, chans, 0)
-    of_heads = lambda a: jnp.pad(lax.dynamic_slice_in_dim(a, first, heads, 0), (0, BLOCK - heads))
-    head_on = (jnp.arange(BLOCK) < jnp.minimum(active - first, heads)).astype(f32)
-    chan_on = (jnp.arange(chans) // HEAD_DIM < active - first).astype(f32)
-    skip_x = jnp.repeat(lax.dynamic_slice_in_dim(d_skip, first, heads, 0), HEAD_DIM)
-    chan = packed_rows([*taps_x, of_chans(conv_b), skip_x, of_chans(gate_gain), chan_on], SUB)
-    bc_par = packed_rows([*conv_w[E:].T, conv_b[E:]], SUB)
-    head = packed_rows([of_heads(dt_bias), of_heads(-jnp.exp(a_log)), head_on], SUB)
-    spread = (jnp.arange(chans)[None, :] // HEAD_DIM == jnp.arange(BLOCK)[:, None]).astype(bf16)
-
-    weights, normed, bgrad, starts_all, *computed = front(
-        w_zx, third_src, w_bc, normed_own, bgrad_own, start_tile, chan, bc_par, head, spread, lanes, heads
+    spread = jnp.asarray(np.arange(chans)[None, :] // HEAD_DIM == np.arange(BLOCK)[:, None], bf16)
+    weights, normed, bgrad, starts_all, chan, head, *computed = front(
+        valid, starts, tokens, cotangent, norm_gain[None], w_bc, w_dt, conv_w.T, conv_b[None], dt_bias[None], a_log[None],
+        d_skip[None], gate_gain[None], spread, w_zx, w_out,
     )
     weights = weights.reshape(model, -1)
     normed, bgrad = normed.reshape(rows, model), bgrad.reshape(rows, model)
     keep = 1.0 - starts_all[:, :lanes, 0]
-    zx, conv, mix, bc, steps = [a.reshape(rows, a.shape[-1]) for a in computed[:5]]
-    state, tail = computed[5:]
-    mixed_grad, sums = run_grad(bgrad, w_out, zx, mix, chan, lanes)
-    sums = summed_small(sums[:, :, :2, :].reshape(-1, BLOCK)).reshape(peers, lanes, 2, BLOCK)
-    gate_rate = lax.rsqrt(sums[:, :, 0] / count + epsilon).reshape(rows, 1)
-    gate_pull = gate_rate * gate_rate * gate_rate * sums[:, :, 1].reshape(rows, 1) / count
-    scale = jnp.pad(jnp.concatenate([gate_rate, gate_pull], axis=1), ((0, 0), (0, SUB - 2)))
-    mixed_low = lax.optimization_barrier(
-        (mix * jax.nn.silu(zx[:, :chans]) * gate_rate * chan[GAIN]).astype(bf16)
-    )
-    branch = lax.psum_scatter(mm(mixed_low, w_out).astype(bf16), "seq", scatter_dimension=0, tiled=True).astype(f32)
+    zx, mix, mixed_grad, scale, mixed_low, part, conv, bc, steps = [a.reshape(rows, a.shape[-1]) for a in computed[:9]]
+    state, tail = computed[9:]
+    branch = lax.psum_scatter(part, "seq", scatter_dimension=0, tiled=True).astype(f32)
     output = (tokens.astype(f32) + row_mask * branch).astype(bf16)
     out_part = mm(mixed_low, bgrad, TN).astype(bf16)
     scale, out_part = lax.optimization_barrier((scale, out_part))

time: 528 us -> 496 us (0.939)
  the two profiles are of different devices: /device:TPU:9 before, /device:TPU:0 now
where the time goes in v4:
time: 496 us; the launch traced here: 487 us
  Pallas kernels  346 us (70%)
  matrix products  44.6 us (9%)
  local copies, waits for them, and re-layouts  41.8 us (8%)
  waiting for transfers between devices  15.5 us (3%)
  between operations  14.9 us (3%)
  other arithmetic  12.3 us (2%)
  starting transfers between devices  11.9 us (2%)
    pallas_call x1, Pallas kernels, front(): pl.pallas_call(partial(front_kernel, peers=peers, widths=widths, lanes=la...  198 us
    pallas_call x1, Pallas kernels, scattered_out(): pl.pallas_call(partial(scatter_kernel, peers=peers, widths=widths), in_sp...  107 us
    dot_general x4, matrix products, mm(): lax.dot_general(left, right, (dims, ((), ())), precision=precision, prefe...  44.6 us
    pallas_call x1, Pallas kernels, run_backward(): pl.pallas_call(partial(backward_kernel, lanes=lanes, heads=heads, blocks=...  34.7 us
    unnamed x44, local copies, waits for them, and re-layouts  20.4 us
    all_to_all x1, waiting for transfers between devices, heads_body(): lax.all_to_all(dbc.reshape(peers, share, rows), 'seq', 0, 0, tiled=True)  12.4 us
  transfers between devices with their start and end apart: 8, of which 3 were waited for; matrix products, arithmetic and copies ran while one was open for 15% of the time, Pallas kernels for 7%

profile of v4, /device:TPU:0, one launch (start us, length us, event | category | flops | bytes accessed | tf_op | source)
XLA Modules:
  0.0 487.2 jit_solution(15769627649945931781)
XLA Ops:
  7.2 1.3 broadcast_in_dim.36.bias_ref
  8.6 1.5 copy.52.dt_ref
  10.1 197.7 %front.1 = (bf16[8,4,64,1408]{3,2,1,0:T(8,128)(2,1)}, bf16[8,256,2048]{2,1,0:T(8,128)(2,1)}, bf16[8,256,2048]{2,1,0:T(8,128)(2,1)}, f32[8,8,128]{2,1,0:T(8,128)}...) custom-call(s32[1,2]{1,0:T(1,128)} %valid_ref.1, ...), custom_call_target="tpu_custom_call" | custom-call | tf_op jit(solution)/shard_map/front/pallas_call | solution.py:691
  207.9 1.5 copy-done.19
  209.4 9.1 %bitcast_convert_fusion = bf16[512,2048]{1,0:T(8,128)(2,1)} fusion(bf16[8,256,512]{2,1,0:T(8,128)(2,1)S(1)} %copy-done.19, bf16[8,256,2048]{2,1,0:T(8,128)(2,1)} %get-tuple-element.72), kind=kOutput, calls=%fused_computation.2 | convolution fusion | flops 4296015872 | bytes 12582912 | tf_op jit(solution)/shard_map/dot_general | solution.py:30
  218.5 3.0 dynamic-slice_bitcast_fusion
  221.6 2.5 collective-permute-start.2
  225.1 2.0 fusion.7
  227.0 1.3 copy.53
  228.4 1.3 slice.121
  232.6 1.2 copy-done.10
  234.5 34.7 %mix_backward.1 = (bf16[2048,1152]{1,0:T(8,128)(2,1)}, bf16[256,2048]{1,0:T(8,128)(2,1)S(1)}, f32[8,512]{1,0:T(8,128)S(1)}, f32[8,128]{1,0:T(8,128)S(1)}) custom-call(f32[8,2]{1,0:T(8,128)S(1)} %copy.55.keep_ref, f32[2048,1408]{1,0:T(8,128)} %bitcast.65, f32[2048,512]{1,0:T(8,128)} %bitcast.78, f32[8,512]{1,0:T(8,128)S(1)} %copy-done.17, ...), custom_call_target="tpu_custom_call" | custom-call | flops 6442450944 | bytes 41943040 | tf_op jit(solution)/shard_map/mix_backward/pallas_call | solution.py:278
  276.2 1.9 add_convert_fusion.1
  278.1 2.5 collective-permute-start.5
  281.6 4.8 all-to-all-start
  286.5 14.0 %fusion.3 = bf16[2048,1024]{1,0:T(8,128)(2,1)} fusion(bf16[2048,2048]{1,0:T(8,128)(2,1)} %bitcast.103, bf16[2048,1152]{1,0:T(8,128)(2,1)} %get-tuple-element.77.ddt_ref), kind=kOutput, calls=%fused_computation.5 | convolution fusion | flops 8592031744 | bytes 16777216 | tf_op jit(solution)/shard_map/dot_general | solution.py:30
  300.5 3.0 collective-permute-done.4
  304.3 2.7 bitcast_convert_fusion.1
  307.0 12.4 %all-to-all-done.got_ref = bf16[8,32,2048]{2,1,0:T(8,128)(2,1)S(1)} async-done(((bf16[8,32,2048]{2,1,0:T(8,128)(2,1)}), bf16[8,32,2048]{2,1,0:T(8,128)(2,1)S(1)}, u32[]{:S(2)}, u32[]{:S(2)}) %all-to-all-start) | async-done | bytes 1048608 | tf_op jit(solution)/shard_map/all_to_all | solution.py:1078
  319.3 4.3 copy-done
  323.6 2.3 copy-done.3
  326.0 1.5 bc_backward.1
  329.7 1.0 concatenate.48
  330.7 4.7 fusion.10
  337.0 16.8 %convolution_convert_fusion = bf16[2048,2048]{1,0:T(8,128)(2,1)} fusion(bf16[2048,1152]{1,0:T(8,128)(2,1)} %constant_dynamic-update-slice_fusion, bf16[2048,1408]{1,0:T(8,128)(2,1)} %bitcast.105), kind=kOutput, calls=%fused_computation | convolution fusion | flops 9667870720 | bytes 17825792 | tf_op jit(solution)/shard_map/dot_general | solution.py:30
  353.8 2.6 add_convert_fusion
  356.4 107.0 %scatter_out.1 = (f32[256,2048]{1,0:T(8,128)S(1)}, bf16[8,4,64,1024]{3,2,1,0:T(8,128)(2,1)}, bf16[8,4,64,128]{3,2,1,0:T(8,128)(2,1)S(1)}) custom-call(bf16[8,256,2048]{2,1,0:T(8,128)(2,1)} %bitcast.74, bf16[8,4,64,1024]{3,2,1,0:T(8,128)(2,1)} %bitcast.76, bf16[8,4,64,128]{3,2,1,0:T(8,128)(2,1)S(1)} %maximum_maximum_fusion.third_ref, ...), custom_call_target="tpu_custom_call" | custom-call | tf_op jit(solution)/shard_map/scatter_out/pallas_call | solution.py:887
  463.4 1.3 copy-done.7
  467.0 2.2 copy-done.1
  469.2 2.2 copy-done.4
  471.4 5.2 %lay_out.1 = (f32[256,8192]{1,0:T(8,128)}, f32[256,256]{1,0:T(8,128)}, f32[256,64]{1,0:T(8,128)S(1)}, f32[256,1]{1,0:T(8,128)S(1)}) custom-call(bf16[8,4,64,1024]{3,2,1,0:T(8,128)(2,1)S(1)} %copy-done.4, bf16[8,4,64,128]{3,2,1,0:T(8,128)(2,1)S(1)} %get-tuple-element.99.third_ref, bf16[256,8192]{1,0:T(8,128)(2,1)S(1)} %copy-done.1, ...), custom_call_target="tpu_custom_call" | custom-call | tf_op jit(solution)/shard_map/lay_out/pallas_call | solution.py:998
  478.6 1.3 copy.84
  (134 shorter events, 21.4 us)
Async XLA Ops:
  7.2 346.6 %reduce-scatter.2.cloned.1.call-start = ((), (), s32[]{:S(2)}) async-start(), calls=%async_computation.2 | async-start | bytes 9437184 | tf_op jit(solution)/shard_map/reduce_scatter | solution.py:1066
  207.8 1.6 copy-start.19
  218.5 11.2 %copy-start.16 = (f32[2048]{0:T(1024)S(1)}, f32[2048]{0:T(1024)}, u32[]{:S(2)}) copy-start(f32[2048]{0:T(1024)} %param.20) | copy-start | bytes 24580
  218.5 14.1 %copy-start.6 = (f32[8,256,256]{2,1,0:T(8,128)S(1)}, f32[8,256,256]{2,1,0:T(8,128)}, u32[]{:S(2)}) copy-start(f32[8,256,256]{2,1,0:T(8,128)} %get-tuple-element.67) | copy-start | bytes 6291460
  218.5 14.1 %copy-start.9 = (f32[8,256,128]{2,1,0:T(8,128)S(1)}, f32[8,256,128]{2,1,0:T(8,128)}, u32[]{:S(2)}) copy-start(f32[8,256,128]{2,1,0:T(8,128)} %get-tuple-element.70) | copy-start | bytes 3145732
  218.5 14.1 %copy-start.14 = (bf16[128,512]{1,0:T(8,128)(2,1)S(1)}, bf16[128,512]{1,0:T(8,128)(2,1)}, u32[]{:S(2)}) copy-start(bf16[128,512]{1,0:T(8,128)(2,1)} %constant.68.clone.spread_ref) | copy-start | bytes 393220
  218.5 14.1 %copy-start.15 = (f32[8,2,8,512]{3,2,1,0:T(8,128)S(1)}, f32[8,2,8,512]{3,2,1,0:T(8,128)}, u32[]{:S(2)}) copy-start(f32[8,2,8,512]{3,2,1,0:T(8,128)} %get-tuple-element.69.tail_ref) | copy-start | bytes 786436
  218.5 14.1 %copy-start.18 = (f32[8,128]{1,0:T(8,128)S(1)}, f32[8,128]{1,0:T(8,128)}, u32[]{:S(2)}) copy-start(f32[8,128]{1,0:T(8,128)} %get-tuple-element.63.head_ref) | copy-start | bytes 12292
  221.6 54.6 %collective-permute-start.2 = (bf16[128,2048]{1,0:T(8,128)(2,1)}, bf16[128,2048]{1,0:T(8,128)(2,1)}, u32[]{:S(2)}, u32[]{:S(2)}) collective-permute-start(bf16[128,2048]{1,0:T(8,128)(2,1)} %get-tuple-element.153), channel_id=1, source_target_pairs={{0,24},{8,16},{16,8},{24,0},{1,25},{9,17},{17,9},{25,1},{2,26},{10... | collective-permute-start | bytes 1572872 | tf_op jit(solution)/shard_map/ppermute | solution.py:1010
  224.0 52.1 %collective-permute-start.1 = (bf16[128,2048]{1,0:T(8,128)(2,1)}, bf16[128,2048]{1,0:T(8,128)(2,1)}, u32[]{:S(2)}, u32[]{:S(2)}) collective-permute-start(bf16[128,2048]{1,0:T(8,128)(2,1)} %get-tuple-element.154), channel_id=1, source_target_pairs={{0,16},{8,24},{16,0},{24,8},{1,17},{9,25},{17,1},{25,9},{2,18},{10... | collective-permute-start | bytes 1572872 | tf_op jit(solution)/shard_map/ppermute | solution.py:1010
  224.5 51.7 %collective-permute-start = (bf16[128,2048]{1,0:T(8,128)(2,1)}, bf16[128,2048]{1,0:T(8,128)(2,1)}, u32[]{:S(2)}, u32[]{:S(2)}) collective-permute-start(bf16[128,2048]{1,0:T(8,128)(2,1)} %get-tuple-element.155), channel_id=1, source_target_pairs={{0,8},{8,0},{16,24},{24,16},{1,9},{9,1},{17,25},{25,17},{2,10},{10... | collective-permute-start | bytes 1572872 | tf_op jit(solution)/shard_map/ppermute | solution.py:1010
  232.6 1.2 copy-start.10
  233.8 0.7 copy-start.17
  269.3 1.0 copy-start.11
  278.1 22.4 %collective-permute-start.5 = (bf16[128,2048]{1,0:T(8,128)(2,1)S(1)}, bf16[128,2048]{1,0:T(8,128)(2,1)S(1)}, u32[]{:S(2)}, u32[]{:S(2)}) collective-permute-start(bf16[128,2048]{1,0:T(8,128)(2,1)S(1)} %add_convert_fusion.1), channel_id=1, source_target_pairs={{0,24},{8,16},{16,8},{24,0},{1,25},{9,17},{17,9},{25,1},{2,26},{10... | collective-permute-start | bytes 1572872 | tf_op jit(solution)/shard_map/ppermute | solution.py:1010
  280.6 22.9 %collective-permute-start.4 = (bf16[128,2048]{1,0:T(8,128)(2,1)S(1)}, bf16[128,2048]{1,0:T(8,128)(2,1)S(1)}, u32[]{:S(2)}, u32[]{:S(2)}) collective-permute-start(bf16[128,2048]{1,0:T(8,128)(2,1)S(1)} %add_convert_fusion.1), channel_id=1, source_target_pairs={{0,16},{8,24},{16,0},{24,8},{1,17},{9,25},{17,1},{25,9},{2,18},{10... | collective-permute-start | bytes 1572872 | tf_op jit(solution)/shard_map/ppermute | solution.py:1010
  281.1 22.5 %collective-permute-start.3 = (bf16[128,2048]{1,0:T(8,128)(2,1)S(1)}, bf16[128,2048]{1,0:T(8,128)(2,1)S(1)}, u32[]{:S(2)}, u32[]{:S(2)}) collective-permute-start(bf16[128,2048]{1,0:T(8,128)(2,1)S(1)} %add_convert_fusion.1), channel_id=1, source_target_pairs={{0,8},{8,0},{16,24},{24,16},{1,9},{9,1},{17,25},{25,17},{2,10},{10... | collective-permute-start | bytes 1572872 | tf_op jit(solution)/shard_map/ppermute | solution.py:1010
  281.6 37.7 %all-to-all-start = ((bf16[8,32,2048]{2,1,0:T(8,128)(2,1)}), bf16[8,32,2048]{2,1,0:T(8,128)(2,1)S(1)}, u32[]{:S(2)}, u32[]{:S(2)}) async-start(bf16[8,32,2048]{2,1,0:T(8,128)(2,1)} %bitcast.71), calls=%async_computation | async-start | bytes 2097152 | tf_op jit(solution)/shard_map/all_to_all | solution.py:1078
  319.3 4.3 copy-start
  323.6 2.3 copy-start.3
  337.0 16.8 %copy-start.2 = (bf16[256,2048]{1,0:T(8,128)(2,1)S(1)}, bf16[256,2048]{1,0:T(8,128)(2,1)}, u32[]{:S(2)}) copy-start(bf16[256,2048]{1,0:T(8,128)(2,1)} %x_ref.3) | copy-start | bytes 3145732
  337.0 19.4 %copy-start.5 = (bf16[256,2048]{1,0:T(8,128)(2,1)S(1)}, bf16[256,2048]{1,0:T(8,128)(2,1)}, u32[]{:S(2)}) copy-start(bf16[256,2048]{1,0:T(8,128)(2,1)} %cot_ref.3) | copy-start | bytes 3145732
  356.4 110.6 %copy-start.12 = (bf16[256,64]{1,0:T(8,128)(2,1)S(1)}, bf16[256,64]{1,0:T(8,128)(2,1)}, u32[]{:S(2)}) copy-start(bf16[256,64]{1,0:T(8,128)(2,1)} %copy.52.dt_ref) | copy-start | bytes 98308
  356.4 110.6 %copy-start.13 = (bf16[256,256]{1,0:T(8,128)(2,1)S(1)}, bf16[256,256]{1,0:T(8,128)(2,1)}, u32[]{:S(2)}) copy-start(bf16[256,256]{1,0:T(8,128)(2,1)} %bc_ref.3) | copy-start | bytes 393220
  463.4 1.3 copy-start.7
  467.0 2.2 copy-start.1
  469.2 2.2 copy-start.4
  471.4 7.2 %copy-start.8 = (f32[256,2048]{1,0:T(8,128)S(1)}, f32[256,2048]{1,0:T(8,128)}, u32[]{:S(2)}) copy-start(f32[256,2048]{1,0:T(8,128)} %copy-done.7) | copy-start | bytes 6291460
Sparse Core Ops, SparseCore 0:
  208.0 95.9 reduce-scatter.1

commit v5 on v4

--- a/solution.py
+++ b/solution.py
@@ -718,206 +718,9 @@
         dst[at] = value.astype(dst.dtype)
 
 
-def scatter_kernel(
-    part_ref, wide_ref, third_ref, x_ref, cot_ref, gain_ref, rows_ref, out_ref, out_third_ref,
-    mine, from_core, up, down, own0, own1, own2, got0, got1, got2, piece0, piece1, piece2,
-    local_sem, core_send, core_recv, up_send, up_recv, down_send, down_recv,
-    own_sem, q_send, q_recv, p_send, p_recv, o_send, o_recv,
-    *, peers, widths,
-):
-    width, place = lax.axis_index("width"), lax.axis_index("seq")
-    chips = peers // 2
-    chip, core = place // 2, lax.rem(place, 2)
-    mate = (width, jnp.bitwise_xor(place, 1))
-    ring = [lax.rem(place + by, peers) for by in range(1, peers)]
-    cross = [jnp.bitwise_xor(width, m) for m in range(1, widths)]
-    others = [(width, s) for s in ring] + [(w, place) for w in cross]
-    greet(others)
-    met(others)
-    half = wide_ref.shape[3] // 2
-    sets = [
-        (wide_ref, out_ref, pl.ds(0, half), own0, got0, piece0),
-        (wide_ref, out_ref, pl.ds(half, half), own1, got1, piece1),
-        (third_ref, out_third_ref, pl.ds(0, BLOCK), own2, got2, piece2),
-    ]
-
-    def remote(src, dst, send, recv, device):
-        return pltpu.make_async_remote_copy(
-            src_ref=src, dst_ref=dst, send_sem=send, recv_sem=recv, device_id=device, device_id_type=MESH
-        )
-
-    locals_ = [pltpu.make_async_copy(part_ref.at[2 * q + core], mine.at[q], local_sem.at[q]) for q in range(chips)]
-    to_core = [
-        remote(part_ref.at[2 * q + 1 - core], from_core.at[q], core_send.at[q], core_recv.at[q], mate) for q in range(chips)
-    ]
-    own_in, to_width = [], []
-    for k, (src, dst, cols, own, got, piece) in enumerate(sets):
-        own_in.append(pltpu.make_async_copy(src.at[:, width, :, cols], own, own_sem.at[0, k]))
-        to_width.append([
-            remote(src.at[:, w, :, cols], got.at[m], q_send.at[k, m], q_recv.at[k, m], (w, place)) for m, w in enumerate(cross)
-        ])
-    for copy in locals_ + to_core + own_in + to_width[0] + to_width[1] + to_width[2]:
-        copy.start()
-    rows = mine.shape[1]
-    for q in range(chips):
-        locals_[q].wait()
-        to_core[q].wait_recv()
-        add_into(mine.at[q], [from_core.at[q]], rows)
-
-    def flow(by):
-        return (up, up_send, up_recv) if by > 0 else (down, down_send, down_recv)
-
-    def sends(by, step):
-        far = chips - step
-        return chip + far < chips if by > 0 else chip >= far
-
-    def later(by):
-        return chip > 0 if by > 0 else chip + 1 < chips
-
-    def hop(src, by, step):
-        buffer, send, recv = flow(by)
-        return remote(
-            src, buffer.at[step - 1], send.at[step - 1], recv.at[step - 1], (width, jnp.clip(place + 2 * by, 0, peers - 1))
-        )
-
-    def staged(by, step):
-        return flow(by)[0].at[step - 2]
-
-    def run_hops(step):
-        for by in (1, -1):
-            owner = jnp.clip(chip + by * (chips - step), 0, chips - 1)
-
-            def direct():
-                hop(mine.at[owner], by, step).start()
-
-            def relayed():
-                hop(staged(by, step), by, step - 1).wait_recv()
-                add_into(staged(by, step), [mine.at[owner]], rows)
-                hop(staged(by, step), by, step).start()
-
-            if step == 1:
-                pl.when(sends(by, step))(direct)
-            else:
-                pl.when(sends(by, step) & jnp.logical_not(later(by)))(direct)
-                pl.when(sends(by, step) & later(by))(relayed)
-
-    to_owner, to_all, kept = [None] * 3, [None] * 3, []
-
-    def exchange(k):
-        src, dst, cols, own, got, piece = sets[k]
-        own_in[k].wait()
-        for copy in to_width[k]:
-            copy.wait_recv()
-        for s in range(peers):
-            add_into(own.at[s], [got.at[m, s] for m in range(widths - 1)], own.shape[1])
-        to_owner[k] = [
-            remote(own.at[s], piece.at[place], p_send.at[k, i], p_recv.at[k, i], (width, s)) for i, s in enumerate(ring)
-        ]
-        keep = pltpu.make_async_copy(own.at[place], piece.at[place], own_sem.at[1, k])
-        for copy in to_owner[k] + [keep]:
-            copy.start()
-        kept.append(keep)
-
-    def spread(k):
-        src, dst, cols, own, got, piece = sets[k]
-        for copy in to_owner[k]:
-            copy.wait_recv()
-        kept[k].wait()
-        to_all[k] = [
-            remote(piece, dst.at[:, width, :, cols], o_send.at[k, m], o_recv.at[k, m], (w, place)) for m, w in enumerate(cross)
-        ]
-        to_all[k].append(pltpu.make_async_copy(piece, dst.at[:, width, :, cols], own_sem.at[2, k]))
-        for copy in to_all[k]:
-            copy.start()
-
-    run_hops(1)
-    exchange(0)
-    if chips > 2:
-        run_hops(2)
-    spread(0)
-    exchange(1)
-    exchange(2)
-    for step in range(3, chips):
-        run_hops(step)
-    spread(1)
-    spread(2)
-
-    for by in (1, -1):
-        @pl.when(later(by))
-        def _():
-            buffer = flow(by)[0].at[chips - 2]
-            hop(buffer, by, chips - 1).wait_recv()
-            add_into(mine.at[chip], [buffer], rows)
-
-    gain = gain_ref[...]
-
-    @pl.loop(0, rows // ROWS_AT_ONCE)
-    def _(i):
-        at = pl.ds(pl.multiple_of(i * ROWS_AT_ONCE, ROWS_AT_ONCE), ROWS_AT_ONCE)
-        x = x_ref[at, :].astype(f32)
-        rate = lax.rsqrt(jnp.mean(x * x, axis=-1, keepdims=True) + epsilon)
-        unit = x * rate
-        pulled = mine[chip, at].astype(f32) * gain
-        inner = jnp.mean(pulled * unit, axis=-1, keepdims=True)
-        rows_ref[at, :] = cot_ref[at, :].astype(f32) + rate * (pulled - unit * inner)
-
-    for step in range(1, chips):
-        for by in (1, -1):
-            @pl.when(sends(by, step))
-            def _():
-                hop(mine.at[0], by, step).wait_send()
-    for copy in to_core:
-        copy.wait_send()
-    for k in range(len(sets)):
-        for copy in to_width[k] + to_owner[k]:
-            copy.wait_send()
-        for copy in to_all[k]:
-            copy.wait()
-
-
-def scattered_out(part, wide, third, x_rows, cotangent, gain):
-    peers, widths = lax.axis_size("seq"), lax.axis_size("width")
-    chips = peers // 2
-    dma = pltpu.SemaphoreType.DMA
-    anywhere = pl.BlockSpec(memory_space=pl.ANY)
-    vmem = pl.BlockSpec(memory_space=pltpu.VMEM)
-    block = part.shape[1:]
-    half = wide.shape[3] // 2
-    pieces = [(peers, wide.shape[2], cols) for cols in (half, half, third.shape[3])]
-    return pl.pallas_call(
-        partial(scatter_kernel, peers=peers, widths=widths),
-        in_specs=[anywhere] * 3 + [vmem] * 3,
-        out_specs=[vmem, anywhere, anywhere],
-        out_shape=[
-            jax.ShapeDtypeStruct(block, f32), jax.ShapeDtypeStruct(wide.shape, bf16), jax.ShapeDtypeStruct(third.shape, bf16)
-        ],
-        scratch_shapes=[
-            pltpu.VMEM((chips,) + block, bf16), pltpu.VMEM((chips,) + block, bf16),
-            pltpu.VMEM((chips - 1,) + block, bf16), pltpu.VMEM((chips - 1,) + block, bf16),
-            *[pltpu.VMEM(piece, bf16) for piece in pieces],
-            *[pltpu.VMEM((widths - 1,) + piece, bf16) for piece in pieces],
-            *[pltpu.VMEM(piece, bf16) for piece in pieces],
-            dma((chips,)), dma((chips,)), dma((chips,)),
-            dma((chips - 1,)), dma((chips - 1,)), dma((chips - 1,)), dma((chips - 1,)),
-            dma((3, 3)), dma((3, widths - 1)), dma((3, widths - 1)), dma((3, peers - 1)), dma((3, peers - 1)),
-            dma((3, widths - 1)), dma((3, widths - 1)),
-        ],
-        compiler_params=pltpu.CompilerParams(collective_id=2, has_side_effects=True, vmem_limit_bytes=48 << 20),
-        name="scatter_out",
-    )(part, wide, third, x_rows, cotangent, gain)
-
-
-def bc_kernel(got_ref, pre_ref, par_ref, keep_ref, ddt_ref, third_ref, dpar_ref, pre_t, *, at):
-    chans, times = pre_t.shape
-    for i in range(times // BLOCK):
-        rows = slice(i * BLOCK, (i + 1) * BLOCK)
-        pre_t[:, rows] = pre_ref[rows, :].T[at : at + chans]
-    dbc = got_ref[0].astype(f32)
-    for s in range(1, got_ref.shape[0]):
-        dbc = dbc + got_ref[s].astype(f32)
-    pre = pre_t[...]
+def bc_back(dbc, pre, par_ref, keep, keep_next):
+    chans, times = pre.shape
     in_block = lax.rem(lax.broadcasted_iota(jnp.int32, (chans, times), 1), BLOCK)
-    keep, keep_next = keep_ref[0:1, :], keep_ref[1:2, :]
     conv = jnp.broadcast_to(par_ref[:, BIAS : BIAS + 1], (chans, times))
     shifted = []
     for j in range(KCONV):
@@ -938,35 +741,286 @@
                 in_block < BLOCK - j, pltpu.roll(dconv, times - j, 1), keep_next * pltpu.roll(dconv, times - BLOCK - j, 1)
             )
             dpre = dpre + back * par_ref[:, KCONV - 1 - j : KCONV - j]
-    dpar_ref[...] = dpar
-    for i in range(times // BLOCK):
-        tile = dpre[:, i * BLOCK : (i + 1) * BLOCK]
-        below = jnp.zeros((BLOCK - at - chans, BLOCK), f32)
-        tile = jnp.concatenate([jnp.zeros((at, BLOCK), f32), tile, below], axis=0).T
-        rows = slice(i * BLOCK, (i + 1) * BLOCK)
-        third_ref[rows, :] = (tile + ddt_ref[rows, :].astype(f32)).astype(bf16)
-
-
-def bc_backward(got, zx, par, keep, dzx, at, chans):
-    rows = dzx.shape[0]
-    share = got.shape[1]
-    third = pl.BlockSpec((rows, BLOCK), lambda i: (0, 2 * chans // BLOCK))
-    whole = lambda a: pl.BlockSpec(a.shape, lambda i: (0,) * a.ndim)
+    return dpre, dpar
+
+
+def scatter_kernel(
+    got_ref, zx_ref, dzx_ref, w_ref, normed_ref, wide_ref, par_ref, keep_ref, small_ref, x_ref, cot_ref, gain_ref,
+    rows_ref, out_ref, out_third_ref,
+    got_v, pre_v, dz_v, w_v, normed_v, third_t, third_g,
+    mine, to_mate, from_core, up, down, own0, own1, own2, got0, got1, got2, piece0, piece1, piece2,
+    load_sem, core_send, core_recv, up_send, up_recv, down_send, down_recv,
+    own_sem, q_send, q_recv, p_send, p_recv, o_send, o_recv,
+    *, peers, widths, heads,
+):
+    width, place = lax.axis_index("width"), lax.axis_index("seq")
+    chips = peers // 2
+    chip, core = place // 2, lax.rem(place, 2)
+    mate = (width, jnp.bitwise_xor(place, 1))
+    ring = [lax.rem(place + by, peers) for by in range(1, peers)]
+    cross = [jnp.bitwise_xor(width, m) for m in range(1, widths)]
+    others = [(width, s) for s in ring] + [(w, place) for w in cross]
+    greet(others)
+    half = wide_ref.shape[3] // 2
+    wide = 2 * half
+    own = mine.shape[1]
+    share, times = got_v.shape[1], got_v.shape[2]
+    loads = [
+        pltpu.make_async_copy(src, dst, load_sem.at[k])
+        for k, (src, dst) in enumerate([
+            (got_ref, got_v), (zx_ref.at[:, :, wide : wide + BLOCK], pre_v), (dzx_ref, dz_v), (w_ref, w_v), (normed_ref, normed_v)
+        ])
+    ]
+    for load in loads:
+        load.start()
+    met(others)
+
+    strip = third_g.shape[0] // widths
+    lanes_of = lambda s: pl.ds(pl.multiple_of(s * own, BLOCK), own)
+    strip_of = lambda w: pl.ds(pl.multiple_of(w * strip, 16), strip)
+    sets = [
+        (lambda w: wide_ref.at[:, w, :, 0:half], own0, got0, lambda s: own0.at[s], piece0, lambda w: out_ref.at[:, w, :, 0:half]),
+        (lambda w: wide_ref.at[:, w, :, half:wide], own1, got1, lambda s: own1.at[s], piece1, lambda w: out_ref.at[:, w, :, half:wide]),
+        (lambda w: third_g.at[strip_of(w)], own2, got2, lambda s: own2.at[:, lanes_of(s)], piece2, lambda w: out_third_ref.at[:, w]),
+    ]
+    own_in, to_width = [None] * 3, [None] * 3
+
+    def begin(k):
+        part, kept, arrived = sets[k][:3]
+        own_in[k] = pltpu.make_async_copy(part(width), kept, own_sem.at[0, k])
+        to_width[k] = [
+            remote(part(w), arrived.at[m], q_send.at[k, m], q_recv.at[k, m], (w, place)) for m, w in enumerate(cross)
+        ]
+        for copy in [own_in[k]] + to_width[k]:
+            copy.start()
+
+    begin(0)
+    begin(1)
+
+    def flow(by):
+        return (up, up_send, up_recv) if by > 0 else (down, down_send, down_recv)
+
+    def sends(by, step):
+        far = chips - step
+        return chip + far < chips if by > 0 else chip >= far
+
+    def later(by):
+        return chip > 0 if by > 0 else chip + 1 < chips
+
+    def hop(src, by, step):
+        buffer, send, recv = flow(by)
+        return remote(
+            src, buffer.at[step - 1], send.at[step - 1], recv.at[step - 1], (width, jnp.clip(place + 2 * by, 0, peers - 1))
+        )
+
+    def staged(by, step):
+        return flow(by)[0].at[step - 2]
+
+    def run_hops(step):
+        for by in (1, -1):
+            owner = jnp.clip(chip + by * (chips - step), 0, chips - 1)
+
+            def direct():
+                hop(mine.at[owner], by, step).start()
+
+            def relayed():
+                hop(staged(by, step), by, step - 1).wait_recv()
+                add_into(staged(by, step), [mine.at[owner]], own)
+                hop(staged(by, step), by, step).start()
+
+            if step == 1:
+                pl.when(sends(by, step))(direct)
+            else:
+                pl.when(sends(by, step) & jnp.logical_not(later(by)))(direct)
+                pl.when(sends(by, step) & later(by))(relayed)
+
+    to_owner, to_all, kept_piece = [None] * 3, [None] * 3, [None] * 3
+
+    def exchange(k):
+        part, kept, arrived, piece_of, piece, out = sets[k]
+        own_in[k].wait()
+        for copy in to_width[k]:
+            copy.wait_recv()
+        if kept.ndim == 3:
+            for s in range(peers):
+                add_into(kept.at[s], [arrived.at[m, s] for m in range(widths - 1)], kept.shape[1])
+        else:
+            add_into(kept, [arrived.at[m] for m in range(widths - 1)], kept.shape[0])
+        to_owner[k] = [
+            remote(piece_of(s), piece.at[place], p_send.at[k, i], p_recv.at[k, i], (width, s)) for i, s in enumerate(ring)
+        ]
+        kept_piece[k] = pltpu.make_async_copy(piece_of(place), piece.at[place], own_sem.at[1, k])
+        for copy in to_owner[k] + [kept_piece[k]]:
+            copy.start()
+
+    def spread(k):
+        piece, out = sets[k][4:]
+        for copy in to_owner[k]:
+            copy.wait_recv()
+        kept_piece[k].wait()
+        to_all[k] = [remote(piece, out(width), o_send.at[k, m], o_recv.at[k, m], (w, place)) for m, w in enumerate(cross)]
+        to_all[k].append(pltpu.make_async_copy(piece, out(width), own_sem.at[2, k]))
+        for copy in to_all[k]:
+            copy.start()
+
+    for load in loads[:3]:
+        load.wait()
+    dbc = got_v[0].astype(f32)
+    for s in range(1, peers):
+        dbc = dbc + got_v[s].astype(f32)
+    block_rows = pre_v.shape[1]
+    spots = [(c, slice(l * BLOCK, (l + 1) * BLOCK)) for c in range(peers) for l in range(block_rows // BLOCK)]
+    pre = jnp.concatenate([pre_v[c, at, :].T[heads : heads + share] for c, at in spots], axis=1)
+    dpre, dpar = bc_back(dbc, pre, par_ref, keep_ref[0:1, :], keep_ref[1:2, :])
+    for i, (c, at) in enumerate(spots):
+        tile = jnp.concatenate(
+            [
+                dz_v[c, at, wide:].astype(f32).T[:heads], dpre[:, i * BLOCK : (i + 1) * BLOCK],
+                jnp.zeros((BLOCK - heads - share, BLOCK), f32),
+            ],
+            axis=0,
+        )
+        third_t[:, i * BLOCK : (i + 1) * BLOCK] = tile.astype(bf16)
+        dz_v[c, at, wide:] = tile.T.astype(bf16)
+    loads[3].wait()
+
+    def partial_rows(s):
+        weights = w_v[...].reshape(w_v.shape[0] * w_v.shape[1] * w_v.shape[2], w_v.shape[3])
+        return mm(dz_v[s], weights[:, : wide + BLOCK], NT).astype(bf16)
+
+    def order(i):
+        return jnp.where(chip < chips // 2, chips - 1 - i, i)
+
+    def over(q):
+        return remote(to_mate.at[q], from_core.at[q], core_send.at[q], core_recv.at[q], mate)
+
+    def whole_sum(q):
+        over(q).wait_recv()
+        add_into(mine.at[q], [from_core.at[q]], own)
+
+    for i in range(chips):
+        q = order(i)
+        to_mate[q] = partial_rows(2 * q + 1 - core)
+        over(q).start()
+        mine[q] = partial_rows(2 * q + core)
+        if i:
+            whole_sum(order(i - 1))
+        if i == 1:
+            run_hops(1)
+    whole_sum(order(chips - 1))
+
+    loads[4].wait()
+    small_at = heads + share
+    used = small_at + small_ref.shape[0]
+    par_rows = jnp.concatenate([dpar, jnp.zeros((BLOCK - share, BLOCK), f32)], axis=0).T[:SUB]
+    par_rows = jnp.concatenate([par_rows, jnp.zeros((SUB, own - BLOCK), f32)], axis=1)
+    grads = mm(third_t[...], normed_v[...].reshape(times, normed_v.shape[2]))
+    tail = [jnp.zeros((third_g.shape[0] - used - SUB, third_g.shape[1]), f32)] if third_g.shape[0] > used + SUB else []
+    third_g[...] = jnp.concatenate(
+        [grads[:small_at], small_ref[...], jnp.concatenate([par_rows] * peers, axis=1), *tail], axis=0
+    ).astype(bf16)
+    begin(2)
+
+    exchange(0)
+    if chips > 2:
+        run_hops(2)
+    spread(0)
+    exchange(1)
+    exchange(2)
+    for step in range(3, chips):
+        run_hops(step)
+    spread(1)
+    spread(2)
+
+    for by in (1, -1):
+        @pl.when(later(by))
+        def _():
+            buffer = flow(by)[0].at[chips - 2]
+            hop(buffer, by, chips - 1).wait_recv()
+            add_into(mine.at[chip], [buffer], own)
+
+    gain = gain_ref[...]
+
+    @pl.loop(0, own // ROWS_AT_ONCE)
+    def _(i):
+        at = pl.ds(pl.multiple_of(i * ROWS_AT_ONCE, ROWS_AT_ONCE), ROWS_AT_ONCE)
+        x = x_ref[at, :].astype(f32)
+        rate = lax.rsqrt(jnp.mean(x * x, axis=-1, keepdims=True) + epsilon)
+        unit = x * rate
+        pulled = mine[chip, at].astype(f32) * gain
+        inner = jnp.mean(pulled * unit, axis=-1, keepdims=True)
+        rows_ref[at, :] = cot_ref[at, :].astype(f32) + rate * (pulled - unit * inner)
+
+    for step in range(1, chips):
+        for by in (1, -1):
+            @pl.when(sends(by, step))
+            def _():
+                hop(mine.at[0], by, step).wait_send()
+    for q in range(chips):
+        over(q).wait_send()
+    for k in range(len(sets)):
+        for copy in to_width[k] + to_owner[k]:
+            copy.wait_send()
+        for copy in to_all[k]:
+            copy.wait()
+
+
+def scattered_out(got, zx, dzx, weights, normed, wide, par, keep, small, x_rows, cotangent, gain, heads):
+    peers, widths = lax.axis_size("seq"), lax.axis_size("width")
+    chips = peers // 2
+    dma = pltpu.SemaphoreType.DMA
+    anywhere = pl.BlockSpec(memory_space=pl.ANY)
+    vmem = pl.BlockSpec(memory_space=pltpu.VMEM)
+    own, model = x_rows.shape
+    half = wide.shape[3] // 2
+    strips = -(-(heads + got.shape[1] + small.shape[0] + SUB) // (16 * widths)) * 16 * widths
+    pieces = [(peers, wide.shape[2], half), (peers, wide.shape[2], half), (peers, strips // widths, own)]
+    kept = pieces[:2] + [(strips // widths, model)]
+    block = (own, model)
+    zx, dzx, normed = [a.reshape(peers, own, a.shape[1]) for a in (zx, dzx, normed)]
     return pl.pallas_call(
-        partial(bc_kernel, at=at),
-        grid=(1,),
-        in_specs=[whole(got), third, whole(par), whole(keep), third],
-        out_specs=[pl.BlockSpec((rows, BLOCK), lambda i: (0, 0)), pl.BlockSpec((share, BLOCK), lambda i: (0, 0))],
-        out_shape=[jax.ShapeDtypeStruct((rows, BLOCK), bf16), jax.ShapeDtypeStruct((share, BLOCK), f32)],
-        scratch_shapes=[pltpu.VMEM((share, rows), f32)],
-        compiler_params=pltpu.CompilerParams(vmem_limit_bytes=32 << 20),
-        name="bc_backward",
-    )(got, zx, par, keep, dzx)
-
-
-def laid_kernel(in_ref, third_ref, w_ref, bc_ref, dt_ref, gain_ref, out_ref, out_bc_ref, out_dt_ref, norm_ref, *, heads, share):
+        partial(scatter_kernel, peers=peers, widths=widths, heads=heads),
+        in_specs=[anywhere] * 6 + [vmem] * 6,
+        out_specs=[vmem, anywhere, anywhere],
+        out_shape=[
+            jax.ShapeDtypeStruct(block, f32), jax.ShapeDtypeStruct(wide.shape, bf16),
+            jax.ShapeDtypeStruct((peers, widths, strips // widths, own), bf16),
+        ],
+        scratch_shapes=[
+            pltpu.VMEM(got.shape, bf16), pltpu.VMEM((peers, own, BLOCK), f32), pltpu.VMEM(dzx.shape, bf16),
+            pltpu.VMEM(weights.shape, bf16), pltpu.VMEM(normed.shape, bf16),
+            pltpu.VMEM((BLOCK, peers * own), bf16), pltpu.VMEM((strips, model), bf16),
+            *[pltpu.VMEM((chips,) + block, bf16)] * 3, *[pltpu.VMEM((chips - 1,) + block, bf16)] * 2,
+            *[pltpu.VMEM(a, bf16) for a in kept],
+            *[pltpu.VMEM((widths - 1,) + a, bf16) for a in kept],
+            *[pltpu.VMEM(a, bf16) for a in pieces],
+            dma((5,)), dma((chips,)), dma((chips,)),
+            dma((chips - 1,)), dma((chips - 1,)), dma((chips - 1,)), dma((chips - 1,)),
+            dma((3, 3)), dma((3, widths - 1)), dma((3, widths - 1)), dma((3, peers - 1)), dma((3, peers - 1)),
+            dma((3, widths - 1)), dma((3, widths - 1)),
+        ],
+        compiler_params=pltpu.CompilerParams(collective_id=2, has_side_effects=True, vmem_limit_bytes=62 << 20),
+        name="scatter_out",
+    )(got, zx, dzx, weights, normed, wide, par, keep, small, x_rows, cotangent, gain)
+
+
+def laid_kernel(in_ref, third_ref, w_ref, bc_ref, dt_ref, gain_ref, out_ref, out_bc_ref, out_dt_ref, norm_ref, rest, *, heads, share):
     peers, rows, wide = in_ref.shape[0], in_ref.shape[2], in_ref.shape[3]
     chans = wide // 2
+    step = pl.program_id(0)
+
+    @pl.when(step == 0)
+    def _():
+        third = [
+            jnp.concatenate([third_ref[s, q].astype(f32) for q in range(third_ref.shape[1])], axis=0) for s in range(peers)
+        ]
+        dt = jnp.concatenate([t[:heads] for t in third], axis=0).T
+        bc = jnp.concatenate([t[heads : heads + share] for t in third], axis=0).T
+        out_bc_ref[...] = bc
+        out_dt_ref[...] = dt
+        total = jnp.sum(bc * bc_ref[...].astype(f32), axis=1, keepdims=True)
+        rest[...] = total + jnp.sum(dt * dt_ref[...].astype(f32), axis=1, keepdims=True)
+
     lane = jnp.zeros((rows, BLOCK), f32)
     for s in range(peers):
         for half in (0, 1):
@@ -976,14 +1030,8 @@
             value = value * w_ref[:, at : at + chans].astype(f32)
             for j in range(chans // BLOCK):
                 lane = lane + value[:, j * BLOCK : (j + 1) * BLOCK]
-    third = [third_ref[s, 0].astype(f32) for s in range(peers)]
-    bc = jnp.concatenate([t[:, heads : heads + share] for t in third], axis=1)
-    dt = jnp.concatenate([t[:, :heads] for t in third], axis=1)
-    out_bc_ref[...] = bc
-    out_dt_ref[...] = dt
-    total = jnp.sum(lane, axis=1, keepdims=True) + jnp.sum(bc * bc_ref[...].astype(f32), axis=1, keepdims=True)
-    total = total + jnp.sum(dt * dt_ref[...].astype(f32), axis=1, keepdims=True)
-    norm_ref[...] = total / gain_ref[...]
+    more = rest[pl.ds(pl.multiple_of(step * rows, SUB), rows), :]
+    norm_ref[...] = (jnp.sum(lane, axis=1, keepdims=True) + more) / gain_ref[...]
 
 
 def laid_out(wide, third, w_zx, w_bc, w_dt, gain, heads):
@@ -993,14 +1041,16 @@
     cut = rows // steps
     share = w_bc.shape[1] // peers
     by_rows = lambda a: pl.BlockSpec((cut, a.shape[1]), lambda i: (i, 0))
-    by_piece = lambda a: pl.BlockSpec((peers, 1, cut, a.shape[3]), lambda i: (0, i // 2, i % 2, 0))
+    whole = lambda a: pl.BlockSpec(a.shape, lambda i: (0,) * len(a.shape))
+    by_piece = pl.BlockSpec((peers, 1, cut, cols), lambda i: (0, i // 2, i % 2, 0))
     shapes = [jax.ShapeDtypeStruct(a.shape, f32) for a in (w_zx, w_bc, w_dt, gain)]
     return pl.pallas_call(
         partial(laid_kernel, heads=heads, share=share),
         grid=(steps,),
-        in_specs=[by_piece(wide), by_piece(third)] + [by_rows(a) for a in (w_zx, w_bc, w_dt, gain)],
-        out_specs=[by_rows(a) for a in shapes],
+        in_specs=[by_piece, whole(third), by_rows(w_zx), whole(w_bc), whole(w_dt), by_rows(gain)],
+        out_specs=[by_rows(w_zx), whole(w_bc), whole(w_dt), by_rows(gain)],
         out_shape=shapes,
+        scratch_shapes=[pltpu.VMEM((rows, 1), f32)],
         compiler_params=pltpu.CompilerParams(vmem_limit_bytes=32 << 20),
         name="lay_out",
     )(wide, third, w_zx, w_bc, w_dt, gain)
@@ -1058,7 +1108,6 @@
         valid, starts, tokens, cotangent, norm_gain[None], w_bc, w_dt, conv_w.T, conv_b[None], dt_bias[None], a_log[None],
         d_skip[None], gate_gain[None], spread, w_zx, w_out,
     )
-    weights = weights.reshape(model, -1)
     normed, bgrad = normed.reshape(rows, model), bgrad.reshape(rows, model)
     keep = 1.0 - starts_all[:, :lanes, 0]
     zx, mix, mixed_grad, scale, mixed_low, part, conv, bc, steps = [a.reshape(rows, a.shape[-1]) for a in computed[:9]]
@@ -1080,40 +1129,39 @@
     share_par = jnp.pad(jnp.concatenate([of_share(conv_w), of_share(conv_b)[:, None]], axis=1), ((0, 0), (0, BLOCK - BIAS - 1)))
     over_time = lambda a: jnp.repeat(a.reshape(-1), BLOCK)
     keep_next = jnp.concatenate([keep[1:], jnp.zeros_like(keep[:1])], axis=0)
-    third, dshare = bc_backward(
-        got, zx, share_par, packed_rows([over_time(keep), over_time(keep_next)], SUB), dzx, heads, chans
-    )
+    keep_rows = packed_rows([over_time(keep), over_time(keep_next)], SUB)
 
     at_heads = lambda a: lax.dynamic_update_slice_in_dim(jnp.zeros((H,), f32), a, first, 0)
     at_chans = lambda a: lax.dynamic_update_slice_in_dim(jnp.zeros((E,), f32), a, first * HEAD_DIM, 0)
-    at_share = lambda a: lax.dynamic_update_slice_in_dim(jnp.zeros((2 * N,), f32), a, place * share, 0)
     skip = jnp.sum(dchan[SKIP].reshape(heads, HEAD_DIM), axis=1)
-    small = [jnp.concatenate([at_chans(dchan[k]), at_share(dshare[:, k])]) for k in range(KCONV + 1)]
+    small = [jnp.pad(at_chans(dchan[k]), (0, 2 * N)) for k in range(KCONV + 1)]
     small += [at_chans(dchan[GAIN]), at_heads(dhead[0, :heads]), at_heads(dhead[1, :heads]), at_heads(skip)]
     sizes = [a.shape[0] // peers for a in small]
     small = jnp.concatenate([a.reshape(peers, -1) for a in small], axis=1)
-    per_row = -(-small.shape[1] // own)
-    small = jnp.pad(small, ((0, 0), (0, own * per_row - small.shape[1]))).reshape(model, per_row)
+    small_rows = -(-small.shape[1] // (own * SUB)) * SUB
+    small = jnp.pad(small, ((0, 0), (0, own * small_rows - small.shape[1])))
+    small = small.reshape(peers, small_rows, own).transpose(1, 0, 2).reshape(small_rows, model)
 
     wide = mm(normed, dzx[:, : 2 * chans], TN).astype(bf16)
     wide, out_pieces = lax.optimization_barrier((wide, out_pieces))
     out_grad = quarters_joined(out_pieces)
-    wide_third = jnp.concatenate(
-        [mm(normed, third, TN)[:, :used], small, jnp.zeros((model, BLOCK - used - per_row), f32)], axis=1
-    ).astype(bf16)
-    part = mm(lax.dynamic_update_slice(dzx, third, (0, 2 * chans)), weights[:, : 2 * chans + BLOCK], NT).astype(bf16)
-    by_owner = lambda a: a.reshape(peers, widths, own // widths, -1)
-    part, output, out_grad = lax.optimization_barrier((part, output, out_grad))
-    input_grad, wide, wide_third = scattered_out(
-        part.reshape(peers, own, model), by_owner(wide), by_owner(wide_third), tokens, cotangent, norm_gain[None]
+    got, output, out_grad = lax.optimization_barrier((got, output, out_grad))
+    input_grad, wide, third = scattered_out(
+        got, zx, dzx, weights, normed, wide.reshape(peers, widths, own // widths, -1), share_par, keep_rows, small,
+        tokens, cotangent, norm_gain[None], heads,
     )
     gain_rows = lax.dynamic_slice_in_dim(norm_gain, place * own, own, 0)[:, None]
-    grad_zx, grad_bc, grad_dt, grad_norm = laid_out(wide, wide_third, w_zx, w_bc, w_dt, gain_rows, heads)
+    grad_zx, grad_bc, grad_dt, grad_norm = laid_out(wide, third, w_zx, w_bc, w_dt, gain_rows, heads)
     grad_norm = grad_norm[:, 0]
-    summed = jnp.sum(wide_third.reshape(peers, own, BLOCK)[:, :, used : used + per_row].astype(f32), axis=0).reshape(-1)
+    third = third.reshape(peers, -1, own)
+    summed = jnp.sum(third[:, used : used + small_rows].astype(f32), axis=0).reshape(-1)
     pieces = [summed[sum(sizes[:i]) : sum(sizes[: i + 1])] for i in range(len(sizes))]
-    grad_taps = jnp.stack(pieces[:KCONV], axis=1)
+    of_bc = third[:, used + small_rows : used + small_rows + KCONV + 1, :share].astype(f32).transpose(1, 0, 2).reshape(KCONV + 1, 2 * N)
+    own_chans = sizes[0]
+    of_bc = lax.dynamic_slice_in_dim(jnp.pad(of_bc, ((0, 0), (E, 0))), place * own_chans, own_chans, 1)
+    grad_taps = jnp.stack(pieces[:KCONV], axis=1) + of_bc[:KCONV].T
     grad_bias, grad_gain, grad_dtb, grad_alog, grad_skip = pieces[KCONV:]
+    grad_bias = grad_bias + of_bc[KCONV]
     return (
         output, input_grad, grad_norm, grad_zx, grad_bc, grad_dt, grad_taps, grad_bias, grad_dtb, grad_alog, grad_skip,
         grad_gain, out_grad,

time: 496 us -> 465 us (0.938)
  the two profiles are of different devices: /device:TPU:0 before, /device:TPU:25 now
where the time goes in v5:
time: 465 us; the launch traced here: 456 us
  Pallas kernels  348 us (75%)
  local copies, waits for them, and re-layouts  36.2 us (8%)
  matrix products  23.1 us (5%)
  other arithmetic  15 us (3%)
  between operations  14.7 us (3%)
  starting transfers between devices  12.4 us (3%)
  waiting for transfers between devices  6.16 us (1%)
    pallas_call x1, Pallas kernels, front(): pl.pallas_call(partial(front_kernel, peers=peers, widths=widths, lanes=la...  196 us
    pallas_call x1, Pallas kernels, scattered_out(): pl.pallas_call(partial(scatter_kernel, peers=peers, widths=widths, heads=...  112 us
    pallas_call x1, Pallas kernels, run_backward(): pl.pallas_call(partial(backward_kernel, lanes=lanes, heads=heads, blocks=...  34.2 us
    dot_general x2, matrix products, mm(): lax.dot_general(left, right, (dims, ((), ())), precision=precision, prefe...  23.1 us
    unnamed x38, local copies, waits for them, and re-layouts  16.6 us
  transfers between devices with their start and end apart: 8, of which 2 were waited for; matrix products, arithmetic and copies ran while one was open for 11% of the time, Pallas kernels for 8%

profile of v5, /device:TPU:25, one launch (start us, length us, event | category | flops | bytes accessed | tf_op | source)
XLA Modules:
  0.0 455.5 jit_solution(725248478980812567)
XLA Ops:
  7.2 1.3 broadcast_in_dim.33.bias_ref
  8.6 1.5 copy.52.dt_ref
  10.1 196.2 %front.1 = (bf16[8,4,64,1408]{3,2,1,0:T(8,128)(2,1)}, bf16[8,256,2048]{2,1,0:T(8,128)(2,1)}, bf16[8,256,2048]{2,1,0:T(8,128)(2,1)}, f32[8,8,128]{2,1,0:T(8,128)}...) custom-call(s32[1,2]{1,0:T(1,128)} %valid_ref.1, ...), custom_call_target="tpu_custom_call" | custom-call | tf_op jit(solution)/shard_map/front/pallas_call | solution.py:691
  206.3 1.5 copy-done.15
  207.8 9.1 %bitcast_convert_fusion = bf16[512,2048]{1,0:T(8,128)(2,1)} fusion(bf16[8,256,512]{2,1,0:T(8,128)(2,1)S(1)} %copy-done.15, bf16[8,256,2048]{2,1,0:T(8,128)(2,1)} %get-tuple-element.70), kind=kOutput, calls=%fused_computation | convolution fusion | flops 4296015872 | bytes 12582912 | tf_op jit(solution)/shard_map/dot_general | solution.py:30
  216.9 3.1 dynamic-slice_bitcast_fusion
  220.0 2.1 collective-permute-start.2
  222.7 2.0 fusion.8
  224.6 1.3 copy.53
  226.0 1.3 slice.104
  227.3 1.3 dynamic_slice.47
  228.6 1.3 copy.55.keep_ref
  231.5 1.2 copy-done.4
  234.1 34.2 %mix_backward.1 = (bf16[2048,1152]{1,0:T(8,128)(2,1)}, bf16[256,2048]{1,0:T(8,128)(2,1)}, f32[8,512]{1,0:T(8,128)S(1)}, f32[8,128]{1,0:T(8,128)S(1)}) custom-call(f32[8,2]{1,0:T(8,128)S(1)} %copy-done.11, f32[2048,1408]{1,0:T(8,128)} %bitcast.78, f32[2048,512]{1,0:T(8,128)} %bitcast.84, f32[8,512]{1,0:T(8,128)S(1)} %copy-done.10, f32[8,128]{1,0:T(8,128)S(1)} %copy-done.12, ...), custom_call_target="tpu_custom_call" | custom-call | flops 6442450944 | bytes 41943040 | tf_op jit(solution)/shard_map/mix_backward/pallas_call | solution.py:278
  268.6 0.8 copy.60.gain_ref
  276.7 1.9 add_convert_fusion.1
  278.5 2.2 collective-permute-start.5
  281.2 7.0 %all-to-all-start = ((bf16[8,32,2048]{2,1,0:T(8,128)(2,1)}), bf16[8,32,2048]{2,1,0:T(8,128)(2,1)S(1)}, u32[]{:S(2)}, u32[]{:S(2)}) async-start(bf16[8,32,2048]{2,1,0:T(8,128)(2,1)} %bitcast.20), calls=%async_computation | async-start | bytes 2097152 | tf_op jit(solution)/shard_map/all_to_all | solution.py:1127
  288.2 14.0 %fusion.2 = bf16[2048,1024]{1,0:T(8,128)(2,1)} fusion(bf16[2048,2048]{1,0:T(8,128)(2,1)} %bitcast.79, bf16[2048,1152]{1,0:T(8,128)(2,1)} %get-tuple-element.78), kind=kOutput, calls=%fused_computation.3 | convolution fusion | flops 8592031744 | bytes 16777216 | tf_op jit(solution)/shard_map/dot_general | solution.py:30
  302.3 2.4 collective-permute-done.4
  304.7 1.3 pad_maximum_fusion
  306.5 2.7 bitcast_convert_fusion.1
  309.2 2.6 add_convert_fusion
  311.8 3.7 all-to-all-done.got_ref
  315.5 1.0 copy-done.14
  316.5 112.2 %scatter_out.1 = (f32[256,2048]{1,0:T(8,128)}, bf16[8,4,64,1024]{3,2,1,0:T(8,128)(2,1)}, bf16[8,4,16,256]{3,2,1,0:T(8,128)(2,1)}) custom-call(bf16[8,32,2048]{2,1,0:T(8,128)(2,1)} %copy-done.14, f32[8,256,1408]{2,1,0:T(8,128)} %get-tuple-element.58.zx_ref, bf16[8,256,1152]{2,1,0:T(8,128)(2,1)} %bitcast.81, bf16[8,4,64,1408]{3,2,1,0:T(8,128)(2,1)} %get-tuple-element.89.w_ref, ...), custom_call_target="tpu_custom_call" | custom-call | tf_op jit(solution)/shard_map/scatter_out/pallas_call | solution.py:981
  429.4 0.9 convert_reduce_fusion
  432.4 2.2 copy-done
  434.6 2.2 copy-done.1
  436.8 0.9 copy-done.8
  437.7 5.4 %lay_out.1 = (f32[256,8192]{1,0:T(8,128)}, f32[256,256]{1,0:T(8,128)}, f32[256,64]{1,0:T(8,128)S(1)}, f32[256,1]{1,0:T(8,128)S(1)}) custom-call(bf16[8,4,64,1024]{3,2,1,0:T(8,128)(2,1)S(1)} %copy-done.1, bf16[8,4,16,256]{3,2,1,0:T(8,128)(2,1)S(1)} %copy-done.8, bf16[256,8192]{1,0:T(8,128)(2,1)S(1)} %copy-done, bf16[256,256]{1,0:T(8,128)(2,1)S(1)} %copy-done.6, ...), custom_call_target="tpu_custom_call" | custom-call | tf_op jit(solution)/shard_map/lay_out/pallas_call | solution.py:1047
  445.1 3.1 copy.86
  (108 shorter events, 16.8 us)
Async XLA Ops:
  7.2 302.0 %reduce-scatter.2.cloned.1.call-start = ((), (), s32[]{:S(2)}) async-start(), calls=%async_computation.2 | async-start | bytes 9437184 | tf_op jit(solution)/shard_map/reduce_scatter | solution.py:1115
  206.2 1.6 copy-start.15
  216.9 14.5 %copy-start.2 = (f32[8,256,256]{2,1,0:T(8,128)S(1)}, f32[8,256,256]{2,1,0:T(8,128)}, u32[]{:S(2)}) copy-start(f32[8,256,256]{2,1,0:T(8,128)} %get-tuple-element.65) | copy-start | bytes 6291460
  216.9 14.5 %copy-start.3 = (f32[8,256,128]{2,1,0:T(8,128)S(1)}, f32[8,256,128]{2,1,0:T(8,128)}, u32[]{:S(2)}) copy-start(f32[8,256,128]{2,1,0:T(8,128)} %get-tuple-element.68) | copy-start | bytes 3145732
  216.9 14.5 %copy-start.7 = (bf16[128,512]{1,0:T(8,128)(2,1)S(1)}, bf16[128,512]{1,0:T(8,128)(2,1)}, u32[]{:S(2)}) copy-start(bf16[128,512]{1,0:T(8,128)(2,1)} %constant.67.clone.spread_ref) | copy-start | bytes 393220
  216.9 14.5 %copy-start.9 = (f32[8,2,8,512]{3,2,1,0:T(8,128)S(1)}, f32[8,2,8,512]{3,2,1,0:T(8,128)}, u32[]{:S(2)}) copy-start(f32[8,2,8,512]{3,2,1,0:T(8,128)} %get-tuple-element.67.tail_ref) | copy-start | bytes 786436
  216.9 14.5 %copy-start.10 = (f32[8,512]{1,0:T(8,128)S(1)}, f32[8,512]{1,0:T(8,128)}, u32[]{:S(2)}) copy-start(f32[8,512]{1,0:T(8,128)} %get-tuple-element.60.chan_ref) | copy-start | bytes 49156
  220.0 56.6 %collective-permute-start.2 = (bf16[128,2048]{1,0:T(8,128)(2,1)}, bf16[128,2048]{1,0:T(8,128)(2,1)}, u32[]{:S(2)}, u32[]{:S(2)}) collective-permute-start(bf16[128,2048]{1,0:T(8,128)(2,1)} %get-tuple-element.144), channel_id=1, source_target_pairs={{0,24},{8,16},{16,8},{24,0},{1,25},{9,17},{17,9},{25,1},{2,26},{10... | collective-permute-start | bytes 1572872 | tf_op jit(solution)/shard_map/ppermute | solution.py:1060
  222.2 54.5 %collective-permute-start.1 = (bf16[128,2048]{1,0:T(8,128)(2,1)}, bf16[128,2048]{1,0:T(8,128)(2,1)}, u32[]{:S(2)}, u32[]{:S(2)}) collective-permute-start(bf16[128,2048]{1,0:T(8,128)(2,1)} %get-tuple-element.145), channel_id=1, source_target_pairs={{0,16},{8,24},{16,0},{24,8},{1,17},{9,25},{17,1},{25,9},{2,18},{10... | collective-permute-start | bytes 1572872 | tf_op jit(solution)/shard_map/ppermute | solution.py:1060
  222.4 54.2 %collective-permute-start = (bf16[128,2048]{1,0:T(8,128)(2,1)}, bf16[128,2048]{1,0:T(8,128)(2,1)}, u32[]{:S(2)}, u32[]{:S(2)}) collective-permute-start(bf16[128,2048]{1,0:T(8,128)(2,1)} %get-tuple-element.146), channel_id=1, source_target_pairs={{0,8},{8,0},{16,24},{24,16},{1,9},{9,1},{17,25},{25,17},{2,10},{10... | collective-permute-start | bytes 1572872 | tf_op jit(solution)/shard_map/ppermute | solution.py:1060
  231.5 1.2 copy-start.4
  232.7 0.7 copy-start.11
  233.4 0.7 copy-start.12
  278.5 23.8 %collective-permute-start.5 = (bf16[128,2048]{1,0:T(8,128)(2,1)S(1)}, bf16[128,2048]{1,0:T(8,128)(2,1)S(1)}, u32[]{:S(2)}, u32[]{:S(2)}) collective-permute-start(bf16[128,2048]{1,0:T(8,128)(2,1)S(1)} %add_convert_fusion.1), channel_id=1, source_target_pairs={{0,24},{8,16},{16,8},{24,0},{1,25},{9,17},{17,9},{25,1},{2,26},{10... | collective-permute-start | bytes 1572872 | tf_op jit(solution)/shard_map/ppermute | solution.py:1060
  280.7 23.9 %collective-permute-start.4 = (bf16[128,2048]{1,0:T(8,128)(2,1)S(1)}, bf16[128,2048]{1,0:T(8,128)(2,1)S(1)}, u32[]{:S(2)}, u32[]{:S(2)}) collective-permute-start(bf16[128,2048]{1,0:T(8,128)(2,1)S(1)} %add_convert_fusion.1), channel_id=1, source_target_pairs={{0,16},{8,24},{16,0},{24,8},{1,17},{9,25},{17,1},{25,9},{2,18},{10... | collective-permute-start | bytes 1572872 | tf_op jit(solution)/shard_map/ppermute | solution.py:1060
  281.0 23.7 %collective-permute-start.3 = (bf16[128,2048]{1,0:T(8,128)(2,1)S(1)}, bf16[128,2048]{1,0:T(8,128)(2,1)}, u32[]{:S(2)}, u32[]{:S(2)}) collective-permute-start(bf16[128,2048]{1,0:T(8,128)(2,1)S(1)} %add_convert_fusion.1), channel_id=1, source_target_pairs={{0,8},{8,0},{16,24},{24,16},{1,9},{9,1},{17,25},{25,17},{2,10},{10... | collective-permute-start | bytes 1572872 | tf_op jit(solution)/shard_map/ppermute | solution.py:1060
  281.2 34.3 %all-to-all-start = ((bf16[8,32,2048]{2,1,0:T(8,128)(2,1)}), bf16[8,32,2048]{2,1,0:T(8,128)(2,1)S(1)}, u32[]{:S(2)}, u32[]{:S(2)}) async-start(bf16[8,32,2048]{2,1,0:T(8,128)(2,1)} %bitcast.20), calls=%async_computation | async-start | bytes 2097152 | tf_op jit(solution)/shard_map/all_to_all | solution.py:1127
  306.5 2.7 copy-start.13
  315.5 1.0 copy-start.14
  316.5 115.9 %copy-start.5 = (bf16[256,64]{1,0:T(8,128)(2,1)S(1)}, bf16[256,64]{1,0:T(8,128)(2,1)}, u32[]{:S(2)}) copy-start(bf16[256,64]{1,0:T(8,128)(2,1)} %copy.52.dt_ref) | copy-start | bytes 98308
  316.5 115.9 %copy-start.6 = (bf16[256,256]{1,0:T(8,128)(2,1)S(1)}, bf16[256,256]{1,0:T(8,128)(2,1)}, u32[]{:S(2)}) copy-start(bf16[256,256]{1,0:T(8,128)(2,1)} %bc_ref.3) | copy-start | bytes 393220
  432.4 2.2 copy-start
  434.6 2.2 copy-start.1
  436.8 0.9 copy-start.8
Sparse Core Ops, SparseCore 0:
  206.4 90.3 reduce-scatter.1

commit v6 on v5

--- a/solution.py
+++ b/solution.py
@@ -143,14 +143,13 @@
 
 
 def backward_kernel(
-    keep_ref, zx_ref, grad_ref, chan_ref, head_ref, spread_ref,
+    start_ref, zx_ref, grad_ref, chan_ref, head_ref, spread_ref,
     conv_ref, mix_ref, bc_ref, step_ref, state_ref, tail_ref, scale_ref,
     dzx_ref, dbc_ref, dchan_ref, dhead_ref,
     state_grad, next_conv, pad_x, pad_d,
-    *, lanes, heads, blocks,
+    *, lanes, heads,
 ):
     lap = pl.program_id(0)
-    c = blocks - 1 - lap
     width = heads * HEAD_DIM
     row, col = grids()
     causal = row >= col
@@ -169,7 +168,7 @@
 
     for lane in range(lanes):
         rows = pl.ds(lane * BLOCK, BLOCK)
-        keep = keep_ref[c, lane]
+        keep = 1.0 - jnp.concatenate([start_ref[0, lane : lane + 1, :]] * (width // BLOCK), axis=1)
         z = zx_ref[rows, :width]
         conv = conv_ref[rows, :]
         mixed = mix_ref[rows, :]
@@ -267,7 +266,7 @@
         dzx_ref[rows, width : 2 * width] = dpre.astype(bf16)
 
 
-def run_backward(keep, zx, grad, chan, head, spread, conv, mix, bc, step_arr, state, tail, scale, lanes, heads):
+def run_backward(starts, zx, grad, chan, head, spread, conv, mix, bc, step_arr, state, tail, scale, lanes, heads):
     rows, width = grad.shape
     step = lanes * BLOCK
     blocks = rows // step
@@ -276,10 +275,10 @@
     fixed = lambda shape: pl.BlockSpec(shape, lambda c: (0,) * len(shape))
     per_lane = lambda r, cols: pl.BlockSpec((1, lanes, r, cols), lambda c: (blocks - 1 - c, 0, 0, 0))
     return pl.pallas_call(
-        partial(backward_kernel, lanes=lanes, heads=heads, blocks=blocks),
+        partial(backward_kernel, lanes=lanes, heads=heads),
         grid=(blocks,),
         in_specs=[
-            pl.BlockSpec(memory_space=pltpu.SMEM), by_block(2 * width + BLOCK), by_block(width),
+            pl.BlockSpec((1, SUB, BLOCK), lambda c: (blocks - 1 - c, 0, 0)), by_block(2 * width + BLOCK), by_block(width),
             whole(chan), whole(head), whole(spread),
             by_block(width), by_block(width), by_block(2 * N), by_block(2 * BLOCK),
             per_lane(N, width), per_lane(SUB, width), by_block(BLOCK),
@@ -300,7 +299,7 @@
         compiler_params=pltpu.CompilerParams(vmem_limit_bytes=48 << 20, dimension_semantics=("arbitrary",)),
         cost_estimate=pl.CostEstimate(flops=rows * width * 6144, bytes_accessed=rows * width * 40, transcendentals=rows * width * 6),
         name="mix_backward",
-    )(keep, zx, grad, chan, head, spread, conv, mix, bc, step_arr, state, tail, scale)
+    )(starts, zx, grad, chan, head, spread, conv, mix, bc, step_arr, state, tail, scale)
 
 
 MESH = pl.DeviceIdType.MESH
@@ -410,12 +409,12 @@
 def front_kernel(
     valid_ref, start_ref, x_ref, cot_ref, norm_gain_ref, bc_ref, dt_ref, taps_ref, bias_ref, dtb_ref, alog_ref, skip_ref,
     gain_ref, spread_ref, zx_ref, wout_ref,
-    w_ref, rows_ref, grads_ref, starts_ref, chan_ref, head_ref,
+    w_ref, rows_ref, grads_ref, starts_ref, chan_ref, head_ref, bc_par,
     out_zx, out_mix, out_grad, out_scale, out_low, out_part, out_conv, out_bc, out_step, out_state, out_tail,
-    w_v, rows_v, starts_v, wout_v, own_v, grad_v, third_v, start_v, bc_par,
+    w_v, rows_v, starts_v, wout_v, own_v, grad_v, third_v, start_v, part_got,
     zx_v, mix_v, mgrad_v, scale_v, low_v, conv_v, bc_v, step_v, state_v, tail_v, sums, sums_got,
     state, tail_x, tail_b, pad_x, pad_b,
-    w_send, w_recv, st_send, st_recv, own_sem, wide_send, wide_recv, in_sem, out_sem, slot_sem, sum_send, sum_recv, *sems,
+    w_send, w_recv, st_send, st_recv, own_sem, wide_send, wide_recv, in_sem, out_sem, slot_sem, part_send, part_recv, part_sem, sum_send, sum_recv, *sems,
     peers, widths, lanes, heads,
 ):
     width, place = lax.axis_index("width"), lax.axis_index("seq")
@@ -636,14 +635,36 @@
                 lane_at == 0, by_time[:, i : i + 1], jnp.where(lane_at == 1, by_time[:, j : j + 1], 0.0)
             )
 
-    @pl.loop(0, peers)
-    def _(c):
-        low = (gated_of(c) * scale_v[c, :, 0:1] * chan_ref[GAIN : GAIN + 1, :]).astype(bf16)
-        low_v[c] = low
-        rows_v[c] = mm(low, wout_v[...]).astype(bf16)
-        out_copy(3, scale_v, out_scale, c).start()
-        out_copy(4, low_v, out_low, c).start()
-        out_copy(5, rows_v, out_part, c).start()
+    core = lax.rem(place, 2)
+
+    def part_over(q):
+        return remote(
+            rows_v.at[2 * q + 1 - core], part_got.at[q], part_send.at[q], part_recv.at[q], (width, jnp.bitwise_xor(place, 1))
+        )
+
+    def part_out(q):
+        return pltpu.make_async_copy(rows_v.at[2 * q + core], out_part.at[q], part_sem.at[q])
+
+    def part_sum(q):
+        part_over(q).wait_recv()
+        add_into(rows_v.at[2 * q + core], [part_got.at[q]], rows_v.shape[1])
+        part_out(q).start()
+
+    @pl.loop(0, chips)
+    def _(q):
+        for c in (2 * q + 1 - core, 2 * q + core):
+            low = (gated_of(c) * scale_v[c, :, 0:1] * chan_ref[GAIN : GAIN + 1, :]).astype(bf16)
+            low_v[c] = low
+            rows_v[c] = mm(low, wout_v[...]).astype(bf16)
+            out_copy(3, scale_v, out_scale, c).start()
+            out_copy(4, low_v, out_low, c).start()
+        part_over(q).start()
+
+        @pl.when(q > 0)
+        def _():
+            part_sum(q - 1)
+
+    part_sum(chips - 1)
 
     for copy in shares + pushes + give:
         copy.wait_send()
@@ -656,9 +677,13 @@
     @pl.loop(0, peers)
     def _(c):
         for k, (src, dst) in enumerate(
-            [(zx_v, out_zx), (mix_v, out_mix), (mgrad_v, out_grad), (scale_v, out_scale), (low_v, out_low), (rows_v, out_part)]
+            [(zx_v, out_zx), (mix_v, out_mix), (mgrad_v, out_grad), (scale_v, out_scale), (low_v, out_low)]
         ):
             out_copy(k, src, dst, c).wait()
+
+    for q in range(chips):
+        part_over(q).wait_send()
+        part_out(q).wait()
 
 
 def front(valid, starts, tokens, cotangent, norm_gain, w_bc, w_dt, taps, bias, dt_bias, a_log, d_skip, gate_gain, spread, w_zx, w_out):
@@ -674,16 +699,17 @@
     smem = pl.BlockSpec(memory_space=pltpu.SMEM)
     w_all = ((peers, widths, quarter, cols), bf16)
     rows_all = ((peers, own, model), bf16)
+    part_all = ((peers // 2, own, model), bf16)
     starts_all = ((peers, SUB, BLOCK), f32)
     per_chan, low = ((peers, own, chans), f32), ((peers, own, chans), bf16)
     whole = [((peers, own, cols), f32), per_chan, per_chan, ((peers, own, BLOCK), f32), low]
     streamed = [
         ((own, chans), f32), ((own, 2 * N), bf16), ((own, 2 * BLOCK), f32), ((lanes, N, chans), f32), ((lanes, SUB, chans), f32)
     ]
-    outs = [w_all, rows_all, rows_all, starts_all, ((SUB, chans), f32), ((SUB, BLOCK), f32), *whole, rows_all]
+    outs = [w_all, rows_all, rows_all, starts_all, ((SUB, chans), f32), ((SUB, BLOCK), f32), ((SUB, 2 * N), f32), *whole, part_all]
     outs += [((peers,) + a[0], a[1]) for a in streamed]
     scratch = [w_all, rows_all, starts_all, ((chans, model), bf16), ((own, model), bf16), ((own, model), bf16)]
-    scratch += [((peers, own, BLOCK), bf16), ((SUB, BLOCK), f32), ((SUB, 2 * N), f32), *whole]
+    scratch += [((peers, own, BLOCK), bf16), ((SUB, BLOCK), f32), part_all, *whole]
     scratch += [((2,) + a[0], a[1]) for a in streamed]
     scratch += [((2, peers * lanes, BLOCK), f32), ((peers - 1, 2, peers * lanes, BLOCK), f32)]
     scratch += [((lanes, N, chans), f32), ((lanes, SUB, chans), f32), ((lanes, SUB, 2 * N), f32)]
@@ -691,13 +717,13 @@
     return pl.pallas_call(
         partial(front_kernel, peers=peers, widths=widths, lanes=lanes, heads=heads),
         in_specs=[smem] * 2 + [vmem] * 12 + [anywhere] * 2,
-        out_specs=[anywhere] * 4 + [vmem] * 2 + [anywhere] * 11,
+        out_specs=[anywhere] * 4 + [vmem] * 3 + [anywhere] * 11,
         out_shape=[jax.ShapeDtypeStruct(*a) for a in outs],
         scratch_shapes=[
             *[pltpu.VMEM(*a) for a in scratch],
             dma((4, peers - 1)), dma((4, peers - 1)), dma((peers - 1,)), dma((peers - 1,)),
-            dma((5,)), dma((widths - 1,)), dma((widths - 1,)), dma((peers,)), dma((6, peers)), dma((5, 2)),
-            dma((peers - 1,)), dma((peers - 1,)),
+            dma((5,)), dma((widths - 1,)), dma((widths - 1,)), dma((peers,)), dma((5, peers)), dma((5, 2)),
+            dma((peers // 2,)), dma((peers // 2,)), dma((peers // 2,)), dma((peers - 1,)), dma((peers - 1,)),
             *row_sems(peers // 2), *row_sems(peers // 2),
         ],
         compiler_params=pltpu.CompilerParams(collective_id=1, has_side_effects=True, vmem_limit_bytes=62 << 20),
@@ -745,9 +771,9 @@
 
 
 def scatter_kernel(
-    got_ref, zx_ref, dzx_ref, w_ref, normed_ref, wide_ref, par_ref, keep_ref, small_ref, x_ref, cot_ref, gain_ref,
+    got_ref, zx_ref, dzx_ref, w_ref, normed_ref, wide_ref, par_ref, start_ref, small_ref,
     rows_ref, out_ref, out_third_ref,
-    got_v, pre_v, dz_v, w_v, normed_v, third_t, third_g,
+    got_v, pre_v, dz_v, w_v, normed_v, third_t, third_g, par_t,
     mine, to_mate, from_core, up, down, own0, own1, own2, got0, got1, got2, piece0, piece1, piece2,
     load_sem, core_send, core_recv, up_send, up_recv, down_send, down_recv,
     own_sem, q_send, q_recv, p_send, p_recv, o_send, o_recv,
@@ -871,7 +897,13 @@
     block_rows = pre_v.shape[1]
     spots = [(c, slice(l * BLOCK, (l + 1) * BLOCK)) for c in range(peers) for l in range(block_rows // BLOCK)]
     pre = jnp.concatenate([pre_v[c, at, :].T[heads : heads + share] for c, at in spots], axis=1)
-    dpre, dpar = bc_back(dbc, pre, par_ref, keep_ref[0:1, :], keep_ref[1:2, :])
+    par = jnp.concatenate([par_ref[...], jnp.zeros((BLOCK - SUB, 2 * N), f32)], axis=0)
+    for i in range(2 * N // BLOCK):
+        par_t[i * BLOCK : (i + 1) * BLOCK, :] = par[:, i * BLOCK : (i + 1) * BLOCK].T
+    keep = [1.0 - start_ref[c, l : l + 1, :] for c in range(peers) for l in range(block_rows // BLOCK)]
+    keep_next = keep[block_rows // BLOCK :] + [jnp.zeros((1, BLOCK), f32)] * (block_rows // BLOCK)
+    own_par = par_t.at[pl.ds(pl.multiple_of(place * share, SUB), share)]
+    dpre, dpar = bc_back(dbc, pre, own_par, jnp.concatenate(keep, axis=1), jnp.concatenate(keep_next, axis=1))
     for i, (c, at) in enumerate(spots):
         tile = jnp.concatenate(
             [
@@ -903,9 +935,10 @@
         to_mate[q] = partial_rows(2 * q + 1 - core)
         over(q).start()
         mine[q] = partial_rows(2 * q + core)
-        if i:
+        if i > 1:
             whole_sum(order(i - 1))
-        if i == 1:
+        if not i:
+            whole_sum(q)
             run_hops(1)
     whole_sum(order(chips - 1))
 
@@ -939,17 +972,7 @@
             hop(buffer, by, chips - 1).wait_recv()
             add_into(mine.at[chip], [buffer], own)
 
-    gain = gain_ref[...]
-
-    @pl.loop(0, own // ROWS_AT_ONCE)
-    def _(i):
-        at = pl.ds(pl.multiple_of(i * ROWS_AT_ONCE, ROWS_AT_ONCE), ROWS_AT_ONCE)
-        x = x_ref[at, :].astype(f32)
-        rate = lax.rsqrt(jnp.mean(x * x, axis=-1, keepdims=True) + epsilon)
-        unit = x * rate
-        pulled = mine[chip, at].astype(f32) * gain
-        inner = jnp.mean(pulled * unit, axis=-1, keepdims=True)
-        rows_ref[at, :] = cot_ref[at, :].astype(f32) + rate * (pulled - unit * inner)
+    rows_ref[...] = mine[chip]
 
     for step in range(1, chips):
         for by in (1, -1):
@@ -965,13 +988,13 @@
             copy.wait()
 
 
-def scattered_out(got, zx, dzx, weights, normed, wide, par, keep, small, x_rows, cotangent, gain, heads):
+def scattered_out(got, zx, dzx, weights, normed, wide, par, starts, small, heads):
     peers, widths = lax.axis_size("seq"), lax.axis_size("width")
     chips = peers // 2
     dma = pltpu.SemaphoreType.DMA
     anywhere = pl.BlockSpec(memory_space=pl.ANY)
     vmem = pl.BlockSpec(memory_space=pltpu.VMEM)
-    own, model = x_rows.shape
+    own, model = normed.shape[0] // peers, normed.shape[1]
     half = wide.shape[3] // 2
     strips = -(-(heads + got.shape[1] + small.shape[0] + SUB) // (16 * widths)) * 16 * widths
     pieces = [(peers, wide.shape[2], half), (peers, wide.shape[2], half), (peers, strips // widths, own)]
@@ -980,16 +1003,16 @@
     zx, dzx, normed = [a.reshape(peers, own, a.shape[1]) for a in (zx, dzx, normed)]
     return pl.pallas_call(
         partial(scatter_kernel, peers=peers, widths=widths, heads=heads),
-        in_specs=[anywhere] * 6 + [vmem] * 6,
+        in_specs=[anywhere] * 6 + [vmem] * 3,
         out_specs=[vmem, anywhere, anywhere],
         out_shape=[
-            jax.ShapeDtypeStruct(block, f32), jax.ShapeDtypeStruct(wide.shape, bf16),
+            jax.ShapeDtypeStruct(block, bf16), jax.ShapeDtypeStruct(wide.shape, bf16),
             jax.ShapeDtypeStruct((peers, widths, strips // widths, own), bf16),
         ],
         scratch_shapes=[
             pltpu.VMEM(got.shape, bf16), pltpu.VMEM((peers, own, BLOCK), f32), pltpu.VMEM(dzx.shape, bf16),
             pltpu.VMEM(weights.shape, bf16), pltpu.VMEM(normed.shape, bf16),
-            pltpu.VMEM((BLOCK, peers * own), bf16), pltpu.VMEM((strips, model), bf16),
+            pltpu.VMEM((BLOCK, peers * own), bf16), pltpu.VMEM((strips, model), bf16), pltpu.VMEM((2 * N, BLOCK), f32),
             *[pltpu.VMEM((chips,) + block, bf16)] * 3, *[pltpu.VMEM((chips - 1,) + block, bf16)] * 2,
             *[pltpu.VMEM(a, bf16) for a in kept],
             *[pltpu.VMEM((widths - 1,) + a, bf16) for a in kept],
@@ -1001,10 +1024,14 @@
         ],
         compiler_params=pltpu.CompilerParams(collective_id=2, has_side_effects=True, vmem_limit_bytes=62 << 20),
         name="scatter_out",
-    )(got, zx, dzx, weights, normed, wide, par, keep, small, x_rows, cotangent, gain)
-
-
-def laid_kernel(in_ref, third_ref, w_ref, bc_ref, dt_ref, gain_ref, out_ref, out_bc_ref, out_dt_ref, norm_ref, rest, *, heads, share):
+    )(got, zx, dzx, weights, normed, wide, par, starts, small)
+
+
+def laid_kernel(
+    in_ref, third_ref, w_ref, bc_ref, dt_ref, gain_ref, rows_ref, x_ref, cot_ref, norm_gain_ref,
+    out_ref, out_bc_ref, out_dt_ref, norm_ref, out_rows_ref, rest,
+    *, heads, share,
+):
     peers, rows, wide = in_ref.shape[0], in_ref.shape[2], in_ref.shape[3]
     chans = wide // 2
     step = pl.program_id(0)
@@ -1030,30 +1057,38 @@
             value = value * w_ref[:, at : at + chans].astype(f32)
             for j in range(chans // BLOCK):
                 lane = lane + value[:, j * BLOCK : (j + 1) * BLOCK]
+    x = x_ref[...].astype(f32)
+    rate = lax.rsqrt(jnp.mean(x * x, axis=-1, keepdims=True) + epsilon)
+    unit = x * rate
+    pulled = rows_ref[...].astype(f32) * norm_gain_ref[...]
+    inner = jnp.mean(pulled * unit, axis=-1, keepdims=True)
+    out_rows_ref[...] = cot_ref[...].astype(f32) + rate * (pulled - unit * inner)
     more = rest[pl.ds(pl.multiple_of(step * rows, SUB), rows), :]
     norm_ref[...] = (jnp.sum(lane, axis=1, keepdims=True) + more) / gain_ref[...]
 
 
-def laid_out(wide, third, w_zx, w_bc, w_dt, gain, heads):
+def laid_out(wide, third, w_zx, w_bc, w_dt, gain, normed_grad, x_rows, cotangent, norm_gain, heads):
     peers, widths, quarter, cols = wide.shape
     rows = widths * quarter
-    steps = 2 * widths
-    cut = rows // steps
+    cut = quarter
     share = w_bc.shape[1] // peers
     by_rows = lambda a: pl.BlockSpec((cut, a.shape[1]), lambda i: (i, 0))
     whole = lambda a: pl.BlockSpec(a.shape, lambda i: (0,) * len(a.shape))
-    by_piece = pl.BlockSpec((peers, 1, cut, cols), lambda i: (0, i // 2, i % 2, 0))
-    shapes = [jax.ShapeDtypeStruct(a.shape, f32) for a in (w_zx, w_bc, w_dt, gain)]
+    by_piece = pl.BlockSpec((peers, 1, cut, cols), lambda i: (0, i, 0, 0))
+    shapes = [jax.ShapeDtypeStruct(a.shape, f32) for a in (w_zx, w_bc, w_dt, gain, x_rows)]
     return pl.pallas_call(
         partial(laid_kernel, heads=heads, share=share),
-        grid=(steps,),
-        in_specs=[by_piece, whole(third), by_rows(w_zx), whole(w_bc), whole(w_dt), by_rows(gain)],
-        out_specs=[by_rows(w_zx), whole(w_bc), whole(w_dt), by_rows(gain)],
+        grid=(widths,),
+        in_specs=[
+            by_piece, whole(third), by_rows(w_zx), whole(w_bc), whole(w_dt), by_rows(gain),
+            by_rows(normed_grad), by_rows(x_rows), by_rows(cotangent), whole(norm_gain),
+        ],
+        out_specs=[by_rows(w_zx), whole(w_bc), whole(w_dt), by_rows(gain), by_rows(x_rows)],
         out_shape=shapes,
         scratch_shapes=[pltpu.VMEM((rows, 1), f32)],
-        compiler_params=pltpu.CompilerParams(vmem_limit_bytes=32 << 20),
+        compiler_params=pltpu.CompilerParams(vmem_limit_bytes=62 << 20),
         name="lay_out",
-    )(wide, third, w_zx, w_bc, w_dt, gain)
+    )(wide, third, w_zx, w_bc, w_dt, gain, normed_grad, x_rows, cotangent, norm_gain)
 
 
 def crossed(value, axis, mask):
@@ -1081,11 +1116,6 @@
     stacked = jnp.stack(pieces)
     whole = jnp.stack([pick(stacked, jnp.bitwise_xor(width, j)) for j in range(len(pieces))])
     return whole.reshape((-1,) + whole.shape[2:]).astype(f32)
-
-
-def packed_rows(rows, count):
-    flat = jnp.stack(rows)
-    return jnp.pad(flat, ((0, count - len(rows)), (0, 0)))
 
 
 def heads_body(
@@ -1104,32 +1134,29 @@
     used = heads + share
     row_mask = (jnp.arange(BLOCK)[None, :] < valid[0][:, None]).astype(f32).reshape(-1, 1)
     spread = jnp.asarray(np.arange(chans)[None, :] // HEAD_DIM == np.arange(BLOCK)[:, None], bf16)
-    weights, normed, bgrad, starts_all, chan, head, *computed = front(
+    weights, normed, bgrad, starts_all, chan, head, bc_par, *computed = front(
         valid, starts, tokens, cotangent, norm_gain[None], w_bc, w_dt, conv_w.T, conv_b[None], dt_bias[None], a_log[None],
         d_skip[None], gate_gain[None], spread, w_zx, w_out,
     )
     normed, bgrad = normed.reshape(rows, model), bgrad.reshape(rows, model)
-    keep = 1.0 - starts_all[:, :lanes, 0]
-    zx, mix, mixed_grad, scale, mixed_low, part, conv, bc, steps = [a.reshape(rows, a.shape[-1]) for a in computed[:9]]
+    zx, mix, mixed_grad, scale, mixed_low = [a.reshape(rows, a.shape[-1]) for a in computed[:5]]
+    part = computed[5].reshape(rows // 2, model)
+    conv, bc, steps = [a.reshape(rows, a.shape[-1]) for a in computed[6:9]]
     state, tail = computed[9:]
-    branch = lax.psum_scatter(part, "seq", scatter_dimension=0, tiled=True).astype(f32)
+    like_cores = [list(range(core, peers, 2)) for core in range(2)]
+    branch = lax.psum_scatter(part, "seq", scatter_dimension=0, axis_index_groups=like_cores, tiled=True).astype(f32)
     output = (tokens.astype(f32) + row_mask * branch).astype(bf16)
     out_part = mm(mixed_low, bgrad, TN).astype(bf16)
     scale, out_part = lax.optimization_barrier((scale, out_part))
     out_quarters = quarters_sent(out_part)
 
     dzx, dbc, dchan, dhead = run_backward(
-        keep, zx, mixed_grad, chan, head, spread, conv, mix, bc, steps, state, tail, scale, lanes, heads
+        starts_all, zx, mixed_grad, chan, head, spread, conv, mix, bc, steps, state, tail, scale, lanes, heads
     )
     dzx, dbc, out_quarters = lax.optimization_barrier((dzx, dbc, out_quarters))
     out_pieces = quarters_back(sum(q.astype(f32) for q in out_quarters).astype(bf16))
 
     got = lax.all_to_all(dbc.reshape(peers, share, rows), "seq", 0, 0, tiled=True)
-    of_share = lambda a: lax.dynamic_slice_in_dim(a, E + place * share, share, 0)
-    share_par = jnp.pad(jnp.concatenate([of_share(conv_w), of_share(conv_b)[:, None]], axis=1), ((0, 0), (0, BLOCK - BIAS - 1)))
-    over_time = lambda a: jnp.repeat(a.reshape(-1), BLOCK)
-    keep_next = jnp.concatenate([keep[1:], jnp.zeros_like(keep[:1])], axis=0)
-    keep_rows = packed_rows([over_time(keep), over_time(keep_next)], SUB)
 
     at_heads = lambda a: lax.dynamic_update_slice_in_dim(jnp.zeros((H,), f32), a, first, 0)
     at_chans = lambda a: lax.dynamic_update_slice_in_dim(jnp.zeros((E,), f32), a, first * HEAD_DIM, 0)
@@ -1146,12 +1173,13 @@
     wide, out_pieces = lax.optimization_barrier((wide, out_pieces))
     out_grad = quarters_joined(out_pieces)
     got, output, out_grad = lax.optimization_barrier((got, output, out_grad))
-    input_grad, wide, third = scattered_out(
-        got, zx, dzx, weights, normed, wide.reshape(peers, widths, own // widths, -1), share_par, keep_rows, small,
-        tokens, cotangent, norm_gain[None], heads,
+    normed_grad, wide, third = scattered_out(
+        got, zx, dzx, weights, normed, wide.reshape(peers, widths, own // widths, -1), bc_par, starts_all, small, heads,
     )
     gain_rows = lax.dynamic_slice_in_dim(norm_gain, place * own, own, 0)[:, None]
-    grad_zx, grad_bc, grad_dt, grad_norm = laid_out(wide, third, w_zx, w_bc, w_dt, gain_rows, heads)
+    grad_zx, grad_bc, grad_dt, grad_norm, input_grad = laid_out(
+        wide, third, w_zx, w_bc, w_dt, gain_rows, normed_grad, tokens, cotangent, norm_gain[None], heads
+    )
     grad_norm = grad_norm[:, 0]
     third = third.reshape(peers, -1, own)
     summed = jnp.sum(third[:, used : used + small_rows].astype(f32), axis=0).reshape(-1)

time: 465 us -> 451 us (0.970)
  local copies, waits for them, and re-layouts: 36.2 us -> 21.7 us
    unnamed x38 -> x28, local copies, waits for them, and re-layouts: 16.6 us -> 9.61 us
  transfers between devices with their start and end apart: 8 -> 8, of which waited for: 2 -> 2; matrix products, arithmetic and copies ran while one was open for 11% -> 9% of each run, Pallas kernels for 8% -> 8%
where the time goes in v6:
time: 451 us; the launch traced here: 442 us
  Pallas kernels  352 us (78%)
  matrix products  23.1 us (5%)
  local copies, waits for them, and re-layouts  21.7 us (5%)
  between operations  14.7 us (3%)
  other arithmetic  13.3 us (3%)
  starting transfers between devices  12.5 us (3%)
  waiting for transfers between devices  4.63 us (1%)
    pallas_call x1, Pallas kernels, front(): pl.pallas_call(partial(front_kernel, peers=peers, widths=widths, lanes=la...  200 us
    pallas_call x1, Pallas kernels, scattered_out(): pl.pallas_call(partial(scatter_kernel, peers=peers, widths=widths, heads=...  109 us
    pallas_call x1, Pallas kernels, run_backward(): pl.pallas_call(partial(backward_kernel, lanes=lanes, heads=heads), grid=(...  34.2 us
    dot_general x2, matrix products, mm(): lax.dot_general(left, right, (dims, ((), ())), precision=precision, prefe...  23.1 us
    unnamed x28, local copies, waits for them, and re-layouts  9.61 us
    pallas_call x1, Pallas kernels, laid_out(): pl.pallas_call(partial(laid_kernel, heads=heads, share=share), grid=(widt...  9.4 us
  transfers between devices with their start and end apart: 8, of which 2 were waited for; matrix products, arithmetic and copies ran while one was open for 9% of the time, Pallas kernels for 8%

profile of v6, /device:TPU:25, one launch (start us, length us, event | category | flops | bytes accessed | tf_op | source)
XLA Modules:
  0.0 442.1 jit_solution(17054262449197838324)
XLA Ops:
  7.2 1.3 broadcast_in_dim.24.bias_ref
  8.6 1.5 copy.34.dt_ref
  10.1 199.9 %front.1 = (bf16[8,4,64,1408]{3,2,1,0:T(8,128)(2,1)}, bf16[8,256,2048]{2,1,0:T(8,128)(2,1)}, bf16[8,256,2048]{2,1,0:T(8,128)(2,1)}, f32[8,8,128]{2,1,0:T(8,128)}...) custom-call(s32[1,2]{1,0:T(1,128)} %valid_ref.1, ...), custom_call_target="tpu_custom_call" | custom-call | tf_op jit(solution)/shard_map/front/pallas_call | solution.py:717
  210.0 1.5 copy-done.11
  211.6 9.1 %bitcast_convert_fusion = bf16[512,2048]{1,0:T(8,128)(2,1)} fusion(bf16[8,256,512]{2,1,0:T(8,128)(2,1)S(1)} %copy-done.11, bf16[8,256,2048]{2,1,0:T(8,128)(2,1)} %get-tuple-element.72), kind=kOutput, calls=%fused_computation | convolution fusion | flops 4296015872 | bytes 12582912 | tf_op jit(solution)/shard_map/dot_general | solution.py:30
  220.7 3.0 dynamic-slice_bitcast_fusion
  223.7 2.2 collective-permute-start.2
  226.4 1.2 copy-done.2
  227.6 0.8 copy-done.5
  228.4 0.7 copy-done.8
  229.1 34.2 %mix_backward.1 = (bf16[2048,1152]{1,0:T(8,128)(2,1)}, bf16[256,2048]{1,0:T(8,128)(2,1)}, f32[8,512]{1,0:T(8,128)S(1)}, f32[8,128]{1,0:T(8,128)S(1)}) custom-call(f32[8,8,128]{2,1,0:T(8,128)S(1)} %copy-done.5, f32[2048,1408]{1,0:T(8,128)} %bitcast.70, f32[2048,512]{1,0:T(8,128)} %bitcast.74, f32[8,512]{1,0:T(8,128)S(1)} %copy-done.6, ...), custom_call_target="tpu_custom_call" | custom-call | flops 6442450944 | bytes 41943040 | tf_op jit(solution)/shard_map/mix_backward/pallas_call | solution.py:277
  264.0 0.8 dynamic_slice.39
  264.8 0.8 copy.37.gain_ref
  265.8 1.0 slice_reduce_fusion.1
  269.4 0.7 copy.41
  270.1 0.7 fusion.7
  270.8 1.9 add_convert_fusion.1
  272.7 2.2 collective-permute-start.5
  275.4 7.1 %all-to-all-start = ((bf16[8,32,2048]{2,1,0:T(8,128)(2,1)}), bf16[8,32,2048]{2,1,0:T(8,128)(2,1)S(1)}, u32[]{:S(2)}, u32[]{:S(2)}) async-start(bf16[8,32,2048]{2,1,0:T(8,128)(2,1)} %bitcast.19), calls=%async_computation | async-start | bytes 2097152 | tf_op jit(solution)/shard_map/all_to_all | solution.py:1159
  282.5 14.0 %fusion.2 = bf16[2048,1024]{1,0:T(8,128)(2,1)} fusion(bf16[2048,2048]{1,0:T(8,128)(2,1)} %bitcast.71, bf16[2048,1152]{1,0:T(8,128)(2,1)} %get-tuple-element.80), kind=kOutput, calls=%fused_computation.3 | convolution fusion | flops 8592031744 | bytes 16777216 | tf_op jit(solution)/shard_map/dot_general | solution.py:30
  296.5 2.3 collective-permute-done.4
  298.8 1.3 pad_maximum_fusion
  300.7 2.7 bitcast_convert_fusion.1
  303.3 2.6 add_convert_fusion
  305.9 2.3 all-to-all-done.got_ref
  308.2 1.0 copy-done.10
  309.2 108.8 %scatter_out.1 = (bf16[256,2048]{1,0:T(8,128)(2,1)}, bf16[8,4,64,1024]{3,2,1,0:T(8,128)(2,1)}, bf16[8,4,16,256]{3,2,1,0:T(8,128)(2,1)}) custom-call(bf16[8,32,2048]{2,1,0:T(8,128)(2,1)} %copy-done.10, f32[8,256,1408]{2,1,0:T(8,128)} %get-tuple-element.60.zx_ref, bf16[8,256,1152]{2,1,0:T(8,128)(2,1)} %bitcast.72, ...), custom_call_target="tpu_custom_call" | custom-call | tf_op jit(solution)/shard_map/scatter_out/pallas_call | solution.py:1004
  417.9 0.7 slice_bitcast_fusion
  418.7 0.9 convert_reduce_fusion
  421.6 9.4 %lay_out.1 = (f32[256,8192]{1,0:T(8,128)}, f32[256,256]{1,0:T(8,128)}, f32[256,64]{1,0:T(8,128)}, f32[256,1]{1,0:T(8,128)}, f32[256,2048]{1,0:T(8,128)}) custom-call(bf16[8,4,64,1024]{3,2,1,0:T(8,128)(2,1)} %get-tuple-element.96.in_ref, bf16[8,4,16,256]{3,2,1,0:T(8,128)(2,1)} %get-tuple-element.97.third_ref, bf16[256,8192]{1,0:T(8,128)(2,1)} %w_ref.1, ...), custom_call_target="tpu_custom_call" | custom-call | tf_op jit(solution)/shard_map/lay_out/pallas_call | solution.py:1079
  431.0 1.6 copy.39
  432.6 1.6 reduce.1
  (82 shorter events, 7.7 us)
Async XLA Ops:
  7.2 296.2 %reduce-scatter.2.cloned.1.call-start = ((), (), s32[]{:S(2)}) async-start(), calls=%async_computation.2 | async-start | bytes 5242880 | tf_op jit(solution)/shard_map/reduce_scatter | solution.py:1147
  210.0 1.6 copy-start.11
  220.7 5.7 %copy-start = (f32[8,256,256]{2,1,0:T(8,128)S(1)}, f32[8,256,256]{2,1,0:T(8,128)}, u32[]{:S(2)}) copy-start(f32[8,256,256]{2,1,0:T(8,128)} %get-tuple-element.67) | copy-start | bytes 6291460
  220.7 5.7 %copy-start.1 = (f32[8,256,128]{2,1,0:T(8,128)S(1)}, f32[8,256,128]{2,1,0:T(8,128)}, u32[]{:S(2)}) copy-start(f32[8,256,128]{2,1,0:T(8,128)} %get-tuple-element.70) | copy-start | bytes 3145732
  220.7 5.7 %copy-start.3 = (bf16[128,512]{1,0:T(8,128)(2,1)S(1)}, bf16[128,512]{1,0:T(8,128)(2,1)}, u32[]{:S(2)}) copy-start(bf16[128,512]{1,0:T(8,128)(2,1)} %constant.60.clone.spread_ref) | copy-start | bytes 393220
  220.7 5.7 %copy-start.4 = (f32[8,2,8,512]{3,2,1,0:T(8,128)S(1)}, f32[8,2,8,512]{3,2,1,0:T(8,128)}, u32[]{:S(2)}) copy-start(f32[8,2,8,512]{3,2,1,0:T(8,128)} %get-tuple-element.69.tail_ref) | copy-start | bytes 786436
  220.7 5.7 %copy-start.6 = (f32[8,512]{1,0:T(8,128)S(1)}, f32[8,512]{1,0:T(8,128)}, u32[]{:S(2)}) copy-start(f32[8,512]{1,0:T(8,128)} %get-tuple-element.62.chan_ref) | copy-start | bytes 49156
  223.7 47.1 %collective-permute-start.2 = (bf16[128,2048]{1,0:T(8,128)(2,1)}, bf16[128,2048]{1,0:T(8,128)(2,1)}, u32[]{:S(2)}, u32[]{:S(2)}) collective-permute-start(bf16[128,2048]{1,0:T(8,128)(2,1)} %get-tuple-element.135), channel_id=1, source_target_pairs={{0,24},{8,16},{16,8},{24,0},{1,25},{9,17},{17,9},{25,1},{2,26},{10... | collective-permute-start | bytes 1572872 | tf_op jit(solution)/shard_map/ppermute | solution.py:1095
  225.9 44.9 %collective-permute-start.1 = (bf16[128,2048]{1,0:T(8,128)(2,1)}, bf16[128,2048]{1,0:T(8,128)(2,1)}, u32[]{:S(2)}, u32[]{:S(2)}) collective-permute-start(bf16[128,2048]{1,0:T(8,128)(2,1)} %get-tuple-element.136), channel_id=1, source_target_pairs={{0,16},{8,24},{16,0},{24,8},{1,17},{9,25},{17,1},{25,9},{2,18},{10... | collective-permute-start | bytes 1572872 | tf_op jit(solution)/shard_map/ppermute | solution.py:1095
  226.1 44.7 %collective-permute-start = (bf16[128,2048]{1,0:T(8,128)(2,1)}, bf16[128,2048]{1,0:T(8,128)(2,1)}, u32[]{:S(2)}, u32[]{:S(2)}) collective-permute-start(bf16[128,2048]{1,0:T(8,128)(2,1)} %get-tuple-element.137), channel_id=1, source_target_pairs={{0,8},{8,0},{16,24},{24,16},{1,9},{9,1},{17,25},{25,17},{2,10},{10... | collective-permute-start | bytes 1572872 | tf_op jit(solution)/shard_map/ppermute | solution.py:1095
  226.4 1.2 copy-start.2
  227.6 0.8 copy-start.5
  228.4 0.7 copy-start.8
  263.3 0.6 copy-start.7
  272.7 23.8 %collective-permute-start.5 = (bf16[128,2048]{1,0:T(8,128)(2,1)S(1)}, bf16[128,2048]{1,0:T(8,128)(2,1)S(1)}, u32[]{:S(2)}, u32[]{:S(2)}) collective-permute-start(bf16[128,2048]{1,0:T(8,128)(2,1)S(1)} %add_convert_fusion.1), channel_id=1, source_target_pairs={{0,24},{8,16},{16,8},{24,0},{1,25},{9,17},{17,9},{25,1},{2,26},{10... | collective-permute-start | bytes 1572872 | tf_op jit(solution)/shard_map/ppermute | solution.py:1095
  274.9 23.9 %collective-permute-start.4 = (bf16[128,2048]{1,0:T(8,128)(2,1)S(1)}, bf16[128,2048]{1,0:T(8,128)(2,1)S(1)}, u32[]{:S(2)}, u32[]{:S(2)}) collective-permute-start(bf16[128,2048]{1,0:T(8,128)(2,1)S(1)} %add_convert_fusion.1), channel_id=1, source_target_pairs={{0,16},{8,24},{16,0},{24,8},{1,17},{9,25},{17,1},{25,9},{2,18},{10... | collective-permute-start | bytes 1572872 | tf_op jit(solution)/shard_map/ppermute | solution.py:1095
  275.1 23.7 %collective-permute-start.3 = (bf16[128,2048]{1,0:T(8,128)(2,1)S(1)}, bf16[128,2048]{1,0:T(8,128)(2,1)}, u32[]{:S(2)}, u32[]{:S(2)}) collective-permute-start(bf16[128,2048]{1,0:T(8,128)(2,1)S(1)} %add_convert_fusion.1), channel_id=1, source_target_pairs={{0,8},{8,0},{16,24},{24,16},{1,9},{9,1},{17,25},{25,17},{2,10},{10... | collective-permute-start | bytes 1572872 | tf_op jit(solution)/shard_map/ppermute | solution.py:1095
  275.4 32.8 %all-to-all-start = ((bf16[8,32,2048]{2,1,0:T(8,128)(2,1)}), bf16[8,32,2048]{2,1,0:T(8,128)(2,1)S(1)}, u32[]{:S(2)}, u32[]{:S(2)}) async-start(bf16[8,32,2048]{2,1,0:T(8,128)(2,1)} %bitcast.19), calls=%async_computation | async-start | bytes 2097152 | tf_op jit(solution)/shard_map/all_to_all | solution.py:1159
  300.6 2.7 copy-start.9
  308.2 1.0 copy-start.10
Sparse Core Ops, SparseCore 0:
  210.1 78.5 reduce-scatter.1

commit v7 on v6

--- a/solution.py
+++ b/solution.py
@@ -320,20 +320,29 @@
     )
 
 
+PARTS = 2
+
+
+def part_of(ref, i):
+    rows = ref.shape[0] // PARTS
+    return ref.at[pl.ds(i * rows, rows)]
+
+
 class Rows:
     def __init__(self, own_ref, all_ref, sems, peers):
         self.own, self.all, self.sems, self.peers = own_ref, all_ref, sems, peers
         self.width, self.place = lax.axis_index("width"), lax.axis_index("seq")
         self.chips, self.chip = peers // 2, self.place // 2
 
-    def hop(self, ref, s, step, by):
+    def hop(self, ref, s, step, by, i):
         send, recv = self.sems[0 if by > 0 else 2], self.sems[1 if by > 0 else 3]
         device = (self.width, jnp.clip(self.place + 2 * by, 0, self.peers - 1))
-        return remote(ref, self.all.at[s], send.at[step], recv.at[step], device)
-
-    def over(self, ref, s, slot):
+        return remote(part_of(ref, i), part_of(self.all.at[s], i), send.at[step, i], recv.at[step, i], device)
+
+    def over(self, ref, s, slot, i):
         device = (self.width, jnp.bitwise_xor(self.place, 1))
-        return remote(ref, self.all.at[s], self.sems[4].at[slot], self.sems[5].at[slot], device)
+        send, recv = self.sems[4].at[slot, i], self.sems[5].at[slot, i]
+        return remote(part_of(ref, i), part_of(self.all.at[s], i), send, recv, device)
 
     def inside(self, by):
         return self.chip + 1 < self.chips if by > 0 else self.chip > 0
@@ -348,40 +357,45 @@
         return pltpu.make_async_copy(self.own, self.all.at[self.place], self.sems[6])
 
     def start(self):
-        self.keep().start()
-        for by in (1, -1):
-            @pl.when(self.inside(by))
-            def _():
-                self.hop(self.own, self.place, 0, by).start()
-        self.over(self.own, self.place, 0).start()
-
-    def pass_on(self, step):
-        for by in (1, -1):
-            @pl.when(self.reached(by, step))
-            def _():
-                s = self.source(by, step)
-                ref = self.all.at[s]
-                self.hop(ref, s, step - 1, by).wait_recv()
-
+        for i in range(PARTS):
+            for by in (1, -1):
                 @pl.when(self.inside(by))
                 def _():
-                    self.hop(ref, s, step, by).start()
-                self.over(ref, s, 2 * step - (by > 0)).start()
+                    self.hop(self.own, self.place, 0, by, i).start()
+        self.keep().start()
+        for copy in self.mate(1, 0):
+            copy.start()
+
+    def pass_on(self, step):
+        for i in range(PARTS):
+            for by in (1, -1):
+                @pl.when(self.reached(by, step))
+                def _():
+                    s = self.source(by, step)
+                    ref = self.all.at[s]
+                    self.hop(ref, s, step - 1, by, i).wait_recv()
+
+                    @pl.when(self.inside(by))
+                    def _():
+                        self.hop(ref, s, step, by, i).start()
+                    self.over(ref, s, 2 * step - (by > 0), i).start()
 
     def mate(self, by, step):
         if not step:
-            return self.over(self.own, self.place, 0)
+            return [self.over(self.own, self.place, 0, i) for i in range(PARTS)]
         s = self.source(by, step)
-        return self.over(self.all.at[s], s, 2 * step - (by > 0))
+        return [self.over(self.all.at[s], s, 2 * step - (by > 0), i) for i in range(PARTS)]
 
     def arrived(self):
         self.keep().wait()
-        self.mate(1, 0).wait_recv()
+        for copy in self.mate(1, 0):
+            copy.wait_recv()
         for step in range(1, self.chips):
             for by in (1, -1):
                 @pl.when(self.reached(by, step))
                 def _():
-                    self.mate(by, step).wait_recv()
+                    for copy in self.mate(by, step):
+                        copy.wait_recv()
 
     def sent(self):
         for step in range(self.chips):
@@ -389,13 +403,16 @@
                 @pl.when(self.inside(by) & self.reached(by, step))
                 def _():
                     s = self.source(by, step)
-                    self.hop(self.all.at[s], s, step, by).wait_send()
-        self.mate(1, 0).wait_send()
+                    for i in range(PARTS):
+                        self.hop(self.all.at[s], s, step, by, i).wait_send()
+        for copy in self.mate(1, 0):
+            copy.wait_send()
         for step in range(1, self.chips):
             for by in (1, -1):
                 @pl.when(self.reached(by, step))
                 def _():
-                    self.mate(by, step).wait_send()
+                    for copy in self.mate(by, step):
+                        copy.wait_send()
 
 
 ROW_SEMS = 7
@@ -403,18 +420,19 @@
 
 def row_sems(chips):
     dma = pltpu.SemaphoreType.DMA
-    return [dma((chips,)), dma((chips,)), dma((chips,)), dma((chips,)), dma((2 * chips,)), dma((2 * chips,)), dma(())]
+    return [dma((chips, PARTS))] * 4 + [dma((2 * chips, PARTS))] * 2 + [dma(())]
 
 
 def front_kernel(
     valid_ref, start_ref, x_ref, cot_ref, norm_gain_ref, bc_ref, dt_ref, taps_ref, bias_ref, dtb_ref, alog_ref, skip_ref,
     gain_ref, spread_ref, zx_ref, wout_ref,
     w_ref, rows_ref, grads_ref, starts_ref, chan_ref, head_ref, bc_par,
-    out_zx, out_mix, out_grad, out_scale, out_low, out_part, out_conv, out_bc, out_step, out_state, out_tail,
+    out_zx, out_mix, out_grad, out_scale, out_wout, out_up, out_down, out_mine, out_conv, out_bc, out_step, out_state, out_tail,
     w_v, rows_v, starts_v, wout_v, own_v, grad_v, third_v, start_v, part_got,
-    zx_v, mix_v, mgrad_v, scale_v, low_v, conv_v, bc_v, step_v, state_v, tail_v, sums, sums_got,
+    z_v, mix_v, scale_v, low_v, zx_v, mgrad_v, conv_v, bc_v, step_v, state_v, tail_v, bgrad_v, up, down, wout_grad, sums, sums_got,
     state, tail_x, tail_b, pad_x, pad_b,
-    w_send, w_recv, st_send, st_recv, own_sem, wide_send, wide_recv, in_sem, out_sem, slot_sem, part_send, part_recv, part_sem, sum_send, sum_recv, *sems,
+    w_send, w_recv, st_send, st_recv, own_sem, wide_send, wide_recv, in_sem, out_sem, slot_sem, grad_sem, part_send, part_recv, branch_sem,
+    up_send, up_recv, down_send, down_recv, sum_send, sum_recv, *sems,
     peers, widths, lanes, heads,
 ):
     width, place = lax.axis_index("width"), lax.axis_index("seq")
@@ -530,7 +548,9 @@
     def out_copy(k, src, dst, c):
         return pltpu.make_async_copy(src.at[c], dst.at[c], out_sem.at[k, c])
 
-    slots = [(conv_v, out_conv), (bc_v, out_bc), (step_v, out_step), (state_v, out_state), (tail_v, out_tail)]
+    slots = [
+        (zx_v, out_zx), (conv_v, out_conv), (bc_v, out_bc), (step_v, out_step), (state_v, out_state), (tail_v, out_tail)
+    ]
 
     def slot_copies(c):
         slot = lax.rem(c, 2)
@@ -546,127 +566,213 @@
                 for copy in slot_copies(c - 2):
                     copy.wait()
             weights = w_v[...].reshape(w_v.shape[0] * w_v.shape[1] * w_v.shape[2], w_v.shape[3])
-            zx_v[c] = mm(rows_v[c], weights)
             slot = lax.rem(c, 2)
+            zx = mm(rows_v[c], weights)
+            zx_v[slot] = zx
+            z_v[c] = zx[:, :chans]
             for lane in range(lanes):
                 forward_block(
-                    1.0 - starts_v[c, lane : lane + 1, :], zx_v.at[c], chan_ref, bc_par, head_ref, spread_ref[...],
+                    1.0 - starts_v[c, lane : lane + 1, :], zx_v.at[slot], chan_ref, bc_par, head_ref, spread_ref[...],
                     conv_v.at[slot], mix_v.at[c], bc_v.at[slot], step_v.at[slot], state_v.at[slot], tail_v.at[slot],
                     state, tail_x, tail_b, pad_x, pad_b, lane=lane, heads=heads,
                 )
-            out_copy(0, zx_v, out_zx, c).start()
-            out_copy(1, mix_v, out_mix, c).start()
+            out_copy(0, mix_v, out_mix, c).start()
             for copy in slot_copies(c):
                 copy.start()
+            gated = gated_of(c)
+            square = mm_right(jnp.ones((SUB, chans), bf16), gated * gated, NT)
+            for lane in range(lanes):
+                sums[0, pl.ds(c * lanes + lane, 1), :] = square[:1, lane * BLOCK : (lane + 1) * BLOCK]
 
     def gated_of(c):
-        z = zx_v[c, :, :chans]
+        z = z_v[c]
         return mix_v[c] * (z * sigmoid(z))
 
-    def mix_grad(s):
-        load(grads_ref, s).wait()
-        grad = mm(rows_v[s], wout_v[...], NT)
-        mgrad_v[s] = grad
-        out_copy(2, mgrad_v, out_grad, s).start()
-        gated = gated_of(s)
-        ones = jnp.ones((SUB, chans), bf16)
-        square = mm_right(ones, gated * gated, NT)
-        pulled = mm_right(ones, grad * chan_ref[GAIN : GAIN + 1, :] * gated, NT)
-        for lane in range(lanes):
-            at = slice(lane * BLOCK, (lane + 1) * BLOCK)
-            sums[0, pl.ds(s * lanes + lane, 1), :] = square[:1, at]
-            sums[1, pl.ds(s * lanes + lane, 1), :] = pulled[:1, at]
-
-    per = -(-peers // 2)
-    for step in range(1, chips):
-        begin, end = min((step - 1) * per, peers), min(step * per, peers)
-        if step == chips - 1:
-            end = peers
-        if begin < end:
-            compute(begin, end)
-        if step < chips - 1:
-            grads.pass_on(step)
-
-    def at_distance(step, act):
+    core = lax.rem(place, 2)
+
+    def give(k):
+        copies = [
+            remote(sums.at[k], sums_got.at[k, i], sum_send.at[k, i], sum_recv.at[k, i], (width, s)) for i, s in enumerate(ring)
+        ]
+        for copy in copies:
+            copy.start()
+        return copies
+
+    def whole(k, copies):
+        total = sums[k]
+        for i, copy in enumerate(copies):
+            copy.wait_recv()
+            total = total + sums_got[k, i]
+        return total
+
+    def by_time(value):
+        return jnp.concatenate([value, jnp.zeros((BLOCK - lanes * peers, BLOCK), f32)], axis=0).T
+
+    def load_grad(s, slot):
+        return pltpu.make_async_copy(grads_ref.at[s], bgrad_v.at[slot], in_sem.at[slot])
+
+    def grad_out(s, slot):
+        return pltpu.make_async_copy(mgrad_v.at[slot], out_grad.at[s], grad_sem.at[slot])
+
+    def mix_grads(q, first):
+        for slot in range(2):
+            load_grad(2 * q + slot, slot).start()
+        for slot in range(2):
+            s = 2 * q + slot
+            load_grad(s, slot).wait()
+            if not first:
+                grad_out(s, slot).wait()
+            grad = mm(bgrad_v[slot], wout_v[...], NT)
+            mgrad_v[slot] = grad
+            grad_out(s, slot).start()
+            pulled = mm_right(jnp.ones((SUB, chans), bf16), grad * chan_ref[GAIN : GAIN + 1, :] * gated_of(s), NT)
+            for lane in range(lanes):
+                sums[1, pl.ds(s * lanes + lane, 1), :] = pulled[:1, lane * BLOCK : (lane + 1) * BLOCK]
+        rows_q = low_v[pl.ds(2 * q, 2)].reshape(2 * low_v.shape[1], chans)
+        both = bgrad_v[...].reshape(2 * bgrad_v.shape[1], bgrad_v.shape[2])
+        part = mm(rows_q, both, TN)
+        wout_grad[...] = part if first else wout_grad[...] + part
+
+    def mine(q):
+        return rows_v.at[2 * q + core]
+
+    def part_over(q):
+        return remote(
+            rows_v.at[2 * q + 1 - core], part_got.at[q], part_send.at[q], part_recv.at[q], (width, jnp.bitwise_xor(place, 1))
+        )
+
+    def part_sum(q):
+        part_over(q).wait_recv()
+        add_into(mine(q), [part_got.at[q]], rows_v.shape[1])
+
+    def sends(by, step):
+        far = chips - step
+        return unit_chip + far < chips if by > 0 else unit_chip >= far
+
+    def later(by):
+        return unit_chip > 0 if by > 0 else unit_chip + 1 < chips
+
+    unit_chip = place // 2
+
+    def branch_hop(src, by, step, i):
+        buffer, send, recv = (up, up_send, up_recv) if by > 0 else (down, down_send, down_recv)
+        return remote(
+            part_of(src, i), part_of(buffer.at[step - 1], i), send.at[step - 1, i], recv.at[step - 1, i],
+            (width, jnp.clip(place + 2 * by, 0, peers - 1)),
+        )
+
+    def branch_stage(by, step):
+        return (up if by > 0 else down).at[step - 2]
+
+    def branch_hops(step):
+        for i in range(PARTS):
+            for by in (1, -1):
+                owner = jnp.clip(unit_chip + by * (chips - step), 0, chips - 1)
+                last = step == chips - 1
+
+                def direct():
+                    branch_hop(mine(owner), by, step, i).start()
+
+                def relayed():
+                    stage = branch_stage(by, step)
+                    branch_hop(stage, by, step - 1, i).wait_recv()
+                    add_into(part_of(stage, i), [part_of(mine(owner), i)], rows_v.shape[1] // PARTS)
+                    if not last:
+                        branch_hop(stage, by, step, i).start()
+
+                if step == 1:
+                    pl.when(sends(by, step))(direct)
+                    continue
+                if not last:
+                    pl.when(sends(by, step) & jnp.logical_not(later(by)))(direct)
+                pl.when(sends(by, step) & later(by))(relayed)
+
+    def branch_out(k, src):
+        return pltpu.make_async_copy(src, (out_mine, out_up, out_down)[k], branch_sem.at[k])
+
+    def branch_outs(act):
+        act(branch_out(0, mine(unit_chip)))
+        for k, by in ((1, 1), (2, -1)):
+            owner = jnp.clip(unit_chip + by, 0, chips - 1)
+
+            @pl.when(later(by))
+            def _():
+                act(branch_out(k, branch_stage(by, chips - 1)))
+
+            @pl.when(jnp.logical_not(later(by)))
+            def _():
+                act(branch_out(k, mine(owner)))
+
+    compute(0, peers)
+    squares = give(0)
+    grads.pass_on(1)
+
+    def mates_here(step):
         if not step:
-            act(place, None)
-            act(jnp.bitwise_xor(place, 1), (1, 0))
+            for copy in grads.mate(1, 0):
+                copy.wait_recv()
         for by in (1, -1):
             if step:
                 @pl.when(grads.reached(by, step))
                 def _():
-                    s = grads.source(by, step)
-                    act(s, None)
-                    act(jnp.bitwise_xor(s, 1), (by, step))
-
-    def begin_load(s, mate):
-        if mate is not None:
-            grads.mate(*mate).wait_recv()
-        load(grads_ref, s).start()
-
+                    for copy in grads.mate(by, step):
+                        copy.wait_recv()
+
+    def at_distance(step):
+        for by in (1, -1):
+            @pl.when(grads.reached(by, step))
+            def _():
+                mix_grads(grads.source(by, step) // 2, False)
+
+    @pl.loop(0, chips)
+    def _(i):
+        q = jnp.where(unit_chip < chips // 2, chips - 1 - i, i)
+        for c in (2 * q + 1 - core, 2 * q + core):
+            low = (gated_of(c) * chan_ref[GAIN : GAIN + 1, :]).astype(bf16)
+            rows_v[c] = mm(low, wout_v[...]).astype(bf16)
+        part_over(q).start()
+
+    for q in range(chips):
+        part_sum(q)
+    branch_hops(1)
+    count = (active * HEAD_DIM).astype(f32)
+    rate = lax.rsqrt(whole(0, squares) / count + epsilon)
+    rate_t = by_time(rate)
+    lane_at = lax.broadcasted_iota(jnp.int32, (BLOCK, BLOCK), 1)
+    spots_of = [(c, slice(lane * BLOCK, (lane + 1) * BLOCK)) for c in range(peers) for lane in range(lanes)]
+    for i, (c, at) in enumerate(spots_of):
+        scale_v[c, at, :] = jnp.where(lane_at == 0, rate_t[:, i : i + 1], 0.0)
+
+    @pl.loop(0, peers)
+    def _(c):
+        low_v[c] = (gated_of(c) * scale_v[c, :, 0:1] * chan_ref[GAIN : GAIN + 1, :]).astype(bf16)
+
+    grads.pass_on(2)
     grads.keep().wait()
-    for step in range(chips - 1):
-        at_distance(step, begin_load)
-    for step in range(chips - 1):
-        at_distance(step, lambda s, mate: mix_grad(s))
+    mates_here(0)
+    mix_grads(unit_chip, True)
+    mates_here(1)
+    at_distance(1)
+    for step in range(2, chips - 1):
+        branch_hops(step)
+        mates_here(step)
+        at_distance(step)
     grads.pass_on(chips - 1)
-    at_distance(chips - 1, begin_load)
-    at_distance(chips - 1, lambda s, mate: mix_grad(s))
-
-    give = [remote(sums, sums_got.at[i], sum_send.at[i], sum_recv.at[i], (width, s)) for i, s in enumerate(ring)]
-    for copy in give:
-        copy.start()
-    for copy in give:
-        copy.wait_recv()
-    total = sums[...]
-    for i in range(peers - 1):
-        total = total + sums_got[i]
-    count = (active * HEAD_DIM).astype(f32)
-    rate = lax.rsqrt(total[0] / count + epsilon)
-    pull = rate * rate * rate * total[1] / count
-    blank = jnp.zeros((BLOCK - 2 * lanes * peers, BLOCK), f32)
-    by_time = jnp.concatenate([rate, pull, blank], axis=0).T
-    lane_at = lax.broadcasted_iota(jnp.int32, (BLOCK, BLOCK), 1)
+    mates_here(chips - 1)
+    at_distance(chips - 1)
+    crosses = give(1)
+    bgrad_v[...] = wout_grad[...].astype(bf16).reshape(bgrad_v.shape)
+    wout_out = pltpu.make_async_copy(bgrad_v, out_wout, own_sem.at[3])
+    wout_out.start()
+    branch_hops(chips - 1)
+    branch_outs(lambda copy: copy.start())
+    pull_t = by_time(rate * rate * rate * whole(1, crosses) / count)
+    for i, (c, at) in enumerate(spots_of):
+        scale_v[c, at, :] = jnp.where(lane_at == 1, pull_t[:, i : i + 1], scale_v[c, at, :])
     for c in range(peers):
-        for lane in range(lanes):
-            i = c * lanes + lane
-            j = lanes * peers + i
-            scale_v[c, lane * BLOCK : (lane + 1) * BLOCK, :] = jnp.where(
-                lane_at == 0, by_time[:, i : i + 1], jnp.where(lane_at == 1, by_time[:, j : j + 1], 0.0)
-            )
-
-    core = lax.rem(place, 2)
-
-    def part_over(q):
-        return remote(
-            rows_v.at[2 * q + 1 - core], part_got.at[q], part_send.at[q], part_recv.at[q], (width, jnp.bitwise_xor(place, 1))
-        )
-
-    def part_out(q):
-        return pltpu.make_async_copy(rows_v.at[2 * q + core], out_part.at[q], part_sem.at[q])
-
-    def part_sum(q):
-        part_over(q).wait_recv()
-        add_into(rows_v.at[2 * q + core], [part_got.at[q]], rows_v.shape[1])
-        part_out(q).start()
-
-    @pl.loop(0, chips)
-    def _(q):
-        for c in (2 * q + 1 - core, 2 * q + core):
-            low = (gated_of(c) * scale_v[c, :, 0:1] * chan_ref[GAIN : GAIN + 1, :]).astype(bf16)
-            low_v[c] = low
-            rows_v[c] = mm(low, wout_v[...]).astype(bf16)
-            out_copy(3, scale_v, out_scale, c).start()
-            out_copy(4, low_v, out_low, c).start()
-        part_over(q).start()
-
-        @pl.when(q > 0)
-        def _():
-            part_sum(q - 1)
-
-    part_sum(chips - 1)
-
-    for copy in shares + pushes + give:
+        out_copy(1, scale_v, out_scale, c).start()
+
+    for copy in shares + pushes + squares + crosses:
         copy.wait_send()
     rows.sent()
     grads.sent()
@@ -676,14 +782,21 @@
 
     @pl.loop(0, peers)
     def _(c):
-        for k, (src, dst) in enumerate(
-            [(zx_v, out_zx), (mix_v, out_mix), (mgrad_v, out_grad), (scale_v, out_scale), (low_v, out_low)]
-        ):
+        for k, (src, dst) in enumerate([(mix_v, out_mix), (scale_v, out_scale)]):
             out_copy(k, src, dst, c).wait()
 
     for q in range(chips):
         part_over(q).wait_send()
-        part_out(q).wait()
+    for step in range(1, chips - 1):
+        for by in (1, -1):
+            @pl.when(sends(by, step))
+            def _():
+                for i in range(PARTS):
+                    branch_hop(mine(0), by, step, i).wait_send()
+    for slot in range(2):
+        grad_out(slot, slot).wait()
+    wout_out.wait()
+    branch_outs(lambda copy: copy.wait())
 
 
 def front(valid, starts, tokens, cotangent, norm_gain, w_bc, w_dt, taps, bias, dt_bias, a_log, d_skip, gate_gain, spread, w_zx, w_out):
@@ -702,28 +815,34 @@
     part_all = ((peers // 2, own, model), bf16)
     starts_all = ((peers, SUB, BLOCK), f32)
     per_chan, low = ((peers, own, chans), f32), ((peers, own, chans), bf16)
-    whole = [((peers, own, cols), f32), per_chan, per_chan, ((peers, own, BLOCK), f32), low]
+    block = ((own, model), bf16)
     streamed = [
-        ((own, chans), f32), ((own, 2 * N), bf16), ((own, 2 * BLOCK), f32), ((lanes, N, chans), f32), ((lanes, SUB, chans), f32)
+        ((own, cols), f32), ((own, chans), f32), ((own, chans), f32), ((own, 2 * N), bf16), ((own, 2 * BLOCK), f32),
+        ((lanes, N, chans), f32), ((lanes, SUB, chans), f32),
     ]
-    outs = [w_all, rows_all, rows_all, starts_all, ((SUB, chans), f32), ((SUB, BLOCK), f32), ((SUB, 2 * N), f32), *whole, part_all]
-    outs += [((peers,) + a[0], a[1]) for a in streamed]
+    scale = ((peers, own, BLOCK), f32)
+    of = lambda count, a: ((count,) + a[0], a[1])
+    outs = [w_all, rows_all, rows_all, starts_all, ((SUB, chans), f32), ((SUB, BLOCK), f32), ((SUB, 2 * N), f32)]
+    outs += [of(peers, streamed[0]), per_chan, per_chan, scale, of(chans // own, block), block, block, block]
+    outs += [of(peers, a) for a in streamed[2:]]
     scratch = [w_all, rows_all, starts_all, ((chans, model), bf16), ((own, model), bf16), ((own, model), bf16)]
-    scratch += [((peers, own, BLOCK), bf16), ((SUB, BLOCK), f32), part_all, *whole]
-    scratch += [((2,) + a[0], a[1]) for a in streamed]
-    scratch += [((2, peers * lanes, BLOCK), f32), ((peers - 1, 2, peers * lanes, BLOCK), f32)]
+    scratch += [((peers, own, BLOCK), bf16), ((SUB, BLOCK), f32), part_all, per_chan, per_chan, scale, low]
+    scratch += [of(2, a) for a in streamed]
+    scratch += [of(2, block)] * 3 + [((chans, model), f32)]
+    scratch += [((2, peers * lanes, BLOCK), f32), ((2, peers - 1, peers * lanes, BLOCK), f32)]
     scratch += [((lanes, N, chans), f32), ((lanes, SUB, chans), f32), ((lanes, SUB, 2 * N), f32)]
     scratch += [((lanes, BLOCK + SUB, chans), f32), ((lanes, BLOCK + SUB, 2 * N), f32)]
     return pl.pallas_call(
         partial(front_kernel, peers=peers, widths=widths, lanes=lanes, heads=heads),
         in_specs=[smem] * 2 + [vmem] * 12 + [anywhere] * 2,
-        out_specs=[anywhere] * 4 + [vmem] * 3 + [anywhere] * 11,
+        out_specs=[anywhere] * 4 + [vmem] * 3 + [anywhere] * 13,
         out_shape=[jax.ShapeDtypeStruct(*a) for a in outs],
         scratch_shapes=[
             *[pltpu.VMEM(*a) for a in scratch],
             dma((4, peers - 1)), dma((4, peers - 1)), dma((peers - 1,)), dma((peers - 1,)),
-            dma((5,)), dma((widths - 1,)), dma((widths - 1,)), dma((peers,)), dma((5, peers)), dma((5, 2)),
-            dma((peers // 2,)), dma((peers // 2,)), dma((peers // 2,)), dma((peers - 1,)), dma((peers - 1,)),
+            dma((5,)), dma((widths - 1,)), dma((widths - 1,)), dma((peers,)), dma((2, peers)), dma((6, 2)), dma((2,)),
+            dma((peers // 2,)), dma((peers // 2,)), dma((3,)), *[dma((2, PARTS))] * 4,
+            dma((2, peers - 1)), dma((2, peers - 1)),
             *row_sems(peers // 2), *row_sems(peers // 2),
         ],
         compiler_params=pltpu.CompilerParams(collective_id=1, has_side_effects=True, vmem_limit_bytes=62 << 20),
@@ -833,32 +952,35 @@
     def later(by):
         return chip > 0 if by > 0 else chip + 1 < chips
 
-    def hop(src, by, step):
+    def hop(src, by, step, i):
         buffer, send, recv = flow(by)
         return remote(
-            src, buffer.at[step - 1], send.at[step - 1], recv.at[step - 1], (width, jnp.clip(place + 2 * by, 0, peers - 1))
+            part_of(src, i), part_of(buffer.at[step - 1], i), send.at[step - 1, i], recv.at[step - 1, i],
+            (width, jnp.clip(place + 2 * by, 0, peers - 1)),
         )
 
     def staged(by, step):
         return flow(by)[0].at[step - 2]
 
     def run_hops(step):
-        for by in (1, -1):
-            owner = jnp.clip(chip + by * (chips - step), 0, chips - 1)
-
-            def direct():
-                hop(mine.at[owner], by, step).start()
-
-            def relayed():
-                hop(staged(by, step), by, step - 1).wait_recv()
-                add_into(staged(by, step), [mine.at[owner]], own)
-                hop(staged(by, step), by, step).start()
-
-            if step == 1:
-                pl.when(sends(by, step))(direct)
-            else:
-                pl.when(sends(by, step) & jnp.logical_not(later(by)))(direct)
-                pl.when(sends(by, step) & later(by))(relayed)
+        for i in range(PARTS):
+            for by in (1, -1):
+                owner = jnp.clip(chip + by * (chips - step), 0, chips - 1)
+
+                def direct():
+                    hop(mine.at[owner], by, step, i).start()
+
+                def relayed():
+                    stage = staged(by, step)
+                    hop(stage, by, step - 1, i).wait_recv()
+                    add_into(part_of(stage, i), [part_of(mine.at[owner], i)], own // PARTS)
+                    hop(stage, by, step, i).start()
+
+                if step == 1:
+                    pl.when(sends(by, step))(direct)
+                else:
+                    pl.when(sends(by, step) & jnp.logical_not(later(by)))(direct)
+                    pl.when(sends(by, step) & later(by))(relayed)
 
     to_owner, to_all, kept_piece = [None] * 3, [None] * 3, [None] * 3
 
@@ -969,8 +1091,9 @@
         @pl.when(later(by))
         def _():
             buffer = flow(by)[0].at[chips - 2]
-            hop(buffer, by, chips - 1).wait_recv()
-            add_into(mine.at[chip], [buffer], own)
+            for i in range(PARTS):
+                hop(buffer, by, chips - 1, i).wait_recv()
+                add_into(part_of(mine.at[chip], i), [part_of(buffer, i)], own // PARTS)
 
     rows_ref[...] = mine[chip]
 
@@ -978,7 +1101,8 @@
         for by in (1, -1):
             @pl.when(sends(by, step))
             def _():
-                hop(mine.at[0], by, step).wait_send()
+                for i in range(PARTS):
+                    hop(mine.at[0], by, step, i).wait_send()
     for q in range(chips):
         over(q).wait_send()
     for k in range(len(sets)):
@@ -1018,7 +1142,7 @@
             *[pltpu.VMEM((widths - 1,) + a, bf16) for a in kept],
             *[pltpu.VMEM(a, bf16) for a in pieces],
             dma((5,)), dma((chips,)), dma((chips,)),
-            dma((chips - 1,)), dma((chips - 1,)), dma((chips - 1,)), dma((chips - 1,)),
+            *[dma((chips - 1, PARTS))] * 4,
             dma((3, 3)), dma((3, widths - 1)), dma((3, widths - 1)), dma((3, peers - 1)), dma((3, peers - 1)),
             dma((3, widths - 1)), dma((3, widths - 1)),
         ],
@@ -1139,17 +1263,13 @@
         d_skip[None], gate_gain[None], spread, w_zx, w_out,
     )
     normed, bgrad = normed.reshape(rows, model), bgrad.reshape(rows, model)
-    zx, mix, mixed_grad, scale, mixed_low = [a.reshape(rows, a.shape[-1]) for a in computed[:5]]
-    part = computed[5].reshape(rows // 2, model)
-    conv, bc, steps = [a.reshape(rows, a.shape[-1]) for a in computed[6:9]]
-    state, tail = computed[9:]
-    like_cores = [list(range(core, peers, 2)) for core in range(2)]
-    branch = lax.psum_scatter(part, "seq", scatter_dimension=0, axis_index_groups=like_cores, tiled=True).astype(f32)
-    output = (tokens.astype(f32) + row_mask * branch).astype(bf16)
-    out_part = mm(mixed_low, bgrad, TN).astype(bf16)
-    scale, out_part = lax.optimization_barrier((scale, out_part))
-    out_quarters = quarters_sent(out_part)
-
+    zx, mix, mixed_grad, scale = [a.reshape(rows, a.shape[-1]) for a in computed[:4]]
+    out_part, up, down, branch = computed[4:8]
+    conv, bc, steps = [a.reshape(rows, a.shape[-1]) for a in computed[8:11]]
+    state, tail = computed[11:]
+    above = lax.ppermute(up, "seq", [(i, i + 2) for i in range(peers - 2)])
+    below = lax.ppermute(down, "seq", [(i + 2, i) for i in range(peers - 2)])
+    out_quarters = quarters_sent(out_part.reshape(chans, model))
     dzx, dbc, dchan, dhead = run_backward(
         starts_all, zx, mixed_grad, chan, head, spread, conv, mix, bc, steps, state, tail, scale, lanes, heads
     )
@@ -1172,6 +1292,9 @@
     wide = mm(normed, dzx[:, : 2 * chans], TN).astype(bf16)
     wide, out_pieces = lax.optimization_barrier((wide, out_pieces))
     out_grad = quarters_joined(out_pieces)
+    branch = branch.astype(f32) + above.astype(f32) + below.astype(f32)
+    own_rate = lax.dynamic_slice(scale, (place * own, 0), (own, 1))
+    output = (tokens.astype(f32) + row_mask * own_rate * branch).astype(bf16)
     got, output, out_grad = lax.optimization_barrier((got, output, out_grad))
     normed_grad, wide, third = scattered_out(
         got, zx, dzx, weights, normed, wide.reshape(peers, widths, own // widths, -1), bc_par, starts_all, small, heads,

time: 451 us -> 426 us (0.945)
  the two profiles are of different devices: /device:TPU:25 before, /device:TPU:9 now
where the time goes in v7:
time: 426 us; the launch traced here: 417 us
  Pallas kernels  352 us (83%)
  local copies, waits for them, and re-layouts  18.9 us (4%)
  starting transfers between devices  17.5 us (4%)
  matrix products  14 us (3%)
  other arithmetic  13 us (3%)
    pallas_call x1, Pallas kernels, front(): pl.pallas_call(partial(front_kernel, peers=peers, widths=widths, lanes=la...  200 us
    pallas_call x1, Pallas kernels, scattered_out(): pl.pallas_call(partial(scatter_kernel, peers=peers, widths=widths, heads=...  108 us
    pallas_call x1, Pallas kernels, run_backward(): pl.pallas_call(partial(backward_kernel, lanes=lanes, heads=heads), grid=(...  34.2 us
    dot_general x1, matrix products, mm(): lax.dot_general(left, right, (dims, ((), ())), precision=precision, prefe...  14 us
    pallas_call x1, Pallas kernels, laid_out(): pl.pallas_call(partial(laid_kernel, heads=heads, share=share), grid=(widt...  9.4 us
  transfers between devices with their start and end apart: 9, of which 1 were waited for; matrix products, arithmetic and copies ran while one was open for 7% of the time, Pallas kernels for 8%

profile of v7, /device:TPU:9, one launch (start us, length us, event | category | flops | bytes accessed | tf_op | source)
XLA Modules:
  0.0 417.5 jit_solution(4811575743589026225)
XLA Ops:
  0.7 1.5 copy.33.dt_ref
  2.2 1.3 broadcast_in_dim.24.bias_ref
  3.5 200.5 %front.1 = (bf16[8,4,64,1408]{3,2,1,0:T(8,128)(2,1)}, bf16[8,256,2048]{2,1,0:T(8,128)(2,1)}, bf16[8,256,2048]{2,1,0:T(8,128)(2,1)}, f32[8,8,128]{2,1,0:T(8,128)}...) custom-call(s32[1,2]{1,0:T(1,128)} %valid_ref.1, ...), custom_call_target="tpu_custom_call" | custom-call | tf_op jit(solution)/shard_map/front/pallas_call | solution.py:835
  204.0 2.9 dynamic-slice_bitcast_fusion
  207.4 1.2 collective-permute-start.1
  208.6 0.9 collective-permute-start.2
  209.6 1.9 collective-permute-start.3
  211.5 4.5 %collective-permute-start.4 = (bf16[256,2048]{1,0:T(8,128)(2,1)}, bf16[256,2048]{1,0:T(8,128)(2,1)}, u32[]{:S(2)}, u32[]{:S(2)}) collective-permute-start(bf16[256,2048]{1,0:T(8,128)(2,1)} %get-tuple-element.76), channel_id=1, source_target_pairs={{2,0},{3,1},{4,2},{5,3},{6,4},{7,5},{10,8},{11,9},{12,10},{13,11},... | collective-permute-start | bytes 3145736 | tf_op jit(solution)/shard_map/ppermute | solution.py:1271
  216.0 0.9 copy-done.4
  217.0 0.7 copy-done.6
  217.7 34.2 %mix_backward.1 = (bf16[2048,1152]{1,0:T(8,128)(2,1)}, bf16[256,2048]{1,0:T(8,128)(2,1)}, f32[8,512]{1,0:T(8,128)S(1)}, f32[8,128]{1,0:T(8,128)S(1)}) custom-call(f32[8,8,128]{2,1,0:T(8,128)S(1)} %copy-done.5, f32[2048,1408]{1,0:T(8,128)} %bitcast.72, f32[2048,512]{1,0:T(8,128)} %bitcast.76, f32[8,512]{1,0:T(8,128)S(1)} %copy-done.6, ...), custom_call_target="tpu_custom_call" | custom-call | flops 6442450944 | bytes 41943040 | tf_op jit(solution)/shard_map/mix_backward/pallas_call | solution.py:277
  255.1 0.7 copy.41
  256.1 0.8 dynamic_slice.43
  256.8 0.8 copy.36.gain_ref
  257.8 1.4 add_convert_fusion.1
  259.7 1.2 collective-permute-start.6
  261.0 0.9 collective-permute-start.7
  261.9 5.7 %all-to-all-start = ((bf16[8,32,2048]{2,1,0:T(8,128)(2,1)}), bf16[8,32,2048]{2,1,0:T(8,128)(2,1)S(1)}, u32[]{:S(2)}, u32[]{:S(2)}) async-start(bf16[8,32,2048]{2,1,0:T(8,128)(2,1)} %bitcast.18), calls=%async_computation | async-start | bytes 2097152 | tf_op jit(solution)/shard_map/all_to_all | solution.py:1279
  267.6 14.0 %fusion.2 = bf16[2048,1024]{1,0:T(8,128)(2,1)} fusion(bf16[2048,2048]{1,0:T(8,128)(2,1)} %bitcast.73, bf16[2048,1152]{1,0:T(8,128)(2,1)} %get-tuple-element.78), kind=kOutput, calls=%fused_computation.2 | convolution fusion | flops 8592031744 | bytes 16777216 | tf_op jit(solution)/shard_map/dot_general | solution.py:30
  281.6 0.9 collective-permute-done.7
  282.6 1.3 pad_maximum_fusion
  284.3 0.9 copy-done.8
  285.6 3.3 add_convert_fusion
  288.9 2.7 bitcast_convert_fusion
  291.6 1.0 copy-done.9
  292.6 107.6 %scatter_out.1 = (bf16[256,2048]{1,0:T(8,128)(2,1)}, bf16[8,4,64,1024]{3,2,1,0:T(8,128)(2,1)}, bf16[8,4,16,256]{3,2,1,0:T(8,128)(2,1)}) custom-call(bf16[8,32,2048]{2,1,0:T(8,128)(2,1)} %copy-done.9, f32[8,256,1408]{2,1,0:T(8,128)} %get-tuple-element.59.zx_ref, bf16[8,256,1152]{2,1,0:T(8,128)(2,1)} %bitcast.74, ...), custom_call_target="tpu_custom_call" | custom-call | tf_op jit(solution)/shard_map/scatter_out/pallas_call | solution.py:1128
  400.1 0.7 slice_bitcast_fusion
  400.9 0.9 convert_reduce_fusion
  401.7 0.6 slice.104
  403.8 9.4 %lay_out.1 = (f32[256,8192]{1,0:T(8,128)}, f32[256,256]{1,0:T(8,128)}, f32[256,64]{1,0:T(8,128)}, f32[256,1]{1,0:T(8,128)}, f32[256,2048]{1,0:T(8,128)}) custom-call(bf16[8,4,64,1024]{3,2,1,0:T(8,128)(2,1)} %get-tuple-element.94.in_ref, bf16[8,4,16,256]{3,2,1,0:T(8,128)(2,1)} %get-tuple-element.95.third_ref, bf16[256,8192]{1,0:T(8,128)(2,1)} %w_ref.1, ...), custom_call_target="tpu_custom_call" | custom-call | tf_op jit(solution)/shard_map/lay_out/pallas_call | solution.py:1203
  413.2 1.6 copy.38
  414.8 1.6 reduce.2
  (85 shorter events, 7.4 us)
Async XLA Ops:
  3.5 212.5 %copy-start.3 = (bf16[128,512]{1,0:T(8,128)(2,1)S(1)}, bf16[128,512]{1,0:T(8,128)(2,1)}, u32[]{:S(2)}) copy-start(bf16[128,512]{1,0:T(8,128)(2,1)} %constant.61.clone.spread_ref) | copy-start | bytes 393220
  204.0 12.0 %copy-start = (f32[8,256,256]{2,1,0:T(8,128)S(1)}, f32[8,256,256]{2,1,0:T(8,128)}, u32[]{:S(2)}) copy-start(f32[8,256,256]{2,1,0:T(8,128)} %get-tuple-element.66) | copy-start | bytes 6291460
  204.0 12.0 %copy-start.1 = (f32[8,256,128]{2,1,0:T(8,128)S(1)}, f32[8,256,128]{2,1,0:T(8,128)}, u32[]{:S(2)}) copy-start(f32[8,256,128]{2,1,0:T(8,128)} %get-tuple-element.69) | copy-start | bytes 3145732
  204.0 12.0 %copy-start.2 = (bf16[8,256,256]{2,1,0:T(8,128)(2,1)S(1)}, bf16[8,256,256]{2,1,0:T(8,128)(2,1)}, u32[]{:S(2)}) copy-start(bf16[8,256,256]{2,1,0:T(8,128)(2,1)} %get-tuple-element.65) | copy-start | bytes 3145732
  204.0 12.0 %copy-start.5 = (f32[8,8,128]{2,1,0:T(8,128)S(1)}, f32[8,8,128]{2,1,0:T(8,128)}, u32[]{:S(2)}) copy-start(f32[8,8,128]{2,1,0:T(8,128)} %get-tuple-element.58.start_ref) | copy-start | bytes 98308
  204.0 12.0 %copy-start.7 = (f32[8,128]{1,0:T(8,128)S(1)}, f32[8,128]{1,0:T(8,128)}, u32[]{:S(2)}) copy-start(f32[8,128]{1,0:T(8,128)} %get-tuple-element.62.head_ref) | copy-start | bytes 12292
  206.9 50.9 %collective-permute-start = (bf16[128,2048]{1,0:T(8,128)(2,1)}, bf16[128,2048]{1,0:T(8,128)(2,1)S(1)}, u32[]{:S(2)}, u32[]{:S(2)}) collective-permute-start(bf16[128,2048]{1,0:T(8,128)(2,1)} %get-tuple-element.135), channel_id=1, source_target_pairs={{0,8},{8,0},{16,24},{24,16},{1,9},{9,1},{17,25},{25,17},{2,10},{10... | collective-permute-start | bytes 1572872 | tf_op jit(solution)/shard_map/ppermute | solution.py:1219
  207.4 50.4 %collective-permute-start.1 = (bf16[128,2048]{1,0:T(8,128)(2,1)}, bf16[128,2048]{1,0:T(8,128)(2,1)S(1)}, u32[]{:S(2)}, u32[]{:S(2)}) collective-permute-start(bf16[128,2048]{1,0:T(8,128)(2,1)} %get-tuple-element.134), channel_id=1, source_target_pairs={{0,16},{8,24},{16,0},{24,8},{1,17},{9,25},{17,1},{25,9},{2,18},{10... | collective-permute-start | bytes 1572872 | tf_op jit(solution)/shard_map/ppermute | solution.py:1219
  208.6 49.1 %collective-permute-start.2 = (bf16[128,2048]{1,0:T(8,128)(2,1)}, bf16[128,2048]{1,0:T(8,128)(2,1)}, u32[]{:S(2)}, u32[]{:S(2)}) collective-permute-start(bf16[128,2048]{1,0:T(8,128)(2,1)} %get-tuple-element.133), channel_id=1, source_target_pairs={{0,24},{8,16},{16,8},{24,0},{1,25},{9,17},{17,9},{25,1},{2,26},{10... | collective-permute-start | bytes 1572872 | tf_op jit(solution)/shard_map/ppermute | solution.py:1219
  209.6 74.8 %collective-permute-start.3 = (bf16[256,2048]{1,0:T(8,128)(2,1)}, bf16[256,2048]{1,0:T(8,128)(2,1)}, u32[]{:S(2)}, u32[]{:S(2)}) collective-permute-start(bf16[256,2048]{1,0:T(8,128)(2,1)} %get-tuple-element.75), channel_id=1, source_target_pairs={{0,2},{1,3},{2,4},{3,5},{4,6},{5,7},{8,10},{9,11},{10,12},{11,13},... | collective-permute-start | bytes 3145736 | tf_op jit(solution)/shard_map/ppermute | solution.py:1270
  211.5 72.9 %collective-permute-start.4 = (bf16[256,2048]{1,0:T(8,128)(2,1)}, bf16[256,2048]{1,0:T(8,128)(2,1)}, u32[]{:S(2)}, u32[]{:S(2)}) collective-permute-start(bf16[256,2048]{1,0:T(8,128)(2,1)} %get-tuple-element.76), channel_id=1, source_target_pairs={{2,0},{3,1},{4,2},{5,3},{6,4},{7,5},{10,8},{11,9},{12,10},{13,11},... | collective-permute-start | bytes 3145736 | tf_op jit(solution)/shard_map/ppermute | solution.py:1271
  216.0 1.0 copy-start.4
  217.0 0.7 copy-start.6
  217.7 38.1 %copy-start.11 = (s32[1,2]{1,0:T(1,128)S(1)}, s32[1,2]{1,0:T(1,128)}, u32[]{:S(2)}) copy-start(s32[1,2]{1,0:T(1,128)} %valid_ref.1) | copy-start | bytes 28
  259.2 22.5 %collective-permute-start.5 = (bf16[128,2048]{1,0:T(8,128)(2,1)S(1)}, bf16[128,2048]{1,0:T(8,128)(2,1)S(1)}, u32[]{:S(2)}, u32[]{:S(2)}) collective-permute-start(bf16[128,2048]{1,0:T(8,128)(2,1)S(1)} %add_convert_fusion.1), channel_id=1, source_target_pairs={{0,8},{8,0},{16,24},{24,16},{1,9},{9,1},{17,25},{25,17},{2,10},{10... | collective-permute-start | bytes 1572872 | tf_op jit(solution)/shard_map/ppermute | solution.py:1219
  259.7 21.9 %collective-permute-start.6 = (bf16[128,2048]{1,0:T(8,128)(2,1)S(1)}, bf16[128,2048]{1,0:T(8,128)(2,1)S(1)}, u32[]{:S(2)}, u32[]{:S(2)}) collective-permute-start(bf16[128,2048]{1,0:T(8,128)(2,1)S(1)} %add_convert_fusion.1), channel_id=1, source_target_pairs={{0,16},{8,24},{16,0},{24,8},{1,17},{9,25},{17,1},{25,9},{2,18},{10... | collective-permute-start | bytes 1572872 | tf_op jit(solution)/shard_map/ppermute | solution.py:1219
  261.0 21.6 %collective-permute-start.7 = (bf16[128,2048]{1,0:T(8,128)(2,1)S(1)}, bf16[128,2048]{1,0:T(8,128)(2,1)}, u32[]{:S(2)}, u32[]{:S(2)}) collective-permute-start(bf16[128,2048]{1,0:T(8,128)(2,1)S(1)} %add_convert_fusion.1), channel_id=1, source_target_pairs={{0,24},{8,16},{16,8},{24,0},{1,25},{9,17},{17,9},{25,1},{2,26},{10... | collective-permute-start | bytes 1572872 | tf_op jit(solution)/shard_map/ppermute | solution.py:1219
  261.9 29.7 %all-to-all-start = ((bf16[8,32,2048]{2,1,0:T(8,128)(2,1)}), bf16[8,32,2048]{2,1,0:T(8,128)(2,1)S(1)}, u32[]{:S(2)}, u32[]{:S(2)}) async-start(bf16[8,32,2048]{2,1,0:T(8,128)(2,1)} %bitcast.18), calls=%async_computation | async-start | bytes 2097152 | tf_op jit(solution)/shard_map/all_to_all | solution.py:1279
  284.0 1.2 copy-start.8
  284.0 1.5 copy-start.10
  291.6 1.0 copy-start.9

commit v8 on v7

--- a/solution.py
+++ b/solution.py
@@ -296,7 +296,7 @@
             pltpu.VMEM((lanes, N, width), f32), pltpu.VMEM((lanes, SUB, width), f32),
             pltpu.VMEM((lanes, BLOCK + SUB, width), f32), pltpu.VMEM((lanes, BLOCK + SUB, width), f32),
         ],
-        compiler_params=pltpu.CompilerParams(vmem_limit_bytes=48 << 20, dimension_semantics=("arbitrary",)),
+        compiler_params=pltpu.CompilerParams(vmem_limit_bytes=62 << 20, dimension_semantics=("arbitrary",)),
         cost_estimate=pl.CostEstimate(flops=rows * width * 6144, bytes_accessed=rows * width * 40, transcendentals=rows * width * 6),
         name="mix_backward",
     )(starts, zx, grad, chan, head, spread, conv, mix, bc, step_arr, state, tail, scale)
@@ -427,7 +427,7 @@
     valid_ref, start_ref, x_ref, cot_ref, norm_gain_ref, bc_ref, dt_ref, taps_ref, bias_ref, dtb_ref, alog_ref, skip_ref,
     gain_ref, spread_ref, zx_ref, wout_ref,
     w_ref, rows_ref, grads_ref, starts_ref, chan_ref, head_ref, bc_par,
-    out_zx, out_mix, out_grad, out_scale, out_wout, out_up, out_down, out_mine, out_conv, out_bc, out_step, out_state, out_tail,
+    out_zx, out_mix, out_grad, out_scale, out_q0, out_q1, out_q2, out_q3, out_up, out_down, out_mine, out_conv, out_bc, out_step, out_state, out_tail,
     w_v, rows_v, starts_v, wout_v, own_v, grad_v, third_v, start_v, part_got,
     z_v, mix_v, scale_v, low_v, zx_v, mgrad_v, conv_v, bc_v, step_v, state_v, tail_v, bgrad_v, up, down, wout_grad, sums, sums_got,
     state, tail_x, tail_b, pad_x, pad_b,
@@ -455,7 +455,7 @@
         grad_v[at, :] = (cot_ref[at, :].astype(f32) * mask).astype(bf16)
         tile = jnp.where(sub == lane, start_ref[0, lane].astype(f32), tile)
     start_v[...] = tile
-    bc, dt = bc_ref[...].astype(f32), dt_ref[...].astype(f32)
+    bc, dt = bc_ref[...].astype(f32), dt_ref[...].astype(f32).T
     share = bc.shape[1] // peers
     rest = jnp.zeros((bc.shape[0], BLOCK - share - heads), f32)
     for s in range(peers):
@@ -762,8 +762,19 @@
     at_distance(chips - 1)
     crosses = give(1)
     bgrad_v[...] = wout_grad[...].astype(bf16).reshape(bgrad_v.shape)
-    wout_out = pltpu.make_async_copy(bgrad_v, out_wout, own_sem.at[3])
-    wout_out.start()
+    wout_rows = chans // widths
+    per_block = bgrad_v.shape[1] // wout_rows
+
+    def wout_quarter(m):
+        j = jnp.bitwise_xor(width, m)
+        rows_j = pl.ds(pl.multiple_of(lax.rem(j, per_block) * wout_rows, 16), wout_rows)
+        return bgrad_v.at[j // per_block, rows_j]
+
+    wout_out = [
+        pltpu.make_async_copy(wout_quarter(m), dst, own_sem.at[m]) for m, dst in enumerate((out_q0, out_q1, out_q2, out_q3))
+    ]
+    for copy in wout_out:
+        copy.start()
     branch_hops(chips - 1)
     branch_outs(lambda copy: copy.start())
     pull_t = by_time(rate * rate * rate * whole(1, crosses) / count)
@@ -795,7 +806,8 @@
                     branch_hop(mine(0), by, step, i).wait_send()
     for slot in range(2):
         grad_out(slot, slot).wait()
-    wout_out.wait()
+    for copy in wout_out:
+        copy.wait()
     branch_outs(lambda copy: copy.wait())
 
 
@@ -823,7 +835,7 @@
     scale = ((peers, own, BLOCK), f32)
     of = lambda count, a: ((count,) + a[0], a[1])
     outs = [w_all, rows_all, rows_all, starts_all, ((SUB, chans), f32), ((SUB, BLOCK), f32), ((SUB, 2 * N), f32)]
-    outs += [of(peers, streamed[0]), per_chan, per_chan, scale, of(chans // own, block), block, block, block]
+    outs += [of(peers, streamed[0]), per_chan, per_chan, scale, *[((chans // widths, model), bf16)] * 4, block, block, block]
     outs += [of(peers, a) for a in streamed[2:]]
     scratch = [w_all, rows_all, starts_all, ((chans, model), bf16), ((own, model), bf16), ((own, model), bf16)]
     scratch += [((peers, own, BLOCK), bf16), ((SUB, BLOCK), f32), part_all, per_chan, per_chan, scale, low]
@@ -835,7 +847,7 @@
     return pl.pallas_call(
         partial(front_kernel, peers=peers, widths=widths, lanes=lanes, heads=heads),
         in_specs=[smem] * 2 + [vmem] * 12 + [anywhere] * 2,
-        out_specs=[anywhere] * 4 + [vmem] * 3 + [anywhere] * 13,
+        out_specs=[anywhere] * 4 + [vmem] * 3 + [anywhere] * 16,
         out_shape=[jax.ShapeDtypeStruct(*a) for a in outs],
         scratch_shapes=[
             *[pltpu.VMEM(*a) for a in scratch],
@@ -890,9 +902,10 @@
 
 
 def scatter_kernel(
-    got_ref, zx_ref, dzx_ref, w_ref, normed_ref, wide_ref, par_ref, start_ref, small_ref,
-    rows_ref, out_ref, out_third_ref,
-    got_v, pre_v, dz_v, w_v, normed_v, third_t, third_g, par_t,
+    valid_ref, got_ref, zx_ref, dzx_ref, w_ref, normed_ref, wide_ref, scale_ref, par_ref, start_ref, dchan_ref, dhead_ref,
+    x_ref, branch_ref, above_ref, below_ref,
+    output_ref, rows_ref, out_ref, out_third_ref,
+    got_v, pre_v, dz_v, w_v, normed_v, third_t, third_g, par_t, rate_v,
     mine, to_mate, from_core, up, down, own0, own1, own2, got0, got1, got2, piece0, piece1, piece2,
     load_sem, core_send, core_recv, up_send, up_recv, down_send, down_recv,
     own_sem, q_send, q_recv, p_send, p_recv, o_send, o_recv,
@@ -913,7 +926,8 @@
     loads = [
         pltpu.make_async_copy(src, dst, load_sem.at[k])
         for k, (src, dst) in enumerate([
-            (got_ref, got_v), (zx_ref.at[:, :, wide : wide + BLOCK], pre_v), (dzx_ref, dz_v), (w_ref, w_v), (normed_ref, normed_v)
+            (got_ref, got_v), (zx_ref.at[:, :, wide : wide + BLOCK], pre_v), (dzx_ref, dz_v), (w_ref, w_v), (normed_ref, normed_v),
+            (scale_ref.at[place], rate_v),
         ])
     ]
     for load in loads:
@@ -1066,13 +1080,17 @@
 
     loads[4].wait()
     small_at = heads + share
-    used = small_at + small_ref.shape[0]
+    chans = dchan_ref.shape[1]
+    more_rows = jnp.concatenate([dhead_ref[0:1], dhead_ref[1:2], jnp.zeros((1, chans - 2 * BLOCK), f32)], axis=1)
+    small = jnp.concatenate([dchan_ref[: SUB - 1], more_rows], axis=0)
+    small = jnp.concatenate([small[:, i : i + own] for i in range(0, chans, own)], axis=0)
+    used = small_at + small.shape[0]
     par_rows = jnp.concatenate([dpar, jnp.zeros((BLOCK - share, BLOCK), f32)], axis=0).T[:SUB]
     par_rows = jnp.concatenate([par_rows, jnp.zeros((SUB, own - BLOCK), f32)], axis=1)
     grads = mm(third_t[...], normed_v[...].reshape(times, normed_v.shape[2]))
     tail = [jnp.zeros((third_g.shape[0] - used - SUB, third_g.shape[1]), f32)] if third_g.shape[0] > used + SUB else []
     third_g[...] = jnp.concatenate(
-        [grads[:small_at], small_ref[...], jnp.concatenate([par_rows] * peers, axis=1), *tail], axis=0
+        [grads[:small_at], jnp.concatenate([small] * peers, axis=1), jnp.concatenate([par_rows] * peers, axis=1), *tail], axis=0
     ).astype(bf16)
     begin(2)
 
@@ -1096,6 +1114,15 @@
                 add_into(part_of(mine.at[chip], i), [part_of(buffer, i)], own // PARTS)
 
     rows_ref[...] = mine[chip]
+    loads[5].wait()
+    for lane in range(block_rows // BLOCK):
+        @pl.loop(0, BLOCK // ROWS_AT_ONCE)
+        def _(i):
+            at = pl.ds(pl.multiple_of(lane * BLOCK + i * ROWS_AT_ONCE, ROWS_AT_ONCE), ROWS_AT_ONCE)
+            row = lax.broadcasted_iota(jnp.int32, (ROWS_AT_ONCE, 1), 0) + i * ROWS_AT_ONCE
+            mask = (row < valid_ref[0, lane]).astype(f32)
+            branch = branch_ref[at, :].astype(f32) + above_ref[at, :].astype(f32) + below_ref[at, :].astype(f32)
+            output_ref[at, :] = (x_ref[at, :].astype(f32) + mask * rate_v[at, 0:1] * branch).astype(bf16)
 
     for step in range(1, chips):
         for by in (1, -1):
@@ -1112,7 +1139,9 @@
             copy.wait()
 
 
-def scattered_out(got, zx, dzx, weights, normed, wide, par, starts, small, heads):
+def scattered_out(
+    valid, got, zx, dzx, weights, normed, wide, scale, par, starts, dchan, dhead, x_rows, branch, above, below, heads
+):
     peers, widths = lax.axis_size("seq"), lax.axis_size("width")
     chips = peers // 2
     dma = pltpu.SemaphoreType.DMA
@@ -1120,40 +1149,42 @@
     vmem = pl.BlockSpec(memory_space=pltpu.VMEM)
     own, model = normed.shape[0] // peers, normed.shape[1]
     half = wide.shape[3] // 2
-    strips = -(-(heads + got.shape[1] + small.shape[0] + SUB) // (16 * widths)) * 16 * widths
+    small_rows = SUB * dchan.shape[1] // own
+    strips = -(-(heads + got.shape[1] + small_rows + SUB) // (16 * widths)) * 16 * widths
     pieces = [(peers, wide.shape[2], half), (peers, wide.shape[2], half), (peers, strips // widths, own)]
     kept = pieces[:2] + [(strips // widths, model)]
     block = (own, model)
-    zx, dzx, normed = [a.reshape(peers, own, a.shape[1]) for a in (zx, dzx, normed)]
+    zx, dzx, normed, scale = [a.reshape(peers, own, a.shape[1]) for a in (zx, dzx, normed, scale)]
     return pl.pallas_call(
         partial(scatter_kernel, peers=peers, widths=widths, heads=heads),
-        in_specs=[anywhere] * 6 + [vmem] * 3,
-        out_specs=[vmem, anywhere, anywhere],
+        in_specs=[pl.BlockSpec(memory_space=pltpu.SMEM)] + [anywhere] * 7 + [vmem] * 8,
+        out_specs=[vmem, vmem, anywhere, anywhere],
         out_shape=[
-            jax.ShapeDtypeStruct(block, bf16), jax.ShapeDtypeStruct(wide.shape, bf16),
+            jax.ShapeDtypeStruct(block, bf16), jax.ShapeDtypeStruct(block, bf16), jax.ShapeDtypeStruct(wide.shape, bf16),
             jax.ShapeDtypeStruct((peers, widths, strips // widths, own), bf16),
         ],
         scratch_shapes=[
             pltpu.VMEM(got.shape, bf16), pltpu.VMEM((peers, own, BLOCK), f32), pltpu.VMEM(dzx.shape, bf16),
             pltpu.VMEM(weights.shape, bf16), pltpu.VMEM(normed.shape, bf16),
             pltpu.VMEM((BLOCK, peers * own), bf16), pltpu.VMEM((strips, model), bf16), pltpu.VMEM((2 * N, BLOCK), f32),
+            pltpu.VMEM((own, BLOCK), f32),
             *[pltpu.VMEM((chips,) + block, bf16)] * 3, *[pltpu.VMEM((chips - 1,) + block, bf16)] * 2,
             *[pltpu.VMEM(a, bf16) for a in kept],
             *[pltpu.VMEM((widths - 1,) + a, bf16) for a in kept],
             *[pltpu.VMEM(a, bf16) for a in pieces],
-            dma((5,)), dma((chips,)), dma((chips,)),
+            dma((6,)), dma((chips,)), dma((chips,)),
             *[dma((chips - 1, PARTS))] * 4,
             dma((3, 3)), dma((3, widths - 1)), dma((3, widths - 1)), dma((3, peers - 1)), dma((3, peers - 1)),
             dma((3, widths - 1)), dma((3, widths - 1)),
         ],
         compiler_params=pltpu.CompilerParams(collective_id=2, has_side_effects=True, vmem_limit_bytes=62 << 20),
         name="scatter_out",
-    )(got, zx, dzx, weights, normed, wide, par, starts, small)
+    )(valid, got, zx, dzx, weights, normed, wide, scale, par, starts, dchan, dhead, x_rows, branch, above, below)
 
 
 def laid_kernel(
-    in_ref, third_ref, w_ref, bc_ref, dt_ref, gain_ref, rows_ref, x_ref, cot_ref, norm_gain_ref,
-    out_ref, out_bc_ref, out_dt_ref, norm_ref, out_rows_ref, rest,
+    in_ref, third_ref, w_ref, bc_ref, dt_ref, rows_ref, x_ref, cot_ref, norm_gain_ref,
+    out_ref, out_bc_ref, out_dt_ref, norm_ref, out_rows_ref, sums,
     *, heads, share,
 ):
     peers, rows, wide = in_ref.shape[0], in_ref.shape[2], in_ref.shape[3]
@@ -1165,12 +1196,12 @@
         third = [
             jnp.concatenate([third_ref[s, q].astype(f32) for q in range(third_ref.shape[1])], axis=0) for s in range(peers)
         ]
-        dt = jnp.concatenate([t[:heads] for t in third], axis=0).T
-        bc = jnp.concatenate([t[heads : heads + share] for t in third], axis=0).T
-        out_bc_ref[...] = bc
+        dt = jnp.concatenate([t[:heads] for t in third], axis=0)
+        bc = jnp.concatenate([t[heads : heads + share] for t in third], axis=0)
         out_dt_ref[...] = dt
-        total = jnp.sum(bc * bc_ref[...].astype(f32), axis=1, keepdims=True)
-        rest[...] = total + jnp.sum(dt * dt_ref[...].astype(f32), axis=1, keepdims=True)
+        out_bc_ref[...] = bc.T
+        norm_ref[...] = jnp.sum(dt * dt_ref[...].astype(f32), axis=0, keepdims=True)
+        norm_ref[...] += jnp.sum(bc * bc_ref[...].astype(f32).T, axis=0, keepdims=True)
 
     lane = jnp.zeros((rows, BLOCK), f32)
     for s in range(peers):
@@ -1187,11 +1218,17 @@
     pulled = rows_ref[...].astype(f32) * norm_gain_ref[...]
     inner = jnp.mean(pulled * unit, axis=-1, keepdims=True)
     out_rows_ref[...] = cot_ref[...].astype(f32) + rate * (pulled - unit * inner)
-    more = rest[pl.ds(pl.multiple_of(step * rows, SUB), rows), :]
-    norm_ref[...] = (jnp.sum(lane, axis=1, keepdims=True) + more) / gain_ref[...]
-
-
-def laid_out(wide, third, w_zx, w_bc, w_dt, gain, normed_grad, x_rows, cotangent, norm_gain, heads):
+    sums[pl.ds(pl.multiple_of(step * rows, SUB), rows), :] = lane
+
+    @pl.when(step == pl.num_programs(0) - 1)
+    def _():
+        own = sums.shape[0]
+        gain = norm_gain_ref[:, pl.ds(pl.multiple_of(lax.axis_index("seq") * own, BLOCK), own)]
+        by_row = [jnp.sum(sums[i : i + BLOCK, :].T, axis=0, keepdims=True) for i in range(0, own, BLOCK)]
+        norm_ref[...] = (norm_ref[...] + jnp.concatenate(by_row, axis=1)) / gain
+
+
+def laid_out(wide, third, w_zx, w_bc, w_dt, normed_grad, x_rows, cotangent, norm_gain, heads):
     peers, widths, quarter, cols = wide.shape
     rows = widths * quarter
     cut = quarter
@@ -1199,20 +1236,21 @@
     by_rows = lambda a: pl.BlockSpec((cut, a.shape[1]), lambda i: (i, 0))
     whole = lambda a: pl.BlockSpec(a.shape, lambda i: (0,) * len(a.shape))
     by_piece = pl.BlockSpec((peers, 1, cut, cols), lambda i: (0, i, 0, 0))
-    shapes = [jax.ShapeDtypeStruct(a.shape, f32) for a in (w_zx, w_bc, w_dt, gain, x_rows)]
+    norm = jax.ShapeDtypeStruct((1, rows), f32)
+    shapes = [jax.ShapeDtypeStruct(a.shape, f32) for a in (w_zx, w_bc, w_dt, norm, x_rows)]
     return pl.pallas_call(
         partial(laid_kernel, heads=heads, share=share),
         grid=(widths,),
         in_specs=[
-            by_piece, whole(third), by_rows(w_zx), whole(w_bc), whole(w_dt), by_rows(gain),
+            by_piece, whole(third), by_rows(w_zx), whole(w_bc), whole(w_dt),
             by_rows(normed_grad), by_rows(x_rows), by_rows(cotangent), whole(norm_gain),
         ],
-        out_specs=[by_rows(w_zx), whole(w_bc), whole(w_dt), by_rows(gain), by_rows(x_rows)],
+        out_specs=[by_rows(w_zx), whole(w_bc), whole(w_dt), whole(norm), by_rows(x_rows)],
         out_shape=shapes,
-        scratch_shapes=[pltpu.VMEM((rows, 1), f32)],
+        scratch_shapes=[pltpu.VMEM((rows, BLOCK), f32)],
         compiler_params=pltpu.CompilerParams(vmem_limit_bytes=62 << 20),
         name="lay_out",
-    )(wide, third, w_zx, w_bc, w_dt, gain, normed_grad, x_rows, cotangent, norm_gain)
+    )(wide, third, w_zx, w_bc, w_dt, normed_grad, x_rows, cotangent, norm_gain)
 
 
 def crossed(value, axis, mask):
@@ -1221,13 +1259,6 @@
 
 def pick(value, index):
     return lax.dynamic_index_in_dim(value, index, 0, False)
-
-
-def quarters_sent(value):
-    widths, width = lax.axis_size("width"), lax.axis_index("width")
-    value = value.reshape((widths, value.shape[0] // widths) + value.shape[1:])
-    sent = [crossed(pick(value, jnp.bitwise_xor(width, m)), "width", m) for m in range(1, widths)]
-    return [pick(value, width)] + sent
 
 
 def quarters_back(total):
@@ -1256,20 +1287,20 @@
     first = place * heads
     share = 2 * N // peers
     used = heads + share
-    row_mask = (jnp.arange(BLOCK)[None, :] < valid[0][:, None]).astype(f32).reshape(-1, 1)
     spread = jnp.asarray(np.arange(chans)[None, :] // HEAD_DIM == np.arange(BLOCK)[:, None], bf16)
     weights, normed, bgrad, starts_all, chan, head, bc_par, *computed = front(
-        valid, starts, tokens, cotangent, norm_gain[None], w_bc, w_dt, conv_w.T, conv_b[None], dt_bias[None], a_log[None],
+        valid, starts, tokens, cotangent, norm_gain[None], w_bc, w_dt.T, conv_w.T, conv_b[None], dt_bias[None], a_log[None],
         d_skip[None], gate_gain[None], spread, w_zx, w_out,
     )
     normed, bgrad = normed.reshape(rows, model), bgrad.reshape(rows, model)
     zx, mix, mixed_grad, scale = [a.reshape(rows, a.shape[-1]) for a in computed[:4]]
-    out_part, up, down, branch = computed[4:8]
-    conv, bc, steps = [a.reshape(rows, a.shape[-1]) for a in computed[8:11]]
-    state, tail = computed[11:]
+    out_parts = computed[4:8]
+    up, down, branch = computed[8:11]
+    conv, bc, steps = [a.reshape(rows, a.shape[-1]) for a in computed[11:14]]
+    state, tail = computed[14:]
     above = lax.ppermute(up, "seq", [(i, i + 2) for i in range(peers - 2)])
     below = lax.ppermute(down, "seq", [(i + 2, i) for i in range(peers - 2)])
-    out_quarters = quarters_sent(out_part.reshape(chans, model))
+    out_quarters = [out_parts[0]] + [crossed(out_parts[m], "width", m) for m in range(1, widths)]
     dzx, dbc, dchan, dhead = run_backward(
         starts_all, zx, mixed_grad, chan, head, spread, conv, mix, bc, steps, state, tail, scale, lanes, heads
     )
@@ -1277,42 +1308,31 @@
     out_pieces = quarters_back(sum(q.astype(f32) for q in out_quarters).astype(bf16))
 
     got = lax.all_to_all(dbc.reshape(peers, share, rows), "seq", 0, 0, tiled=True)
-
-    at_heads = lambda a: lax.dynamic_update_slice_in_dim(jnp.zeros((H,), f32), a, first, 0)
-    at_chans = lambda a: lax.dynamic_update_slice_in_dim(jnp.zeros((E,), f32), a, first * HEAD_DIM, 0)
-    skip = jnp.sum(dchan[SKIP].reshape(heads, HEAD_DIM), axis=1)
-    small = [jnp.pad(at_chans(dchan[k]), (0, 2 * N)) for k in range(KCONV + 1)]
-    small += [at_chans(dchan[GAIN]), at_heads(dhead[0, :heads]), at_heads(dhead[1, :heads]), at_heads(skip)]
-    sizes = [a.shape[0] // peers for a in small]
-    small = jnp.concatenate([a.reshape(peers, -1) for a in small], axis=1)
-    small_rows = -(-small.shape[1] // (own * SUB)) * SUB
-    small = jnp.pad(small, ((0, 0), (0, own * small_rows - small.shape[1])))
-    small = small.reshape(peers, small_rows, own).transpose(1, 0, 2).reshape(small_rows, model)
 
     wide = mm(normed, dzx[:, : 2 * chans], TN).astype(bf16)
     wide, out_pieces = lax.optimization_barrier((wide, out_pieces))
     out_grad = quarters_joined(out_pieces)
-    branch = branch.astype(f32) + above.astype(f32) + below.astype(f32)
-    own_rate = lax.dynamic_slice(scale, (place * own, 0), (own, 1))
-    output = (tokens.astype(f32) + row_mask * own_rate * branch).astype(bf16)
-    got, output, out_grad = lax.optimization_barrier((got, output, out_grad))
-    normed_grad, wide, third = scattered_out(
-        got, zx, dzx, weights, normed, wide.reshape(peers, widths, own // widths, -1), bc_par, starts_all, small, heads,
-    )
-    gain_rows = lax.dynamic_slice_in_dim(norm_gain, place * own, own, 0)[:, None]
+    got, out_grad = lax.optimization_barrier((got, out_grad))
+    output, normed_grad, wide, third = scattered_out(
+        valid, got, zx, dzx, weights, normed, wide.reshape(peers, widths, own // widths, -1), scale, bc_par, starts_all, dchan,
+        dhead, tokens, branch, above, below, heads,
+    )
     grad_zx, grad_bc, grad_dt, grad_norm, input_grad = laid_out(
-        wide, third, w_zx, w_bc, w_dt, gain_rows, normed_grad, tokens, cotangent, norm_gain[None], heads
-    )
-    grad_norm = grad_norm[:, 0]
-    third = third.reshape(peers, -1, own)
-    summed = jnp.sum(third[:, used : used + small_rows].astype(f32), axis=0).reshape(-1)
-    pieces = [summed[sum(sizes[:i]) : sum(sizes[: i + 1])] for i in range(len(sizes))]
-    of_bc = third[:, used + small_rows : used + small_rows + KCONV + 1, :share].astype(f32).transpose(1, 0, 2).reshape(KCONV + 1, 2 * N)
-    own_chans = sizes[0]
-    of_bc = lax.dynamic_slice_in_dim(jnp.pad(of_bc, ((0, 0), (E, 0))), place * own_chans, own_chans, 1)
-    grad_taps = jnp.stack(pieces[:KCONV], axis=1) + of_bc[:KCONV].T
-    grad_bias, grad_gain, grad_dtb, grad_alog, grad_skip = pieces[KCONV:]
-    grad_bias = grad_bias + of_bc[KCONV]
+        wide, third, w_zx, w_bc, w_dt.T, normed_grad, tokens, cotangent, norm_gain[None], heads
+    )
+    grad_dt = grad_dt.T
+    grad_norm = grad_norm[0]
+    third = third.reshape(peers, -1, own).astype(f32)
+    small_rows = SUB * chans // own
+    small = third[:, used : used + small_rows].reshape(peers, chans // own, SUB, own).transpose(2, 0, 1, 3).reshape(SUB, peers, chans)
+    of_bc = third[:, used + small_rows : used + small_rows + KCONV + 1, :share].transpose(1, 0, 2).reshape(KCONV + 1, 2 * N)
+    of_conv = jnp.concatenate([small[: KCONV + 1].reshape(KCONV + 1, E), of_bc], axis=1)
+    mine = lambda a, axis: lax.dynamic_slice_in_dim(a, place * (a.shape[axis] // peers), a.shape[axis] // peers, axis)
+    of_conv = mine(of_conv, 1)
+    grad_taps, grad_bias = of_conv[:KCONV].T, of_conv[BIAS]
+    kept = pick(small.transpose(1, 0, 2), place)
+    grad_gain, grad_skip = kept[GAIN], jnp.sum(kept[SKIP].reshape(heads, HEAD_DIM), axis=1)
+    grad_dtb, grad_alog = kept[SUB - 1, :heads], kept[SUB - 1, BLOCK : BLOCK + heads]
     return (
         output, input_grad, grad_norm, grad_zx, grad_bc, grad_dt, grad_taps, grad_bias, grad_dtb, grad_alog, grad_skip,
         grad_gain, out_grad,

time: 426 us -> 414 us (0.972)
  local copies, waits for them, and re-layouts: 18.9 us -> 6.3 us
  other arithmetic: 13 us -> 7.32 us
    unnamed x30 -> x8, local copies, waits for them, and re-layouts: 7.9 us -> 1.94 us
  transfers between devices with their start and end apart: 9 -> 9, of which waited for: 1 -> 2; matrix products, arithmetic and copies ran while one was open for 7% -> 5% of each run, Pallas kernels for 8% -> 9%
where the time goes in v8:
time: 414 us; the launch traced here: 406 us
  Pallas kernels  355 us (86%)
  starting transfers between devices  17.3 us (4%)
  matrix products  14 us (3%)
  other arithmetic  7.32 us (2%)
  local copies, waits for them, and re-layouts  6.3 us (2%)
  waiting for transfers between devices  4.46 us (1%)
    pallas_call x1, Pallas kernels, front(): pl.pallas_call(partial(front_kernel, peers=peers, widths=widths, lanes=la...  201 us
    pallas_call x1, Pallas kernels, scattered_out(): pl.pallas_call(partial(scatter_kernel, peers=peers, widths=widths, heads=...  110 us
    pallas_call x1, Pallas kernels, run_backward(): pl.pallas_call(partial(backward_kernel, lanes=lanes, heads=heads), grid=(...  34.8 us
    dot_general x1, matrix products, mm(): lax.dot_general(left, right, (dims, ((), ())), precision=precision, prefe...  14 us
    pallas_call x1, Pallas kernels, laid_out(): pl.pallas_call(partial(laid_kernel, heads=heads, share=share), grid=(widt...  9.78 us
  transfers between devices with their start and end apart: 9, of which 2 were waited for; matrix products, arithmetic and copies ran while one was open for 5% of the time, Pallas kernels for 9%

profile of v8, /device:TPU:9, one launch (start us, length us, event | category | flops | bytes accessed | tf_op | source)
XLA Modules:
  0.0 406.0 jit_solution(17963705521780549616)
XLA Ops:
  0.6 1.3 broadcast_in_dim.20.bias_ref
  2.0 200.8 %front.1 = (bf16[8,4,64,1408]{3,2,1,0:T(8,128)(2,1)}, bf16[8,256,2048]{2,1,0:T(8,128)(2,1)}, bf16[8,256,2048]{2,1,0:T(8,128)(2,1)}, f32[8,8,128]{2,1,0:T(8,128)}...) custom-call(s32[1,2]{1,0:T(1,128)} %valid_ref.3, ...), custom_call_target="tpu_custom_call" | custom-call | tf_op jit(solution)/shard_map/front/pallas_call | solution.py:847
  202.8 0.4 collective-permute-start
  203.3 1.2 collective-permute-start.1
  204.5 1.0 collective-permute-start.2
  205.6 1.9 collective-permute-start.6
  207.5 4.3 %collective-permute-start.7 = (bf16[256,2048]{1,0:T(8,128)(2,1)}, bf16[256,2048]{1,0:T(8,128)(2,1)}, u32[]{:S(2)}, u32[]{:S(2)}) collective-permute-start(bf16[256,2048]{1,0:T(8,128)(2,1)} %get-tuple-element.98), channel_id=1, source_target_pairs={{2,0},{3,1},{4,2},{5,3},{6,4},{7,5},{10,8},{11,9},{12,10},{13,11},... | collective-permute-start | bytes 3145736 | tf_op jit(solution)/shard_map/ppermute | solution.py:1302
  211.9 34.8 %mix_backward.1 = (bf16[2048,1152]{1,0:T(8,128)(2,1)}, bf16[256,2048]{1,0:T(8,128)(2,1)}, f32[8,512]{1,0:T(8,128)}, f32[8,128]{1,0:T(8,128)}) custom-call(f32[8,8,128]{2,1,0:T(8,128)} %get-tuple-element.61.start_ref, f32[2048,1408]{1,0:T(8,128)} %bitcast.50, f32[2048,512]{1,0:T(8,128)} %bitcast.54, f32[8,512]{1,0:T(8,128)} %get-tuple-element.64.chan_ref, ...), custom_call_target="tpu_custom_call" | custom-call | flops 6442450944 | bytes 41943040 | tf_op jit(solution)/shard_map/mix_backward/pallas_call | solution.py:277
  246.7 1.4 add_convert_fusion
  248.1 0.4 collective-permute-start.3
  248.5 1.3 collective-permute-start.4
  249.8 1.0 collective-permute-start.5
  250.8 5.7 %all-to-all-start = ((bf16[8,32,2048]{2,1,0:T(8,128)(2,1)}), bf16[8,32,2048]{2,1,0:T(8,128)(2,1)S(1)}, u32[]{:S(2)}, u32[]{:S(2)}) async-start(bf16[8,32,2048]{2,1,0:T(8,128)(2,1)} %bitcast.61), calls=%async_computation | async-start | bytes 2097152 | tf_op jit(solution)/shard_map/all_to_all | solution.py:1310
  256.5 14.0 %fusion.2 = bf16[2048,1024]{1,0:T(8,128)(2,1)} fusion(bf16[2048,2048]{1,0:T(8,128)(2,1)} %bitcast.51, bf16[2048,1152]{1,0:T(8,128)(2,1)} %get-tuple-element.81), kind=kOutput, calls=%fused_computation.2 | convolution fusion | flops 8592031744 | bytes 16777216 | tf_op jit(solution)/shard_map/dot_general | solution.py:30
  270.5 1.0 collective-permute-done.5
  271.5 1.3 pad_maximum_fusion
  272.8 0.2 constant_dynamic-slice_fusion.4
  273.1 0.3 pad_maximum_fusion.1
  273.3 2.7 bitcast_convert_fusion
  276.0 3.5 all-to-all-done.got_ref
  279.5 1.0 copy-done
  280.4 109.8 %scatter_out.1 = (bf16[256,2048]{1,0:T(8,128)(2,1)}, bf16[256,2048]{1,0:T(8,128)(2,1)}, bf16[8,4,64,1024]{3,2,1,0:T(8,128)(2,1)}, bf16[8,4,16,256]{3,2,1,0:T(8,128)(2,1)}) custom-call(s32[1,2]{1,0:T(1,128)} %valid_ref.3, bf16[8,32,2048]{2,1,0:T(8,128)(2,1)} %copy-done, f32[8,256,1408]{2,1,0:T(8,128)} %get-tuple-element.62.zx_ref, ...), custom_call_target="tpu_custom_call" | custom-call | tf_op jit(solution)/shard_map/scatter_out/pallas_call | solution.py:1158
  390.2 1.0 bitcast_convert_fusion.1
  391.5 0.1 fusion.5
  391.6 0.6 slice_bitcast_fusion.2
  392.2 0.6 slice_reduce_fusion
  392.8 0.1 reshape.99
  393.0 0.6 fusion.6
  393.6 0.5 slice_bitcast_fusion.3
  394.2 9.8 %lay_out.1 = (f32[256,8192]{1,0:T(8,128)}, f32[256,256]{1,0:T(8,128)}, f32[64,256]{1,0:T(8,128)}, f32[1,256]{1,0:T(1,128)}, f32[256,2048]{1,0:T(8,128)}) custom-call(bf16[8,4,64,1024]{3,2,1,0:T(8,128)(2,1)} %get-tuple-element.100.in_ref, bf16[8,4,16,256]{3,2,1,0:T(8,128)(2,1)} %get-tuple-element.101.third_ref, bf16[256,8192]{1,0:T(8,128)(2,1)} %w_ref.1, ...), custom_call_target="tpu_custom_call" | custom-call | tf_op jit(solution)/shard_map/lay_out/pallas_call | solution.py:1241
  403.9 0.6 reduce_sum.9
  404.6 1.0 copy.39
  (22 shorter events, 0.4 us)
Async XLA Ops:
  202.8 43.8 %collective-permute-start = (bf16[128,2048]{1,0:T(8,128)(2,1)}, bf16[128,2048]{1,0:T(8,128)(2,1)S(1)}, u32[]{:S(2)}, u32[]{:S(2)}) collective-permute-start(bf16[128,2048]{1,0:T(8,128)(2,1)} %get-tuple-element.76), channel_id=1, source_target_pairs={{0,8},{8,0},{16,24},{24,16},{1,9},{9,1},{17,25},{25,17},{2,10},{10... | collective-permute-start | bytes 1572872 | tf_op jit(solution)/shard_map/ppermute | solution.py:1257
  203.3 43.4 %collective-permute-start.1 = (bf16[128,2048]{1,0:T(8,128)(2,1)}, bf16[128,2048]{1,0:T(8,128)(2,1)S(1)}, u32[]{:S(2)}, u32[]{:S(2)}) collective-permute-start(bf16[128,2048]{1,0:T(8,128)(2,1)} %get-tuple-element.77), channel_id=1, source_target_pairs={{0,16},{8,24},{16,0},{24,8},{1,17},{9,25},{17,1},{25,9},{2,18},{10... | collective-permute-start | bytes 1572872 | tf_op jit(solution)/shard_map/ppermute | solution.py:1257
  204.5 42.2 %collective-permute-start.2 = (bf16[128,2048]{1,0:T(8,128)(2,1)}, bf16[128,2048]{1,0:T(8,128)(2,1)}, u32[]{:S(2)}, u32[]{:S(2)}) collective-permute-start(bf16[128,2048]{1,0:T(8,128)(2,1)} %get-tuple-element.78), channel_id=1, source_target_pairs={{0,24},{8,16},{16,8},{24,0},{1,25},{9,17},{17,9},{25,1},{2,26},{10... | collective-permute-start | bytes 1572872 | tf_op jit(solution)/shard_map/ppermute | solution.py:1257
  205.6 73.9 %collective-permute-start.6 = (bf16[256,2048]{1,0:T(8,128)(2,1)}, bf16[256,2048]{1,0:T(8,128)(2,1)}, u32[]{:S(2)}, u32[]{:S(2)}) collective-permute-start(bf16[256,2048]{1,0:T(8,128)(2,1)} %get-tuple-element.97), channel_id=1, source_target_pairs={{0,2},{1,3},{2,4},{3,5},{4,6},{5,7},{8,10},{9,11},{10,12},{11,13},... | collective-permute-start | bytes 3145736 | tf_op jit(solution)/shard_map/ppermute | solution.py:1301
  207.5 72.0 %collective-permute-start.7 = (bf16[256,2048]{1,0:T(8,128)(2,1)}, bf16[256,2048]{1,0:T(8,128)(2,1)}, u32[]{:S(2)}, u32[]{:S(2)}) collective-permute-start(bf16[256,2048]{1,0:T(8,128)(2,1)} %get-tuple-element.98), channel_id=1, source_target_pairs={{2,0},{3,1},{4,2},{5,3},{6,4},{7,5},{10,8},{11,9},{12,10},{13,11},... | collective-permute-start | bytes 3145736 | tf_op jit(solution)/shard_map/ppermute | solution.py:1302
  211.8 34.9 %copy-start.2 = (bf16[128,2048]{1,0:T(8,128)(2,1)S(1)}, bf16[128,2048]{1,0:T(8,128)(2,1)}, u32[]{:S(2)}) copy-start(bf16[128,2048]{1,0:T(8,128)(2,1)} %get-tuple-element.82) | copy-start | bytes 1572868
  248.1 22.4 %collective-permute-start.3 = (bf16[128,2048]{1,0:T(8,128)(2,1)S(1)}, bf16[128,2048]{1,0:T(8,128)(2,1)S(1)}, u32[]{:S(2)}, u32[]{:S(2)}) collective-permute-start(bf16[128,2048]{1,0:T(8,128)(2,1)S(1)} %add_convert_fusion), channel_id=1, source_target_pairs={{0,8},{8,0},{16,24},{24,16},{1,9},{9,1},{17,25},{25,17},{2,10},{10... | collective-permute-start | bytes 1572872 | tf_op jit(solution)/shard_map/ppermute | solution.py:1257
  248.5 22.0 %collective-permute-start.4 = (bf16[128,2048]{1,0:T(8,128)(2,1)S(1)}, bf16[128,2048]{1,0:T(8,128)(2,1)S(1)}, u32[]{:S(2)}, u32[]{:S(2)}) collective-permute-start(bf16[128,2048]{1,0:T(8,128)(2,1)S(1)} %add_convert_fusion), channel_id=1, source_target_pairs={{0,16},{8,24},{16,0},{24,8},{1,17},{9,25},{17,1},{25,9},{2,18},{10... | collective-permute-start | bytes 1572872 | tf_op jit(solution)/shard_map/ppermute | solution.py:1257
  249.8 21.7 %collective-permute-start.5 = (bf16[128,2048]{1,0:T(8,128)(2,1)S(1)}, bf16[128,2048]{1,0:T(8,128)(2,1)}, u32[]{:S(2)}, u32[]{:S(2)}) collective-permute-start(bf16[128,2048]{1,0:T(8,128)(2,1)S(1)} %add_convert_fusion), channel_id=1, source_target_pairs={{0,24},{8,16},{16,8},{24,0},{1,25},{9,17},{17,9},{25,1},{2,26},{10... | collective-permute-start | bytes 1572872 | tf_op jit(solution)/shard_map/ppermute | solution.py:1257
  250.8 28.6 %all-to-all-start = ((bf16[8,32,2048]{2,1,0:T(8,128)(2,1)}), bf16[8,32,2048]{2,1,0:T(8,128)(2,1)S(1)}, u32[]{:S(2)}, u32[]{:S(2)}) async-start(bf16[8,32,2048]{2,1,0:T(8,128)(2,1)} %bitcast.61), calls=%async_computation | async-start | bytes 2097152 | tf_op jit(solution)/shard_map/all_to_all | solution.py:1310
  279.5 1.0 copy-start
  394.2 10.4 %copy-start.1 = (bf16[256,2048]{1,0:T(8,128)(2,1)S(1)}, bf16[256,2048]{1,0:T(8,128)(2,1)}, u32[]{:S(2)}) copy-start(bf16[256,2048]{1,0:T(8,128)(2,1)} %get-tuple-element.132) | copy-start | bytes 3145732

commit v9 on v8

--- a/solution.py
+++ b/solution.py
@@ -52,7 +52,7 @@
 
 
 def sigmoid(v):
-    return 1.0 / (1.0 + jnp.exp(-v))
+    return 0.5 + 0.5 * jnp.tanh(0.5 * v)
 
 
 def grids():
@@ -235,10 +235,10 @@
         db = db + mm(di_high, c_low, TN) + mm(di_low, c_low, TN)
         dbc_ref[:N, rows] = db.T.astype(bf16)
         dbc_ref[N:, rows] = dc.T.astype(bf16)
-        dweighted = mm(b_low, sg_high) + mm(b_low, sg_low)
+        dweighted = mm(b_low, sg_high)
         dx = dx_within + dweighted * end_x
         dcum = mm_left(dlow_f * (mixed - skip * x_f) - x_f * dx, spread, NT)
-        dend = mm_left(dweighted * x_f, spread, NT)
+        dend = mm((dweighted * x_f).astype(bf16), spread, NT)
         touch = jnp.broadcast_to(total(sgrad * state_in), (SUB, width))
         dlast = total(dend * to_last * dt) + jnp.exp(last) * mm_left(touch, spread, NT)[0:1]
         dlog = mm(triu, dcum, precision=highest) + dlast
@@ -249,7 +249,7 @@
         dzx_ref[rows, 2 * width :] = draw.astype(bf16)
         dhead_ref[0:1, :] += total(draw)
         dhead_ref[1:2, :] += total(dlog * neg_a * dt)
-        state_grad[lane] = keep * (mm(c_low, dc_high, TN) + mm(c_low, dc_low, TN) + last_x * sgrad)
+        state_grad[lane] = keep * (mm(c_low, dc_high, TN) + last_x * sgrad)
 
         dx = dx + skip * dmixed
         dconv = dx * chan_ref[MASK : MASK + 1, :] * (act * (1.0 + conv * (1.0 - act)))
@@ -938,9 +938,12 @@
     lanes_of = lambda s: pl.ds(pl.multiple_of(s * own, BLOCK), own)
     strip_of = lambda w: pl.ds(pl.multiple_of(w * strip, 16), strip)
     sets = [
-        (lambda w: wide_ref.at[:, w, :, 0:half], own0, got0, lambda s: own0.at[s], piece0, lambda w: out_ref.at[:, w, :, 0:half]),
-        (lambda w: wide_ref.at[:, w, :, half:wide], own1, got1, lambda s: own1.at[s], piece1, lambda w: out_ref.at[:, w, :, half:wide]),
-        (lambda w: third_g.at[strip_of(w)], own2, got2, lambda s: own2.at[:, lanes_of(s)], piece2, lambda w: out_third_ref.at[:, w]),
+        (lambda w: wide_ref.at[:, w, :, 0:half], own0, got0, lambda s: own0.at[s], piece0,
+         lambda w, at: out_ref.at[at, w, :, 0:half]),
+        (lambda w: wide_ref.at[:, w, :, half:wide], own1, got1, lambda s: own1.at[s], piece1,
+         lambda w, at: out_ref.at[at, w, :, half:wide]),
+        (lambda w: third_g.at[strip_of(w)], own2, got2, lambda s: own2.at[:, lanes_of(s)], piece2,
+         lambda w, at: out_third_ref.at[at, w]),
     ]
     own_in, to_width = [None] * 3, [None] * 3
 
@@ -1015,15 +1018,29 @@
         for copy in to_owner[k] + [kept_piece[k]]:
             copy.start()
 
+    everything, relays = pl.ds(0, peers), [None] * 3
+    over_x, over_y = jnp.bitwise_xor(width, 1), jnp.bitwise_xor(width, 2)
+
     def spread(k):
         piece, out = sets[k][4:]
         for copy in to_owner[k]:
             copy.wait_recv()
         kept_piece[k].wait()
-        to_all[k] = [remote(piece, out(width), o_send.at[k, m], o_recv.at[k, m], (w, place)) for m, w in enumerate(cross)]
-        to_all[k].append(pltpu.make_async_copy(piece, out(width), own_sem.at[2, k]))
+        to_all[k] = [
+            remote(piece, out(width, everything), o_send.at[k, i], o_recv.at[k, i], (w, place)) for i, w in enumerate((over_x, over_y))
+        ]
+        to_all[k].append(pltpu.make_async_copy(piece, out(width, everything), own_sem.at[2, k]))
         for copy in to_all[k]:
             copy.start()
+
+    def relay(k):
+        out = sets[k][5]
+        relays[k] = []
+        for i, (origin, target) in enumerate(((over_x, over_y), (over_y, over_x))):
+            to_all[k][i].wait_recv()
+            rows = out(origin, pl.ds(i * peers // 2, peers // 2))
+            relays[k].append(remote(rows, rows, o_send.at[k, 2 + i], o_recv.at[k, 2 + i], (target, place)))
+            relays[k][i].start()
 
     for load in loads[:3]:
         load.wait()
@@ -1102,8 +1119,11 @@
     exchange(2)
     for step in range(3, chips):
         run_hops(step)
+    relay(0)
     spread(1)
     spread(2)
+    relay(1)
+    relay(2)
 
     for by in (1, -1):
         @pl.when(later(by))
@@ -1133,9 +1153,10 @@
     for q in range(chips):
         over(q).wait_send()
     for k in range(len(sets)):
-        for copy in to_width[k] + to_owner[k]:
+        for copy in to_width[k] + to_owner[k] + to_all[k][:2]:
             copy.wait_send()
-        for copy in to_all[k]:
+        to_all[k][2].wait()
+        for copy in relays[k]:
             copy.wait()
 
 
@@ -1175,7 +1196,7 @@
             dma((6,)), dma((chips,)), dma((chips,)),
             *[dma((chips - 1, PARTS))] * 4,
             dma((3, 3)), dma((3, widths - 1)), dma((3, widths - 1)), dma((3, peers - 1)), dma((3, peers - 1)),
-            dma((3, widths - 1)), dma((3, widths - 1)),
+            dma((3, widths)), dma((3, widths)),
         ],
         compiler_params=pltpu.CompilerParams(collective_id=2, has_side_effects=True, vmem_limit_bytes=62 << 20),
         name="scatter_out",
@@ -1736,5 +1757,5 @@
         P("seq"),
         P("seq", None),
     )
-    body = heads_body if H % (2 * mesh.shape["seq"]) == 0 else rows_body
+    body = heads_body if mesh.shape["width"] == 4 and H % (2 * mesh.shape["seq"]) == 0 else rows_body
     return jax.shard_map(body, mesh=mesh, in_specs=in_specs, out_specs=out_specs, check_vma=False)

time: 414 us -> 409 us (0.988)
  transfers between devices with their start and end apart: 9 -> 9, of which waited for: 2 -> 2; matrix products, arithmetic and copies ran while one was open for 5% -> 5% of each run, Pallas kernels for 9% -> 8%
where the time goes in v9:
time: 409 us; the launch traced here: 401 us
  Pallas kernels  351 us (86%)
  starting transfers between devices  17.1 us (4%)
  matrix products  14 us (3%)
  other arithmetic  7.32 us (2%)
  local copies, waits for them, and re-layouts  6.3 us (2%)
  waiting for transfers between devices  4.5 us (1%)
    pallas_call x1, Pallas kernels, front(): pl.pallas_call(partial(front_kernel, peers=peers, widths=widths, lanes=la...  201 us
    pallas_call x1, Pallas kernels, scattered_out(): pl.pallas_call(partial(scatter_kernel, peers=peers, widths=widths, heads=...  107 us
    pallas_call x1, Pallas kernels, run_backward(): pl.pallas_call(partial(backward_kernel, lanes=lanes, heads=heads), grid=(...  33.7 us
    dot_general x1, matrix products, mm(): lax.dot_general(left, right, (dims, ((), ())), precision=precision, prefe...  14 us
    pallas_call x1, Pallas kernels, laid_out(): pl.pallas_call(partial(laid_kernel, heads=heads, share=share), grid=(widt...  9.78 us
  transfers between devices with their start and end apart: 9, of which 2 were waited for; matrix products, arithmetic and copies ran while one was open for 5% of the time, Pallas kernels for 8%

profile of v9, /device:TPU:9, one launch (start us, length us, event | category | flops | bytes accessed | tf_op | source)
XLA Modules:
  0.0 401.1 jit_solution(17117627888656853124)
XLA Ops:
  0.6 1.3 broadcast_in_dim.20.bias_ref
  2.0 200.5 %front.1 = (bf16[8,4,64,1408]{3,2,1,0:T(8,128)(2,1)}, bf16[8,256,2048]{2,1,0:T(8,128)(2,1)}, bf16[8,256,2048]{2,1,0:T(8,128)(2,1)}, f32[8,8,128]{2,1,0:T(8,128)}...) custom-call(s32[1,2]{1,0:T(1,128)} %valid_ref.3, ...), custom_call_target="tpu_custom_call" | custom-call | tf_op jit(solution)/shard_map/front/pallas_call | solution.py:847
  202.5 0.4 collective-permute-start
  203.0 1.2 collective-permute-start.1
  204.2 1.0 collective-permute-start.2
  205.2 1.9 collective-permute-start.6
  207.2 4.3 %collective-permute-start.7 = (bf16[256,2048]{1,0:T(8,128)(2,1)}, bf16[256,2048]{1,0:T(8,128)(2,1)}, u32[]{:S(2)}, u32[]{:S(2)}) collective-permute-start(bf16[256,2048]{1,0:T(8,128)(2,1)} %get-tuple-element.98), channel_id=1, source_target_pairs={{2,0},{3,1},{4,2},{5,3},{6,4},{7,5},{10,8},{11,9},{12,10},{13,11},... | collective-permute-start | bytes 3145736 | tf_op jit(solution)/shard_map/ppermute | solution.py:1323
  211.5 33.7 %mix_backward.1 = (bf16[2048,1152]{1,0:T(8,128)(2,1)}, bf16[256,2048]{1,0:T(8,128)(2,1)}, f32[8,512]{1,0:T(8,128)}, f32[8,128]{1,0:T(8,128)}) custom-call(f32[8,8,128]{2,1,0:T(8,128)} %get-tuple-element.61.start_ref, f32[2048,1408]{1,0:T(8,128)} %bitcast.50, f32[2048,512]{1,0:T(8,128)} %bitcast.54, f32[8,512]{1,0:T(8,128)} %get-tuple-element.64.chan_ref, ...), custom_call_target="tpu_custom_call" | custom-call | flops 6442450944 | bytes 41943040 | tf_op jit(solution)/shard_map/mix_backward/pallas_call | solution.py:277
  245.3 1.4 add_convert_fusion
  246.7 0.4 collective-permute-start.3
  247.1 1.2 collective-permute-start.4
  248.4 1.0 collective-permute-start.5
  249.4 5.4 %all-to-all-start = ((bf16[8,32,2048]{2,1,0:T(8,128)(2,1)}), bf16[8,32,2048]{2,1,0:T(8,128)(2,1)S(1)}, u32[]{:S(2)}, u32[]{:S(2)}) async-start(bf16[8,32,2048]{2,1,0:T(8,128)(2,1)} %bitcast.61), calls=%async_computation | async-start | bytes 2097152 | tf_op jit(solution)/shard_map/all_to_all | solution.py:1331
  254.8 14.0 %fusion.2 = bf16[2048,1024]{1,0:T(8,128)(2,1)} fusion(bf16[2048,2048]{1,0:T(8,128)(2,1)} %bitcast.51, bf16[2048,1152]{1,0:T(8,128)(2,1)} %get-tuple-element.81), kind=kOutput, calls=%fused_computation.2 | convolution fusion | flops 8592031744 | bytes 16777216 | tf_op jit(solution)/shard_map/dot_general | solution.py:30
  268.9 1.3 collective-permute-done.5
  270.1 1.3 pad_maximum_fusion
  271.4 0.2 constant_dynamic-slice_fusion.4
  271.7 0.3 pad_maximum_fusion.1
  272.0 2.7 bitcast_convert_fusion
  274.6 3.2 all-to-all-done.got_ref
  277.9 1.0 copy-done
  278.8 106.6 %scatter_out.1 = (bf16[256,2048]{1,0:T(8,128)(2,1)}, bf16[256,2048]{1,0:T(8,128)(2,1)}, bf16[8,4,64,1024]{3,2,1,0:T(8,128)(2,1)}, bf16[8,4,16,256]{3,2,1,0:T(8,128)(2,1)}) custom-call(s32[1,2]{1,0:T(1,128)} %valid_ref.3, bf16[8,32,2048]{2,1,0:T(8,128)(2,1)} %copy-done, f32[8,256,1408]{2,1,0:T(8,128)} %get-tuple-element.62.zx_ref, ...), custom_call_target="tpu_custom_call" | custom-call | tf_op jit(solution)/shard_map/scatter_out/pallas_call | solution.py:1179
  385.4 1.0 bitcast_convert_fusion.1
  386.7 0.1 fusion.5
  386.8 0.6 slice_bitcast_fusion.2
  387.4 0.6 slice_reduce_fusion
  388.0 0.1 reshape.99
  388.1 0.6 fusion.6
  388.8 0.5 slice_bitcast_fusion.3
  389.3 9.8 %lay_out.1 = (f32[256,8192]{1,0:T(8,128)}, f32[256,256]{1,0:T(8,128)}, f32[64,256]{1,0:T(8,128)}, f32[1,256]{1,0:T(1,128)}, f32[256,2048]{1,0:T(8,128)}) custom-call(bf16[8,4,64,1024]{3,2,1,0:T(8,128)(2,1)} %get-tuple-element.100.in_ref, bf16[8,4,16,256]{3,2,1,0:T(8,128)(2,1)} %get-tuple-element.101.third_ref, bf16[256,8192]{1,0:T(8,128)(2,1)} %w_ref.1, ...), custom_call_target="tpu_custom_call" | custom-call | tf_op jit(solution)/shard_map/lay_out/pallas_call | solution.py:1262
  399.1 0.6 reduce_sum.9
  399.7 1.0 copy.39
  (22 shorter events, 0.4 us)
Async XLA Ops:
  202.5 42.8 %collective-permute-start = (bf16[128,2048]{1,0:T(8,128)(2,1)}, bf16[128,2048]{1,0:T(8,128)(2,1)S(1)}, u32[]{:S(2)}, u32[]{:S(2)}) collective-permute-start(bf16[128,2048]{1,0:T(8,128)(2,1)} %get-tuple-element.76), channel_id=1, source_target_pairs={{0,8},{8,0},{16,24},{24,16},{1,9},{9,1},{17,25},{25,17},{2,10},{10... | collective-permute-start | bytes 1572872 | tf_op jit(solution)/shard_map/ppermute | solution.py:1278
  203.0 42.3 %collective-permute-start.1 = (bf16[128,2048]{1,0:T(8,128)(2,1)}, bf16[128,2048]{1,0:T(8,128)(2,1)S(1)}, u32[]{:S(2)}, u32[]{:S(2)}) collective-permute-start(bf16[128,2048]{1,0:T(8,128)(2,1)} %get-tuple-element.77), channel_id=1, source_target_pairs={{0,16},{8,24},{16,0},{24,8},{1,17},{9,25},{17,1},{25,9},{2,18},{10... | collective-permute-start | bytes 1572872 | tf_op jit(solution)/shard_map/ppermute | solution.py:1278
  204.2 41.1 %collective-permute-start.2 = (bf16[128,2048]{1,0:T(8,128)(2,1)}, bf16[128,2048]{1,0:T(8,128)(2,1)}, u32[]{:S(2)}, u32[]{:S(2)}) collective-permute-start(bf16[128,2048]{1,0:T(8,128)(2,1)} %get-tuple-element.78), channel_id=1, source_target_pairs={{0,24},{8,16},{16,8},{24,0},{1,25},{9,17},{17,9},{25,1},{2,26},{10... | collective-permute-start | bytes 1572872 | tf_op jit(solution)/shard_map/ppermute | solution.py:1278
  205.2 72.6 %collective-permute-start.6 = (bf16[256,2048]{1,0:T(8,128)(2,1)}, bf16[256,2048]{1,0:T(8,128)(2,1)}, u32[]{:S(2)}, u32[]{:S(2)}) collective-permute-start(bf16[256,2048]{1,0:T(8,128)(2,1)} %get-tuple-element.97), channel_id=1, source_target_pairs={{0,2},{1,3},{2,4},{3,5},{4,6},{5,7},{8,10},{9,11},{10,12},{11,13},... | collective-permute-start | bytes 3145736 | tf_op jit(solution)/shard_map/ppermute | solution.py:1322
  207.2 70.7 %collective-permute-start.7 = (bf16[256,2048]{1,0:T(8,128)(2,1)}, bf16[256,2048]{1,0:T(8,128)(2,1)}, u32[]{:S(2)}, u32[]{:S(2)}) collective-permute-start(bf16[256,2048]{1,0:T(8,128)(2,1)} %get-tuple-element.98), channel_id=1, source_target_pairs={{2,0},{3,1},{4,2},{5,3},{6,4},{7,5},{10,8},{11,9},{12,10},{13,11},... | collective-permute-start | bytes 3145736 | tf_op jit(solution)/shard_map/ppermute | solution.py:1323
  211.5 33.8 %copy-start.2 = (bf16[128,2048]{1,0:T(8,128)(2,1)S(1)}, bf16[128,2048]{1,0:T(8,128)(2,1)}, u32[]{:S(2)}) copy-start(bf16[128,2048]{1,0:T(8,128)(2,1)} %get-tuple-element.82) | copy-start | bytes 1572868
  246.7 22.1 %collective-permute-start.3 = (bf16[128,2048]{1,0:T(8,128)(2,1)S(1)}, bf16[128,2048]{1,0:T(8,128)(2,1)S(1)}, u32[]{:S(2)}, u32[]{:S(2)}) collective-permute-start(bf16[128,2048]{1,0:T(8,128)(2,1)S(1)} %add_convert_fusion), channel_id=1, source_target_pairs={{0,8},{8,0},{16,24},{24,16},{1,9},{9,1},{17,25},{25,17},{2,10},{10... | collective-permute-start | bytes 1572872 | tf_op jit(solution)/shard_map/ppermute | solution.py:1278
  247.1 21.7 %collective-permute-start.4 = (bf16[128,2048]{1,0:T(8,128)(2,1)S(1)}, bf16[128,2048]{1,0:T(8,128)(2,1)S(1)}, u32[]{:S(2)}, u32[]{:S(2)}) collective-permute-start(bf16[128,2048]{1,0:T(8,128)(2,1)S(1)} %add_convert_fusion), channel_id=1, source_target_pairs={{0,16},{8,24},{16,0},{24,8},{1,17},{9,25},{17,1},{25,9},{2,18},{10... | collective-permute-start | bytes 1572872 | tf_op jit(solution)/shard_map/ppermute | solution.py:1278
  248.4 21.7 %collective-permute-start.5 = (bf16[128,2048]{1,0:T(8,128)(2,1)S(1)}, bf16[128,2048]{1,0:T(8,128)(2,1)}, u32[]{:S(2)}, u32[]{:S(2)}) collective-permute-start(bf16[128,2048]{1,0:T(8,128)(2,1)S(1)} %add_convert_fusion), channel_id=1, source_target_pairs={{0,24},{8,16},{16,8},{24,0},{1,25},{9,17},{17,9},{25,1},{2,26},{10... | collective-permute-start | bytes 1572872 | tf_op jit(solution)/shard_map/ppermute | solution.py:1278
  249.4 28.4 %all-to-all-start = ((bf16[8,32,2048]{2,1,0:T(8,128)(2,1)}), bf16[8,32,2048]{2,1,0:T(8,128)(2,1)S(1)}, u32[]{:S(2)}, u32[]{:S(2)}) async-start(bf16[8,32,2048]{2,1,0:T(8,128)(2,1)} %bitcast.61), calls=%async_computation | async-start | bytes 2097152 | tf_op jit(solution)/shard_map/all_to_all | solution.py:1331
  277.9 1.0 copy-start
  389.3 10.4 %copy-start.1 = (bf16[256,2048]{1,0:T(8,128)(2,1)S(1)}, bf16[256,2048]{1,0:T(8,128)(2,1)}, u32[]{:S(2)}) copy-start(bf16[256,2048]{1,0:T(8,128)(2,1)} %get-tuple-element.132) | copy-start | bytes 3145732

commit v10 on v9

--- a/solution.py
+++ b/solution.py
@@ -223,15 +223,14 @@
 
         state_in = state_ref[0, lane]
         sgrad = state_grad[lane]
-        in_high, in_low = split2(state_in)
-        sg_high, sg_low = split2(sgrad)
+        in_high, sg_high = state_in.astype(bf16), sgrad.astype(bf16)
         dcarry = dlow_f * carry_x
-        dc_high, dc_low = split2(dcarry)
+        dc_high = dcarry.astype(bf16)
         di_high, di_low = split2(dinner)
-        dc = mm(dc_high, in_high, NT) + mm(dc_high, in_low, NT) + mm(dc_low, in_high, NT)
+        dc = mm(dc_high, in_high, NT)
         dc = dc + mm(di_high, b_low) + mm(di_low, b_low)
         weighted = (x_f * end_x).astype(bf16)
-        db = mm(weighted, sg_high, NT) + mm(weighted, sg_low, NT)
+        db = mm(weighted, sg_high, NT)
         db = db + mm(di_high, c_low, TN) + mm(di_low, c_low, TN)
         dbc_ref[:N, rows] = db.T.astype(bf16)
         dbc_ref[N:, rows] = dc.T.astype(bf16)
@@ -506,11 +505,14 @@
     head_lane = lax.broadcasted_iota(jnp.int32, (SUB, BLOCK), 1)
     head_ref[...] = jnp.where((sub == HEAD_MASK) & (head_lane + first >= active), 0.0, per_head)
     on_chans = mm(head_ref[...], spread.astype(f32), precision=highest)
+    bias_rows = bias_ref[pl.ds(place * (chans // BLOCK), chans // BLOCK), :]
+    bias_here = jnp.concatenate([bias_rows[i : i + 1] for i in range(chans // BLOCK)], axis=1)
+    bias_bc = jnp.concatenate([bias_ref[i : i + 1, :] for i in range(E // BLOCK, (E + 2 * N) // BLOCK)], axis=1)
     chan_ref[...] = jnp.concatenate(
-        [taps_ref[:, here], bias_ref[:, here], on_chans[3:4], gain_ref[:, here], on_chans[HEAD_MASK : HEAD_MASK + 1]], axis=0
+        [taps_ref[:, here], bias_here, on_chans[3:4], gain_ref[:, here], on_chans[HEAD_MASK : HEAD_MASK + 1]], axis=0
     )
     bc_par[...] = jnp.concatenate(
-        [taps_ref[:, E:], bias_ref[:, E:], jnp.zeros((SUB - KCONV - 1, 2 * N), f32)], axis=0
+        [taps_ref[:, E:], bias_bc, jnp.zeros((SUB - KCONV - 1, 2 * N), f32)], axis=0
     )
 
     for push in pushes:
@@ -614,8 +616,8 @@
     def grad_out(s, slot):
         return pltpu.make_async_copy(mgrad_v.at[slot], out_grad.at[s], grad_sem.at[slot])
 
-    def mix_grads(q, first):
-        for slot in range(2):
+    def mix_grads(q, first, begun=False):
+        for slot in (1 - core,) if begun else range(2):
             load_grad(2 * q + slot, slot).start()
         for slot in range(2):
             s = 2 * q + slot
@@ -718,11 +720,11 @@
                     for copy in grads.mate(by, step):
                         copy.wait_recv()
 
-    def at_distance(step):
+    def at_distance(step, begun=False):
         for by in (1, -1):
             @pl.when(grads.reached(by, step))
             def _():
-                mix_grads(grads.source(by, step) // 2, False)
+                mix_grads(grads.source(by, step) // 2, False, begun)
 
     @pl.loop(0, chips)
     def _(i):
@@ -758,8 +760,12 @@
         mates_here(step)
         at_distance(step)
     grads.pass_on(chips - 1)
+    for by in (1, -1):
+        @pl.when(grads.reached(by, chips - 1))
+        def _():
+            load_grad(grads.source(by, chips - 1), core).start()
     mates_here(chips - 1)
-    at_distance(chips - 1)
+    at_distance(chips - 1, True)
     crosses = give(1)
     bgrad_v[...] = wout_grad[...].astype(bf16).reshape(bgrad_v.shape)
     wout_rows = chans // widths
@@ -1310,7 +1316,7 @@
     used = heads + share
     spread = jnp.asarray(np.arange(chans)[None, :] // HEAD_DIM == np.arange(BLOCK)[:, None], bf16)
     weights, normed, bgrad, starts_all, chan, head, bc_par, *computed = front(
-        valid, starts, tokens, cotangent, norm_gain[None], w_bc, w_dt.T, conv_w.T, conv_b[None], dt_bias[None], a_log[None],
+        valid, starts, tokens, cotangent, norm_gain[None], w_bc, w_dt.T, conv_w.T, conv_b.reshape(-1, BLOCK), dt_bias[None], a_log[None],
         d_skip[None], gate_gain[None], spread, w_zx, w_out,
     )
     normed, bgrad = normed.reshape(rows, model), bgrad.reshape(rows, model)

time: 409 us -> 407 us (level)
  no operation moved by 1% of the time
where the time goes in v10:
time: 407 us; the launch traced here: 400 us
  Pallas kernels  350 us (86%)
  starting transfers between devices  17.3 us (4%)
  matrix products  14 us (3%)
  other arithmetic  7.32 us (2%)
  local copies, waits for them, and re-layouts  4.95 us (1%)
  waiting for transfers between devices  4.46 us (1%)
    pallas_call x1, Pallas kernels, front(): pl.pallas_call(partial(front_kernel, peers=peers, widths=widths, lanes=la...  201 us
    pallas_call x1, Pallas kernels, scattered_out(): pl.pallas_call(partial(scatter_kernel, peers=peers, widths=widths, heads=...  107 us
    pallas_call x1, Pallas kernels, run_backward(): pl.pallas_call(partial(backward_kernel, lanes=lanes, heads=heads), grid=(...  33.1 us
    dot_general x1, matrix products, mm(): lax.dot_general(left, right, (dims, ((), ())), precision=precision, prefe...  14 us
    pallas_call x1, Pallas kernels, laid_out(): pl.pallas_call(partial(laid_kernel, heads=heads, share=share), grid=(widt...  9.78 us
  transfers between devices with their start and end apart: 9, of which 2 were waited for; matrix products, arithmetic and copies ran while one was open for 5% of the time, Pallas kernels for 8%

profile of v10, /device:TPU:9, one launch (start us, length us, event | category | flops | bytes accessed | tf_op | source)
XLA Modules:
  0.0 399.6 jit_solution(13427078855361049949)
XLA Ops:
  0.6 200.8 %front.1 = (bf16[8,4,64,1408]{3,2,1,0:T(8,128)(2,1)}, bf16[8,256,2048]{2,1,0:T(8,128)(2,1)}, bf16[8,256,2048]{2,1,0:T(8,128)(2,1)}, f32[8,8,128]{2,1,0:T(8,128)}...) custom-call(s32[1,2]{1,0:T(1,128)} %valid_ref.3, ...), custom_call_target="tpu_custom_call" | custom-call | tf_op jit(solution)/shard_map/front/pallas_call | solution.py:853
  201.4 0.4 collective-permute-start
  201.8 1.2 collective-permute-start.1
  203.1 1.0 collective-permute-start.2
  204.1 1.9 collective-permute-start.6
  206.0 4.3 %collective-permute-start.7 = (bf16[256,2048]{1,0:T(8,128)(2,1)}, bf16[256,2048]{1,0:T(8,128)(2,1)}, u32[]{:S(2)}, u32[]{:S(2)}) collective-permute-start(bf16[256,2048]{1,0:T(8,128)(2,1)} %get-tuple-element.98), channel_id=1, source_target_pairs={{2,0},{3,1},{4,2},{5,3},{6,4},{7,5},{10,8},{11,9},{12,10},{13,11},... | collective-permute-start | bytes 3145736 | tf_op jit(solution)/shard_map/ppermute | solution.py:1329
  210.4 33.1 %mix_backward.1 = (bf16[2048,1152]{1,0:T(8,128)(2,1)}, bf16[256,2048]{1,0:T(8,128)(2,1)}, f32[8,512]{1,0:T(8,128)}, f32[8,128]{1,0:T(8,128)}) custom-call(f32[8,8,128]{2,1,0:T(8,128)} %get-tuple-element.61.start_ref, f32[2048,1408]{1,0:T(8,128)} %bitcast.51, f32[2048,512]{1,0:T(8,128)} %bitcast.55, f32[8,512]{1,0:T(8,128)} %get-tuple-element.64.chan_ref, ...), custom_call_target="tpu_custom_call" | custom-call | flops 6442450944 | bytes 41943040 | tf_op jit(solution)/shard_map/mix_backward/pallas_call | solution.py:276
  243.6 1.4 add_convert_fusion
  245.0 0.4 collective-permute-start.3
  245.4 1.2 collective-permute-start.4
  246.7 1.0 collective-permute-start.5
  247.7 5.7 %all-to-all-start = ((bf16[8,32,2048]{2,1,0:T(8,128)(2,1)}), bf16[8,32,2048]{2,1,0:T(8,128)(2,1)S(1)}, u32[]{:S(2)}, u32[]{:S(2)}) async-start(bf16[8,32,2048]{2,1,0:T(8,128)(2,1)} %bitcast.62), calls=%async_computation | async-start | bytes 2097152 | tf_op jit(solution)/shard_map/all_to_all | solution.py:1337
  253.4 14.0 %fusion.2 = bf16[2048,1024]{1,0:T(8,128)(2,1)} fusion(bf16[2048,2048]{1,0:T(8,128)(2,1)} %bitcast.52, bf16[2048,1152]{1,0:T(8,128)(2,1)} %get-tuple-element.81), kind=kOutput, calls=%fused_computation.2 | convolution fusion | flops 8592031744 | bytes 16777216 | tf_op jit(solution)/shard_map/dot_general | solution.py:30
  267.4 1.0 collective-permute-done.5
  268.4 1.3 pad_maximum_fusion
  269.7 0.2 constant_dynamic-slice_fusion.4
  270.0 0.3 pad_maximum_fusion.1
  270.3 2.7 bitcast_convert_fusion
  272.9 3.4 all-to-all-done.got_ref
  276.4 1.0 copy-done
  277.3 106.6 %scatter_out.1 = (bf16[256,2048]{1,0:T(8,128)(2,1)}, bf16[256,2048]{1,0:T(8,128)(2,1)}, bf16[8,4,64,1024]{3,2,1,0:T(8,128)(2,1)}, bf16[8,4,16,256]{3,2,1,0:T(8,128)(2,1)}) custom-call(s32[1,2]{1,0:T(1,128)} %valid_ref.3, bf16[8,32,2048]{2,1,0:T(8,128)(2,1)} %copy-done, f32[8,256,1408]{2,1,0:T(8,128)} %get-tuple-element.62.zx_ref, ...), custom_call_target="tpu_custom_call" | custom-call | tf_op jit(solution)/shard_map/scatter_out/pallas_call | solution.py:1185
  383.9 1.0 bitcast_convert_fusion.1
  385.2 0.1 fusion.5
  385.2 0.6 slice_bitcast_fusion.2
  385.9 0.6 slice_reduce_fusion
  386.5 0.1 reshape.103
  386.6 0.6 fusion.6
  387.2 0.1 reshape_squeeze.3
  387.3 0.5 slice_bitcast_fusion.3
  387.8 9.8 %lay_out.1 = (f32[256,8192]{1,0:T(8,128)}, f32[256,256]{1,0:T(8,128)}, f32[64,256]{1,0:T(8,128)}, f32[1,256]{1,0:T(1,128)}, f32[256,2048]{1,0:T(8,128)}) custom-call(bf16[8,4,64,1024]{3,2,1,0:T(8,128)(2,1)} %get-tuple-element.100.in_ref, bf16[8,4,16,256]{3,2,1,0:T(8,128)(2,1)} %get-tuple-element.101.third_ref, bf16[256,8192]{1,0:T(8,128)(2,1)} %w_ref.1, ...), custom_call_target="tpu_custom_call" | custom-call | tf_op jit(solution)/shard_map/lay_out/pallas_call | solution.py:1268
  397.6 0.6 reduce_sum.9
  398.2 1.0 copy.39
  (21 shorter events, 0.3 us)
Async XLA Ops:
  201.4 42.1 %collective-permute-start = (bf16[128,2048]{1,0:T(8,128)(2,1)}, bf16[128,2048]{1,0:T(8,128)(2,1)S(1)}, u32[]{:S(2)}, u32[]{:S(2)}) collective-permute-start(bf16[128,2048]{1,0:T(8,128)(2,1)} %get-tuple-element.76), channel_id=1, source_target_pairs={{0,8},{8,0},{16,24},{24,16},{1,9},{9,1},{17,25},{25,17},{2,10},{10... | collective-permute-start | bytes 1572872 | tf_op jit(solution)/shard_map/ppermute | solution.py:1284
  201.8 41.7 %collective-permute-start.1 = (bf16[128,2048]{1,0:T(8,128)(2,1)}, bf16[128,2048]{1,0:T(8,128)(2,1)S(1)}, u32[]{:S(2)}, u32[]{:S(2)}) collective-permute-start(bf16[128,2048]{1,0:T(8,128)(2,1)} %get-tuple-element.77), channel_id=1, source_target_pairs={{0,16},{8,24},{16,0},{24,8},{1,17},{9,25},{17,1},{25,9},{2,18},{10... | collective-permute-start | bytes 1572872 | tf_op jit(solution)/shard_map/ppermute | solution.py:1284
  203.1 40.5 %collective-permute-start.2 = (bf16[128,2048]{1,0:T(8,128)(2,1)}, bf16[128,2048]{1,0:T(8,128)(2,1)}, u32[]{:S(2)}, u32[]{:S(2)}) collective-permute-start(bf16[128,2048]{1,0:T(8,128)(2,1)} %get-tuple-element.78), channel_id=1, source_target_pairs={{0,24},{8,16},{16,8},{24,0},{1,25},{9,17},{17,9},{25,1},{2,26},{10... | collective-permute-start | bytes 1572872 | tf_op jit(solution)/shard_map/ppermute | solution.py:1284
  204.1 72.2 %collective-permute-start.6 = (bf16[256,2048]{1,0:T(8,128)(2,1)}, bf16[256,2048]{1,0:T(8,128)(2,1)}, u32[]{:S(2)}, u32[]{:S(2)}) collective-permute-start(bf16[256,2048]{1,0:T(8,128)(2,1)} %get-tuple-element.97), channel_id=1, source_target_pairs={{0,2},{1,3},{2,4},{3,5},{4,6},{5,7},{8,10},{9,11},{10,12},{11,13},... | collective-permute-start | bytes 3145736 | tf_op jit(solution)/shard_map/ppermute | solution.py:1328
  206.0 70.3 %collective-permute-start.7 = (bf16[256,2048]{1,0:T(8,128)(2,1)}, bf16[256,2048]{1,0:T(8,128)(2,1)}, u32[]{:S(2)}, u32[]{:S(2)}) collective-permute-start(bf16[256,2048]{1,0:T(8,128)(2,1)} %get-tuple-element.98), channel_id=1, source_target_pairs={{2,0},{3,1},{4,2},{5,3},{6,4},{7,5},{10,8},{11,9},{12,10},{13,11},... | collective-permute-start | bytes 3145736 | tf_op jit(solution)/shard_map/ppermute | solution.py:1329
  210.4 33.2 %copy-start.2 = (bf16[128,2048]{1,0:T(8,128)(2,1)S(1)}, bf16[128,2048]{1,0:T(8,128)(2,1)}, u32[]{:S(2)}) copy-start(bf16[128,2048]{1,0:T(8,128)(2,1)} %get-tuple-element.82) | copy-start | bytes 1572868
  245.0 22.4 %collective-permute-start.3 = (bf16[128,2048]{1,0:T(8,128)(2,1)S(1)}, bf16[128,2048]{1,0:T(8,128)(2,1)S(1)}, u32[]{:S(2)}, u32[]{:S(2)}) collective-permute-start(bf16[128,2048]{1,0:T(8,128)(2,1)S(1)} %add_convert_fusion), channel_id=1, source_target_pairs={{0,8},{8,0},{16,24},{24,16},{1,9},{9,1},{17,25},{25,17},{2,10},{10... | collective-permute-start | bytes 1572872 | tf_op jit(solution)/shard_map/ppermute | solution.py:1284
  245.4 22.0 %collective-permute-start.4 = (bf16[128,2048]{1,0:T(8,128)(2,1)S(1)}, bf16[128,2048]{1,0:T(8,128)(2,1)S(1)}, u32[]{:S(2)}, u32[]{:S(2)}) collective-permute-start(bf16[128,2048]{1,0:T(8,128)(2,1)S(1)} %add_convert_fusion), channel_id=1, source_target_pairs={{0,16},{8,24},{16,0},{24,8},{1,17},{9,25},{17,1},{25,9},{2,18},{10... | collective-permute-start | bytes 1572872 | tf_op jit(solution)/shard_map/ppermute | solution.py:1284
  246.7 21.8 %collective-permute-start.5 = (bf16[128,2048]{1,0:T(8,128)(2,1)S(1)}, bf16[128,2048]{1,0:T(8,128)(2,1)}, u32[]{:S(2)}, u32[]{:S(2)}) collective-permute-start(bf16[128,2048]{1,0:T(8,128)(2,1)S(1)} %add_convert_fusion), channel_id=1, source_target_pairs={{0,24},{8,16},{16,8},{24,0},{1,25},{9,17},{17,9},{25,1},{2,26},{10... | collective-permute-start | bytes 1572872 | tf_op jit(solution)/shard_map/ppermute | solution.py:1284
  247.7 28.6 %all-to-all-start = ((bf16[8,32,2048]{2,1,0:T(8,128)(2,1)}), bf16[8,32,2048]{2,1,0:T(8,128)(2,1)S(1)}, u32[]{:S(2)}, u32[]{:S(2)}) async-start(bf16[8,32,2048]{2,1,0:T(8,128)(2,1)} %bitcast.62), calls=%async_computation | async-start | bytes 2097152 | tf_op jit(solution)/shard_map/all_to_all | solution.py:1337
  276.3 1.0 copy-start
  387.8 10.4 %copy-start.1 = (bf16[256,2048]{1,0:T(8,128)(2,1)S(1)}, bf16[256,2048]{1,0:T(8,128)(2,1)}, u32[]{:S(2)}) copy-start(bf16[256,2048]{1,0:T(8,128)(2,1)} %get-tuple-element.132) | copy-start | bytes 3145732
